TPU v7x, 32 devices: a whole 2x2x4 slice. The times are simulated.
32 devices in a mesh: tile: 4 (over x, core), lev: 4 (over z), sec: 2 (over y).
Axes of the slice: x: 2, y: 2, z: 4, core: 2. Of those that a mesh axis runs over, the one named last changes fastest.
Arguments:
- forcing: float32 [8, 72, 160, 384], P('sec', 'lev', 'tile'), may hold values from -6 to 6
- courant_x: bfloat16 [72, 160, 384], P('lev', 'tile'), may hold values from -0.44921875 to 0.44921875
- courant_y: bfloat16 [72, 160, 384], P('lev', 'tile'), may hold values from -0.44921875 to 0.44921875
- mass_flux: bfloat16 [72, 160, 384], P('lev', 'tile'), may hold values from 0 to 0.59765625
- limiter_code: int32 [72, 160, 384], P('lev', 'tile'), may hold values from 0 to 15
- seam_code: int32 [4, 2], replicated, may hold values from 0 to 1
- level_weight: float32 [72], P('lev'), may hold values from 0.02 to 0.5
- sector_share: float32 [8, 160, 384], P('sec', 'tile'), may hold values from 0.1 to 1
- flux_cell: int32 [16, 3840], P('tile'), may hold values from 0 to 15359
Outputs:
- adjoint_start: float32 [8, 72, 160, 384], P('sec', 'lev', 'tile')
- flux_sensitivity: float32 [61440], P('tile')
All inputs are finite; a program needn't handle non-finite values.
Results may differ from a plain program's by a relative error of at most 0.0003.
Values sent between devices are 32-bit elements; how exact they have to be, the bound alone decides.
No kernel may reach another device: no remote copies, remote signals or barrier semaphores. Data moves between devices by JAX's collectives and lax.ppermute only.
A program may use at most 128 MiB of HBM per device.

v0:
```python
import jax
import jax.numpy as jnp
from jax import lax
from jax.sharding import PartitionSpec as P

FL_DEV = 15360


def from_behind(value, axis, steps):
    count = lax.axis_size(axis)
    initial, last = (max(0, -steps), min(count, count - steps))
    return lax.ppermute(value, axis, [(source, source + steps) for source in range(initial, last)])


def extended_2(value, sides, width):
    for axis, dim in sides:
        devices, length = (lax.axis_size(axis), value.shape[dim])
        up = [(i, (i + 1) % devices) for i in range(devices)]
        down = [(j, i) for i, j in up]
        last = lax.slice_in_dim(value, length - width, length, axis=dim)
        initial = lax.slice_in_dim(value, 0, width, axis=dim)
        before = lax.ppermute(last, axis, up)
        after = lax.ppermute(initial, axis, down)
        value = jnp.concatenate([before, value, after], axis=dim)
    return value


def coefficients(courant, codes, bit):
    value = courant.astype(jnp.float32)
    limited = jnp.bitwise_and(jnp.right_shift(codes, bit), 1).astype(jnp.float32)
    spread = 0.5 * jnp.abs(value) * (1.0 - jnp.abs(value))
    ahead = jnp.maximum(value, 0.0) - limited * spread
    behind = jnp.minimum(value, 0.0) + limited * spread
    return (ahead, behind)


def flipped(rim, flag):
    return jnp.where(flag, rim[..., ::-1], rim)


def vertical(adjoint, mixing, at_top):
    above = from_behind(adjoint[:, :1], "lev", -1)
    above = jnp.where(at_top, adjoint[:, -1:], above)
    upper = jnp.concatenate([adjoint[:, 1:], above], axis=1)
    return adjoint + mixing * (upper - adjoint)


def sweep_second(adjoint, courant, codes, bit):
    ahead, behind = coefficients(courant, codes, bit)
    following = jnp.concatenate([adjoint[..., 1:], adjoint[..., -1:]], axis=-1)
    previous = jnp.concatenate([adjoint[..., :1], adjoint[..., :-1]], axis=-1)
    return adjoint + ahead * (following - adjoint) + behind * (adjoint - previous)


def sweep_first(adjoint, courant, codes, bit, flip_left, flip_right):
    ahead, behind = coefficients(courant, codes, bit)
    extended = extended_2(adjoint, (("tile", 2),), 1)
    left_rim = flipped(extended[:, :, :1], flip_left)
    right_rim = flipped(extended[:, :, -1:], flip_right)
    following = jnp.concatenate([adjoint[:, :, 1:], right_rim], axis=2)
    previous = jnp.concatenate([left_rim, adjoint[:, :, :-1]], axis=2)
    return adjoint + ahead * (following - adjoint) + behind * (adjoint - previous)


def shards(
    forcing,
    courant_x,
    courant_y,
    mass_flux,
    limiter_code,
    seam_code,
    level_weight,
    sector_share,
    flux_cell,
):
    mixing = mass_flux.astype(jnp.float32)
    at_top = lax.axis_index("lev") == lax.axis_size("lev") - 1
    tile_count = lax.axis_size("tile")
    tile_rank = lax.axis_index("tile")
    place = jnp.remainder(tile_rank + tile_count, tile_count)
    seams_here = lax.dynamic_index_in_dim(seam_code, place, 0, keepdims=False) == 1
    adjoint = forcing
    for turn_index in (1, 0):
        adjoint = vertical(adjoint, mixing, at_top)
        adjoint = sweep_second(adjoint, courant_y, limiter_code, 2 * turn_index + 1)
        adjoint = sweep_first(
            adjoint, courant_x, limiter_code, 2 * turn_index, seams_here[0], seams_here[1]
        )
    partial_value = jnp.einsum(
        "sxy,l,slxy->xy", sector_share, level_weight, adjoint, precision=lax.Precision.HIGHEST
    )
    columns = partial_value.reshape(tile_count, -1)
    totals = lax.psum(columns, ("lev", "sec"))
    received = lax.all_to_all(totals, "tile", split_axis=0, concat_axis=0, tiled=True)
    flux_sensitivity = jax.ops.segment_sum(
        received.reshape(-1), flux_cell.reshape(-1), num_segments=FL_DEV
    )
    return (adjoint, flux_sensitivity)


def solution(mesh):
    placed = (
        P("sec", "lev", "tile", None),
        P("lev", "tile", None),
        P("lev", "tile", None),
        P("lev", "tile", None),
        P("lev", "tile", None),
        P(),
        P("lev"),
        P("sec", "tile", None),
        P("tile", None),
    )
    return jax.shard_map(
        shards,
        mesh=mesh,
        in_specs=placed,
        out_specs=(P("sec", "lev", "tile", None), P("tile")),
        check_vma=False,
    )
```

profile of v0, /device:TPU:0, one launch (start us, length us, event | category | flops | bytes accessed | tf_op | source)
XLA Modules:
  0.0 203.3 jit_solution(576393310717845087)
XLA Ops:
  0.7 1.1 slice.78
  1.8 1.4 collective-permute-start
  3.2 5.8 %fusion.28 = (f32[18,40,384]{2,1,0:T(8,128)}, f32[18,40,384]{2,1,0:T(8,128)}, f32[18,40,384]{2,1,0:T(8,128)}, f32[18,40,384]{2,1,0:T(8,128)}, f32[18,40,384]{2,1...) fusion(bf16[18,40,384]{2,1,0:T(8,128)(2,1)} %param.10, ...), kind=kLoop, calls=%fused_computation.45 | loop fusion | flops 10506240 | bytes 11059200 | tf_op jit(solution)/shard_map/sub | solution.py:32
  9.1 2.3 %slice.76 = f32[4,17,40,384]{3,2,1,0:T(8,128)} slice(f32[4,18,40,384]{3,2,1,0:T(8,128)S(1)} %bitcast.19), slice={[0:4], [1:18], [0:40], [0:384]} | slice | bytes 8355840 | tf_op jit(solution)/shard_map/slice | solution.py:44
  12.0 0.8 collective-permute-done
  12.8 1.0 slice_select_fusion.1
  13.8 4.2 %fusion.3 = f32[4,18,40,384]{3,2,1,0:T(8,128)S(1)} fusion(f32[4,18,40,384]{3,2,1,0:T(8,128)} %param.9, f32[4,1,40,384]{3,2,1,0:T(8,128)S(1)} %slice_select_fusion.1, f32[4,17,40,384]{3,2,1,0:T(8,128)} %slice.76, f32[18,40,384]{2,1,0:T(8,128)S(1)} %convert_element_type.23), kind=kLoop, calls=%fused_computation.5 | loop fusion | flops 4423680 | bytes 14376960 | tf_op jit(solution)/shard_map/add | solution.py:45
  18.0 1.6 fusion.46
  19.5 1.4 fusion.47
  21.0 3.7 %fusion.6 = f32[4,18,40,384]{3,2,1,0:T(8,128)S(1)} fusion(f32[4,18,40,384]{3,2,1,0:T(8,128)S(1)} %fusion.3, f32[4,18,40,1]{3,2,1,0:T(8,128)} %get-tuple-element.17, f32[4,18,40,383]{3,2,1,0:T(8,128)S(1)} %get-tuple-element.19, f32[4,18,40,383]{3,2,1,0:T(8,128)S(1)} %get-tuple-element.18, f32[4,18,40,1]{3,2,1,0:T(8,128)S(1)} %get-tuple-element.16, ...), kind=kLoop, calls=%fused_computation.9 | loop fusion | flops 8847360 | bytes 19906560 | tf_op jit(solution)/shard_map/add | solution.py:52
  24.9 1.7 collective-permute-start.1
  26.6 4.1 %fusion.45 = (f32[4,18,39,384]{3,2,1,0:T(8,128)}, f32[4,18,39,384]{3,2,1,0:T(8,128)}) fusion(f32[4,18,40,384]{3,2,1,0:T(8,128)S(1)} %fusion.6), kind=kLoop, calls=%fused_computation.74 | loop fusion | bytes 17252352 | tf_op jit(solution)/shard_map/slice | solution.py:61
  30.8 0.7 rev.12
  32.6 0.7 broadcast_select_fusion.3
  33.4 0.8 broadcast_select_fusion.1
  34.2 5.9 %fusion.10 = f32[4,18,40,384]{3,2,1,0:T(8,128)S(1)} fusion(f32[4,18,40,384]{3,2,1,0:T(8,128)} %copy-done.2, f32[4,18,1,384]{3,2,1,0:T(1,128)S(1)} %broadcast_select_fusion.3, f32[4,18,39,384]{3,2,1,0:T(8,128)} %get-tuple-element.15, f32[4,18,39,384]{3,2,1,0:T(8,128)} %get-tuple-element.14, f32[4,18,1,384]{3,2,1,0:T(1,128)S(1)} %broadcast_select_fusion.1, ...), kind=kLoop, calls=%fused_computation.15 | loop fusion | flops 8847360 | bytes 19906560 | tf_op jit(solution)/shard_map/add | solution.py:62
  40.1 1.5 collective-permute-start.3
  41.8 9.3 %collective-permute-done.3 = f32[4,1,40,384]{3,2,1,0:T(8,128)S(1)} collective-permute-done((f32[4,1,40,384]{3,2,1,0:T(8,128)S(1)}, f32[4,1,40,384]{3,2,1,0:T(8,128)S(1)}, u32[]{:S(2)}, u32[]{:S(2)}) %collective-permute-start.3) | collective-permute-done | bytes 245792 | tf_op jit(solution)/shard_map/ppermute | solution.py:12
  52.4 1.4 fusion.43
  53.8 3.5 %fusion.16 = f32[4,18,40,384]{3,2,1,0:T(8,128)S(1)} fusion(f32[4,18,40,384]{3,2,1,0:T(8,128)S(1)} %fusion.13, f32[4,18,40,1]{3,2,1,0:T(8,128)S(1)} %get-tuple-element.9, f32[4,18,40,383]{3,2,1,0:T(8,128)S(1)} %get-tuple-element.11, f32[4,18,40,383]{3,2,1,0:T(8,128)S(1)} %get-tuple-element.10, f32[4,18,40,1]{3,2,1,0:T(8,128)S(1)} %get-tuple-element.8, ...), kind=kLoop, calls=%fused_computation.24 | loop fusion | flops 8847360 | bytes 19906560 | tf_op jit(solution)/shard_map/add | solution.py:52
  57.5 1.2 collective-permute-start.4
  58.8 4.1 %fusion.41 = (f32[4,18,39,384]{3,2,1,0:T(8,128)}, f32[4,18,39,384]{3,2,1,0:T(8,128)}) fusion(f32[4,18,40,384]{3,2,1,0:T(8,128)S(1)} %fusion.16), kind=kLoop, calls=%fused_computation.70 | loop fusion | bytes 17252352 | tf_op jit(solution)/shard_map/slice | solution.py:61
  63.8 0.7 rev.15
  64.5 0.7 broadcast_select_fusion.2
  65.2 0.8 broadcast_select_fusion
  66.1 5.7 %fusion.20 = f32[4,18,40,384]{3,2,1,0:T(8,128)S(1)} fusion(f32[4,18,40,384]{3,2,1,0:T(8,128)} %copy-done.1, f32[4,18,1,384]{3,2,1,0:T(1,128)S(1)} %broadcast_select_fusion.2, f32[4,18,39,384]{3,2,1,0:T(8,128)} %get-tuple-element.7, f32[4,18,39,384]{3,2,1,0:T(8,128)} %get-tuple-element.6, f32[4,18,1,384]{3,2,1,0:T(1,128)S(1)} %broadcast_select_fusion, ...), kind=kLoop, calls=%fused_computation.30 | loop fusion | flops 8847360 | bytes 19906560 | tf_op jit(solution)/shard_map/add | solution.py:62
  71.8 2.1 %copy-done.3 = f32[4,18,40,384]{3,2,1,0:T(8,128)} copy-done((f32[4,18,40,384]{3,2,1,0:T(8,128)}, f32[4,18,40,384]{3,2,1,0:T(8,128)S(1)}, u32[]{:S(2)}) %copy-start.3) | copy-done | bytes 4423704
  73.9 4.4 %fusion = f32[1,4,40,384]{3,0,2,1:T(1,128)S(1)} fusion(f32[4,18,40,384]{3,2,1,0:T(8,128)S(1)} %fusion.20, f32[18]{0:T(128)S(1)} %copy-done), kind=kOutput, calls=%fused_computation.1 | convolution fusion | flops 13271040 | bytes 4669512 | tf_op jit(solution)/shard_map/sxy,l,slxy->xy/dot_general | solution.py:89
  78.3 36.6 %psum.7 = f32[4,1,3840]{2,1,0:T(1,128)} all-reduce(f32[4,1,3840]{2,1,0:T(1,128)S(1)} %all_to_all.6), channel_id=1, replica_groups=mesh['tile'=4,'lev'=4,'sec'=2] {'lev','sec'}, use_global_device_ids=true, to_apply=%region_0.1 | all-reduce | flops 15360 | bytes 122880 | tf_op jit(solution)/shard_map/psum | solution.py:93
  114.9 3.3 %all-to-all-start = ((f32[4,1,3840]{2,1,0:T(1,128)}), f32[4,1,3840]{2,1,0:T(1,128)S(1)}, u32[]{:S(2)}, u32[]{:S(2)}) async-start(f32[4,1,3840]{2,1,0:T(1,128)} %psum.7), calls=%async_computation | async-start | bytes 122880 | tf_op jit(solution)/shard_map/all_to_all | solution.py:94
  118.3 4.0 %all-to-all-done = f32[4,1,3840]{2,1,0:T(1,128)S(1)} async-done(((f32[4,1,3840]{2,1,0:T(1,128)}), f32[4,1,3840]{2,1,0:T(1,128)S(1)}, u32[]{:S(2)}, u32[]{:S(2)}) %all-to-all-start) | async-done | bytes 61472 | tf_op jit(solution)/shard_map/all_to_all | solution.py:94
  122.3 81.0 %scatter_custom_fusion = f32[15360]{0:T(1024)} fusion(s32[15360]{0:T(1024)S(1)} %reshape.33, f32[15360]{0:T(1024)S(1)} %bitcast.20, f32[]{:T(128)} %constant.18.clone.1), kind=kCustom, calls=%fused_computation.65 | custom fusion | flops 15360 | bytes 61444 | tf_op jit(solution)/shard_map/scatter-add | solution.py:95
  (55 shorter events, 5.0 us)
Async XLA Ops:
  0.6 73.2 %copy-start = (f32[18]{0:T(128)S(1)}, f32[18]{0:T(128)}, u32[]{:S(2)}) copy-start(f32[18]{0:T(128)} %param.15) | copy-start | bytes 220
  0.6 8.4 %slice-start = ((s8[4423680]{0:T(1024)(128)(4,1)}), s8[4194304]{0:T(1024)(128)(4,1)S(1)}, s32[]{:S(2)}) async-start(s8[4423680]{0:T(1024)(128)(4,1)} %bitcast.18), calls=%async_computation.1 | async-start | bytes 8388608
  1.8 7.3 %slice-start.1 = ((s8[4423680]{0:T(1024)(128)(4,1)}), s8[229376]{0:T(1024)(128)(4,1)S(1)}, s32[]{:S(2)}) async-start(s8[4423680]{0:T(1024)(128)(4,1)} %bitcast.18), calls=%async_computation.2 | async-start | bytes 458752
  1.8 11.0 %collective-permute-start = (f32[4,1,40,384]{3,2,1,0:T(8,128)S(1)}, f32[4,1,40,384]{3,2,1,0:T(8,128)S(1)}, u32[]{:S(2)}, u32[]{:S(2)}) collective-permute-start(f32[4,1,40,384]{3,2,1,0:T(8,128)S(1)} %slice.78), channel_id=1, source_target_pairs={{2,0},{4,2},{6,4},{3,1},{5,3},{7,5},{10,8},{12,10},{14,12},{11,9},... | collective-permute-start | bytes 737288 | tf_op jit(solution)/shard_map/ppermute | solution.py:12
  9.0 2.3 %copy-start.7 = (bf16[18,40,384]{2,1,0:T(8,128)(2,1)S(1)}, bf16[18,40,384]{2,1,0:T(8,128)(2,1)}, u32[]{:S(2)}) copy-start(bf16[18,40,384]{2,1,0:T(8,128)(2,1)} %param.12) | copy-start | bytes 1658884
  9.0 2.4 %copy-start.10 = (s32[4,2]{0,1:T(2,128)S(1)}, s32[4,2]{0,1:T(2,128)}, u32[]{:S(2)}) copy-start(s32[4,2]{0,1:T(2,128)} %param.14) | copy-start | bytes 100
  24.7 6.0 %copy-start.2 = (f32[4,18,40,384]{3,2,1,0:T(8,128)}, f32[4,18,40,384]{3,2,1,0:T(8,128)S(1)}, u32[]{:S(2)}) copy-start(f32[4,18,40,384]{3,2,1,0:T(8,128)S(1)} %fusion.6) | copy-start | bytes 13271044
  24.9 5.8 %collective-permute-start.1 = (f32[4,18,1,384]{3,1,2,0:T(8,128)S(1)}, f32[4,18,1,384]{3,1,2,0:T(8,128)S(1)}, u32[]{:S(2)}, u32[]{:S(2)}) collective-permute-start(f32[4,18,1,384]{3,1,2,0:T(8,128)S(1)} %copy.26), channel_id=1, source_target_pairs={{8,0},{16,8},{24,16},{0,24},{9,1},{17,9},{25,17},{1,25},{10,2},{18... | collective-permute-start | bytes 331784 | tf_op jit(solution)/shard_map/ppermute | solution.py:23
  26.6 7.6 %copy-start.6 = (f32[18,40,384]{2,1,0:T(8,128)S(1)}, f32[18,40,384]{2,1,0:T(8,128)}, u32[]{:S(2)}) copy-start(f32[18,40,384]{2,1,0:T(8,128)} %get-tuple-element.22) | copy-start | bytes 3317764
  26.6 5.2 %collective-permute-start.2 = (f32[4,18,1,384]{3,1,2,0:T(8,128)S(1)}, f32[4,18,1,384]{3,1,2,0:T(8,128)S(1)}, u32[]{:S(2)}, u32[]{:S(2)}) collective-permute-start(f32[4,18,1,384]{3,1,2,0:T(8,128)S(1)} %copy.29), channel_id=1, source_target_pairs={{0,8},{8,16},{16,24},{24,0},{1,9},{9,17},{17,25},{25,1},{2,10},{10... | collective-permute-start | bytes 331784 | tf_op jit(solution)/shard_map/ppermute | solution.py:22
  40.1 11.1 %collective-permute-start.3 = (f32[4,1,40,384]{3,2,1,0:T(8,128)S(1)}, f32[4,1,40,384]{3,2,1,0:T(8,128)S(1)}, u32[]{:S(2)}, u32[]{:S(2)}) collective-permute-start(f32[4,1,40,384]{3,2,1,0:T(8,128)S(1)} %slice.110), channel_id=1, source_target_pairs={{2,0},{4,2},{6,4},{3,1},{5,3},{7,5},{10,8},{12,10},{14,12},{11,9},... | collective-permute-start | bytes 737288 | tf_op jit(solution)/shard_map/ppermute | solution.py:12
  57.3 5.6 %copy-start.1 = (f32[4,18,40,384]{3,2,1,0:T(8,128)}, f32[4,18,40,384]{3,2,1,0:T(8,128)S(1)}, u32[]{:S(2)}) copy-start(f32[4,18,40,384]{3,2,1,0:T(8,128)S(1)} %fusion.16) | copy-start | bytes 13271044
  57.5 5.4 %collective-permute-start.4 = (f32[4,18,1,384]{3,1,2,0:T(8,128)S(1)}, f32[4,18,1,384]{3,1,2,0:T(8,128)S(1)}, u32[]{:S(2)}, u32[]{:S(2)}) collective-permute-start(f32[4,18,1,384]{3,1,2,0:T(8,128)S(1)} %copy.32), channel_id=1, source_target_pairs={{8,0},{16,8},{24,16},{0,24},{9,1},{17,9},{25,17},{1,25},{10,2},{18... | collective-permute-start | bytes 331784 | tf_op jit(solution)/shard_map/ppermute | solution.py:23
  58.7 7.4 %copy-start.4 = (f32[18,40,384]{2,1,0:T(8,128)S(1)}, f32[18,40,384]{2,1,0:T(8,128)}, u32[]{:S(2)}) copy-start(f32[18,40,384]{2,1,0:T(8,128)} %get-tuple-element.20) | copy-start | bytes 3317764
  58.7 7.4 %copy-start.5 = (f32[18,40,384]{2,1,0:T(8,128)S(1)}, f32[18,40,384]{2,1,0:T(8,128)}, u32[]{:S(2)}) copy-start(f32[18,40,384]{2,1,0:T(8,128)} %get-tuple-element.21) | copy-start | bytes 3317764
  58.7 5.0 %collective-permute-start.5 = (f32[4,18,1,384]{3,1,2,0:T(8,128)S(1)}, f32[4,18,1,384]{3,1,2,0:T(8,128)S(1)}, u32[]{:S(2)}, u32[]{:S(2)}) collective-permute-start(f32[4,18,1,384]{3,1,2,0:T(8,128)S(1)} %copy.35), channel_id=1, source_target_pairs={{0,8},{8,16},{16,24},{24,0},{1,9},{9,17},{17,25},{25,1},{2,10},{10... | collective-permute-start | bytes 331784 | tf_op jit(solution)/shard_map/ppermute | solution.py:22
  71.8 2.1 %copy-start.3 = (f32[4,18,40,384]{3,2,1,0:T(8,128)}, f32[4,18,40,384]{3,2,1,0:T(8,128)S(1)}, u32[]{:S(2)}) copy-start(f32[4,18,40,384]{3,2,1,0:T(8,128)S(1)} %fusion.20) | copy-start | bytes 13271044
  73.9 4.4 %copy-start.8 = (f32[4,40,384]{2,1,0:T(8,128)S(1)}, f32[4,40,384]{2,1,0:T(8,128)}, u32[]{:S(2)}) copy-start(f32[4,40,384]{2,1,0:T(8,128)} %param.16) | copy-start | bytes 737284
  73.9 44.4 %copy-start.9 = (s32[4,3840]{1,0:T(4,128)S(1)}, s32[4,3840]{1,0:T(4,128)}, u32[]{:S(2)}) copy-start(s32[4,3840]{1,0:T(4,128)} %param.17) | copy-start | bytes 184324
  114.9 7.4 %all-to-all-start = ((f32[4,1,3840]{2,1,0:T(1,128)}), f32[4,1,3840]{2,1,0:T(1,128)S(1)}, u32[]{:S(2)}, u32[]{:S(2)}) async-start(f32[4,1,3840]{2,1,0:T(1,128)} %psum.7), calls=%async_computation | async-start | bytes 122880 | tf_op jit(solution)/shard_map/all_to_all | solution.py:94
where the time goes:
time: 204 us; the launch traced here: 203 us
  other arithmetic  115 us (56%)
  blocking collectives  36.6 us (18%)
  local copies, waits for them, and re-layouts  23.1 us (11%)
  waiting for transfers between devices  14.4 us (7%)
  starting transfers between devices  9.16 us (4%)
  matrix products  4.36 us (2%)
    scatter-add x1, other arithmetic, shards(): jax.ops.segment_sum(received.reshape(-1), flux_cell.reshape(-1), num_segm...  81 us
    psum x1, blocking collectives, shards(): totals = lax.psum(columns, ('lev', 'sec'))  36.6 us
    add x2, other arithmetic, sweep_first(): adjoint + ahead * (following - adjoint) + behind * (adjoint - previous)  11.6 us
    ppermute x2, waiting for transfers between devices, from_behind(): lax.ppermute(value, axis, [(source, source + steps) for source in range(i...  10.1 us
    slice x2, local copies, waits for them, and re-layouts, sweep_first(): previous = jnp.concatenate([left_rim, adjoint[:, :, :-1]], axis=2)  8.14 us
    add x2, other arithmetic, sweep_second(): adjoint + ahead * (following - adjoint) + behind * (adjoint - previous)  7.2 us
    sub x1, other arithmetic, coefficients(): ahead = jnp.maximum(value, 0.0) - limited * spread  5.8 us
    add x2, other arithmetic, vertical(): return adjoint + mixing * (upper - adjoint)  4.88 us
  transfers between devices with their start and end apart: 7, of which 4 were waited for; matrix products, arithmetic and copies ran while one was open for 9% of the time, Pallas kernels for 0%

commit v1 on v0

--- a/solution.py
+++ b/solution.py
@@ -1,6 +1,8 @@
 import jax
 import jax.numpy as jnp
 from jax import lax
+from jax.experimental import pallas as pl
+from jax.experimental.pallas import tpu as pltpu
 from jax.sharding import PartitionSpec as P
 
 FL_DEV = 15360
@@ -62,6 +64,55 @@
     return adjoint + ahead * (following - adjoint) + behind * (adjoint - previous)
 
 
+def scatter_kernel(cells_ref, values_ref, out_ref):
+    rows, lanes = out_ref.shape
+    count = cells_ref.shape[0]
+    high_iota = lax.broadcasted_iota(jnp.int32, (rows, lanes), 0)
+    low_iota = lax.broadcasted_iota(jnp.int32, (lanes, lanes), 0)
+    total = jnp.zeros((2 * rows, lanes), jnp.float32)
+    for pair in range(0, count, 2):
+        lefts, rights = [], []
+        for row in (pair, pair + 1):
+            cells = cells_ref[row : row + 1, :]
+            value = values_ref[row : row + 1, :]
+            coarse = value.astype(jnp.bfloat16).astype(jnp.float32)
+            fine = value - coarse
+            here = jnp.right_shift(cells, 7) == high_iota
+            lefts.append(
+                jnp.concatenate(
+                    [jnp.where(here, coarse, 0.0), jnp.where(here, fine, 0.0)], axis=0
+                ).astype(jnp.bfloat16)
+            )
+            match = jnp.bitwise_and(cells, 127) == low_iota
+            rights.append(jnp.where(match, 1.0, 0.0).astype(jnp.bfloat16))
+        total += lax.dot_general(
+            jnp.concatenate(lefts, axis=1),
+            jnp.concatenate(rights, axis=1),
+            (((1,), (1,)), ((), ())),
+            preferred_element_type=jnp.float32,
+        )
+    out_ref[...] = total[:rows] + total[rows:]
+
+
+def remapped(partial_value, flux_cell):
+    tiles, share = flux_cell.shape
+    group = lax.axis_size("lev") * lax.axis_size("sec")
+    piece = share // group
+    sent = partial_value.reshape(tiles * group, piece)
+    received = lax.all_to_all(
+        sent, ("tile", "lev", "sec"), split_axis=0, concat_axis=0, tiled=True
+    )
+    summed = jnp.sum(received.reshape(tiles, group, piece), axis=1)
+    gathered = lax.all_gather(summed, ("lev", "sec"))
+    cells = flux_cell.reshape(tiles, group, piece).transpose(1, 0, 2)
+    out = pl.pallas_call(
+        scatter_kernel,
+        out_shape=jax.ShapeDtypeStruct((FL_DEV // 128, 128), jnp.float32),
+        compiler_params=pltpu.CompilerParams(vmem_limit_bytes=48 * 2**20),
+    )(cells.reshape(-1, 128), gathered.reshape(-1, 128))
+    return out.reshape(-1)
+
+
 def shards(
     forcing,
     courant_x,
@@ -89,12 +140,7 @@
     partial_value = jnp.einsum(
         "sxy,l,slxy->xy", sector_share, level_weight, adjoint, precision=lax.Precision.HIGHEST
     )
-    columns = partial_value.reshape(tile_count, -1)
-    totals = lax.psum(columns, ("lev", "sec"))
-    received = lax.all_to_all(totals, "tile", split_axis=0, concat_axis=0, tiled=True)
-    flux_sensitivity = jax.ops.segment_sum(
-        received.reshape(-1), flux_cell.reshape(-1), num_segments=FL_DEV
-    )
+    flux_sensitivity = remapped(partial_value, flux_cell)
     return (adjoint, flux_sensitivity)
 
 

time: 204 us -> 126 us (0.62)
  other arithmetic: 115 us -> 33.7 us
  blocking collectives: 36.6 us -> 30.7 us
  Pallas kernels: 0 us -> 3.25 us
  waiting for transfers between devices: 14.4 us -> 17.4 us
    scatter-add x1 -> x0, other arithmetic: 81 us -> none  [shards(): jax.ops.segment_sum(received.reshape(-1), flux_cell.reshape(-1), num_segm...]
    psum x1 -> x0, blocking collectives: 36.6 us -> none  [shards(): totals = lax.psum(columns, ('lev', 'sec'))]
    all_gather x0 -> x1, blocking collectives: none -> 30.7 us  [remapped(): gathered = lax.all_gather(summed, ('lev', 'sec'))]
    pallas_call x0 -> x1, Pallas kernels: none -> 3.25 us  [remapped(): pl.pallas_call(scatter_kernel, out_shape=jax.ShapeDtypeStruct((FL_DEV //...]
    all_to_all x1, waiting for transfers between devices: 4.02 us -> 6.98 us  [remapped(): lax.all_to_all(sent, ('tile', 'lev', 'sec'), split_axis=0, concat_axis=0,...]
    all_to_all x1, starting transfers between devices: 3.28 us -> 5.35 us  [remapped(): lax.all_to_all(sent, ('tile', 'lev', 'sec'), split_axis=0, concat_axis=0,...]
  transfers between devices with their start and end apart: 7 -> 7, of which waited for: 4 -> 4; matrix products, arithmetic and copies ran while one was open for 9% -> 15% of each run, Pallas kernels for 0% -> 0%
where the time goes in v1:
time: 126 us
  other arithmetic  33.7 us (27%)
  blocking collectives  30.7 us (24%)
  local copies, waits for them, and re-layouts  24.2 us (19%)
  waiting for transfers between devices  17.4 us (14%)
  starting transfers between devices  11.2 us (9%)
  matrix products  4.36 us (3%)
  Pallas kernels  3.25 us (3%)
    all_gather x1, blocking collectives, remapped(): gathered = lax.all_gather(summed, ('lev', 'sec'))  30.7 us
    add x2, other arithmetic, sweep_first(): adjoint + ahead * (following - adjoint) + behind * (adjoint - previous)  11.6 us
    ppermute x2, waiting for transfers between devices, from_behind(): lax.ppermute(value, axis, [(source, source + steps) for source in range(i...  10.1 us
    slice x2, local copies, waits for them, and re-layouts, sweep_first(): previous = jnp.concatenate([left_rim, adjoint[:, :, :-1]], axis=2)  8.18 us
    add x2, other arithmetic, sweep_second(): adjoint + ahead * (following - adjoint) + behind * (adjoint - previous)  7.2 us
    all_to_all x1, waiting for transfers between devices, remapped(): lax.all_to_all(sent, ('tile', 'lev', 'sec'), split_axis=0, concat_axis=0,...  6.98 us
    sub x1, other arithmetic, coefficients(): ahead = jnp.maximum(value, 0.0) - limited * spread  5.77 us
    all_to_all x1, starting transfers between devices, remapped(): lax.all_to_all(sent, ('tile', 'lev', 'sec'), split_axis=0, concat_axis=0,...  5.35 us
  transfers between devices with their start and end apart: 7, of which 4 were waited for; matrix products, arithmetic and copies ran while one was open for 15% of the time, Pallas kernels for 0%

profile of v1, /device:TPU:0, one launch (start us, length us, event | category | flops | bytes accessed | tf_op | source)
XLA Modules:
  0.0 125.9 jit_solution(16337762631974234213)
XLA Ops:
  0.7 1.1 slice.78
  1.8 1.4 %collective-permute-start = (f32[4,1,40,384]{3,2,1,0:T(8,128)S(1)}, f32[4,1,40,384]{3,2,1,0:T(8,128)S(1)}, u32[]{:S(2)}, u32[]{:S(2)}) collective-permute-start(f32[4,1,40,384]{3,2,1,0:T(8,128)S(1)} %slice.78), channel_id=1, source_target_pairs={{2,0},{4,2},{6,4},{3,1},{5,3},{7,5},{10,8},{12,10},{14,12},{11,9},... | collective-permute-start | bytes 737288 | tf_op jit(solution)/shard_map/ppermute | solution.py:14
  3.2 5.8 %fusion.28 = (f32[18,40,384]{2,1,0:T(8,128)}, f32[18,40,384]{2,1,0:T(8,128)}, f32[18,40,384]{2,1,0:T(8,128)}, f32[18,40,384]{2,1,0:T(8,128)}, f32[18,40,384]{2,1...) fusion(bf16[18,40,384]{2,1,0:T(8,128)(2,1)} %param.10, ...), kind=kLoop, calls=%fused_computation.44 | loop fusion | flops 10506240 | bytes 11059200 | tf_op jit(solution)/shard_map/sub | solution.py:34
  9.0 2.3 %slice.76 = f32[4,17,40,384]{3,2,1,0:T(8,128)} slice(f32[4,18,40,384]{3,2,1,0:T(8,128)S(1)} %bitcast.25), slice={[0:4], [1:18], [0:40], [0:384]} | slice | bytes 8355840 | tf_op jit(solution)/shard_map/slice | solution.py:46
  12.0 0.8 collective-permute-done
  12.8 1.0 slice_select_fusion.1
  13.8 4.2 %fusion.3 = f32[4,18,40,384]{3,2,1,0:T(8,128)S(1)} fusion(f32[4,18,40,384]{3,2,1,0:T(8,128)} %param.9, f32[4,1,40,384]{3,2,1,0:T(8,128)S(1)} %slice_select_fusion.1, f32[4,17,40,384]{3,2,1,0:T(8,128)} %slice.76, f32[18,40,384]{2,1,0:T(8,128)S(1)} %convert_element_type.23), kind=kLoop, calls=%fused_computation.4 | loop fusion | flops 4423680 | bytes 14376960 | tf_op jit(solution)/shard_map/add | solution.py:47
  18.0 1.6 %fusion.44 = (f32[4,18,40,1]{3,2,1,0:T(8,128)S(1)}, f32[4,18,40,1]{3,2,1,0:T(8,128)}) fusion(f32[4,18,40,384]{3,2,1,0:T(8,128)S(1)} %fusion.3), kind=kLoop, calls=%fused_computation.74 | loop fusion | bytes 46080 | tf_op jit(solution)/shard_map/slice | solution.py:53
  19.5 1.4 %fusion.45 = (f32[4,18,40,383]{3,2,1,0:T(8,128)S(1)}, f32[4,18,40,383]{3,2,1,0:T(8,128)S(1)}) fusion(f32[4,18,40,384]{3,2,1,0:T(8,128)S(1)} %fusion.3), kind=kLoop, calls=%fused_computation.75 | loop fusion | bytes 17648640 | tf_op jit(solution)/shard_map/slice | solution.py:53
  21.0 3.7 %fusion.6 = f32[4,18,40,384]{3,2,1,0:T(8,128)S(1)} fusion(f32[4,18,40,384]{3,2,1,0:T(8,128)S(1)} %fusion.3, f32[4,18,40,1]{3,2,1,0:T(8,128)} %get-tuple-element.17, f32[4,18,40,383]{3,2,1,0:T(8,128)S(1)} %get-tuple-element.19, f32[4,18,40,383]{3,2,1,0:T(8,128)S(1)} %get-tuple-element.18, f32[4,18,40,1]{3,2,1,0:T(8,128)S(1)} %get-tuple-element.16, ...), kind=kLoop, calls=%fused_computation.8 | loop fusion | flops 8847360 | bytes 19906560 | tf_op jit(solution)/shard_map/add | solution.py:54
  24.9 1.6 %collective-permute-start.1 = (f32[4,18,1,384]{3,1,2,0:T(8,128)S(1)}, f32[4,18,1,384]{3,1,2,0:T(8,128)S(1)}, u32[]{:S(2)}, u32[]{:S(2)}) collective-permute-start(f32[4,18,1,384]{3,1,2,0:T(8,128)S(1)} %copy.28), channel_id=1, source_target_pairs={{8,0},{16,8},{24,16},{0,24},{9,1},{17,9},{25,17},{1,25},{10,2},{18... | collective-permute-start | bytes 331784 | tf_op jit(solution)/shard_map/ppermute | solution.py:25
  26.6 4.1 %fusion.43 = (f32[4,18,39,384]{3,2,1,0:T(8,128)}, f32[4,18,39,384]{3,2,1,0:T(8,128)}) fusion(f32[4,18,40,384]{3,2,1,0:T(8,128)S(1)} %fusion.6), kind=kLoop, calls=%fused_computation.73 | loop fusion | bytes 17252352 | tf_op jit(solution)/shard_map/slice | solution.py:63
  32.6 0.8 broadcast_select_fusion.3
  33.4 0.8 broadcast_select_fusion.1
  34.2 5.9 %fusion.10 = f32[4,18,40,384]{3,2,1,0:T(8,128)S(1)} fusion(f32[4,18,40,384]{3,2,1,0:T(8,128)} %copy-done.2, f32[4,18,1,384]{3,2,1,0:T(1,128)S(1)} %broadcast_select_fusion.3, f32[4,18,39,384]{3,2,1,0:T(8,128)} %get-tuple-element.15, f32[4,18,39,384]{3,2,1,0:T(8,128)} %get-tuple-element.14, f32[4,18,1,384]{3,2,1,0:T(1,128)S(1)} %broadcast_select_fusion.1, ...), kind=kLoop, calls=%fused_computation.14 | loop fusion | flops 8847360 | bytes 19906560 | tf_op jit(solution)/shard_map/add | solution.py:64
  40.1 1.5 %collective-permute-start.3 = (f32[4,1,40,384]{3,2,1,0:T(8,128)S(1)}, f32[4,1,40,384]{3,2,1,0:T(8,128)S(1)}, u32[]{:S(2)}, u32[]{:S(2)}) collective-permute-start(f32[4,1,40,384]{3,2,1,0:T(8,128)S(1)} %slice.110), channel_id=1, source_target_pairs={{2,0},{4,2},{6,4},{3,1},{5,3},{7,5},{10,8},{12,10},{14,12},{11,9},... | collective-permute-start | bytes 737288 | tf_op jit(solution)/shard_map/ppermute | solution.py:14
  41.9 9.4 %collective-permute-done.3 = f32[4,1,40,384]{3,2,1,0:T(8,128)S(1)} collective-permute-done((f32[4,1,40,384]{3,2,1,0:T(8,128)S(1)}, f32[4,1,40,384]{3,2,1,0:T(8,128)S(1)}, u32[]{:S(2)}, u32[]{:S(2)}) %collective-permute-start.3) | collective-permute-done | bytes 245792 | tf_op jit(solution)/shard_map/ppermute | solution.py:14
  52.4 1.4 %fusion.41 = (f32[4,18,40,383]{3,2,1,0:T(8,128)S(1)}, f32[4,18,40,383]{3,2,1,0:T(8,128)S(1)}) fusion(f32[4,18,40,384]{3,2,1,0:T(8,128)S(1)} %fusion.13), kind=kLoop, calls=%fused_computation.71 | loop fusion | bytes 17648640 | tf_op jit(solution)/shard_map/slice | solution.py:53
  53.8 3.5 %fusion.16 = f32[4,18,40,384]{3,2,1,0:T(8,128)S(1)} fusion(f32[4,18,40,384]{3,2,1,0:T(8,128)S(1)} %fusion.13, f32[4,18,40,1]{3,2,1,0:T(8,128)S(1)} %get-tuple-element.9, f32[4,18,40,383]{3,2,1,0:T(8,128)S(1)} %get-tuple-element.11, f32[4,18,40,383]{3,2,1,0:T(8,128)S(1)} %get-tuple-element.10, f32[4,18,40,1]{3,2,1,0:T(8,128)S(1)} %get-tuple-element.8, ...), kind=kLoop, calls=%fused_computation.23 | loop fusion | flops 8847360 | bytes 19906560 | tf_op jit(solution)/shard_map/add | solution.py:54
  57.5 1.2 collective-permute-start.4
  58.8 4.1 %fusion.39 = (f32[4,18,39,384]{3,2,1,0:T(8,128)}, f32[4,18,39,384]{3,2,1,0:T(8,128)}) fusion(f32[4,18,40,384]{3,2,1,0:T(8,128)S(1)} %fusion.16), kind=kLoop, calls=%fused_computation.69 | loop fusion | bytes 17252352 | tf_op jit(solution)/shard_map/slice | solution.py:63
  63.9 0.7 rev.15
  64.6 0.8 broadcast_select_fusion.2
  65.4 0.8 broadcast_select_fusion
  66.2 5.7 %fusion.20 = f32[4,18,40,384]{3,2,1,0:T(8,128)S(1)} fusion(f32[4,18,40,384]{3,2,1,0:T(8,128)} %copy-done.1, f32[4,18,1,384]{3,2,1,0:T(1,128)S(1)} %broadcast_select_fusion.2, f32[4,18,39,384]{3,2,1,0:T(8,128)} %get-tuple-element.7, f32[4,18,39,384]{3,2,1,0:T(8,128)} %get-tuple-element.6, f32[4,18,1,384]{3,2,1,0:T(1,128)S(1)} %broadcast_select_fusion, ...), kind=kLoop, calls=%fused_computation.29 | loop fusion | flops 8847360 | bytes 19906560 | tf_op jit(solution)/shard_map/add | solution.py:64
  71.9 2.1 %copy-done.3 = f32[4,18,40,384]{3,2,1,0:T(8,128)} copy-done((f32[4,18,40,384]{3,2,1,0:T(8,128)}, f32[4,18,40,384]{3,2,1,0:T(8,128)S(1)}, u32[]{:S(2)}) %copy-start.3) | copy-done | bytes 4423704
  74.0 4.4 %fusion = f32[1,4,40,384]{3,0,2,1:T(1,128)S(1)} fusion(f32[4,18,40,384]{3,2,1,0:T(8,128)S(1)} %fusion.20, f32[18]{0:T(128)S(1)} %copy-done), kind=kOutput, calls=%fused_computation | convolution fusion | flops 13271040 | bytes 4669512 | tf_op jit(solution)/shard_map/sxy,l,slxy->xy/dot_general | solution.py:140
  78.4 0.8 all_to_all.6
  79.1 5.4 %all-to-all-start = ((f32[32,1,480]{2,1,0:T(1,128)}), f32[32,1,480]{2,1,0:T(1,128)S(1)}, u32[]{:S(2)}, u32[]{:S(2)}) async-start(f32[32,1,480]{2,1,0:T(1,128)} %all_to_all.6), calls=%async_computation | async-start | bytes 131072 | tf_op jit(solution)/shard_map/all_to_all | solution.py:102
  84.8 7.0 %all-to-all-done = f32[32,1,480]{2,1,0:T(1,128)S(1)} async-done(((f32[32,1,480]{2,1,0:T(1,128)}), f32[32,1,480]{2,1,0:T(1,128)S(1)}, u32[]{:S(2)}, u32[]{:S(2)}) %all-to-all-start) | async-done | bytes 61472 | tf_op jit(solution)/shard_map/all_to_all | solution.py:102
  91.8 30.7 %all-gather.1 = f32[8,4,480]{2,1,0:T(4,128)S(1)} all-gather(f32[1,4,480]{2,1,0:T(4,128)S(1)} %bitcast.28), channel_id=2, replica_groups=mesh['tile'=4,'lev'=4,'sec'=2] {'lev','sec'}, dimensions={0}, use_global_device_ids=true | all-gather | bytes 69120 | tf_op jit(solution)/shard_map/all_gather | solution.py:106
  122.7 3.3 %shard_map.104 = f32[120,128]{1,0:T(8,128)} custom-call(s32[120,128]{1,0:T(8,128)S(1)} %reshape.40.cells_ref, f32[120,128]{1,0:T(8,128)S(1)} %reshape.42.values_ref), custom_call_target="tpu_custom_call" | custom-call | tf_op jit(solution)/shard_map/pallas_call | solution.py:108
  (59 shorter events, 6.0 us)
Async XLA Ops:
  0.6 73.4 %copy-start = (f32[18]{0:T(128)S(1)}, f32[18]{0:T(128)}, u32[]{:S(2)}) copy-start(f32[18]{0:T(128)} %param.15) | copy-start | bytes 220
  0.6 8.4 %slice-start = ((s8[4423680]{0:T(1024)(128)(4,1)}), s8[4194304]{0:T(1024)(128)(4,1)S(1)}, s32[]{:S(2)}) async-start(s8[4423680]{0:T(1024)(128)(4,1)} %bitcast.24), calls=%async_computation.1 | async-start | bytes 8388608
  1.8 7.2 %slice-start.1 = ((s8[4423680]{0:T(1024)(128)(4,1)}), s8[229376]{0:T(1024)(128)(4,1)S(1)}, s32[]{:S(2)}) async-start(s8[4423680]{0:T(1024)(128)(4,1)} %bitcast.24), calls=%async_computation.2 | async-start | bytes 458752
  1.8 11.0 %collective-permute-start = (f32[4,1,40,384]{3,2,1,0:T(8,128)S(1)}, f32[4,1,40,384]{3,2,1,0:T(8,128)S(1)}, u32[]{:S(2)}, u32[]{:S(2)}) collective-permute-start(f32[4,1,40,384]{3,2,1,0:T(8,128)S(1)} %slice.78), channel_id=1, source_target_pairs={{2,0},{4,2},{6,4},{3,1},{5,3},{7,5},{10,8},{12,10},{14,12},{11,9},... | collective-permute-start | bytes 737288 | tf_op jit(solution)/shard_map/ppermute | solution.py:14
  9.0 2.3 %copy-start.7 = (bf16[18,40,384]{2,1,0:T(8,128)(2,1)S(1)}, bf16[18,40,384]{2,1,0:T(8,128)(2,1)}, u32[]{:S(2)}) copy-start(bf16[18,40,384]{2,1,0:T(8,128)(2,1)} %param.12) | copy-start | bytes 1658884
  9.0 2.4 %copy-start.10 = (s32[4,2]{0,1:T(2,128)S(1)}, s32[4,2]{0,1:T(2,128)}, u32[]{:S(2)}) copy-start(s32[4,2]{0,1:T(2,128)} %param.14) | copy-start | bytes 100
  24.7 6.0 %copy-start.2 = (f32[4,18,40,384]{3,2,1,0:T(8,128)}, f32[4,18,40,384]{3,2,1,0:T(8,128)S(1)}, u32[]{:S(2)}) copy-start(f32[4,18,40,384]{3,2,1,0:T(8,128)S(1)} %fusion.6) | copy-start | bytes 13271044
  24.9 5.8 %collective-permute-start.1 = (f32[4,18,1,384]{3,1,2,0:T(8,128)S(1)}, f32[4,18,1,384]{3,1,2,0:T(8,128)S(1)}, u32[]{:S(2)}, u32[]{:S(2)}) collective-permute-start(f32[4,18,1,384]{3,1,2,0:T(8,128)S(1)} %copy.28), channel_id=1, source_target_pairs={{8,0},{16,8},{24,16},{0,24},{9,1},{17,9},{25,17},{1,25},{10,2},{18... | collective-permute-start | bytes 331784 | tf_op jit(solution)/shard_map/ppermute | solution.py:25
  26.5 7.7 %copy-start.6 = (f32[18,40,384]{2,1,0:T(8,128)S(1)}, f32[18,40,384]{2,1,0:T(8,128)}, u32[]{:S(2)}) copy-start(f32[18,40,384]{2,1,0:T(8,128)} %get-tuple-element.22) | copy-start | bytes 3317764
  26.5 5.2 %collective-permute-start.2 = (f32[4,18,1,384]{3,1,2,0:T(8,128)S(1)}, f32[4,18,1,384]{3,1,2,0:T(8,128)S(1)}, u32[]{:S(2)}, u32[]{:S(2)}) collective-permute-start(f32[4,18,1,384]{3,1,2,0:T(8,128)S(1)} %copy.31), channel_id=1, source_target_pairs={{0,8},{8,16},{16,24},{24,0},{1,9},{9,17},{17,25},{25,1},{2,10},{10... | collective-permute-start | bytes 331784 | tf_op jit(solution)/shard_map/ppermute | solution.py:24
  40.1 11.1 %collective-permute-start.3 = (f32[4,1,40,384]{3,2,1,0:T(8,128)S(1)}, f32[4,1,40,384]{3,2,1,0:T(8,128)S(1)}, u32[]{:S(2)}, u32[]{:S(2)}) collective-permute-start(f32[4,1,40,384]{3,2,1,0:T(8,128)S(1)} %slice.110), channel_id=1, source_target_pairs={{2,0},{4,2},{6,4},{3,1},{5,3},{7,5},{10,8},{12,10},{14,12},{11,9},... | collective-permute-start | bytes 737288 | tf_op jit(solution)/shard_map/ppermute | solution.py:14
  57.3 5.6 %copy-start.1 = (f32[4,18,40,384]{3,2,1,0:T(8,128)}, f32[4,18,40,384]{3,2,1,0:T(8,128)S(1)}, u32[]{:S(2)}) copy-start(f32[4,18,40,384]{3,2,1,0:T(8,128)S(1)} %fusion.16) | copy-start | bytes 13271044
  57.5 5.4 %collective-permute-start.4 = (f32[4,18,1,384]{3,1,2,0:T(8,128)S(1)}, f32[4,18,1,384]{3,1,2,0:T(8,128)S(1)}, u32[]{:S(2)}, u32[]{:S(2)}) collective-permute-start(f32[4,18,1,384]{3,1,2,0:T(8,128)S(1)} %copy.34), channel_id=1, source_target_pairs={{8,0},{16,8},{24,16},{0,24},{9,1},{17,9},{25,17},{1,25},{10,2},{18... | collective-permute-start | bytes 331784 | tf_op jit(solution)/shard_map/ppermute | solution.py:25
  58.7 7.5 %copy-start.4 = (f32[18,40,384]{2,1,0:T(8,128)S(1)}, f32[18,40,384]{2,1,0:T(8,128)}, u32[]{:S(2)}) copy-start(f32[18,40,384]{2,1,0:T(8,128)} %get-tuple-element.20) | copy-start | bytes 3317764
  58.7 7.5 %copy-start.5 = (f32[18,40,384]{2,1,0:T(8,128)S(1)}, f32[18,40,384]{2,1,0:T(8,128)}, u32[]{:S(2)}) copy-start(f32[18,40,384]{2,1,0:T(8,128)} %get-tuple-element.21) | copy-start | bytes 3317764
  58.7 5.0 %collective-permute-start.5 = (f32[4,18,1,384]{3,1,2,0:T(8,128)S(1)}, f32[4,18,1,384]{3,1,2,0:T(8,128)S(1)}, u32[]{:S(2)}, u32[]{:S(2)}) collective-permute-start(f32[4,18,1,384]{3,1,2,0:T(8,128)S(1)} %copy.37), channel_id=1, source_target_pairs={{0,8},{8,16},{16,24},{24,0},{1,9},{9,17},{17,25},{25,1},{2,10},{10... | collective-permute-start | bytes 331784 | tf_op jit(solution)/shard_map/ppermute | solution.py:24
  71.9 2.1 %copy-start.3 = (f32[4,18,40,384]{3,2,1,0:T(8,128)}, f32[4,18,40,384]{3,2,1,0:T(8,128)S(1)}, u32[]{:S(2)}) copy-start(f32[4,18,40,384]{3,2,1,0:T(8,128)S(1)} %fusion.20) | copy-start | bytes 13271044
  74.0 4.4 %copy-start.8 = (f32[4,40,384]{2,1,0:T(8,128)S(1)}, f32[4,40,384]{2,1,0:T(8,128)}, u32[]{:S(2)}) copy-start(f32[4,40,384]{2,1,0:T(8,128)} %param.16) | copy-start | bytes 737284
  74.0 10.5 %copy-start.9 = (s32[4,3840]{1,0:T(4,128)S(1)}, s32[4,3840]{1,0:T(4,128)}, u32[]{:S(2)}) copy-start(s32[4,3840]{1,0:T(4,128)} %param.17) | copy-start | bytes 184324
  79.1 12.6 %all-to-all-start = ((f32[32,1,480]{2,1,0:T(1,128)}), f32[32,1,480]{2,1,0:T(1,128)S(1)}, u32[]{:S(2)}, u32[]{:S(2)}) async-start(f32[32,1,480]{2,1,0:T(1,128)} %all_to_all.6), calls=%async_computation | async-start | bytes 131072 | tf_op jit(solution)/shard_map/all_to_all | solution.py:102

commit v2 on v1

v2 whole, which is shorter than its diff:
```python
import functools

import jax
import jax.numpy as jnp
from jax import lax
from jax.experimental import pallas as pl
from jax.experimental.pallas import tpu as pltpu
from jax.sharding import PartitionSpec as P

FL_DEV = 15360
LANES = 128
ROWS = 8
MIB = 2**20
VM = pl.BlockSpec(memory_space=pltpu.VMEM)
HBM = pl.BlockSpec(memory_space=pltpu.HBM)


def call(kernel, out_shape, in_specs, out_specs, operands, scratch=(), mib=16):
    return pl.pallas_call(
        kernel,
        out_shape=out_shape,
        in_specs=in_specs,
        out_specs=out_specs,
        scratch_shapes=list(scratch),
        compiler_params=pltpu.CompilerParams(vmem_limit_bytes=mib * MIB),
    )(*operands)


def f32(*shape):
    return jax.ShapeDtypeStruct(shape, jnp.float32)


def cut(value, xt, j):
    return value[xt * ROWS : (xt + 1) * ROWS, j * LANES : (j + 1) * LANES]


def weights(courant, codes, bit):
    size = jnp.abs(courant)
    half = (0.5 * size) * (1.0 - size)
    limited = jnp.where(jnp.bitwise_and(codes, 1 << bit) != 0, half, 0.0)
    ahead = jnp.maximum(courant, 0.0) - limited
    back = jnp.maximum(-courant, 0.0) - limited
    return ahead, back


def second_weights(cy, codes, bit, xt, tiles):
    lane = lax.broadcasted_iota(jnp.int32, (ROWS, LANES), 1)
    out = []
    for j in range(tiles):
        ahead, back = weights(cut(cy, xt, j), cut(codes, xt, j), bit)
        if j == 0:
            back = jnp.where(lane == 0, 0.0, back)
        if j == tiles - 1:
            ahead = jnp.where(lane == LANES - 1, 0.0, ahead)
        out.append((ahead, back, (1.0 - ahead) - back))
    return out


def second_sweep(parts, factors):
    lane = lax.broadcasted_iota(jnp.int32, (ROWS, LANES), 1)
    tiles = len(parts)
    later = [pltpu.roll(part, LANES - 1, 1) for part in parts]
    sooner = [pltpu.roll(part, 1, 1) for part in parts]
    out = []
    for j in range(tiles):
        following, previous = later[j], sooner[j]
        if j + 1 < tiles:
            following = jnp.where(lane == LANES - 1, later[j + 1], following)
        if j > 0:
            previous = jnp.where(lane == 0, sooner[j - 1], previous)
        ahead, back, own = factors[j]
        out.append(own * parts[j] + ahead * following + back * previous)
    return out


def first_sweep(field, s, j, xt, last, factors, left_row, right_row):
    start = ROWS * (xt + 1)
    sub = lax.broadcasted_iota(jnp.int32, (ROWS, LANES), 0)
    own_value = field(s, j, start)
    following = field(s, j, start + 1)
    previous = field(s, j, start - 1)
    if xt == 0:
        previous = jnp.where(sub == 0, left_row(s, j), previous)
    if xt == last:
        following = jnp.where(sub == ROWS - 1, right_row(s, j), following)
    ahead, back, own = factors
    return own * own_value + ahead * following + back * previous


def turned(source_ref, flag, target_ref):
    tiles, rows, _ = source_ref.shape
    for j in range(tiles):
        for start in range(0, rows, ROWS):
            count = min(ROWS, rows - start)
            index = (LANES - 1) - lax.broadcasted_iota(jnp.int32, (count, LANES), 1)
            straight = source_ref[j, start : start + count, :]
            other = source_ref[tiles - 1 - j, start : start + count, :]
            mirrored = jnp.take_along_axis(other, index, axis=1, mode="promise_in_bounds")
            target_ref[j, start : start + count, :] = jnp.where(flag[:count], mirrored, straight)


def store_padded(ref, index, s, j, xt, value):
    start = ROWS * (xt + 1)
    ref[(*index, s, j, slice(start, start + ROWS), slice(None))] = value


def store_rims(first_ref, last_ref, row, j, xt, last, value):
    if xt == 0:
        first_ref[j, pl.ds(row, 1), :] = value[:1]
    if xt == last:
        last_ref[j, pl.ds(row, 1), :] = value[ROWS - 1 :]


def flags(seam_ref):
    return seam_ref[0] == 1, seam_ref[1] == 1


def lower_kernel(
    f_hbm, mf_hbm, cy_hbm, code_hbm,
    v_ref, first_ref, last_ref, top_ref,
    f_ref, mf_ref, cy_ref, code_ref, sems,
):
    sectors, levels, columns, width = f_hbm.shape
    tiles, strips = width // LANES, columns // ROWS

    def fetch(k):
        return pltpu.make_async_copy(f_hbm.at[:, k], f_ref.at[k], sems.at[0, k])

    def fetch_code(k):
        return pltpu.make_async_copy(code_hbm.at[k], code_ref.at[k], sems.at[1, k])

    fetch_mf = pltpu.make_async_copy(mf_hbm, mf_ref, sems.at[2, 0])
    fetch_cy = pltpu.make_async_copy(cy_hbm, cy_ref, sems.at[2, 1])
    fetch(0).start()
    fetch_mf.start()
    fetch_cy.start()
    for k in range(levels - 1):
        fetch_code(k).start()
        fetch(k + 1).start()
    fetch(0).wait()
    fetch_mf.wait()
    fetch_cy.wait()

    def level(k, _):
        fetch_code(k).wait()
        fetch(k + 1).wait()
        mf = mf_ref[k].astype(jnp.float32)
        cy = cy_ref[k].astype(jnp.float32)
        codes = code_ref[k]
        for xt in range(strips):
            factors = second_weights(cy, codes, 3, xt, tiles)
            rows = slice(xt * ROWS, (xt + 1) * ROWS)
            for s in range(sectors):
                parts = []
                for j in range(tiles):
                    lanes = slice(j * LANES, (j + 1) * LANES)
                    here = f_ref[k, s, rows, lanes]
                    upper = f_ref[k + 1, s, rows, lanes]
                    parts.append(here + cut(mf, xt, j) * (upper - here))
                for j, value in enumerate(second_sweep(parts, factors)):
                    store_padded(v_ref, (k,), s, j, xt, value)
                    store_rims(first_ref, last_ref, k * sectors + s, j, xt, strips - 1, value)
        return 0

    lax.fori_loop(0, levels - 1, level, 0)
    top_ref[...] = f_ref[levels - 1]


def upper_kernel(bit, here_ref, above_ref, mf_ref, cy_ref, code_ref, v_ref, first_ref, last_ref):
    sectors, columns, width = above_ref.shape
    level = mf_ref.shape[0] - 1
    tiles, strips = width // LANES, columns // ROWS
    at_top = lax.axis_index("lev") == lax.axis_size("lev") - 1
    mf = mf_ref[level].astype(jnp.float32)
    cy = cy_ref[level].astype(jnp.float32)
    codes = code_ref[level]
    for xt in range(strips):
        factors = second_weights(cy, codes, bit, xt, tiles)
        rows = slice(xt * ROWS, (xt + 1) * ROWS)
        for s in range(sectors):
            parts = []
            for j in range(tiles):
                lanes = slice(j * LANES, (j + 1) * LANES)
                here = here_ref[s, rows, lanes]
                upper = jnp.where(at_top, here, above_ref[s, rows, lanes])
                parts.append(here + cut(mf, xt, j) * (upper - here))
            for j, value in enumerate(second_sweep(parts, factors)):
                store_padded(v_ref, (), s, j, xt, value)
                store_rims(first_ref, last_ref, s, j, xt, strips - 1, value)


def first_weights(cx, codes, bit, xt, j):
    ahead, back = weights(cut(cx, xt, j), cut(codes, xt, j), bit)
    return ahead, back, (1.0 - ahead) - back


def lowest_kernel(v_ref, left_ref, right_ref, seam_ref, cx_ref, code_ref, out_ref, lrow_ref, rrow_ref):
    _, sectors, tiles, _, _ = v_ref.shape
    columns = out_ref.shape[1]
    strips = columns // ROWS
    flip_left, flip_right = flags(seam_ref)
    turned(left_ref.at[:, :ROWS], flip_left, lrow_ref)
    turned(right_ref.at[:, :ROWS], flip_right, rrow_ref)
    cx = cx_ref[0].astype(jnp.float32)
    codes = code_ref[0]
    for xt in range(strips):
        for j in range(tiles):
            factors = first_weights(cx, codes, 2, xt, j)
            for s in range(sectors):
                value = first_sweep(
                    lambda s, j, start: v_ref[0, s, j, start : start + ROWS, :],
                    s, j, xt, strips - 1, factors,
                    lambda s, j: lrow_ref[j, s : s + 1, :],
                    lambda s, j: rrow_ref[j, s : s + 1, :],
                )
                out_ref[s, xt * ROWS : (xt + 1) * ROWS, j * LANES : (j + 1) * LANES] = value


def middle_kernel(
    v_ref, vt_ref, left_ref, right_ref, left_top_ref, right_top_ref, seam_ref,
    cx_ref, mf_ref, cy_ref, code_ref,
    out_ref, first_ref, last_ref, top_ref,
    lrow_ref, rrow_ref, ltop_ref, rtop_ref, a_ref,
):
    below, sectors, tiles, padded, _ = v_ref.shape
    strips = (padded - 2 * ROWS) // ROWS
    flip_left, flip_right = flags(seam_ref)
    turned(left_ref, flip_left, lrow_ref)
    turned(right_ref, flip_right, rrow_ref)
    turned(left_top_ref, flip_left, ltop_ref)
    turned(right_top_ref, flip_right, rtop_ref)

    cx = cx_ref[below].astype(jnp.float32)
    codes = code_ref[below]
    for xt in range(strips):
        for j in range(tiles):
            factors = first_weights(cx, codes, 2, xt, j)
            for s in range(sectors):
                value = first_sweep(
                    lambda s, j, start: vt_ref[s, j, start : start + ROWS, :],
                    s, j, xt, strips - 1, factors,
                    lambda s, j: ltop_ref[j, s : s + 1, :],
                    lambda s, j: rtop_ref[j, s : s + 1, :],
                )
                a_ref[below, s, j, xt * ROWS : (xt + 1) * ROWS, :] = value
                top_ref[s, xt * ROWS : (xt + 1) * ROWS, j * LANES : (j + 1) * LANES] = value

    def level(step, _):
        k = below - 1 - step
        cx = cx_ref[k].astype(jnp.float32)
        mf = mf_ref[k].astype(jnp.float32)
        cy = cy_ref[k].astype(jnp.float32)
        codes = code_ref[k]
        for xt in range(strips):
            along = [first_weights(cx, codes, 2, xt, j) for j in range(tiles)]
            across = second_weights(cy, codes, 1, xt, tiles)
            rows = slice(xt * ROWS, (xt + 1) * ROWS)
            for s in range(sectors):
                parts = []
                for j in range(tiles):
                    here = first_sweep(
                        lambda s, j, start: v_ref[k, s, j, start : start + ROWS, :],
                        s, j, xt, strips - 1, along[j],
                        lambda s, j: lrow_ref[j, pl.ds(k * sectors + s, 1), :],
                        lambda s, j: rrow_ref[j, pl.ds(k * sectors + s, 1), :],
                    )
                    upper = a_ref[k + 1, s, j, rows, :]
                    a_ref[k, s, j, rows, :] = here
                    parts.append(here + cut(mf, xt, j) * (upper - here))
                for j, value in enumerate(second_sweep(parts, across)):
                    store_padded(out_ref, (k,), s, j, xt, value)
                    store_rims(first_ref, last_ref, k * sectors + s, j, xt, strips - 1, value)
        return 0

    lax.fori_loop(0, below, level, 0)


def final_kernel(
    v_ref, vt_ref, left_ref, right_ref, left_top_ref, right_top_ref, seam_ref,
    cx_ref, code_ref, weight_ref, share_ref,
    out_hbm, sens_ref,
    lrow_ref, rrow_ref, ltop_ref, rtop_ref, out_ref, sems,
):
    below, sectors, tiles, padded, _ = v_ref.shape
    strips = (padded - 2 * ROWS) // ROWS
    flip_left, flip_right = flags(seam_ref)
    turned(left_ref, flip_left, lrow_ref)
    turned(right_ref, flip_right, rrow_ref)
    turned(left_top_ref, flip_left, ltop_ref)
    turned(right_top_ref, flip_right, rtop_ref)

    def send(k):
        return pltpu.make_async_copy(out_ref.at[k], out_hbm.at[:, k], sems.at[k])

    def level(k, field, left_row, right_row, start_sum):
        cx = cx_ref[k].astype(jnp.float32)
        codes = code_ref[k]
        factor = weight_ref[pl.ds(k, 1), :]
        for xt in range(strips):
            rows = slice(xt * ROWS, (xt + 1) * ROWS)
            for j in range(tiles):
                lanes = slice(j * LANES, (j + 1) * LANES)
                factors = first_weights(cx, codes, 0, xt, j)
                total = 0.0
                for s in range(sectors):
                    value = first_sweep(
                        field, s, j, xt, strips - 1, factors, left_row, right_row
                    )
                    out_ref[k, s, rows, lanes] = value
                    total = total + share_ref[s, rows, lanes] * value
                if start_sum:
                    sens_ref[rows, lanes] = factor * total
                else:
                    sens_ref[rows, lanes] += factor * total
        send(k).start()

    level(
        below,
        lambda s, j, start: vt_ref[s, j, start : start + ROWS, :],
        lambda s, j: ltop_ref[j, s : s + 1, :],
        lambda s, j: rtop_ref[j, s : s + 1, :],
        True,
    )

    def step(k, _):
        level(
            k,
            lambda s, j, start: v_ref[k, s, j, start : start + ROWS, :],
            lambda s, j: lrow_ref[j, pl.ds(k * sectors + s, 1), :],
            lambda s, j: rrow_ref[j, pl.ds(k * sectors + s, 1), :],
            False,
        )
        return 0

    lax.fori_loop(0, below, step, 0)
    for k in range(below + 1):
        send(k).wait()


def scatter_kernel(cells_ref, values_ref, out_ref):
    rows, lanes = out_ref.shape
    count = cells_ref.shape[0]
    high_iota = lax.broadcasted_iota(jnp.int32, (rows, lanes), 0)
    low_iota = lax.broadcasted_iota(jnp.int32, (lanes, lanes), 0)
    total = jnp.zeros((2 * rows, lanes), jnp.float32)
    for pair in range(0, count, 2):
        lefts, rights = [], []
        for row in (pair, pair + 1):
            cells = cells_ref[row : row + 1, :]
            value = values_ref[row : row + 1, :]
            coarse = value.astype(jnp.bfloat16).astype(jnp.float32)
            fine = value - coarse
            here = jnp.right_shift(cells, 7) == high_iota
            lefts.append(
                jnp.concatenate(
                    [jnp.where(here, coarse, 0.0), jnp.where(here, fine, 0.0)], axis=0
                ).astype(jnp.bfloat16)
            )
            match = jnp.bitwise_and(cells, 127) == low_iota
            rights.append(jnp.where(match, 1.0, 0.0).astype(jnp.bfloat16))
        total += lax.dot_general(
            jnp.concatenate(lefts, axis=1),
            jnp.concatenate(rights, axis=1),
            (((1,), (1,)), ((), ())),
            preferred_element_type=jnp.float32,
        )
    out_ref[...] = total[:rows] + total[rows:]


def remapped(partial_value, flux_cell):
    tiles, share = flux_cell.shape
    group = lax.axis_size("lev") * lax.axis_size("sec")
    piece = share // group
    sent = partial_value.reshape(tiles * group, piece)
    received = lax.all_to_all(
        sent, ("tile", "lev", "sec"), split_axis=0, concat_axis=0, tiled=True
    )
    summed = jnp.sum(received.reshape(tiles, group, piece), axis=1)
    copies = jnp.broadcast_to(summed.reshape(1, tiles * piece), (group, tiles * piece))
    gathered = lax.all_to_all(copies, ("lev", "sec"), split_axis=0, concat_axis=0, tiled=True)
    cells = flux_cell.reshape(tiles, group, piece).transpose(1, 0, 2)
    out = call(
        scatter_kernel,
        f32(FL_DEV // LANES, LANES),
        [VM, VM],
        VM,
        (cells.reshape(-1, LANES), gathered.reshape(-1, LANES)),
    )
    return out.reshape(-1)


def around(first, last):
    count = lax.axis_size("tile")
    up = [(i, (i + 1) % count) for i in range(count)]
    down = [(j, i) for i, j in up]
    return lax.ppermute(last, "tile", up), lax.ppermute(first, "tile", down)


def from_above(value):
    count = lax.axis_size("lev")
    return lax.ppermute(value, "lev", [(i + 1, i) for i in range(count - 1)])


def shards(
    forcing, courant_x, courant_y, mass_flux, limiter_code, seam_code, level_weight, sector_share, flux_cell
):
    sectors, levels, columns, width = forcing.shape
    tiles, below = width // LANES, levels - 1
    padded = columns + 2 * ROWS
    field = f32(below, sectors, tiles, padded, LANES)
    field_top = f32(sectors, tiles, padded, LANES)
    plane = f32(sectors, columns, width)
    rim = f32(tiles, below * sectors, LANES)
    rim_top = f32(tiles, sectors, LANES)
    rim_scratch = pltpu.VMEM(rim.shape, jnp.float32)
    top_scratch = pltpu.VMEM(rim_top.shape, jnp.float32)

    seam = lax.dynamic_index_in_dim(seam_code, lax.axis_index("tile"), 0, keepdims=False)
    seam = jnp.broadcast_to(seam[:, None, None], (2, ROWS, LANES))
    weight = jnp.broadcast_to(level_weight[:, None], (levels, LANES))

    above = from_above(forcing[:, 0])
    v, first, last, top = call(
        lower_kernel,
        (field, rim, rim, plane),
        [HBM] * 4,
        [VM] * 4,
        (forcing, mass_flux, courant_y, limiter_code),
        [
            pltpu.VMEM((levels, sectors, columns, width), jnp.float32),
            pltpu.VMEM((levels, columns, width), jnp.bfloat16),
            pltpu.VMEM((levels, columns, width), jnp.bfloat16),
            pltpu.VMEM((below, columns, width), jnp.int32),
            pltpu.SemaphoreType.DMA((3, levels)),
        ],
    )
    left, right = around(first, last)
    lowest = call(
        lowest_kernel,
        plane,
        [VM] * 6,
        VM,
        (v, left, right, seam, courant_x, limiter_code),
        [pltpu.VMEM((tiles, ROWS, LANES), jnp.float32)] * 2,
    )
    vt, first_top, last_top = call(
        functools.partial(upper_kernel, 3),
        (field_top, rim_top, rim_top),
        [VM] * 5,
        [VM] * 3,
        (top, above, mass_flux, courant_y, limiter_code),
    )
    left_top, right_top = around(first_top, last_top)
    above = from_above(lowest)

    v, first, last, top = call(
        middle_kernel,
        (field, rim, rim, plane),
        [VM] * 11,
        [VM] * 4,
        (
            v, vt, left, right, left_top, right_top, seam,
            courant_x, mass_flux, courant_y, limiter_code,
        ),
        [
            rim_scratch, rim_scratch, top_scratch, top_scratch,
            pltpu.VMEM((levels, sectors, tiles, columns, LANES), jnp.float32),
        ],
    )
    left, right = around(first, last)
    vt, first_top, last_top = call(
        functools.partial(upper_kernel, 1),
        (field_top, rim_top, rim_top),
        [VM] * 5,
        [VM] * 3,
        (top, above, mass_flux, courant_y, limiter_code),
    )
    left_top, right_top = around(first_top, last_top)
    adjoint, sensitivity = call(
        final_kernel,
        (f32(*forcing.shape), f32(columns, width)),
        [VM] * 11,
        [HBM, VM],
        (
            v, vt, left, right, left_top, right_top, seam,
            courant_x, limiter_code, weight, sector_share,
        ),
        [
            rim_scratch, rim_scratch, top_scratch, top_scratch,
            pltpu.VMEM((levels, sectors, columns, width), jnp.float32),
            pltpu.SemaphoreType.DMA((levels,)),
        ],
    )
    return (adjoint, remapped(sensitivity, flux_cell))


def solution(mesh):
    placed = (
        P("sec", "lev", "tile", None),
        P("lev", "tile", None),
        P("lev", "tile", None),
        P("lev", "tile", None),
        P("lev", "tile", None),
        P(),
        P("lev"),
        P("sec", "tile", None),
        P("tile", None),
    )
    return jax.shard_map(
        shards,
        mesh=mesh,
        in_specs=placed,
        out_specs=(P("sec", "lev", "tile", None), P("tile")),
        check_vma=False,
    )
```

time: 126 us -> 74.8 us (0.59)
  other arithmetic: 33.7 us -> 0.03 us
  blocking collectives: 30.7 us -> 12.1 us
  Pallas kernels: 3.25 us -> 20.2 us
  local copies, waits for them, and re-layouts: 24.2 us -> 13 us
  matrix products: 4.36 us -> 0 us
  waiting for transfers between devices: 17.4 us -> 14 us
  starting transfers between devices: 11.2 us -> 14.3 us
    all_gather x1 -> x0, blocking collectives: 30.7 us -> none  [remapped(): gathered = lax.all_gather(summed, ('lev', 'sec'))]
    add x6 -> x0, other arithmetic: 23.7 us -> none  [the longest x2 11.6 us: sweep_first(): adjoint + ahead * (following - adjoint) + behind * (adjoint - previous)]
    slice x17 -> x0, local copies, waits for them, and re-layouts: 17.6 us -> none  [the longest x2 8.18 us: sweep_first(): previous = jnp.concatenate([left_rim, adjoint[:, :, :-1]], axis=2)]
    pallas_call x1 -> x7, Pallas kernels: 3.25 us -> 20.2 us  [call(): pl.pallas_call(kernel, out_shape=out_shape, in_specs=in_specs, out_specs=...]
    all_to_all x0 -> x1, blocking collectives: none -> 12.1 us  [remapped(): lax.all_to_all(sent, ('tile', 'lev', 'sec'), split_axis=0, concat_axis=0,...]
    unnamed x26 -> x30, local copies, waits for them, and re-layouts: 2.15 us -> 10.8 us
    sub x1 -> x0, other arithmetic: 5.77 us -> none  [coefficients(): ahead = jnp.maximum(value, 0.0) - limited * spread]
    ppermute x6 -> x10, starting transfers between devices: 5.83 us -> 10.9 us  [the longest x8 8.08 us: around(): return (lax.ppermute(last, 'tile', up), lax.ppermute(first, 'tile', down))]
  transfers between devices with their start and end apart: 7 -> 11, of which waited for: 4 -> 6; matrix products, arithmetic and copies ran while one was open for 15% -> 2% of each run, Pallas kernels for 0% -> 9%
where the time goes in v2:
time: 74.8 us; the launch traced here: 74.4 us
  Pallas kernels  20.2 us (27%)
  starting transfers between devices  14.3 us (19%)
  waiting for transfers between devices  14 us (19%)
  local copies, waits for them, and re-layouts  13 us (17%)
  blocking collectives  12.1 us (16%)
  between operations  0.81 us (1%)
    pallas_call x7, Pallas kernels, call(): pl.pallas_call(kernel, out_shape=out_shape, in_specs=in_specs, out_specs=...  20.2 us
    all_to_all x1, blocking collectives, remapped(): lax.all_to_all(sent, ('tile', 'lev', 'sec'), split_axis=0, concat_axis=0,...  12.1 us
    unnamed x30, local copies, waits for them, and re-layouts  10.8 us
    ppermute x8, starting transfers between devices, around(): return (lax.ppermute(last, 'tile', up), lax.ppermute(first, 'tile', down))  8.08 us
    all_to_all x1, waiting for transfers between devices, remapped(): lax.all_to_all(copies, ('lev', 'sec'), split_axis=0, concat_axis=0, tiled...  6.52 us
    ppermute x8, waiting for transfers between devices, around(): return (lax.ppermute(last, 'tile', up), lax.ppermute(first, 'tile', down))  4.32 us
    all_to_all x1, starting transfers between devices, remapped(): lax.all_to_all(copies, ('lev', 'sec'), split_axis=0, concat_axis=0, tiled...  3.35 us
    ppermute x2, waiting for transfers between devices, from_above(): return lax.ppermute(value, 'lev', [(i + 1, i) for i in range(count - 1)])  3.19 us
  transfers between devices with their start and end apart: 11, of which 6 were waited for; matrix products, arithmetic and copies ran while one was open for 2% of the time, Pallas kernels for 9%

profile of v2, /device:TPU:0, one launch (start us, length us, event | category | flops | bytes accessed | tf_op | source)
XLA Modules:
  0.0 74.4 jit_solution(15668271665408540475)
XLA Ops:
  0.7 1.2 %copy-done.1 = s32[18,40,384]{2,1,0:T(8,128)S(1)} copy-done((s32[18,40,384]{2,1,0:T(8,128)S(1)}, s32[18,40,384]{2,1,0:T(8,128)}, u32[]{:S(2)}) %copy-start.1) | copy-done | bytes 1105944
  1.9 1.0 %copy-done.6 = bf16[18,40,384]{2,1,0:T(8,128)(2,1)S(1)} copy-done((bf16[18,40,384]{2,1,0:T(8,128)(2,1)S(1)}, bf16[18,40,384]{2,1,0:T(8,128)(2,1)}, u32[]{:S(2)}) %copy-start.6) | copy-done | bytes 552984
  3.0 1.0 %copy-done.8 = bf16[18,40,384]{2,1,0:T(8,128)(2,1)S(1)} copy-done((bf16[18,40,384]{2,1,0:T(8,128)(2,1)S(1)}, bf16[18,40,384]{2,1,0:T(8,128)(2,1)}, u32[]{:S(2)}) %copy-start.8) | copy-done | bytes 552984
  4.0 2.3 %copy-done.11 = f32[4,18,40,384]{3,2,1,0:T(8,128)S(1)} copy-done((f32[4,18,40,384]{3,2,1,0:T(8,128)S(1)}, f32[4,18,40,384]{3,2,1,0:T(8,128)}, u32[]{:S(2)}) %copy-start.11) | copy-done | bytes 4423704
  6.3 7.6 %shard_map.104 = (f32[17,4,3,56,128]{4,3,2,1,0:T(8,128)S(1)}, f32[3,68,128]{2,1,0:T(8,128)}, f32[3,68,128]{2,1,0:T(8,128)}, f32[4,40,384]{2,1,0:T(8,128)S(1)}) custom-call(f32[4,18,40,384]{3,2,1,0:T(8,128)S(1)} %copy-done.11, bf16[18,40,384]{2,1,0:T(8,128)(2,1)S(1)} %copy-done.6, bf16[18,40,384]{2,1,0:T(8,128)(2,1)S(1)} %copy-done.8, ...), custom_call_target="tpu_custom_call" | custom-call | tf_op jit(solution)/shard_map/pallas_call | solution.py:19
  13.8 2.5 %copy-done.3 = f32[17,4,3,56,128]{4,3,2,1,0:T(8,128)} copy-done((f32[17,4,3,56,128]{4,3,2,1,0:T(8,128)}, f32[17,4,3,56,128]{4,3,2,1,0:T(8,128)S(1)}, u32[]{:S(2)}) %copy-start.3) | copy-done | bytes 5849112
  16.4 0.5 collective-permute-start.1
  16.8 1.9 %collective-permute-start.2 = (f32[3,68,128]{2,1,0:T(8,128)}, f32[3,68,128]{2,1,0:T(8,128)S(1)}, u32[]{:S(2)}, u32[]{:S(2)}) collective-permute-start(f32[3,68,128]{2,1,0:T(8,128)} %get-tuple-element.22), channel_id=1, source_target_pairs={{8,0},{16,8},{24,16},{0,24},{9,1},{17,9},{25,17},{1,25},{10,2},{18... | collective-permute-start | bytes 313352 | tf_op jit(solution)/shard_map/ppermute | solution.py:396
  18.7 0.7 slice_bitcast_fusion
  19.4 1.3 %collective-permute-start = (f32[4,40,384]{2,1,0:T(8,128)}, f32[4,40,384]{2,1,0:T(8,128)S(1)}, u32[]{:S(2)}, u32[]{:S(2)}) collective-permute-start(f32[4,40,384]{2,1,0:T(8,128)} %slice_bitcast_fusion), channel_id=1, source_target_pairs={{2,0},{4,2},{6,4},{3,1},{5,3},{7,5},{10,8},{12,10},{14,12},{11,9},... | collective-permute-start | bytes 737288 | tf_op jit(solution)/shard_map/ppermute | solution.py:401
  20.8 0.2 dynamic-slice_reduce_fusion
  20.9 0.4 collective-permute-done.1.left_ref
  21.4 1.1 %collective-permute-done.2.right_ref = f32[3,68,128]{2,1,0:T(8,128)S(1)} collective-permute-done((f32[3,68,128]{2,1,0:T(8,128)}, f32[3,68,128]{2,1,0:T(8,128)S(1)}, u32[]{:S(2)}, u32[]{:S(2)}) %collective-permute-start.2) | collective-permute-done | bytes 104480 | tf_op jit(solution)/shard_map/ppermute | solution.py:396
  22.6 2.7 %copy-done.4 = f32[17,4,3,56,128]{4,3,2,1,0:T(8,128)S(1)} copy-done((f32[17,4,3,56,128]{4,3,2,1,0:T(8,128)S(1)}, f32[17,4,3,56,128]{4,3,2,1,0:T(8,128)}, u32[]{:S(2)}) %copy-start.4) | copy-done | bytes 5849112
  25.3 1.6 %collective-permute-start.5 = (f32[4,40,384]{2,1,0:T(8,128)S(1)}, f32[4,40,384]{2,1,0:T(8,128)S(1)}, u32[]{:S(2)}, u32[]{:S(2)}) collective-permute-start(f32[4,40,384]{2,1,0:T(8,128)S(1)} %shard_map.107), channel_id=1, source_target_pairs={{2,0},{4,2},{6,4},{3,1},{5,3},{7,5},{10,8},{12,10},{14,12},{11,9},... | collective-permute-start | bytes 737288 | tf_op jit(solution)/shard_map/ppermute | solution.py:401
  26.9 3.2 %collective-permute-done.above_ref = f32[4,40,384]{2,1,0:T(8,128)S(1)} collective-permute-done((f32[4,40,384]{2,1,0:T(8,128)}, f32[4,40,384]{2,1,0:T(8,128)S(1)}, u32[]{:S(2)}, u32[]{:S(2)}) %collective-permute-start) | collective-permute-done | bytes 245792 | tf_op jit(solution)/shard_map/ppermute | solution.py:401
  30.1 0.2 shard_map.105
  30.4 1.7 %collective-permute-start.4 = (f32[3,4,128]{2,1,0:T(4,128)S(1)}, f32[3,4,128]{2,1,0:T(4,128)S(1)}, u32[]{:S(2)}, u32[]{:S(2)}) collective-permute-start(f32[3,4,128]{2,1,0:T(4,128)S(1)} %get-tuple-element.24), channel_id=1, source_target_pairs={{8,0},{16,8},{24,16},{0,24},{9,1},{17,9},{25,17},{1,25},{10,2},{18... | collective-permute-start | bytes 18440 | tf_op jit(solution)/shard_map/ppermute | solution.py:396
  32.1 1.3 %collective-permute-done.3.left_top_ref = f32[3,4,128]{2,1,0:T(4,128)S(1)} collective-permute-done((f32[3,4,128]{2,1,0:T(4,128)S(1)}, f32[3,4,128]{2,1,0:T(4,128)S(1)}, u32[]{:S(2)}, u32[]{:S(2)}) %collective-permute-start.3) | collective-permute-done | bytes 6176 | tf_op jit(solution)/shard_map/ppermute | solution.py:396
  33.4 6.0 %shard_map.106 = (f32[17,4,3,56,128]{4,3,2,1,0:T(8,128)S(1)}, f32[3,68,128]{2,1,0:T(8,128)S(1)}, f32[3,68,128]{2,1,0:T(8,128)S(1)}, f32[4,40,384]{2,1,0:T(8,128)S(1)}) custom-call(f32[17,4,3,56,128]{4,3,2,1,0:T(8,128)S(1)} %copy-done.5, f32[4,3,56,128]{3,2,1,0:T(8,128)S(1)} %get-tuple-element.20.vt_ref, f32[3,68,128]{2,1,0:T(8,128)S(1)} %collective-permute-done.1.left_ref, ...), custom_call_target="tpu_custom_call" | custom-call | tf_op jit(solution)/shard_map/pallas_call | solution.py:19
  39.4 0.8 %collective-permute-start.6 = (f32[3,68,128]{2,1,0:T(8,128)S(1)}, f32[3,68,128]{2,1,0:T(8,128)S(1)}, u32[]{:S(2)}, u32[]{:S(2)}) collective-permute-start(f32[3,68,128]{2,1,0:T(8,128)S(1)} %get-tuple-element.28), channel_id=1, source_target_pairs={{0,8},{8,16},{16,24},{24,0},{1,9},{9,17},{17,25},{25,1},{2,10},{10... | collective-permute-start | bytes 313352 | tf_op jit(solution)/shard_map/ppermute | solution.py:396
  40.3 1.3 %collective-permute-start.7 = (f32[3,68,128]{2,1,0:T(8,128)S(1)}, f32[3,68,128]{2,1,0:T(8,128)S(1)}, u32[]{:S(2)}, u32[]{:S(2)}) collective-permute-start(f32[3,68,128]{2,1,0:T(8,128)S(1)} %get-tuple-element.29), channel_id=1, source_target_pairs={{8,0},{16,8},{24,16},{0,24},{9,1},{17,9},{25,17},{1,25},{10,2},{18... | collective-permute-start | bytes 313352 | tf_op jit(solution)/shard_map/ppermute | solution.py:396
  41.6 0.2 shard_map.108
  41.8 1.7 %collective-permute-start.9 = (f32[3,4,128]{2,1,0:T(4,128)S(1)}, f32[3,4,128]{2,1,0:T(4,128)S(1)}, u32[]{:S(2)}, u32[]{:S(2)}) collective-permute-start(f32[3,4,128]{2,1,0:T(4,128)S(1)} %get-tuple-element.31), channel_id=1, source_target_pairs={{8,0},{16,8},{24,16},{0,24},{9,1},{17,9},{25,17},{1,25},{10,2},{18... | collective-permute-start | bytes 18440 | tf_op jit(solution)/shard_map/ppermute | solution.py:396
  43.6 1.4 %collective-permute-done.8.left_top_ref = f32[3,4,128]{2,1,0:T(4,128)S(1)} collective-permute-done((f32[3,4,128]{2,1,0:T(4,128)S(1)}, f32[3,4,128]{2,1,0:T(4,128)S(1)}, u32[]{:S(2)}, u32[]{:S(2)}) %collective-permute-start.8) | collective-permute-done | bytes 6176 | tf_op jit(solution)/shard_map/ppermute | solution.py:396
  45.1 2.9 %shard_map.109 = (f32[4,18,40,384]{3,2,1,0:T(8,128)}, f32[40,384]{1,0:T(8,128)S(1)}) custom-call(f32[17,4,3,56,128]{4,3,2,1,0:T(8,128)S(1)} %get-tuple-element.25.v_ref, f32[4,3,56,128]{3,2,1,0:T(8,128)S(1)} %get-tuple-element.27.vt_ref, f32[3,68,128]{2,1,0:T(8,128)S(1)} %collective-permute-done.6.left_ref, ...), custom_call_target="tpu_custom_call" | custom-call | tf_op jit(solution)/shard_map/pallas_call | solution.py:19
  48.0 0.1 all_to_all.13
  48.1 12.1 %all_to_all.16 = f32[32,1,480]{2,1,0:T(1,128)S(1)} all-to-all(f32[32,1,480]{2,1,0:T(1,128)S(1)} %all_to_all.13), channel_id=1, replica_groups=mesh['tile'=4,'lev'=4,'sec'=2] {'tile','lev','sec'}, dimensions={0} | all-to-all | bytes 122880 | tf_op jit(solution)/shard_map/all_to_all | solution.py:375
  60.3 0.7 broadcast_in_dim.25
  60.9 3.4 %all-to-all-start.1 = ((f32[8,1,1920]{2,1,0:T(1,128)}), f32[8,1,1920]{2,1,0:T(1,128)S(1)}, u32[]{:S(2)}, u32[]{:S(2)}) async-start(f32[8,1,1920]{2,1,0:T(1,128)} %broadcast_in_dim.25), calls=%async_computation.1 | async-start | bytes 122880 | tf_op jit(solution)/shard_map/all_to_all | solution.py:380
  64.6 6.5 %all-to-all-done.1 = f32[8,1,1920]{2,1,0:T(1,128)S(1)} async-done(((f32[8,1,1920]{2,1,0:T(1,128)}), f32[8,1,1920]{2,1,0:T(1,128)S(1)}, u32[]{:S(2)}, u32[]{:S(2)}) %all-to-all-start.1) | async-done | bytes 61472 | tf_op jit(solution)/shard_map/all_to_all | solution.py:380
  71.1 3.3 %shard_map.110 = f32[120,128]{1,0:T(8,128)} custom-call(s32[120,128]{1,0:T(8,128)S(1)} %reshape.38.cells_ref, f32[120,128]{1,0:T(8,128)S(1)} %bitcast.11), custom_call_target="tpu_custom_call" | custom-call | tf_op jit(solution)/shard_map/pallas_call | solution.py:19
  (39 shorter events, 0.8 us)
Async XLA Ops:
  0.6 20.1 %copy-start = (s32[4,2]{0,1:T(2,128)S(1)}, s32[4,2]{0,1:T(2,128)}, u32[]{:S(2)}) copy-start(s32[4,2]{0,1:T(2,128)} %param.14) | copy-start | bytes 100
  0.6 1.3 %copy-start.1 = (s32[18,40,384]{2,1,0:T(8,128)S(1)}, s32[18,40,384]{2,1,0:T(8,128)}, u32[]{:S(2)}) copy-start(s32[18,40,384]{2,1,0:T(8,128)} %code_ref.9) | copy-start | bytes 3317764
  1.9 1.1 %copy-start.6 = (bf16[18,40,384]{2,1,0:T(8,128)(2,1)S(1)}, bf16[18,40,384]{2,1,0:T(8,128)(2,1)}, u32[]{:S(2)}) copy-start(bf16[18,40,384]{2,1,0:T(8,128)(2,1)} %mf_ref.5) | copy-start | bytes 1658884
  3.0 1.1 %copy-start.8 = (bf16[18,40,384]{2,1,0:T(8,128)(2,1)S(1)}, bf16[18,40,384]{2,1,0:T(8,128)(2,1)}, u32[]{:S(2)}) copy-start(bf16[18,40,384]{2,1,0:T(8,128)(2,1)} %cy_ref.5) | copy-start | bytes 1658884
  4.0 2.3 %copy-start.11 = (f32[4,18,40,384]{3,2,1,0:T(8,128)S(1)}, f32[4,18,40,384]{3,2,1,0:T(8,128)}, u32[]{:S(2)}) copy-start(f32[4,18,40,384]{3,2,1,0:T(8,128)} %f_hbm.1) | copy-start | bytes 13271044
  6.3 16.3 %copy-start.2 = (s32[18,40,384]{2,1,0:T(8,128)S(1)}, s32[18,40,384]{2,1,0:T(8,128)}, u32[]{:S(2)}) copy-start(s32[18,40,384]{2,1,0:T(8,128)} %code_ref.9) | copy-start | bytes 3317764
  6.3 16.3 %copy-start.10 = (bf16[18,40,384]{2,1,0:T(8,128)(2,1)S(1)}, bf16[18,40,384]{2,1,0:T(8,128)(2,1)}, u32[]{:S(2)}) copy-start(bf16[18,40,384]{2,1,0:T(8,128)(2,1)} %cx_ref.5) | copy-start | bytes 1658884
  6.3 23.8 %copy-start.7 = (bf16[18,40,384]{2,1,0:T(8,128)(2,1)S(1)}, bf16[18,40,384]{2,1,0:T(8,128)(2,1)}, u32[]{:S(2)}) copy-start(bf16[18,40,384]{2,1,0:T(8,128)(2,1)} %mf_ref.5) | copy-start | bytes 1658884
  6.3 23.8 %copy-start.9 = (bf16[18,40,384]{2,1,0:T(8,128)(2,1)S(1)}, bf16[18,40,384]{2,1,0:T(8,128)(2,1)}, u32[]{:S(2)}) copy-start(bf16[18,40,384]{2,1,0:T(8,128)(2,1)} %cy_ref.5) | copy-start | bytes 1658884
  13.8 2.5 %copy-start.3 = (f32[17,4,3,56,128]{4,3,2,1,0:T(8,128)}, f32[17,4,3,56,128]{4,3,2,1,0:T(8,128)S(1)}, u32[]{:S(2)}) copy-start(f32[17,4,3,56,128]{4,3,2,1,0:T(8,128)S(1)} %get-tuple-element.18.v_ref) | copy-start | bytes 17547268
  16.4 5.0 %collective-permute-start.1 = (f32[3,68,128]{2,1,0:T(8,128)}, f32[3,68,128]{2,1,0:T(8,128)S(1)}, u32[]{:S(2)}, u32[]{:S(2)}) collective-permute-start(f32[3,68,128]{2,1,0:T(8,128)} %get-tuple-element.21), channel_id=1, source_target_pairs={{0,8},{8,16},{16,24},{24,0},{1,9},{9,17},{17,25},{25,1},{2,10},{10... | collective-permute-start | bytes 313352 | tf_op jit(solution)/shard_map/ppermute | solution.py:396
  16.8 5.7 %collective-permute-start.2 = (f32[3,68,128]{2,1,0:T(8,128)}, f32[3,68,128]{2,1,0:T(8,128)S(1)}, u32[]{:S(2)}, u32[]{:S(2)}) collective-permute-start(f32[3,68,128]{2,1,0:T(8,128)} %get-tuple-element.22), channel_id=1, source_target_pairs={{8,0},{16,8},{24,16},{0,24},{9,1},{17,9},{25,17},{1,25},{10,2},{18... | collective-permute-start | bytes 313352 | tf_op jit(solution)/shard_map/ppermute | solution.py:396
  19.4 10.6 %collective-permute-start = (f32[4,40,384]{2,1,0:T(8,128)}, f32[4,40,384]{2,1,0:T(8,128)S(1)}, u32[]{:S(2)}, u32[]{:S(2)}) collective-permute-start(f32[4,40,384]{2,1,0:T(8,128)} %slice_bitcast_fusion), channel_id=1, source_target_pairs={{2,0},{4,2},{6,4},{3,1},{5,3},{7,5},{10,8},{12,10},{14,12},{11,9},... | collective-permute-start | bytes 737288 | tf_op jit(solution)/shard_map/ppermute | solution.py:401
  22.6 2.7 %copy-start.4 = (f32[17,4,3,56,128]{4,3,2,1,0:T(8,128)S(1)}, f32[17,4,3,56,128]{4,3,2,1,0:T(8,128)}, u32[]{:S(2)}) copy-start(f32[17,4,3,56,128]{4,3,2,1,0:T(8,128)} %copy-done.3) | copy-start | bytes 17547268
  25.2 8.2 %copy-start.5 = (f32[17,4,3,56,128]{4,3,2,1,0:T(8,128)S(1)}, f32[17,4,3,56,128]{4,3,2,1,0:T(8,128)}, u32[]{:S(2)}) copy-start(f32[17,4,3,56,128]{4,3,2,1,0:T(8,128)} %copy-done.3) | copy-start | bytes 17547268
  25.3 16.2 %collective-permute-start.5 = (f32[4,40,384]{2,1,0:T(8,128)S(1)}, f32[4,40,384]{2,1,0:T(8,128)S(1)}, u32[]{:S(2)}, u32[]{:S(2)}) collective-permute-start(f32[4,40,384]{2,1,0:T(8,128)S(1)} %shard_map.107), channel_id=1, source_target_pairs={{2,0},{4,2},{6,4},{3,1},{5,3},{7,5},{10,8},{12,10},{14,12},{11,9},... | collective-permute-start | bytes 737288 | tf_op jit(solution)/shard_map/ppermute | solution.py:401
  30.3 3.1 %collective-permute-start.3 = (f32[3,4,128]{2,1,0:T(4,128)S(1)}, f32[3,4,128]{2,1,0:T(4,128)S(1)}, u32[]{:S(2)}, u32[]{:S(2)}) collective-permute-start(f32[3,4,128]{2,1,0:T(4,128)S(1)} %get-tuple-element.23), channel_id=1, source_target_pairs={{0,8},{8,16},{16,24},{24,0},{1,9},{9,17},{17,25},{25,1},{2,10},{10... | collective-permute-start | bytes 18440 | tf_op jit(solution)/shard_map/ppermute | solution.py:396
  30.4 3.1 %collective-permute-start.4 = (f32[3,4,128]{2,1,0:T(4,128)S(1)}, f32[3,4,128]{2,1,0:T(4,128)S(1)}, u32[]{:S(2)}, u32[]{:S(2)}) collective-permute-start(f32[3,4,128]{2,1,0:T(4,128)S(1)} %get-tuple-element.24), channel_id=1, source_target_pairs={{8,0},{16,8},{24,16},{0,24},{9,1},{17,9},{25,17},{1,25},{10,2},{18... | collective-permute-start | bytes 18440 | tf_op jit(solution)/shard_map/ppermute | solution.py:396
  33.4 11.6 %copy-start.14 = (f32[18]{0:T(128)S(1)}, f32[18]{0:T(128)}, u32[]{:S(2)}) copy-start(f32[18]{0:T(128)} %param.15) | copy-start | bytes 220
  33.4 11.6 %copy-start.12 = (f32[4,40,384]{2,1,0:T(8,128)S(1)}, f32[4,40,384]{2,1,0:T(8,128)}, u32[]{:S(2)}) copy-start(f32[4,40,384]{2,1,0:T(8,128)} %share_ref.1) | copy-start | bytes 737284
  39.4 5.6 %collective-permute-start.6 = (f32[3,68,128]{2,1,0:T(8,128)S(1)}, f32[3,68,128]{2,1,0:T(8,128)S(1)}, u32[]{:S(2)}, u32[]{:S(2)}) collective-permute-start(f32[3,68,128]{2,1,0:T(8,128)S(1)} %get-tuple-element.28), channel_id=1, source_target_pairs={{0,8},{8,16},{16,24},{24,0},{1,9},{9,17},{17,25},{25,1},{2,10},{10... | collective-permute-start | bytes 313352 | tf_op jit(solution)/shard_map/ppermute | solution.py:396
  40.3 4.7 %collective-permute-start.7 = (f32[3,68,128]{2,1,0:T(8,128)S(1)}, f32[3,68,128]{2,1,0:T(8,128)S(1)}, u32[]{:S(2)}, u32[]{:S(2)}) collective-permute-start(f32[3,68,128]{2,1,0:T(8,128)S(1)} %get-tuple-element.29), channel_id=1, source_target_pairs={{8,0},{16,8},{24,16},{0,24},{9,1},{17,9},{25,17},{1,25},{10,2},{18... | collective-permute-start | bytes 313352 | tf_op jit(solution)/shard_map/ppermute | solution.py:396
  41.8 3.2 %collective-permute-start.8 = (f32[3,4,128]{2,1,0:T(4,128)S(1)}, f32[3,4,128]{2,1,0:T(4,128)S(1)}, u32[]{:S(2)}, u32[]{:S(2)}) collective-permute-start(f32[3,4,128]{2,1,0:T(4,128)S(1)} %get-tuple-element.30), channel_id=1, source_target_pairs={{0,8},{8,16},{16,24},{24,0},{1,9},{9,17},{17,25},{25,1},{2,10},{10... | collective-permute-start | bytes 18440 | tf_op jit(solution)/shard_map/ppermute | solution.py:396
  41.8 3.2 %collective-permute-start.9 = (f32[3,4,128]{2,1,0:T(4,128)S(1)}, f32[3,4,128]{2,1,0:T(4,128)S(1)}, u32[]{:S(2)}, u32[]{:S(2)}) collective-permute-start(f32[3,4,128]{2,1,0:T(4,128)S(1)} %get-tuple-element.31), channel_id=1, source_target_pairs={{8,0},{16,8},{24,16},{0,24},{9,1},{17,9},{25,17},{1,25},{10,2},{18... | collective-permute-start | bytes 18440 | tf_op jit(solution)/shard_map/ppermute | solution.py:396
  45.1 19.2 %copy-start.13 = (s32[4,3840]{1,0:T(4,128)S(1)}, s32[4,3840]{1,0:T(4,128)}, u32[]{:S(2)}) copy-start(s32[4,3840]{1,0:T(4,128)} %param.17) | copy-start | bytes 184324
  60.9 10.2 %all-to-all-start.1 = ((f32[8,1,1920]{2,1,0:T(1,128)}), f32[8,1,1920]{2,1,0:T(1,128)S(1)}, u32[]{:S(2)}, u32[]{:S(2)}) async-start(f32[8,1,1920]{2,1,0:T(1,128)} %broadcast_in_dim.25), calls=%async_computation.1 | async-start | bytes 122880 | tf_op jit(solution)/shard_map/all_to_all | solution.py:380

commit v3 on v2

--- a/solution.py
+++ b/solution.py
@@ -22,8 +22,17 @@
         in_specs=in_specs,
         out_specs=out_specs,
         scratch_shapes=list(scratch),
+        cost_estimate=pl.CostEstimate(flops=1, transcendentals=0, bytes_accessed=1),
         compiler_params=pltpu.CompilerParams(vmem_limit_bytes=mib * MIB),
     )(*operands)
+
+
+def in_hbm(*arrays):
+    return tuple(pltpu.with_memory_space_constraint(a, pltpu.HBM) for a in arrays)
+
+
+def kept(*shape):
+    return pltpu.VMEM(shape, jnp.float32)
 
 
 def f32(*shape):
@@ -116,9 +125,9 @@
 
 
 def lower_kernel(
-    f_hbm, mf_hbm, cy_hbm, code_hbm,
-    v_ref, first_ref, last_ref, top_ref,
-    f_ref, mf_ref, cy_ref, code_ref, sems,
+    f_hbm, mf_hbm, cy_hbm, code_hbm, cx_hbm,
+    v_ref, first_ref, last_ref, top_ref, mf_ref, cy_ref, code_ref, cx_ref,
+    f_ref, sems,
 ):
     sectors, levels, columns, width = f_hbm.shape
     tiles, strips = width // LANES, columns // ROWS
@@ -131,12 +140,15 @@
 
     fetch_mf = pltpu.make_async_copy(mf_hbm, mf_ref, sems.at[2, 0])
     fetch_cy = pltpu.make_async_copy(cy_hbm, cy_ref, sems.at[2, 1])
+    fetch_cx = pltpu.make_async_copy(cx_hbm, cx_ref, sems.at[2, 2])
     fetch(0).start()
     fetch_mf.start()
     fetch_cy.start()
     for k in range(levels - 1):
         fetch_code(k).start()
         fetch(k + 1).start()
+    fetch_code(levels - 1).start()
+    fetch_cx.start()
     fetch(0).wait()
     fetch_mf.wait()
     fetch_cy.wait()
@@ -164,29 +176,8 @@
 
     lax.fori_loop(0, levels - 1, level, 0)
     top_ref[...] = f_ref[levels - 1]
-
-
-def upper_kernel(bit, here_ref, above_ref, mf_ref, cy_ref, code_ref, v_ref, first_ref, last_ref):
-    sectors, columns, width = above_ref.shape
-    level = mf_ref.shape[0] - 1
-    tiles, strips = width // LANES, columns // ROWS
-    at_top = lax.axis_index("lev") == lax.axis_size("lev") - 1
-    mf = mf_ref[level].astype(jnp.float32)
-    cy = cy_ref[level].astype(jnp.float32)
-    codes = code_ref[level]
-    for xt in range(strips):
-        factors = second_weights(cy, codes, bit, xt, tiles)
-        rows = slice(xt * ROWS, (xt + 1) * ROWS)
-        for s in range(sectors):
-            parts = []
-            for j in range(tiles):
-                lanes = slice(j * LANES, (j + 1) * LANES)
-                here = here_ref[s, rows, lanes]
-                upper = jnp.where(at_top, here, above_ref[s, rows, lanes])
-                parts.append(here + cut(mf, xt, j) * (upper - here))
-            for j, value in enumerate(second_sweep(parts, factors)):
-                store_padded(v_ref, (), s, j, xt, value)
-                store_rims(first_ref, last_ref, s, j, xt, strips - 1, value)
+    fetch_code(levels - 1).wait()
+    fetch_cx.wait()
 
 
 def first_weights(cx, codes, bit, xt, j):
@@ -194,7 +185,11 @@
     return ahead, back, (1.0 - ahead) - back
 
 
-def lowest_kernel(v_ref, left_ref, right_ref, seam_ref, cx_ref, code_ref, out_ref, lrow_ref, rrow_ref):
+def ends_kernel(
+    v_ref, left_ref, right_ref, seam_ref, cx_ref, code_ref, here_ref, above_ref, mf_ref, cy_ref,
+    out_ref, top_ref, first_ref, last_ref,
+    lrow_ref, rrow_ref,
+):
     _, sectors, tiles, _, _ = v_ref.shape
     columns = out_ref.shape[1]
     strips = columns // ROWS
@@ -215,64 +210,110 @@
                 )
                 out_ref[s, xt * ROWS : (xt + 1) * ROWS, j * LANES : (j + 1) * LANES] = value
 
+    level = mf_ref.shape[0] - 1
+    at_top = lax.axis_index("lev") == lax.axis_size("lev") - 1
+    mf = mf_ref[level].astype(jnp.float32)
+    cy = cy_ref[level].astype(jnp.float32)
+    codes = code_ref[level]
+    for xt in range(strips):
+        factors = second_weights(cy, codes, 3, xt, tiles)
+        rows = slice(xt * ROWS, (xt + 1) * ROWS)
+        for s in range(sectors):
+            parts = []
+            for j in range(tiles):
+                lanes = slice(j * LANES, (j + 1) * LANES)
+                here = here_ref[s, rows, lanes]
+                upper = jnp.where(at_top, here, above_ref[s, rows, lanes])
+                parts.append(here + cut(mf, xt, j) * (upper - here))
+            for j, value in enumerate(second_sweep(parts, factors)):
+                store_padded(top_ref, (), s, j, xt, value)
+                store_rims(first_ref, last_ref, s, j, xt, strips - 1, value)
+
 
 def middle_kernel(
-    v_ref, vt_ref, left_ref, right_ref, left_top_ref, right_top_ref, seam_ref,
-    cx_ref, mf_ref, cy_ref, code_ref,
+    v_ref, left_ref, right_ref, lowest_ref, seam_ref, cx_ref, mf_ref, cy_ref, code_ref,
     out_ref, first_ref, last_ref, top_ref,
-    lrow_ref, rrow_ref, ltop_ref, rtop_ref, a_ref,
+    lrow_ref, rrow_ref, a_ref,
 ):
     below, sectors, tiles, padded, _ = v_ref.shape
     strips = (padded - 2 * ROWS) // ROWS
     flip_left, flip_right = flags(seam_ref)
     turned(left_ref, flip_left, lrow_ref)
     turned(right_ref, flip_right, rrow_ref)
-    turned(left_top_ref, flip_left, ltop_ref)
-    turned(right_top_ref, flip_right, rtop_ref)
-
-    cx = cx_ref[below].astype(jnp.float32)
-    codes = code_ref[below]
-    for xt in range(strips):
+    for s in range(sectors):
         for j in range(tiles):
-            factors = first_weights(cx, codes, 2, xt, j)
-            for s in range(sectors):
-                value = first_sweep(
-                    lambda s, j, start: vt_ref[s, j, start : start + ROWS, :],
-                    s, j, xt, strips - 1, factors,
-                    lambda s, j: ltop_ref[j, s : s + 1, :],
-                    lambda s, j: rtop_ref[j, s : s + 1, :],
-                )
-                a_ref[below, s, j, xt * ROWS : (xt + 1) * ROWS, :] = value
-                top_ref[s, xt * ROWS : (xt + 1) * ROWS, j * LANES : (j + 1) * LANES] = value
-
-    def level(step, _):
-        k = below - 1 - step
-        cx = cx_ref[k].astype(jnp.float32)
+            a_ref[0, s, j] = lowest_ref[s, :, j * LANES : (j + 1) * LANES]
+
+    def level(k, _):
+        cx = cx_ref[k + 1].astype(jnp.float32)
         mf = mf_ref[k].astype(jnp.float32)
         cy = cy_ref[k].astype(jnp.float32)
-        codes = code_ref[k]
+        codes_x = code_ref[k + 1]
+        codes_y = code_ref[k]
+        slot = lax.rem(k, 2)
         for xt in range(strips):
-            along = [first_weights(cx, codes, 2, xt, j) for j in range(tiles)]
-            across = second_weights(cy, codes, 1, xt, tiles)
+            along = [first_weights(cx, codes_x, 2, xt, j) for j in range(tiles)]
+            across = second_weights(cy, codes_y, 1, xt, tiles)
             rows = slice(xt * ROWS, (xt + 1) * ROWS)
             for s in range(sectors):
                 parts = []
                 for j in range(tiles):
-                    here = first_sweep(
-                        lambda s, j, start: v_ref[k, s, j, start : start + ROWS, :],
+                    upper = first_sweep(
+                        lambda s, j, start: v_ref[k + 1, s, j, start : start + ROWS, :],
                         s, j, xt, strips - 1, along[j],
-                        lambda s, j: lrow_ref[j, pl.ds(k * sectors + s, 1), :],
-                        lambda s, j: rrow_ref[j, pl.ds(k * sectors + s, 1), :],
+                        lambda s, j: lrow_ref[j, pl.ds((k + 1) * sectors + s, 1), :],
+                        lambda s, j: rrow_ref[j, pl.ds((k + 1) * sectors + s, 1), :],
                     )
-                    upper = a_ref[k + 1, s, j, rows, :]
-                    a_ref[k, s, j, rows, :] = here
+                    here = a_ref[slot, s, j, rows, :]
+                    a_ref[1 - slot, s, j, rows, :] = upper
                     parts.append(here + cut(mf, xt, j) * (upper - here))
                 for j, value in enumerate(second_sweep(parts, across)):
                     store_padded(out_ref, (k,), s, j, xt, value)
                     store_rims(first_ref, last_ref, k * sectors + s, j, xt, strips - 1, value)
         return 0
 
-    lax.fori_loop(0, below, level, 0)
+    lax.fori_loop(0, below - 1, level, 0)
+    top_ref[...] = a_ref[(below - 1) % 2]
+
+
+def highest_kernel(
+    vt_ref, left_ref, right_ref, lower_ref, above_ref, seam_ref, cx_ref, mf_ref, cy_ref, code_ref,
+    out_ref, first_ref, last_ref,
+    lrow_ref, rrow_ref,
+):
+    sectors, tiles, padded, _ = vt_ref.shape
+    strips = (padded - 2 * ROWS) // ROWS
+    top = mf_ref.shape[0] - 1
+    at_top = lax.axis_index("lev") == lax.axis_size("lev") - 1
+    flip_left, flip_right = flags(seam_ref)
+    turned(left_ref, flip_left, lrow_ref)
+    turned(right_ref, flip_right, rrow_ref)
+    cx = cx_ref[top].astype(jnp.float32)
+    mixing = [mf_ref[top - 1].astype(jnp.float32), mf_ref[top].astype(jnp.float32)]
+    cys = [cy_ref[top - 1].astype(jnp.float32), cy_ref[top].astype(jnp.float32)]
+    codes = [code_ref[top - 1], code_ref[top]]
+    for xt in range(strips):
+        along = [first_weights(cx, codes[1], 2, xt, j) for j in range(tiles)]
+        across = [second_weights(cys[i], codes[i], 1, xt, tiles) for i in range(2)]
+        rows = slice(xt * ROWS, (xt + 1) * ROWS)
+        for s in range(sectors):
+            low, high = [], []
+            for j in range(tiles):
+                here = first_sweep(
+                    lambda s, j, start: vt_ref[s, j, start : start + ROWS, :],
+                    s, j, xt, strips - 1, along[j],
+                    lambda s, j: lrow_ref[j, s : s + 1, :],
+                    lambda s, j: rrow_ref[j, s : s + 1, :],
+                )
+                lower = lower_ref[s, j, rows, :]
+                low.append(lower + cut(mixing[0], xt, j) * (here - lower))
+                upper = above_ref[s, rows, j * LANES : (j + 1) * LANES]
+                upper = jnp.where(at_top, here, upper)
+                high.append(here + cut(mixing[1], xt, j) * (upper - here))
+            for i, parts in enumerate((low, high)):
+                for j, value in enumerate(second_sweep(parts, across[i])):
+                    store_padded(out_ref, (i,), s, j, xt, value)
+                    store_rims(first_ref, last_ref, i * sectors + s, j, xt, strips - 1, value)
 
 
 def final_kernel(
@@ -314,13 +355,14 @@
                     sens_ref[rows, lanes] += factor * total
         send(k).start()
 
-    level(
-        below,
-        lambda s, j, start: vt_ref[s, j, start : start + ROWS, :],
-        lambda s, j: ltop_ref[j, s : s + 1, :],
-        lambda s, j: rtop_ref[j, s : s + 1, :],
-        True,
-    )
+    for i in range(2):
+        level(
+            below + i,
+            lambda s, j, start: vt_ref[i, s, j, start : start + ROWS, :],
+            lambda s, j: ltop_ref[j, i * sectors + s : i * sectors + s + 1, :],
+            lambda s, j: rtop_ref[j, i * sectors + s : i * sectors + s + 1, :],
+            i == 0,
+        )
 
     def step(k, _):
         level(
@@ -333,11 +375,12 @@
         return 0
 
     lax.fori_loop(0, below, step, 0)
-    for k in range(below + 1):
+    for k in range(below + 2):
         send(k).wait()
 
 
-def scatter_kernel(cells_ref, values_ref, out_ref):
+def scatter_kernel(cells_ref, *refs):
+    *value_refs, out_ref = refs
     rows, lanes = out_ref.shape
     count = cells_ref.shape[0]
     high_iota = lax.broadcasted_iota(jnp.int32, (rows, lanes), 0)
@@ -347,7 +390,8 @@
         lefts, rights = [], []
         for row in (pair, pair + 1):
             cells = cells_ref[row : row + 1, :]
-            value = values_ref[row : row + 1, :]
+            part, line = divmod(row, value_refs[0].shape[0])
+            value = value_refs[part][line : line + 1, :]
             coarse = value.astype(jnp.bfloat16).astype(jnp.float32)
             fine = value - coarse
             here = jnp.right_shift(cells, 7) == high_iota
@@ -376,15 +420,23 @@
         sent, ("tile", "lev", "sec"), split_axis=0, concat_axis=0, tiled=True
     )
     summed = jnp.sum(received.reshape(tiles, group, piece), axis=1)
-    copies = jnp.broadcast_to(summed.reshape(1, tiles * piece), (group, tiles * piece))
-    gathered = lax.all_to_all(copies, ("lev", "sec"), split_axis=0, concat_axis=0, tiled=True)
-    cells = flux_cell.reshape(tiles, group, piece).transpose(1, 0, 2)
+    own = summed.reshape(-1, LANES)
+    rank = lax.axis_index(("lev", "sec"))
+    parts = [own]
+    for apart in range(1, group):
+        pairs = [(i, i ^ apart) for i in range(group)]
+        parts.append(lax.ppermute(own, ("lev", "sec"), pairs))
+    cells = flux_cell.reshape(tiles, group, piece).transpose(1, 0, 2).reshape(group, -1, LANES)
+    order = jnp.bitwise_xor(rank, jnp.arange(group, dtype=jnp.int32))
+    cells = jnp.concatenate(
+        [lax.dynamic_slice_in_dim(cells, order[i], 1, axis=0)[0] for i in range(group)], axis=0
+    )
     out = call(
         scatter_kernel,
         f32(FL_DEV // LANES, LANES),
-        [VM, VM],
+        [VM] * (group + 1),
         VM,
-        (cells.reshape(-1, LANES), gathered.reshape(-1, LANES)),
+        (cells, *parts),
     )
     return out.reshape(-1)
 
@@ -407,73 +459,73 @@
     sectors, levels, columns, width = forcing.shape
     tiles, below = width // LANES, levels - 1
     padded = columns + 2 * ROWS
-    field = f32(below, sectors, tiles, padded, LANES)
-    field_top = f32(sectors, tiles, padded, LANES)
-    plane = f32(sectors, columns, width)
-    rim = f32(tiles, below * sectors, LANES)
-    rim_top = f32(tiles, sectors, LANES)
-    rim_scratch = pltpu.VMEM(rim.shape, jnp.float32)
-    top_scratch = pltpu.VMEM(rim_top.shape, jnp.float32)
+    field = kept(below, sectors, tiles, padded, LANES)
+    field_top = kept(sectors, tiles, padded, LANES)
+    plane = kept(sectors, columns, width)
+    rim = kept(tiles, below * sectors, LANES)
+    rim_top = kept(tiles, sectors, LANES)
+    rim_next = kept(tiles, (below - 1) * sectors, LANES)
+    rim_pair = kept(tiles, 2 * sectors, LANES)
+    rim_scratch = pltpu.VMEM((tiles, below * sectors, LANES), jnp.float32)
 
     seam = lax.dynamic_index_in_dim(seam_code, lax.axis_index("tile"), 0, keepdims=False)
     seam = jnp.broadcast_to(seam[:, None, None], (2, ROWS, LANES))
     weight = jnp.broadcast_to(level_weight[:, None], (levels, LANES))
 
     above = from_above(forcing[:, 0])
-    v, first, last, top = call(
+    narrow = pltpu.VMEM((levels, columns, width), jnp.bfloat16)
+    v, first, last, top, mass_flux, courant_y, limiter_code, courant_x = call(
         lower_kernel,
-        (field, rim, rim, plane),
-        [HBM] * 4,
-        [VM] * 4,
-        (forcing, mass_flux, courant_y, limiter_code),
+        (
+            field, rim, rim, plane,
+            narrow, narrow, pltpu.VMEM((levels, columns, width), jnp.int32), narrow,
+        ),
+        [HBM] * 5,
+        [VM] * 8,
+        in_hbm(forcing, mass_flux, courant_y, limiter_code, courant_x),
         [
             pltpu.VMEM((levels, sectors, columns, width), jnp.float32),
-            pltpu.VMEM((levels, columns, width), jnp.bfloat16),
-            pltpu.VMEM((levels, columns, width), jnp.bfloat16),
-            pltpu.VMEM((below, columns, width), jnp.int32),
             pltpu.SemaphoreType.DMA((3, levels)),
         ],
     )
     left, right = around(first, last)
-    lowest = call(
-        lowest_kernel,
-        plane,
-        [VM] * 6,
-        VM,
-        (v, left, right, seam, courant_x, limiter_code),
+    lowest, vt, first_top, last_top = call(
+        ends_kernel,
+        (plane, field_top, rim_top, rim_top),
+        [VM] * 10,
+        [VM] * 4,
+        (
+            v, left, right, seam, courant_x, limiter_code, top, above, mass_flux, courant_y,
+        ),
         [pltpu.VMEM((tiles, ROWS, LANES), jnp.float32)] * 2,
     )
-    vt, first_top, last_top = call(
-        functools.partial(upper_kernel, 3),
-        (field_top, rim_top, rim_top),
-        [VM] * 5,
-        [VM] * 3,
-        (top, above, mass_flux, courant_y, limiter_code),
-    )
+    above = from_above(lowest)
     left_top, right_top = around(first_top, last_top)
-    above = from_above(lowest)
 
     v, first, last, top = call(
         middle_kernel,
-        (field, rim, rim, plane),
-        [VM] * 11,
+        (
+            kept(below - 1, sectors, tiles, padded, LANES),
+            rim_next,
+            rim_next,
+            kept(sectors, tiles, columns, LANES),
+        ),
+        [VM] * 9,
         [VM] * 4,
+        (v, left, right, lowest, seam, courant_x, mass_flux, courant_y, limiter_code),
+        [rim_scratch, rim_scratch, pltpu.VMEM((2, sectors, tiles, columns, LANES), jnp.float32)],
+    )
+    left, right = around(first, last)
+    vt, first_top, last_top = call(
+        highest_kernel,
+        (kept(2, sectors, tiles, padded, LANES), rim_pair, rim_pair),
+        [VM] * 10,
+        [VM] * 3,
         (
-            v, vt, left, right, left_top, right_top, seam,
+            vt, left_top, right_top, top, above, seam,
             courant_x, mass_flux, courant_y, limiter_code,
         ),
-        [
-            rim_scratch, rim_scratch, top_scratch, top_scratch,
-            pltpu.VMEM((levels, sectors, tiles, columns, LANES), jnp.float32),
-        ],
-    )
-    left, right = around(first, last)
-    vt, first_top, last_top = call(
-        functools.partial(upper_kernel, 1),
-        (field_top, rim_top, rim_top),
-        [VM] * 5,
-        [VM] * 3,
-        (top, above, mass_flux, courant_y, limiter_code),
+        [pltpu.VMEM((tiles, sectors, LANES), jnp.float32)] * 2,
     )
     left_top, right_top = around(first_top, last_top)
     adjoint, sensitivity = call(
@@ -486,7 +538,10 @@
             courant_x, limiter_code, weight, sector_share,
         ),
         [
-            rim_scratch, rim_scratch, top_scratch, top_scratch,
+            pltpu.VMEM((tiles, (below - 1) * sectors, LANES), jnp.float32),
+            pltpu.VMEM((tiles, (below - 1) * sectors, LANES), jnp.float32),
+            pltpu.VMEM((tiles, 2 * sectors, LANES), jnp.float32),
+            pltpu.VMEM((tiles, 2 * sectors, LANES), jnp.float32),
             pltpu.VMEM((levels, sectors, columns, width), jnp.float32),
             pltpu.SemaphoreType.DMA((levels,)),
         ],

time: 74.8 us -> 89.4 us (1.20)
  starting transfers between devices: 14.3 us -> 30 us
  between operations: 0.81 us -> 16.1 us
  blocking collectives: 12.1 us -> 0 us
  local copies, waits for them, and re-layouts: 13 us -> 9.8 us
  Pallas kernels: 20.2 us -> 17.6 us
  waiting for transfers between devices: 14 us -> 15.5 us
    all_to_all x1 -> x0, blocking collectives: 12.1 us -> none  [remapped(): lax.all_to_all(sent, ('tile', 'lev', 'sec'), split_axis=0, concat_axis=0,...]
    ppermute x0 -> x7, starting transfers between devices: none -> 11.2 us  [remapped(): parts.append(lax.ppermute(own, ('lev', 'sec'), pairs))]
    unnamed x30 -> x12, local copies, waits for them, and re-layouts: 10.8 us -> 5.21 us
    all_to_all x1, starting transfers between devices: 3.35 us -> 7.67 us  [remapped(): lax.all_to_all(sent, ('tile', 'lev', 'sec'), split_axis=0, concat_axis=0,...]
    ppermute x2, waiting for transfers between devices: 3.19 us -> 0.01 us  [from_above(): return lax.ppermute(value, 'lev', [(i + 1, i) for i in range(count - 1)])]
    pallas_call x7 -> x6, Pallas kernels: 20.2 us -> 17.6 us  [call(): pl.pallas_call(kernel, out_shape=out_shape, in_specs=in_specs, out_specs=...]
    ppermute x8, waiting for transfers between devices: 4.32 us -> 6.31 us  [around(): return (lax.ppermute(last, 'tile', up), lax.ppermute(first, 'tile', down))]
    ppermute x0 -> x7, waiting for transfers between devices: none -> 1.92 us  [remapped(): parts.append(lax.ppermute(own, ('lev', 'sec'), pairs))]
  transfers between devices with their start and end apart: 11 -> 18, of which waited for: 6 -> 8; matrix products, arithmetic and copies ran while one was open for 2% -> 2% of each run, Pallas kernels for 9% -> 13%
where the time goes in v3:
time: 89.4 us; the launch traced here: 89 us
  starting transfers between devices  30 us (34%)
  Pallas kernels  17.6 us (20%)
  between operations  16.1 us (18%)
  waiting for transfers between devices  15.5 us (17%)
  local copies, waits for them, and re-layouts  9.8 us (11%)
    pallas_call x6, Pallas kernels, call(): pl.pallas_call(kernel, out_shape=out_shape, in_specs=in_specs, out_specs=...  17.6 us
    ppermute x7, starting transfers between devices, remapped(): parts.append(lax.ppermute(own, ('lev', 'sec'), pairs))  11.2 us
    ppermute x8, starting transfers between devices, around(): return (lax.ppermute(last, 'tile', up), lax.ppermute(first, 'tile', down))  8.41 us
    all_to_all x1, starting transfers between devices, remapped(): lax.all_to_all(sent, ('tile', 'lev', 'sec'), split_axis=0, concat_axis=0,...  7.67 us
    all_to_all x1, waiting for transfers between devices, remapped(): lax.all_to_all(sent, ('tile', 'lev', 'sec'), split_axis=0, concat_axis=0,...  7.26 us
    ppermute x8, waiting for transfers between devices, around(): return (lax.ppermute(last, 'tile', up), lax.ppermute(first, 'tile', down))  6.31 us
    unnamed x12, local copies, waits for them, and re-layouts  5.21 us
    ppermute x2, starting transfers between devices, from_above(): return lax.ppermute(value, 'lev', [(i + 1, i) for i in range(count - 1)])  2.7 us
  transfers between devices with their start and end apart: 18, of which 8 were waited for; matrix products, arithmetic and copies ran while one was open for 2% of the time, Pallas kernels for 13%

profile of v3, /device:TPU:0, one launch (start us, length us, event | category | flops | bytes accessed | tf_op | source)
XLA Modules:
  0.0 89.0 jit_solution(4011648020440913486)
XLA Ops:
  0.6 1.7 %slice_bitcast_fusion = f32[4,40,384]{2,1,0:T(8,128)} fusion(f32[4,18,40,384]{3,2,1,0:T(8,128)} %f_hbm.1), kind=kLoop, calls=%fused_computation | loop fusion | bytes 491520 | tf_op jit(solution)/shard_map/squeeze | solution.py:475
  2.3 1.3 %collective-permute-start.2 = (f32[4,40,384]{2,1,0:T(8,128)}, f32[4,40,384]{2,1,0:T(8,128)S(1)}, u32[]{:S(2)}, u32[]{:S(2)}) collective-permute-start(f32[4,40,384]{2,1,0:T(8,128)} %slice_bitcast_fusion), channel_id=1, source_target_pairs={{2,0},{4,2},{6,4},{3,1},{5,3},{7,5},{10,8},{12,10},{14,12},{11,9},... | collective-permute-start | bytes 737288 | tf_op jit(solution)/shard_map/ppermute | solution.py:453
  3.6 6.1 %shard_map.104 = (f32[17,4,3,56,128]{4,3,2,1,0:T(8,128)S(1)}, f32[3,68,128]{2,1,0:T(8,128)}, f32[3,68,128]{2,1,0:T(8,128)}, f32[4,40,384]{2,1,0:T(8,128)S(1)}, b...) custom-call(f32[4,18,40,384]{3,2,1,0:T(8,128)} %f_hbm.1, ...), custom_call_target="tpu_custom_call" | custom-call | flops 1 | bytes 1 | tf_op jit(solution)/shard_map/pallas_call | solution.py:19
  9.7 2.5 %copy-done.1 = f32[17,4,3,56,128]{4,3,2,1,0:T(8,128)} copy-done((f32[17,4,3,56,128]{4,3,2,1,0:T(8,128)}, f32[17,4,3,56,128]{4,3,2,1,0:T(8,128)S(1)}, u32[]{:S(2)}) %copy-start.1) | copy-done | bytes 5849112
  12.2 0.5 collective-permute-start
  12.7 1.9 %collective-permute-start.1 = (f32[3,68,128]{2,1,0:T(8,128)}, f32[3,68,128]{2,1,0:T(8,128)S(1)}, u32[]{:S(2)}, u32[]{:S(2)}) collective-permute-start(f32[3,68,128]{2,1,0:T(8,128)} %get-tuple-element.25), channel_id=1, source_target_pairs={{8,0},{16,8},{24,16},{0,24},{9,1},{17,9},{25,17},{1,25},{10,2},{18... | collective-permute-start | bytes 313352 | tf_op jit(solution)/shard_map/ppermute | solution.py:448
  14.8 2.5 %collective-permute-done.left_ref = f32[3,68,128]{2,1,0:T(8,128)S(1)} collective-permute-done((f32[3,68,128]{2,1,0:T(8,128)}, f32[3,68,128]{2,1,0:T(8,128)S(1)}, u32[]{:S(2)}, u32[]{:S(2)}) %collective-permute-start) | collective-permute-done | bytes 104480 | tf_op jit(solution)/shard_map/ppermute | solution.py:448
  17.3 1.1 %collective-permute-done.1.right_ref = f32[3,68,128]{2,1,0:T(8,128)S(1)} collective-permute-done((f32[3,68,128]{2,1,0:T(8,128)}, f32[3,68,128]{2,1,0:T(8,128)S(1)}, u32[]{:S(2)}, u32[]{:S(2)}) %collective-permute-start.1) | collective-permute-done | bytes 104480 | tf_op jit(solution)/shard_map/ppermute | solution.py:448
  18.4 2.7 %copy-done.2 = f32[17,4,3,56,128]{4,3,2,1,0:T(8,128)S(1)} copy-done((f32[17,4,3,56,128]{4,3,2,1,0:T(8,128)S(1)}, f32[17,4,3,56,128]{4,3,2,1,0:T(8,128)}, u32[]{:S(2)}) %copy-start.2) | copy-done | bytes 5849112
  21.4 1.4 %collective-permute-start.5 = (f32[4,40,384]{2,1,0:T(8,128)S(1)}, f32[4,40,384]{2,1,0:T(8,128)S(1)}, u32[]{:S(2)}, u32[]{:S(2)}) collective-permute-start(f32[4,40,384]{2,1,0:T(8,128)S(1)} %get-tuple-element.31.lowest_ref), channel_id=1, source_target_pairs={{2,0},{4,2},{6,4},{3,1},{5,3},{7,5},{10,8},{12,10},{14,12},{11,9},... | collective-permute-start | bytes 737288 | tf_op jit(solution)/shard_map/ppermute | solution.py:453
  22.8 4.6 %shard_map.106 = (f32[16,4,3,56,128]{4,3,2,1,0:T(8,128)S(1)}, f32[3,64,128]{2,1,0:T(8,128)S(1)}, f32[3,64,128]{2,1,0:T(8,128)S(1)}, f32[4,3,40,128]{3,2,1,0:T(8,128)S(1)}) custom-call(f32[17,4,3,56,128]{4,3,2,1,0:T(8,128)S(1)} %copy-done.2, f32[3,68,128]{2,1,0:T(8,128)S(1)} %collective-permute-done.left_ref, ...), custom_call_target="tpu_custom_call" | custom-call | flops 1 | bytes 1 | tf_op jit(solution)/shard_map/pallas_call | solution.py:19
  27.5 1.4 %collective-permute-start.6 = (f32[3,64,128]{2,1,0:T(8,128)S(1)}, f32[3,64,128]{2,1,0:T(8,128)S(1)}, u32[]{:S(2)}, u32[]{:S(2)}) collective-permute-start(f32[3,64,128]{2,1,0:T(8,128)S(1)} %get-tuple-element.38), channel_id=1, source_target_pairs={{0,8},{8,16},{16,24},{24,0},{1,9},{9,17},{17,25},{25,1},{2,10},{10... | collective-permute-start | bytes 294920 | tf_op jit(solution)/shard_map/ppermute | solution.py:448
  28.8 0.8 collective-permute-start.7
  30.0 1.4 %collective-permute-start.4 = (f32[3,4,128]{2,1,0:T(4,128)S(1)}, f32[3,4,128]{2,1,0:T(4,128)S(1)}, u32[]{:S(2)}, u32[]{:S(2)}) collective-permute-start(f32[3,4,128]{2,1,0:T(4,128)S(1)} %get-tuple-element.35), channel_id=1, source_target_pairs={{8,0},{16,8},{24,16},{0,24},{9,1},{17,9},{25,17},{1,25},{10,2},{18... | collective-permute-start | bytes 18440 | tf_op jit(solution)/shard_map/ppermute | solution.py:448
  31.4 1.3 %collective-permute-done.3.left_ref = f32[3,4,128]{2,1,0:T(4,128)S(1)} collective-permute-done((f32[3,4,128]{2,1,0:T(4,128)S(1)}, f32[3,4,128]{2,1,0:T(4,128)S(1)}, u32[]{:S(2)}, u32[]{:S(2)}) %collective-permute-start.3) | collective-permute-done | bytes 6176 | tf_op jit(solution)/shard_map/ppermute | solution.py:448
  33.2 2.1 %collective-permute-start.8 = (f32[3,8,128]{2,1,0:T(8,128)S(1)}, f32[3,8,128]{2,1,0:T(8,128)S(1)}, u32[]{:S(2)}, u32[]{:S(2)}) collective-permute-start(f32[3,8,128]{2,1,0:T(8,128)S(1)} %get-tuple-element.40), channel_id=1, source_target_pairs={{0,8},{8,16},{16,24},{24,0},{1,9},{9,17},{17,25},{25,1},{2,10},{10... | collective-permute-start | bytes 36872 | tf_op jit(solution)/shard_map/ppermute | solution.py:448
  35.3 1.1 %collective-permute-done.8.left_top_ref = f32[3,8,128]{2,1,0:T(8,128)S(1)} collective-permute-done((f32[3,8,128]{2,1,0:T(8,128)S(1)}, f32[3,8,128]{2,1,0:T(8,128)S(1)}, u32[]{:S(2)}, u32[]{:S(2)}) %collective-permute-start.8) | collective-permute-done | bytes 12320 | tf_op jit(solution)/shard_map/ppermute | solution.py:448
  36.8 2.9 %shard_map.108 = (f32[4,18,40,384]{3,2,1,0:T(8,128)}, f32[40,384]{1,0:T(8,128)S(1)}) custom-call(f32[16,4,3,56,128]{4,3,2,1,0:T(8,128)S(1)} %get-tuple-element.32.v_ref, f32[2,4,3,56,128]{4,3,2,1,0:T(8,128)S(1)} %get-tuple-element.37.vt_ref, f32[3,64,128]{2,1,0:T(8,128)S(1)} %collective-permute-done.6.left_ref, ...), custom_call_target="tpu_custom_call" | custom-call | flops 1 | bytes 1 | tf_op jit(solution)/shard_map/pallas_call | solution.py:19
  39.7 0.8 all_to_all.8
  40.4 7.7 %all-to-all-start = ((f32[32,1,480]{2,1,0:T(1,128)}), f32[32,1,480]{2,1,0:T(1,128)S(1)}, u32[]{:S(2)}, u32[]{:S(2)}) async-start(f32[32,1,480]{2,1,0:T(1,128)} %all_to_all.8), calls=%async_computation | async-start | bytes 131072 | tf_op jit(solution)/shard_map/all_to_all | solution.py:419
  48.1 7.3 %all-to-all-done = f32[32,1,480]{2,1,0:T(1,128)S(1)} async-done(((f32[32,1,480]{2,1,0:T(1,128)}), f32[32,1,480]{2,1,0:T(1,128)S(1)}, u32[]{:S(2)}, u32[]{:S(2)}) %all-to-all-start) | async-done | bytes 61472 | tf_op jit(solution)/shard_map/all_to_all | solution.py:419
  55.5 0.8 collective-permute-start.10
  56.3 0.6 collective-permute-start.11
  56.9 0.7 fusion.1
  73.1 2.2 %collective-permute-start.12 = (f32[15,128]{1,0:T(8,128)S(1)}, f32[15,128]{1,0:T(8,128)S(1)}, u32[]{:S(2)}, u32[]{:S(2)}) collective-permute-start(f32[15,128]{1,0:T(8,128)S(1)} %reshape.30.refs_0_), channel_id=1, source_target_pairs={{0,3},{1,2},{2,1},{3,0},{4,7},{5,6},{6,5},{7,4},{8,11},{9,10},{10,... | collective-permute-start | bytes 23048 | tf_op jit(solution)/shard_map/ppermute | solution.py:428
  75.3 0.8 collective-permute-start.13
  76.1 2.3 %collective-permute-start.14 = (f32[15,128]{1,0:T(8,128)S(1)}, f32[15,128]{1,0:T(8,128)S(1)}, u32[]{:S(2)}, u32[]{:S(2)}) collective-permute-start(f32[15,128]{1,0:T(8,128)S(1)} %reshape.30.refs_0_), channel_id=1, source_target_pairs={{0,5},{1,4},{2,7},{3,6},{4,1},{5,0},{6,3},{7,2},{8,13},{9,12},{10,... | collective-permute-start | bytes 23048 | tf_op jit(solution)/shard_map/ppermute | solution.py:428
  78.4 0.9 %collective-permute-start.15 = (f32[15,128]{1,0:T(8,128)S(1)}, f32[15,128]{1,0:T(8,128)S(1)}, u32[]{:S(2)}, u32[]{:S(2)}) collective-permute-start(f32[15,128]{1,0:T(8,128)S(1)} %reshape.30.refs_0_), channel_id=1, source_target_pairs={{0,6},{1,7},{2,4},{3,5},{4,2},{5,3},{6,0},{7,1},{8,14},{9,15},{10,... | collective-permute-start | bytes 23048 | tf_op jit(solution)/shard_map/ppermute | solution.py:428
  79.4 3.6 %collective-permute-start.16 = (f32[15,128]{1,0:T(8,128)S(1)}, f32[15,128]{1,0:T(8,128)S(1)}, u32[]{:S(2)}, u32[]{:S(2)}) collective-permute-start(f32[15,128]{1,0:T(8,128)S(1)} %reshape.30.refs_0_), channel_id=1, source_target_pairs={{0,7},{1,6},{2,5},{3,4},{4,3},{5,2},{6,1},{7,0},{8,15},{9,14},{10,... | collective-permute-start | bytes 23048 | tf_op jit(solution)/shard_map/ppermute | solution.py:428
  83.0 0.8 concatenate.3.cells_ref
  83.9 1.8 %collective-permute-done.16.refs_7_ = f32[15,128]{1,0:T(8,128)S(1)} collective-permute-done((f32[15,128]{1,0:T(8,128)S(1)}, f32[15,128]{1,0:T(8,128)S(1)}, u32[]{:S(2)}, u32[]{:S(2)}) %collective-permute-start.16) | collective-permute-done | bytes 7712 | tf_op jit(solution)/shard_map/ppermute | solution.py:428
  85.7 3.3 %shard_map.109 = f32[120,128]{1,0:T(8,128)} custom-call(s32[120,128]{1,0:T(8,128)S(1)} %concatenate.3.cells_ref, f32[15,128]{1,0:T(8,128)S(1)} %reshape.30.refs_0_, f32[15,128]{1,0:T(8,128)S(1)} %collective-permute-done.10.refs_1_, f32[15,128]{1,0:T(8,128)S(1)} %collective-permute-done.11.refs_2_, f32[15,128]{1,0:T(8,128)S(1)} %collective-permute-done.12.refs_3_, ...), custom_call_target="tpu_custom_call" | custom-call | flops 1 | bytes 1 | tf_op jit(solution)/shard_map/pallas_call | solution.py:19
  (36 shorter events, 2.2 us)
Async XLA Ops:
  0.6 14.0 %copy-start = (s32[4,2]{0,1:T(2,128)S(1)}, s32[4,2]{0,1:T(2,128)}, u32[]{:S(2)}) copy-start(s32[4,2]{0,1:T(2,128)} %param.14) | copy-start | bytes 100
  2.3 16.1 %collective-permute-start.2 = (f32[4,40,384]{2,1,0:T(8,128)}, f32[4,40,384]{2,1,0:T(8,128)S(1)}, u32[]{:S(2)}, u32[]{:S(2)}) collective-permute-start(f32[4,40,384]{2,1,0:T(8,128)} %slice_bitcast_fusion), channel_id=1, source_target_pairs={{2,0},{4,2},{6,4},{3,1},{5,3},{7,5},{10,8},{12,10},{14,12},{11,9},... | collective-permute-start | bytes 737288 | tf_op jit(solution)/shard_map/ppermute | solution.py:453
  9.7 2.5 %copy-start.1 = (f32[17,4,3,56,128]{4,3,2,1,0:T(8,128)}, f32[17,4,3,56,128]{4,3,2,1,0:T(8,128)S(1)}, u32[]{:S(2)}) copy-start(f32[17,4,3,56,128]{4,3,2,1,0:T(8,128)S(1)} %get-tuple-element.23.v_ref) | copy-start | bytes 17547268
  12.2 5.0 %collective-permute-start = (f32[3,68,128]{2,1,0:T(8,128)}, f32[3,68,128]{2,1,0:T(8,128)S(1)}, u32[]{:S(2)}, u32[]{:S(2)}) collective-permute-start(f32[3,68,128]{2,1,0:T(8,128)} %get-tuple-element.24), channel_id=1, source_target_pairs={{0,8},{8,16},{16,24},{24,0},{1,9},{9,17},{17,25},{25,1},{2,10},{10... | collective-permute-start | bytes 313352 | tf_op jit(solution)/shard_map/ppermute | solution.py:448
  12.7 5.7 %collective-permute-start.1 = (f32[3,68,128]{2,1,0:T(8,128)}, f32[3,68,128]{2,1,0:T(8,128)S(1)}, u32[]{:S(2)}, u32[]{:S(2)}) collective-permute-start(f32[3,68,128]{2,1,0:T(8,128)} %get-tuple-element.25), channel_id=1, source_target_pairs={{8,0},{16,8},{24,16},{0,24},{9,1},{17,9},{25,17},{1,25},{10,2},{18... | collective-permute-start | bytes 313352 | tf_op jit(solution)/shard_map/ppermute | solution.py:448
  18.4 2.7 %copy-start.2 = (f32[17,4,3,56,128]{4,3,2,1,0:T(8,128)S(1)}, f32[17,4,3,56,128]{4,3,2,1,0:T(8,128)}, u32[]{:S(2)}) copy-start(f32[17,4,3,56,128]{4,3,2,1,0:T(8,128)} %copy-done.1) | copy-start | bytes 17547268
  21.4 15.3 %copy-start.5 = (f32[18]{0:T(128)S(1)}, f32[18]{0:T(128)}, u32[]{:S(2)}) copy-start(f32[18]{0:T(128)} %param.15) | copy-start | bytes 220
  21.4 15.4 %copy-start.3 = (f32[4,40,384]{2,1,0:T(8,128)S(1)}, f32[4,40,384]{2,1,0:T(8,128)}, u32[]{:S(2)}) copy-start(f32[4,40,384]{2,1,0:T(8,128)} %share_ref.1) | copy-start | bytes 737284
  21.4 11.4 %collective-permute-start.5 = (f32[4,40,384]{2,1,0:T(8,128)S(1)}, f32[4,40,384]{2,1,0:T(8,128)S(1)}, u32[]{:S(2)}, u32[]{:S(2)}) collective-permute-start(f32[4,40,384]{2,1,0:T(8,128)S(1)} %get-tuple-element.31.lowest_ref), channel_id=1, source_target_pairs={{2,0},{4,2},{6,4},{3,1},{5,3},{7,5},{10,8},{12,10},{14,12},{11,9},... | collective-permute-start | bytes 737288 | tf_op jit(solution)/shard_map/ppermute | solution.py:453
  27.5 7.8 %collective-permute-start.6 = (f32[3,64,128]{2,1,0:T(8,128)S(1)}, f32[3,64,128]{2,1,0:T(8,128)S(1)}, u32[]{:S(2)}, u32[]{:S(2)}) collective-permute-start(f32[3,64,128]{2,1,0:T(8,128)S(1)} %get-tuple-element.38), channel_id=1, source_target_pairs={{0,8},{8,16},{16,24},{24,0},{1,9},{9,17},{17,25},{25,1},{2,10},{10... | collective-permute-start | bytes 294920 | tf_op jit(solution)/shard_map/ppermute | solution.py:448
  28.8 6.5 %collective-permute-start.7 = (f32[3,64,128]{2,1,0:T(8,128)S(1)}, f32[3,64,128]{2,1,0:T(8,128)S(1)}, u32[]{:S(2)}, u32[]{:S(2)}) collective-permute-start(f32[3,64,128]{2,1,0:T(8,128)S(1)} %get-tuple-element.39), channel_id=1, source_target_pairs={{8,0},{16,8},{24,16},{0,24},{9,1},{17,9},{25,17},{1,25},{10,2},{18... | collective-permute-start | bytes 294920 | tf_op jit(solution)/shard_map/ppermute | solution.py:448
  29.7 3.1 %collective-permute-start.3 = (f32[3,4,128]{2,1,0:T(4,128)S(1)}, f32[3,4,128]{2,1,0:T(4,128)S(1)}, u32[]{:S(2)}, u32[]{:S(2)}) collective-permute-start(f32[3,4,128]{2,1,0:T(4,128)S(1)} %get-tuple-element.34), channel_id=1, source_target_pairs={{0,8},{8,16},{16,24},{24,0},{1,9},{9,17},{17,25},{25,1},{2,10},{10... | collective-permute-start | bytes 18440 | tf_op jit(solution)/shard_map/ppermute | solution.py:448
  30.0 2.8 %collective-permute-start.4 = (f32[3,4,128]{2,1,0:T(4,128)S(1)}, f32[3,4,128]{2,1,0:T(4,128)S(1)}, u32[]{:S(2)}, u32[]{:S(2)}) collective-permute-start(f32[3,4,128]{2,1,0:T(4,128)S(1)} %get-tuple-element.35), channel_id=1, source_target_pairs={{8,0},{16,8},{24,16},{0,24},{9,1},{17,9},{25,17},{1,25},{10,2},{18... | collective-permute-start | bytes 18440 | tf_op jit(solution)/shard_map/ppermute | solution.py:448
  33.2 34.6 %copy-start.4 = (s32[4,3840]{1,0:T(4,128)S(1)}, s32[4,3840]{1,0:T(4,128)}, u32[]{:S(2)}) copy-start(s32[4,3840]{1,0:T(4,128)} %param.17) | copy-start | bytes 184324
  33.2 3.2 %collective-permute-start.8 = (f32[3,8,128]{2,1,0:T(8,128)S(1)}, f32[3,8,128]{2,1,0:T(8,128)S(1)}, u32[]{:S(2)}, u32[]{:S(2)}) collective-permute-start(f32[3,8,128]{2,1,0:T(8,128)S(1)} %get-tuple-element.40), channel_id=1, source_target_pairs={{0,8},{8,16},{16,24},{24,0},{1,9},{9,17},{17,25},{25,1},{2,10},{10... | collective-permute-start | bytes 36872 | tf_op jit(solution)/shard_map/ppermute | solution.py:448
  35.3 1.4 %collective-permute-start.9 = (f32[3,8,128]{2,1,0:T(8,128)S(1)}, f32[3,8,128]{2,1,0:T(8,128)S(1)}, u32[]{:S(2)}, u32[]{:S(2)}) collective-permute-start(f32[3,8,128]{2,1,0:T(8,128)S(1)} %get-tuple-element.41), channel_id=1, source_target_pairs={{8,0},{16,8},{24,16},{0,24},{9,1},{17,9},{25,17},{1,25},{10,2},{18... | collective-permute-start | bytes 36872 | tf_op jit(solution)/shard_map/ppermute | solution.py:448
  40.4 15.0 %all-to-all-start = ((f32[32,1,480]{2,1,0:T(1,128)}), f32[32,1,480]{2,1,0:T(1,128)S(1)}, u32[]{:S(2)}, u32[]{:S(2)}) async-start(f32[32,1,480]{2,1,0:T(1,128)} %all_to_all.8), calls=%async_computation | async-start | bytes 131072 | tf_op jit(solution)/shard_map/all_to_all | solution.py:419
  55.5 22.9 %collective-permute-start.10 = (f32[15,128]{1,0:T(8,128)S(1)}, f32[15,128]{1,0:T(8,128)S(1)}, u32[]{:S(2)}, u32[]{:S(2)}) collective-permute-start(f32[15,128]{1,0:T(8,128)S(1)} %reshape.30.refs_0_), channel_id=1, source_target_pairs={{0,1},{1,0},{2,3},{3,2},{4,5},{5,4},{6,7},{7,6},{8,9},{9,8},{10,11... | collective-permute-start | bytes 23048 | tf_op jit(solution)/shard_map/ppermute | solution.py:428
  56.3 23.1 %collective-permute-start.11 = (f32[15,128]{1,0:T(8,128)S(1)}, f32[15,128]{1,0:T(8,128)S(1)}, u32[]{:S(2)}, u32[]{:S(2)}) collective-permute-start(f32[15,128]{1,0:T(8,128)S(1)} %reshape.30.refs_0_), channel_id=1, source_target_pairs={{0,2},{1,3},{2,0},{3,1},{4,6},{5,7},{6,4},{7,5},{8,10},{9,11},{10,... | collective-permute-start | bytes 23048 | tf_op jit(solution)/shard_map/ppermute | solution.py:428
  73.1 10.6 %collective-permute-start.12 = (f32[15,128]{1,0:T(8,128)S(1)}, f32[15,128]{1,0:T(8,128)S(1)}, u32[]{:S(2)}, u32[]{:S(2)}) collective-permute-start(f32[15,128]{1,0:T(8,128)S(1)} %reshape.30.refs_0_), channel_id=1, source_target_pairs={{0,3},{1,2},{2,1},{3,0},{4,7},{5,6},{6,5},{7,4},{8,11},{9,10},{10,... | collective-permute-start | bytes 23048 | tf_op jit(solution)/shard_map/ppermute | solution.py:428
  75.3 8.5 %collective-permute-start.13 = (f32[15,128]{1,0:T(8,128)S(1)}, f32[15,128]{1,0:T(8,128)S(1)}, u32[]{:S(2)}, u32[]{:S(2)}) collective-permute-start(f32[15,128]{1,0:T(8,128)S(1)} %reshape.30.refs_0_), channel_id=1, source_target_pairs={{0,4},{1,5},{2,6},{3,7},{4,0},{5,1},{6,2},{7,3},{8,12},{9,13},{10,... | collective-permute-start | bytes 23048 | tf_op jit(solution)/shard_map/ppermute | solution.py:428
  76.1 7.6 %collective-permute-start.14 = (f32[15,128]{1,0:T(8,128)S(1)}, f32[15,128]{1,0:T(8,128)S(1)}, u32[]{:S(2)}, u32[]{:S(2)}) collective-permute-start(f32[15,128]{1,0:T(8,128)S(1)} %reshape.30.refs_0_), channel_id=1, source_target_pairs={{0,5},{1,4},{2,7},{3,6},{4,1},{5,0},{6,3},{7,2},{8,13},{9,12},{10,... | collective-permute-start | bytes 23048 | tf_op jit(solution)/shard_map/ppermute | solution.py:428
  78.4 5.4 %collective-permute-start.15 = (f32[15,128]{1,0:T(8,128)S(1)}, f32[15,128]{1,0:T(8,128)S(1)}, u32[]{:S(2)}, u32[]{:S(2)}) collective-permute-start(f32[15,128]{1,0:T(8,128)S(1)} %reshape.30.refs_0_), channel_id=1, source_target_pairs={{0,6},{1,7},{2,4},{3,5},{4,2},{5,3},{6,0},{7,1},{8,14},{9,15},{10,... | collective-permute-start | bytes 23048 | tf_op jit(solution)/shard_map/ppermute | solution.py:428
  79.4 6.3 %collective-permute-start.16 = (f32[15,128]{1,0:T(8,128)S(1)}, f32[15,128]{1,0:T(8,128)S(1)}, u32[]{:S(2)}, u32[]{:S(2)}) collective-permute-start(f32[15,128]{1,0:T(8,128)S(1)} %reshape.30.refs_0_), channel_id=1, source_target_pairs={{0,7},{1,6},{2,5},{3,4},{4,3},{5,2},{6,1},{7,0},{8,15},{9,14},{10,... | collective-permute-start | bytes 23048 | tf_op jit(solution)/shard_map/ppermute | solution.py:428

commit v4 on v3

--- a/solution.py
+++ b/solution.py
@@ -105,7 +105,7 @@
             straight = source_ref[j, start : start + count, :]
             other = source_ref[tiles - 1 - j, start : start + count, :]
             mirrored = jnp.take_along_axis(other, index, axis=1, mode="promise_in_bounds")
-            target_ref[j, start : start + count, :] = jnp.where(flag[:count], mirrored, straight)
+            target_ref[j, start : start + count, :] = jnp.where(flag, mirrored, straight)
 
 
 def store_padded(ref, index, s, j, xt, value):
@@ -121,7 +121,14 @@
 
 
 def flags(seam_ref):
-    return seam_ref[0] == 1, seam_ref[1] == 1
+    tile = lax.axis_index("tile")
+    return seam_ref[tile, 0:1, :] == 1, seam_ref[tile, 1:2, :] == 1
+
+
+def start_kernel(f_hbm, out_ref, sem):
+    copy = pltpu.make_async_copy(f_hbm.at[:, 0], out_ref, sem)
+    copy.start()
+    copy.wait()
 
 
 def lower_kernel(
@@ -138,22 +145,26 @@
     def fetch_code(k):
         return pltpu.make_async_copy(code_hbm.at[k], code_ref.at[k], sems.at[1, k])
 
-    fetch_mf = pltpu.make_async_copy(mf_hbm, mf_ref, sems.at[2, 0])
-    fetch_cy = pltpu.make_async_copy(cy_hbm, cy_ref, sems.at[2, 1])
-    fetch_cx = pltpu.make_async_copy(cx_hbm, cx_ref, sems.at[2, 2])
+    def fetch_mf(k):
+        return pltpu.make_async_copy(mf_hbm.at[k], mf_ref.at[k], sems.at[2, k])
+
+    def fetch_cy(k):
+        return pltpu.make_async_copy(cy_hbm.at[k], cy_ref.at[k], sems.at[3, k])
+
+    fetch_cx = pltpu.make_async_copy(cx_hbm, cx_ref, sems.at[4, 0])
     fetch(0).start()
-    fetch_mf.start()
-    fetch_cy.start()
-    for k in range(levels - 1):
+    for k in range(levels):
+        fetch_mf(k).start()
+        fetch_cy(k).start()
         fetch_code(k).start()
-        fetch(k + 1).start()
-    fetch_code(levels - 1).start()
+        if k < levels - 1:
+            fetch(k + 1).start()
     fetch_cx.start()
     fetch(0).wait()
-    fetch_mf.wait()
-    fetch_cy.wait()
 
     def level(k, _):
+        fetch_mf(k).wait()
+        fetch_cy(k).wait()
         fetch_code(k).wait()
         fetch(k + 1).wait()
         mf = mf_ref[k].astype(jnp.float32)
@@ -176,6 +187,8 @@
 
     lax.fori_loop(0, levels - 1, level, 0)
     top_ref[...] = f_ref[levels - 1]
+    fetch_mf(levels - 1).wait()
+    fetch_cy(levels - 1).wait()
     fetch_code(levels - 1).wait()
     fetch_cx.wait()
 
@@ -276,52 +289,72 @@
     top_ref[...] = a_ref[(below - 1) % 2]
 
 
-def highest_kernel(
-    vt_ref, left_ref, right_ref, lower_ref, above_ref, seam_ref, cx_ref, mf_ref, cy_ref, code_ref,
-    out_ref, first_ref, last_ref,
+def second_last_kernel(
+    vt_ref, left_ref, right_ref, lower_ref, first_in, last_in, seam_ref, cx_ref, mf_ref, cy_ref, code_ref,
+    out_ref, first_ref, last_ref, top_ref,
     lrow_ref, rrow_ref,
 ):
     sectors, tiles, padded, _ = vt_ref.shape
     strips = (padded - 2 * ROWS) // ROWS
     top = mf_ref.shape[0] - 1
-    at_top = lax.axis_index("lev") == lax.axis_size("lev") - 1
+    done = first_in.shape[1]
     flip_left, flip_right = flags(seam_ref)
     turned(left_ref, flip_left, lrow_ref)
     turned(right_ref, flip_right, rrow_ref)
+    first_ref[:, :done] = first_in[...]
+    last_ref[:, :done] = last_in[...]
     cx = cx_ref[top].astype(jnp.float32)
-    mixing = [mf_ref[top - 1].astype(jnp.float32), mf_ref[top].astype(jnp.float32)]
-    cys = [cy_ref[top - 1].astype(jnp.float32), cy_ref[top].astype(jnp.float32)]
-    codes = [code_ref[top - 1], code_ref[top]]
+    mf = mf_ref[top - 1].astype(jnp.float32)
+    cy = cy_ref[top - 1].astype(jnp.float32)
     for xt in range(strips):
-        along = [first_weights(cx, codes[1], 2, xt, j) for j in range(tiles)]
-        across = [second_weights(cys[i], codes[i], 1, xt, tiles) for i in range(2)]
+        along = [first_weights(cx, code_ref[top], 2, xt, j) for j in range(tiles)]
+        across = second_weights(cy, code_ref[top - 1], 1, xt, tiles)
         rows = slice(xt * ROWS, (xt + 1) * ROWS)
         for s in range(sectors):
-            low, high = [], []
+            parts = []
             for j in range(tiles):
-                here = first_sweep(
+                upper = first_sweep(
                     lambda s, j, start: vt_ref[s, j, start : start + ROWS, :],
                     s, j, xt, strips - 1, along[j],
                     lambda s, j: lrow_ref[j, s : s + 1, :],
                     lambda s, j: rrow_ref[j, s : s + 1, :],
                 )
-                lower = lower_ref[s, j, rows, :]
-                low.append(lower + cut(mixing[0], xt, j) * (here - lower))
+                top_ref[s, j, rows, :] = upper
+                here = lower_ref[s, j, rows, :]
+                parts.append(here + cut(mf, xt, j) * (upper - here))
+            for j, value in enumerate(second_sweep(parts, across)):
+                store_padded(out_ref, (), s, j, xt, value)
+                store_rims(first_ref, last_ref, done + s, j, xt, strips - 1, value)
+
+
+def highest_kernel(here_ref, above_ref, mf_ref, cy_ref, code_ref, out_ref, first_ref, last_ref):
+    sectors, tiles, columns, _ = here_ref.shape
+    strips = columns // ROWS
+    top = mf_ref.shape[0] - 1
+    at_top = lax.axis_index("lev") == lax.axis_size("lev") - 1
+    mf = mf_ref[top].astype(jnp.float32)
+    cy = cy_ref[top].astype(jnp.float32)
+    for xt in range(strips):
+        across = second_weights(cy, code_ref[top], 1, xt, tiles)
+        rows = slice(xt * ROWS, (xt + 1) * ROWS)
+        for s in range(sectors):
+            parts = []
+            for j in range(tiles):
+                here = here_ref[s, j, rows, :]
                 upper = above_ref[s, rows, j * LANES : (j + 1) * LANES]
                 upper = jnp.where(at_top, here, upper)
-                high.append(here + cut(mixing[1], xt, j) * (upper - here))
-            for i, parts in enumerate((low, high)):
-                for j, value in enumerate(second_sweep(parts, across[i])):
-                    store_padded(out_ref, (i,), s, j, xt, value)
-                    store_rims(first_ref, last_ref, i * sectors + s, j, xt, strips - 1, value)
+                parts.append(here + cut(mf, xt, j) * (upper - here))
+            for j, value in enumerate(second_sweep(parts, across)):
+                store_padded(out_ref, (), s, j, xt, value)
+                store_rims(first_ref, last_ref, s, j, xt, strips - 1, value)
 
 
 def final_kernel(
-    v_ref, vt_ref, left_ref, right_ref, left_top_ref, right_top_ref, seam_ref,
+    v_ref, vs_ref, vt_ref, left_ref, right_ref, left_top_ref, right_top_ref, seam_ref,
     cx_ref, code_ref, weight_ref, share_ref,
-    out_hbm, sens_ref,
-    lrow_ref, rrow_ref, ltop_ref, rtop_ref, out_ref, sems,
+    out_hbm, *refs,
 ):
+    *piece_refs, lrow_ref, rrow_ref, ltop_ref, rtop_ref, out_ref, sens_ref, packed_ref, sems = refs
     below, sectors, tiles, padded, _ = v_ref.shape
     strips = (padded - 2 * ROWS) // ROWS
     flip_left, flip_right = flags(seam_ref)
@@ -355,14 +388,20 @@
                     sens_ref[rows, lanes] += factor * total
         send(k).start()
 
-    for i in range(2):
-        level(
-            below + i,
-            lambda s, j, start: vt_ref[i, s, j, start : start + ROWS, :],
-            lambda s, j: ltop_ref[j, i * sectors + s : i * sectors + s + 1, :],
-            lambda s, j: rtop_ref[j, i * sectors + s : i * sectors + s + 1, :],
-            i == 0,
-        )
+    level(
+        below + 1,
+        lambda s, j, start: vt_ref[s, j, start : start + ROWS, :],
+        lambda s, j: ltop_ref[j, s : s + 1, :],
+        lambda s, j: rtop_ref[j, s : s + 1, :],
+        True,
+    )
+    level(
+        below,
+        lambda s, j, start: vs_ref[s, j, start : start + ROWS, :],
+        lambda s, j: lrow_ref[j, below * sectors + s : below * sectors + s + 1, :],
+        lambda s, j: rrow_ref[j, below * sectors + s : below * sectors + s + 1, :],
+        False,
+    )
 
     def step(k, _):
         level(
@@ -375,6 +414,23 @@
         return 0
 
     lax.fori_loop(0, below, step, 0)
+    if len(piece_refs) == 1:
+        piece_refs[0][...] = sens_ref[...]
+    else:
+        owners, group, depth, _ = packed_ref.shape
+        share = strips * ROWS * tiles // owners
+        rank = lax.axis_index("lev")
+        for o in range(owners):
+            for place in range(group * depth):
+                piece, line = divmod(place, depth)
+                if place < share:
+                    x, j = divmod(o * share + place, tiles)
+                    row = sens_ref[x : x + 1, j * LANES : (j + 1) * LANES]
+                else:
+                    row = jnp.zeros((1, LANES), jnp.float32)
+                packed_ref[o, piece, line : line + 1, :] = row
+        for apart, ref in enumerate(piece_refs):
+            ref[...] = packed_ref[:, jnp.bitwise_xor(rank, apart)]
     for k in range(below + 2):
         send(k).wait()
 
@@ -382,16 +438,18 @@
 def scatter_kernel(cells_ref, *refs):
     *value_refs, out_ref = refs
     rows, lanes = out_ref.shape
-    count = cells_ref.shape[0]
+    group, owners, depth, _ = cells_ref.shape
+    tile, rank = lax.axis_index("tile"), lax.axis_index("lev")
     high_iota = lax.broadcasted_iota(jnp.int32, (rows, lanes), 0)
     low_iota = lax.broadcasted_iota(jnp.int32, (lanes, lanes), 0)
     total = jnp.zeros((2 * rows, lanes), jnp.float32)
-    for pair in range(0, count, 2):
+    lines = [(i, o, r) for i in range(group) for o in range(owners) for r in range(depth)]
+    for pair in range(0, len(lines), 2):
         lefts, rights = [], []
-        for row in (pair, pair + 1):
-            cells = cells_ref[row : row + 1, :]
-            part, line = divmod(row, value_refs[0].shape[0])
-            value = value_refs[part][line : line + 1, :]
+        for part, owner, line in lines[pair : pair + 2]:
+            source = lax.rem(tile + owners - owner, owners)
+            cells = cells_ref[jnp.bitwise_xor(rank, part), source, line : line + 1, :]
+            value = value_refs[part][owner, line : line + 1, :]
             coarse = value.astype(jnp.bfloat16).astype(jnp.float32)
             fine = value - coarse
             here = jnp.right_shift(cells, 7) == high_iota
@@ -411,32 +469,46 @@
     out_ref[...] = total[:rows] + total[rows:]
 
 
-def remapped(partial_value, flux_cell):
-    tiles, share = flux_cell.shape
-    group = lax.axis_size("lev") * lax.axis_size("sec")
-    piece = share // group
-    sent = partial_value.reshape(tiles * group, piece)
-    received = lax.all_to_all(
-        sent, ("tile", "lev", "sec"), split_axis=0, concat_axis=0, tiled=True
-    )
-    summed = jnp.sum(received.reshape(tiles, group, piece), axis=1)
-    own = summed.reshape(-1, LANES)
-    rank = lax.axis_index(("lev", "sec"))
-    parts = [own]
-    for apart in range(1, group):
-        pairs = [(i, i ^ apart) for i in range(group)]
-        parts.append(lax.ppermute(own, ("lev", "sec"), pairs))
-    cells = flux_cell.reshape(tiles, group, piece).transpose(1, 0, 2).reshape(group, -1, LANES)
-    order = jnp.bitwise_xor(rank, jnp.arange(group, dtype=jnp.int32))
-    cells = jnp.concatenate(
-        [lax.dynamic_slice_in_dim(cells, order[i], 1, axis=0)[0] for i in range(group)], axis=0
-    )
+def choose_kernel(mine_ref, other_ref, *out_refs):
+    owners = mine_ref.shape[0]
+    tile = lax.axis_index("tile")
+    for apart, ref in enumerate(out_refs):
+        owner = lax.rem(tile + apart, owners)
+        ref[...] = mine_ref[owner] + other_ref[owner]
+
+
+def exchanged(value, axis, apart):
+    count = lax.axis_size(axis)
+    return lax.ppermute(value, axis, [(i, i ^ apart) for i in range(count)])
+
+
+def remapped(pieces, flux_cell):
+    owners, share = flux_cell.shape
+    group = lax.axis_size("lev")
+    depth = pieces[0].shape[1]
+    mine = pieces[0]
+    arrived = [exchanged(pieces[d], "lev", d) for d in range(1, group)]
+    for other in arrived:
+        mine = mine + other
+    other = exchanged(mine, "sec", 1)
+    if owners <= 8:
+        sent = call(
+            choose_kernel, (f32(depth, LANES),) * owners, [VM] * 2, [VM] * owners, (mine, other)
+        )
+        got = [sent[0]]
+        for d in range(1, owners):
+            hops = [(i, (i + d) % owners) for i in range(owners)]
+            got.append(lax.ppermute(sent[d], "tile", hops))
+        own = jnp.stack(got)
+    else:
+        own = lax.all_to_all(mine + other, "tile", split_axis=0, concat_axis=0, tiled=True)
+        order = jnp.remainder(lax.axis_index("tile") - jnp.arange(owners), owners)
+        own = jnp.take(own, order, axis=0)
+    parts = [own] + [exchanged(own, "lev", d) for d in range(1, group)]
+    cells = jnp.pad(flux_cell, ((0, 0), (0, group * depth * LANES - share)))
+    cells = cells.reshape(owners, group, depth, LANES).transpose(1, 0, 2, 3)
     out = call(
-        scatter_kernel,
-        f32(FL_DEV // LANES, LANES),
-        [VM] * (group + 1),
-        VM,
-        (cells, *parts),
+        scatter_kernel, f32(FL_DEV // LANES, LANES), [VM] * (group + 1), VM, (cells, *parts)
     )
     return out.reshape(-1)
 
@@ -465,14 +537,14 @@
     rim = kept(tiles, below * sectors, LANES)
     rim_top = kept(tiles, sectors, LANES)
     rim_next = kept(tiles, (below - 1) * sectors, LANES)
-    rim_pair = kept(tiles, 2 * sectors, LANES)
     rim_scratch = pltpu.VMEM((tiles, below * sectors, LANES), jnp.float32)
 
-    seam = lax.dynamic_index_in_dim(seam_code, lax.axis_index("tile"), 0, keepdims=False)
-    seam = jnp.broadcast_to(seam[:, None, None], (2, ROWS, LANES))
+    seam = jnp.broadcast_to(seam_code[:, :, None], (*seam_code.shape, LANES))
     weight = jnp.broadcast_to(level_weight[:, None], (levels, LANES))
 
-    above = from_above(forcing[:, 0])
+    above = from_above(
+        call(start_kernel, plane, [HBM], VM, in_hbm(forcing), [pltpu.SemaphoreType.DMA])
+    )
     narrow = pltpu.VMEM((levels, columns, width), jnp.bfloat16)
     v, first, last, top, mass_flux, courant_y, limiter_code, courant_x = call(
         lower_kernel,
@@ -485,7 +557,7 @@
         in_hbm(forcing, mass_flux, courant_y, limiter_code, courant_x),
         [
             pltpu.VMEM((levels, sectors, columns, width), jnp.float32),
-            pltpu.SemaphoreType.DMA((3, levels)),
+            pltpu.SemaphoreType.DMA((5, levels)),
         ],
     )
     left, right = around(first, last)
@@ -515,38 +587,62 @@
         (v, left, right, lowest, seam, courant_x, mass_flux, courant_y, limiter_code),
         [rim_scratch, rim_scratch, pltpu.VMEM((2, sectors, tiles, columns, LANES), jnp.float32)],
     )
+    vs, first, last, top = call(
+        second_last_kernel,
+        (field_top, rim, rim, kept(sectors, tiles, columns, LANES)),
+        [VM] * 11,
+        [VM] * 4,
+        (
+            vt, left_top, right_top, top, first, last, seam,
+            courant_x, mass_flux, courant_y, limiter_code,
+        ),
+        [pltpu.VMEM((tiles, sectors, LANES), jnp.float32)] * 2,
+    )
     left, right = around(first, last)
     vt, first_top, last_top = call(
         highest_kernel,
-        (kept(2, sectors, tiles, padded, LANES), rim_pair, rim_pair),
-        [VM] * 10,
+        (field_top, rim_top, rim_top),
+        [VM] * 5,
         [VM] * 3,
+        (top, above, mass_flux, courant_y, limiter_code),
+    )
+    left_top, right_top = around(first_top, last_top)
+
+    owners, share = flux_cell.shape
+    group = lax.axis_size("lev")
+    depth = -(-share // (group * LANES))
+    aligned = share % LANES == 0 and width % LANES == 0
+    pieces = (f32(owners, depth, LANES),) * group if aligned else (f32(columns, width),)
+    adjoint, *pieces = call(
+        final_kernel,
+        (f32(*forcing.shape), *pieces),
+        [VM] * 12,
+        [HBM] + [VM] * len(pieces),
         (
-            vt, left_top, right_top, top, above, seam,
-            courant_x, mass_flux, courant_y, limiter_code,
-        ),
-        [pltpu.VMEM((tiles, sectors, LANES), jnp.float32)] * 2,
-    )
-    left_top, right_top = around(first_top, last_top)
-    adjoint, sensitivity = call(
-        final_kernel,
-        (f32(*forcing.shape), f32(columns, width)),
-        [VM] * 11,
-        [HBM, VM],
-        (
-            v, vt, left, right, left_top, right_top, seam,
+            v, vs, vt, left, right, left_top, right_top, seam,
             courant_x, limiter_code, weight, sector_share,
         ),
         [
-            pltpu.VMEM((tiles, (below - 1) * sectors, LANES), jnp.float32),
-            pltpu.VMEM((tiles, (below - 1) * sectors, LANES), jnp.float32),
-            pltpu.VMEM((tiles, 2 * sectors, LANES), jnp.float32),
-            pltpu.VMEM((tiles, 2 * sectors, LANES), jnp.float32),
+            rim_scratch, rim_scratch,
+            pltpu.VMEM((tiles, sectors, LANES), jnp.float32),
+            pltpu.VMEM((tiles, sectors, LANES), jnp.float32),
             pltpu.VMEM((levels, sectors, columns, width), jnp.float32),
+            pltpu.VMEM((columns, width), jnp.float32),
+            pltpu.VMEM((owners, group, depth, LANES), jnp.float32),
             pltpu.SemaphoreType.DMA((levels,)),
         ],
     )
-    return (adjoint, remapped(sensitivity, flux_cell))
+    if not aligned:
+        packed = jnp.pad(
+            pieces[0].reshape(owners, share), ((0, 0), (0, group * depth * LANES - share))
+        ).reshape(owners, group, depth, LANES)
+        rank = lax.axis_index("lev")
+        pieces = [
+            lax.dynamic_index_in_dim(packed, jnp.bitwise_xor(rank, d), 1, keepdims=False)
+            for d in range(group)
+        ]
+    flux_cell, pieces = lax.optimization_barrier((flux_cell, pieces))
+    return (adjoint, remapped(pieces, flux_cell))
 
 
 def solution(mesh):

time: 89.4 us -> 68 us (0.76)
  between operations: 16.1 us -> 0.79 us
  starting transfers between devices: 30 us -> 25.1 us
  local copies, waits for them, and re-layouts: 9.8 us -> 5.44 us
  Pallas kernels: 17.6 us -> 19.5 us
  waiting for transfers between devices: 15.5 us -> 16.9 us
    ppermute x7 -> x10, waiting for transfers between devices: 1.92 us -> 11.3 us  [the longest x7 10 us: exchanged(): return lax.ppermute(value, axis, [(i, i ^ apart) for i in range(count)])]
    all_to_all x1 -> x0, starting transfers between devices: 7.67 us -> none  [remapped(): lax.all_to_all(sent, ('tile', 'lev', 'sec'), split_axis=0, concat_axis=0,...]
    all_to_all x1 -> x0, waiting for transfers between devices: 7.26 us -> none  [remapped(): lax.all_to_all(sent, ('tile', 'lev', 'sec'), split_axis=0, concat_axis=0,...]
    ppermute x7 -> x10, starting transfers between devices: 11.2 us -> 14.4 us  [the longest x7 11.3 us: exchanged(): return lax.ppermute(value, axis, [(i, i ^ apart) for i in range(count)])]
    pallas_call x6 -> x9, Pallas kernels: 17.6 us -> 19.5 us  [call(): pl.pallas_call(kernel, out_shape=out_shape, in_specs=in_specs, out_specs=...]
    squeeze x2 -> x0, local copies, waits for them, and re-layouts: 1.67 us -> none  [the longest x1 1.66 us: shards(): above = from_above(forcing[:, 0])]
    ppermute x8, waiting for transfers between devices: 6.31 us -> 5.03 us  [around(): return (lax.ppermute(last, 'tile', up), lax.ppermute(first, 'tile', down))]
    unnamed x12 -> x14, local copies, waits for them, and re-layouts: 5.21 us -> 5.29 us
  transfers between devices with their start and end apart: 18 -> 20, of which waited for: 8 -> 12; matrix products, arithmetic and copies ran while one was open for 2% -> 0% of each run, Pallas kernels for 13% -> 17%
where the time goes in v4:
time: 68 us; the launch traced here: 67.8 us
  starting transfers between devices  25.1 us (37%)
  Pallas kernels  19.5 us (29%)
  waiting for transfers between devices  16.9 us (25%)
  local copies, waits for them, and re-layouts  5.44 us (8%)
  between operations  0.79 us (1%)
    pallas_call x9, Pallas kernels, call(): pl.pallas_call(kernel, out_shape=out_shape, in_specs=in_specs, out_specs=...  19.5 us
    ppermute x7, starting transfers between devices, exchanged(): return lax.ppermute(value, axis, [(i, i ^ apart) for i in range(count)])  11.3 us
    ppermute x7, waiting for transfers between devices, exchanged(): return lax.ppermute(value, axis, [(i, i ^ apart) for i in range(count)])  10 us
    ppermute x8, starting transfers between devices, around(): return (lax.ppermute(last, 'tile', up), lax.ppermute(first, 'tile', down))  8.16 us
    unnamed x14, local copies, waits for them, and re-layouts  5.29 us
    ppermute x8, waiting for transfers between devices, around(): return (lax.ppermute(last, 'tile', up), lax.ppermute(first, 'tile', down))  5.03 us
    ppermute x3, starting transfers between devices, remapped(): got.append(lax.ppermute(sent[d], 'tile', hops))  3.05 us
    ppermute x2, starting transfers between devices, from_above(): return lax.ppermute(value, 'lev', [(i + 1, i) for i in range(count - 1)])  2.58 us
  transfers between devices with their start and end apart: 20, of which 12 were waited for; matrix products, arithmetic and copies ran while one was open for 0% of the time, Pallas kernels for 17%

profile of v4, /device:TPU:0, one launch (start us, length us, event | category | flops | bytes accessed | tf_op | source)
XLA Modules:
  0.0 67.8 jit_solution(6724184730788747850)
XLA Ops:
  0.6 1.6 %shard_map.105 = f32[4,40,384]{2,1,0:T(8,128)} custom-call(f32[4,18,40,384]{3,2,1,0:T(8,128)} %f_hbm.3), custom_call_target="tpu_custom_call" | custom-call | flops 1 | bytes 1 | tf_op jit(solution)/shard_map/pallas_call | solution.py:19
  2.3 1.3 %collective-permute-start.2 = (f32[4,40,384]{2,1,0:T(8,128)}, f32[4,40,384]{2,1,0:T(8,128)S(1)}, u32[]{:S(2)}, u32[]{:S(2)}) collective-permute-start(f32[4,40,384]{2,1,0:T(8,128)} %shard_map.105), channel_id=1, source_target_pairs={{2,0},{4,2},{6,4},{3,1},{5,3},{7,5},{10,8},{12,10},{14,12},{11,9},... | collective-permute-start | bytes 737288 | tf_op jit(solution)/shard_map/ppermute | solution.py:525
  3.6 6.2 %shard_map.104 = (f32[17,4,3,56,128]{4,3,2,1,0:T(8,128)S(1)}, f32[3,68,128]{2,1,0:T(8,128)}, f32[3,68,128]{2,1,0:T(8,128)}, f32[4,40,384]{2,1,0:T(8,128)S(1)}, b...) custom-call(f32[4,18,40,384]{3,2,1,0:T(8,128)} %f_hbm.3, ...), custom_call_target="tpu_custom_call" | custom-call | flops 1 | bytes 1 | tf_op jit(solution)/shard_map/pallas_call | solution.py:19
  9.8 2.5 %copy-done = f32[17,4,3,56,128]{4,3,2,1,0:T(8,128)} copy-done((f32[17,4,3,56,128]{4,3,2,1,0:T(8,128)}, f32[17,4,3,56,128]{4,3,2,1,0:T(8,128)S(1)}, u32[]{:S(2)}) %copy-start) | copy-done | bytes 5849112
  12.8 1.9 %collective-permute-start.1 = (f32[3,68,128]{2,1,0:T(8,128)}, f32[3,68,128]{2,1,0:T(8,128)S(1)}, u32[]{:S(2)}, u32[]{:S(2)}) collective-permute-start(f32[3,68,128]{2,1,0:T(8,128)} %get-tuple-element.41), channel_id=1, source_target_pairs={{8,0},{16,8},{24,16},{0,24},{9,1},{17,9},{25,17},{1,25},{10,2},{18... | collective-permute-start | bytes 313352 | tf_op jit(solution)/shard_map/ppermute | solution.py:520
  14.8 2.5 %collective-permute-done.left_ref = f32[3,68,128]{2,1,0:T(8,128)S(1)} collective-permute-done((f32[3,68,128]{2,1,0:T(8,128)}, f32[3,68,128]{2,1,0:T(8,128)S(1)}, u32[]{:S(2)}, u32[]{:S(2)}) %collective-permute-start) | collective-permute-done | bytes 104480 | tf_op jit(solution)/shard_map/ppermute | solution.py:520
  17.3 1.1 %collective-permute-done.1.right_ref = f32[3,68,128]{2,1,0:T(8,128)S(1)} collective-permute-done((f32[3,68,128]{2,1,0:T(8,128)}, f32[3,68,128]{2,1,0:T(8,128)S(1)}, u32[]{:S(2)}, u32[]{:S(2)}) %collective-permute-start.1) | collective-permute-done | bytes 104480 | tf_op jit(solution)/shard_map/ppermute | solution.py:520
  18.5 2.7 %copy-done.1 = f32[17,4,3,56,128]{4,3,2,1,0:T(8,128)S(1)} copy-done((f32[17,4,3,56,128]{4,3,2,1,0:T(8,128)S(1)}, f32[17,4,3,56,128]{4,3,2,1,0:T(8,128)}, u32[]{:S(2)}) %copy-start.1) | copy-done | bytes 5849112
  21.4 1.3 %collective-permute-start.5 = (f32[4,40,384]{2,1,0:T(8,128)S(1)}, f32[4,40,384]{2,1,0:T(8,128)S(1)}, u32[]{:S(2)}, u32[]{:S(2)}) collective-permute-start(f32[4,40,384]{2,1,0:T(8,128)S(1)} %get-tuple-element.47.lowest_ref), channel_id=1, source_target_pairs={{2,0},{4,2},{6,4},{3,1},{5,3},{7,5},{10,8},{12,10},{14,12},{11,9},... | collective-permute-start | bytes 737288 | tf_op jit(solution)/shard_map/ppermute | solution.py:525
  22.7 1.4 %collective-permute-start.3 = (f32[3,4,128]{2,1,0:T(4,128)S(1)}, f32[3,4,128]{2,1,0:T(4,128)S(1)}, u32[]{:S(2)}, u32[]{:S(2)}) collective-permute-start(f32[3,4,128]{2,1,0:T(4,128)S(1)} %get-tuple-element.50), channel_id=1, source_target_pairs={{0,8},{8,16},{16,24},{24,0},{1,9},{9,17},{17,25},{25,1},{2,10},{10... | collective-permute-start | bytes 18440 | tf_op jit(solution)/shard_map/ppermute | solution.py:520
  24.1 0.8 %collective-permute-start.4 = (f32[3,4,128]{2,1,0:T(4,128)S(1)}, f32[3,4,128]{2,1,0:T(4,128)S(1)}, u32[]{:S(2)}, u32[]{:S(2)}) collective-permute-start(f32[3,4,128]{2,1,0:T(4,128)S(1)} %get-tuple-element.51), channel_id=1, source_target_pairs={{8,0},{16,8},{24,16},{0,24},{9,1},{17,9},{25,17},{1,25},{10,2},{18... | collective-permute-start | bytes 18440 | tf_op jit(solution)/shard_map/ppermute | solution.py:520
  24.9 4.6 %shard_map.107 = (f32[16,4,3,56,128]{4,3,2,1,0:T(8,128)S(1)}, f32[3,64,128]{2,1,0:T(8,128)S(1)}, f32[3,64,128]{2,1,0:T(8,128)S(1)}, f32[4,3,40,128]{3,2,1,0:T(8,128)S(1)}) custom-call(f32[17,4,3,56,128]{4,3,2,1,0:T(8,128)S(1)} %copy-done.1, f32[3,68,128]{2,1,0:T(8,128)S(1)} %collective-permute-done.left_ref, ...), custom_call_target="tpu_custom_call" | custom-call | flops 1 | bytes 1 | tf_op jit(solution)/shard_map/pallas_call | solution.py:19
  30.2 1.4 %collective-permute-start.7 = (f32[3,68,128]{2,1,0:T(8,128)S(1)}, f32[3,68,128]{2,1,0:T(8,128)S(1)}, u32[]{:S(2)}, u32[]{:S(2)}) collective-permute-start(f32[3,68,128]{2,1,0:T(8,128)S(1)} %get-tuple-element.59), channel_id=1, source_target_pairs={{8,0},{16,8},{24,16},{0,24},{9,1},{17,9},{25,17},{1,25},{10,2},{18... | collective-permute-start | bytes 313352 | tf_op jit(solution)/shard_map/ppermute | solution.py:520
  31.7 0.6 collective-permute-done.5.above_ref
  32.9 1.4 %collective-permute-start.9 = (f32[3,4,128]{2,1,0:T(4,128)S(1)}, f32[3,4,128]{2,1,0:T(4,128)S(1)}, u32[]{:S(2)}, u32[]{:S(2)}) collective-permute-start(f32[3,4,128]{2,1,0:T(4,128)S(1)} %get-tuple-element.61), channel_id=1, source_target_pairs={{8,0},{16,8},{24,16},{0,24},{9,1},{17,9},{25,17},{1,25},{10,2},{18... | collective-permute-start | bytes 18440 | tf_op jit(solution)/shard_map/ppermute | solution.py:520
  34.2 0.5 collective-permute-done.7.right_ref
  34.8 0.9 %collective-permute-done.8.left_top_ref = f32[3,4,128]{2,1,0:T(4,128)S(1)} collective-permute-done((f32[3,4,128]{2,1,0:T(4,128)S(1)}, f32[3,4,128]{2,1,0:T(4,128)S(1)}, u32[]{:S(2)}, u32[]{:S(2)}) %collective-permute-start.8) | collective-permute-done | bytes 6176 | tf_op jit(solution)/shard_map/ppermute | solution.py:520
  35.7 2.9 %shard_map.110 = (f32[4,18,40,384]{3,2,1,0:T(8,128)}, f32[4,8,128]{2,1,0:T(8,128)S(1)}, f32[4,8,128]{2,1,0:T(8,128)S(1)}, f32[4,8,128]{2,1,0:T(8,128)S(1)}, f32[4,8,128]{2,1,0:T(8,128)S(1)}) custom-call(f32[16,4,3,56,128]{4,3,2,1,0:T(8,128)S(1)} %get-tuple-element.48.v_ref, f32[4,3,56,128]{3,2,1,0:T(8,128)S(1)} %get-tuple-element.55.vs_ref, ...), custom_call_target="tpu_custom_call" | custom-call | flops 1 | bytes 1 | tf_op jit(solution)/shard_map/pallas_call | solution.py:19
  38.6 2.5 %collective-permute-start.10 = (f32[4,8,128]{2,1,0:T(8,128)S(1)}, f32[4,8,128]{2,1,0:T(8,128)S(1)}, u32[]{:S(2)}, u32[]{:S(2)}) collective-permute-start(f32[4,8,128]{2,1,0:T(8,128)S(1)} %get-tuple-element.69), channel_id=1, source_target_pairs={{0,2},{2,0},{4,6},{6,4},{1,3},{3,1},{5,7},{7,5},{8,10},{10,8},{12,... | collective-permute-start | bytes 49160 | tf_op jit(solution)/shard_map/ppermute | solution.py:482
  41.1 2.9 %collective-permute-start.11 = (f32[4,8,128]{2,1,0:T(8,128)S(1)}, f32[4,8,128]{2,1,0:T(8,128)S(1)}, u32[]{:S(2)}, u32[]{:S(2)}) collective-permute-start(f32[4,8,128]{2,1,0:T(8,128)S(1)} %get-tuple-element.70), channel_id=1, source_target_pairs={{0,4},{2,6},{4,0},{6,2},{1,5},{3,7},{5,1},{7,3},{8,12},{10,14},{12... | collective-permute-start | bytes 49160 | tf_op jit(solution)/shard_map/ppermute | solution.py:482
  44.0 1.9 %collective-permute-done.11 = f32[4,8,128]{2,1,0:T(8,128)S(1)} collective-permute-done((f32[4,8,128]{2,1,0:T(8,128)S(1)}, f32[4,8,128]{2,1,0:T(8,128)S(1)}, u32[]{:S(2)}, u32[]{:S(2)}) %collective-permute-start.11) | collective-permute-done | bytes 16416 | tf_op jit(solution)/shard_map/ppermute | solution.py:482
  45.9 3.7 %collective-permute-done.12 = f32[4,8,128]{2,1,0:T(8,128)S(1)} collective-permute-done((f32[4,8,128]{2,1,0:T(8,128)S(1)}, f32[4,8,128]{2,1,0:T(8,128)S(1)}, u32[]{:S(2)}, u32[]{:S(2)}) %collective-permute-start.12) | collective-permute-done | bytes 16416 | tf_op jit(solution)/shard_map/ppermute | solution.py:482
  49.6 1.5 %collective-permute-start.13 = (f32[4,8,128]{2,1,0:T(8,128)S(1)}, f32[4,8,128]{2,1,0:T(8,128)S(1)}, u32[]{:S(2)}, u32[]{:S(2)}) collective-permute-start(f32[4,8,128]{2,1,0:T(8,128)S(1)} %add_add_fusion.mine_ref), channel_id=1, source_target_pairs={{0,1},{1,0},{2,3},{3,2},{4,5},{5,4},{6,7},{7,6},{8,9},{9,8},{10,11... | collective-permute-start | bytes 49160 | tf_op jit(solution)/shard_map/ppermute | solution.py:482
  51.2 2.2 %collective-permute-done.13.other_ref = f32[4,8,128]{2,1,0:T(8,128)S(1)} collective-permute-done((f32[4,8,128]{2,1,0:T(8,128)S(1)}, f32[4,8,128]{2,1,0:T(8,128)S(1)}, u32[]{:S(2)}, u32[]{:S(2)}) %collective-permute-start.13) | collective-permute-done | bytes 16416 | tf_op jit(solution)/shard_map/ppermute | solution.py:482
  53.5 1.6 %collective-permute-start.15 = (f32[8,128]{1,0:T(8,128)S(1)}, f32[8,128]{1,0:T(8,128)S(1)}, u32[]{:S(2)}, u32[]{:S(2)}) collective-permute-start(f32[8,128]{1,0:T(8,128)S(1)} %get-tuple-element.74), channel_id=1, source_target_pairs={{0,16},{8,24},{16,0},{24,8},{1,17},{9,25},{17,1},{25,9},{2,18},{10... | collective-permute-start | bytes 12296 | tf_op jit(solution)/shard_map/ppermute | solution.py:501
  55.1 1.4 %collective-permute-start.16 = (f32[8,128]{1,0:T(8,128)S(1)}, f32[8,128]{1,0:T(8,128)S(1)}, u32[]{:S(2)}, u32[]{:S(2)}) collective-permute-start(f32[8,128]{1,0:T(8,128)S(1)} %get-tuple-element.75), channel_id=1, source_target_pairs={{0,24},{8,0},{16,8},{24,16},{1,25},{9,1},{17,9},{25,17},{2,26},{10... | collective-permute-start | bytes 12296 | tf_op jit(solution)/shard_map/ppermute | solution.py:501
  56.5 0.7 collective-permute-done.15
  57.1 0.6 collective-permute-done.16
  57.8 1.0 %collective-permute-start.18 = (f32[4,8,128]{2,1,0:T(8,128)S(1)}, f32[4,8,128]{2,1,0:T(8,128)S(1)}, u32[]{:S(2)}, u32[]{:S(2)}) collective-permute-start(f32[4,8,128]{2,1,0:T(8,128)S(1)} %pad_maximum_fusion.refs_0_), channel_id=1, source_target_pairs={{0,4},{2,6},{4,0},{6,2},{1,5},{3,7},{5,1},{7,3},{8,12},{10,14},{12... | collective-permute-start | bytes 49160 | tf_op jit(solution)/shard_map/ppermute | solution.py:482
  58.8 3.4 %collective-permute-start.19 = (f32[4,8,128]{2,1,0:T(8,128)S(1)}, f32[4,8,128]{2,1,0:T(8,128)S(1)}, u32[]{:S(2)}, u32[]{:S(2)}) collective-permute-start(f32[4,8,128]{2,1,0:T(8,128)S(1)} %pad_maximum_fusion.refs_0_), channel_id=1, source_target_pairs={{0,6},{2,4},{4,2},{6,0},{1,7},{3,5},{5,3},{7,1},{8,14},{10,12},{12... | collective-permute-start | bytes 49160 | tf_op jit(solution)/shard_map/ppermute | solution.py:482
  62.5 1.9 %collective-permute-done.19.refs_3_ = f32[4,8,128]{2,1,0:T(8,128)S(1)} collective-permute-done((f32[4,8,128]{2,1,0:T(8,128)S(1)}, f32[4,8,128]{2,1,0:T(8,128)S(1)}, u32[]{:S(2)}, u32[]{:S(2)}) %collective-permute-start.19) | collective-permute-done | bytes 16416 | tf_op jit(solution)/shard_map/ppermute | solution.py:482
  64.4 3.4 %shard_map.112 = f32[120,128]{1,0:T(8,128)} custom-call(s32[4,4,8,128]{3,2,1,0:T(8,128)S(1)} %copy_bitcast_fusion.1.cells_ref, f32[4,8,128]{2,1,0:T(8,128)S(1)} %pad_maximum_fusion.refs_0_, f32[4,8,128]{2,1,0:T(8,128)S(1)} %collective-permute-done.17.refs_1_, f32[4,8,128]{2,1,0:T(8,128)S(1)} %collective-permute-done.18.refs_2_, ...), custom_call_target="tpu_custom_call" | custom-call | flops 1 | bytes 1 | tf_op jit(solution)/shard_map/pallas_call | solution.py:19
  (36 shorter events, 2.7 us)
Async XLA Ops:
  2.3 12.4 %copy-start.4 = (s32[4,2]{0,1:T(2,128)S(1)}, s32[4,2]{0,1:T(2,128)}, u32[]{:S(2)}) copy-start(s32[4,2]{0,1:T(2,128)} %param.14) | copy-start | bytes 100
  2.3 16.1 %collective-permute-start.2 = (f32[4,40,384]{2,1,0:T(8,128)}, f32[4,40,384]{2,1,0:T(8,128)S(1)}, u32[]{:S(2)}, u32[]{:S(2)}) collective-permute-start(f32[4,40,384]{2,1,0:T(8,128)} %shard_map.105), channel_id=1, source_target_pairs={{2,0},{4,2},{6,4},{3,1},{5,3},{7,5},{10,8},{12,10},{14,12},{11,9},... | collective-permute-start | bytes 737288 | tf_op jit(solution)/shard_map/ppermute | solution.py:525
  9.8 2.5 %copy-start = (f32[17,4,3,56,128]{4,3,2,1,0:T(8,128)}, f32[17,4,3,56,128]{4,3,2,1,0:T(8,128)S(1)}, u32[]{:S(2)}) copy-start(f32[17,4,3,56,128]{4,3,2,1,0:T(8,128)S(1)} %get-tuple-element.39.v_ref) | copy-start | bytes 17547268
  12.3 5.0 %collective-permute-start = (f32[3,68,128]{2,1,0:T(8,128)}, f32[3,68,128]{2,1,0:T(8,128)S(1)}, u32[]{:S(2)}, u32[]{:S(2)}) collective-permute-start(f32[3,68,128]{2,1,0:T(8,128)} %get-tuple-element.40), channel_id=1, source_target_pairs={{0,8},{8,16},{16,24},{24,0},{1,9},{9,17},{17,25},{25,1},{2,10},{10... | collective-permute-start | bytes 313352 | tf_op jit(solution)/shard_map/ppermute | solution.py:520
  12.8 5.7 %collective-permute-start.1 = (f32[3,68,128]{2,1,0:T(8,128)}, f32[3,68,128]{2,1,0:T(8,128)S(1)}, u32[]{:S(2)}, u32[]{:S(2)}) collective-permute-start(f32[3,68,128]{2,1,0:T(8,128)} %get-tuple-element.41), channel_id=1, source_target_pairs={{8,0},{16,8},{24,16},{0,24},{9,1},{17,9},{25,17},{1,25},{10,2},{18... | collective-permute-start | bytes 313352 | tf_op jit(solution)/shard_map/ppermute | solution.py:520
  18.5 2.7 %copy-start.1 = (f32[17,4,3,56,128]{4,3,2,1,0:T(8,128)S(1)}, f32[17,4,3,56,128]{4,3,2,1,0:T(8,128)}, u32[]{:S(2)}) copy-start(f32[17,4,3,56,128]{4,3,2,1,0:T(8,128)} %copy-done) | copy-start | bytes 17547268
  21.4 10.8 %collective-permute-start.5 = (f32[4,40,384]{2,1,0:T(8,128)S(1)}, f32[4,40,384]{2,1,0:T(8,128)S(1)}, u32[]{:S(2)}, u32[]{:S(2)}) collective-permute-start(f32[4,40,384]{2,1,0:T(8,128)S(1)} %get-tuple-element.47.lowest_ref), channel_id=1, source_target_pairs={{2,0},{4,2},{6,4},{3,1},{5,3},{7,5},{10,8},{12,10},{14,12},{11,9},... | collective-permute-start | bytes 737288 | tf_op jit(solution)/shard_map/ppermute | solution.py:525
  22.7 6.9 %collective-permute-start.3 = (f32[3,4,128]{2,1,0:T(4,128)S(1)}, f32[3,4,128]{2,1,0:T(4,128)S(1)}, u32[]{:S(2)}, u32[]{:S(2)}) collective-permute-start(f32[3,4,128]{2,1,0:T(4,128)S(1)} %get-tuple-element.50), channel_id=1, source_target_pairs={{0,8},{8,16},{16,24},{24,0},{1,9},{9,17},{17,25},{25,1},{2,10},{10... | collective-permute-start | bytes 18440 | tf_op jit(solution)/shard_map/ppermute | solution.py:520
  24.1 5.5 %collective-permute-start.4 = (f32[3,4,128]{2,1,0:T(4,128)S(1)}, f32[3,4,128]{2,1,0:T(4,128)S(1)}, u32[]{:S(2)}, u32[]{:S(2)}) collective-permute-start(f32[3,4,128]{2,1,0:T(4,128)S(1)} %get-tuple-element.51), channel_id=1, source_target_pairs={{8,0},{16,8},{24,16},{0,24},{9,1},{17,9},{25,17},{1,25},{10,2},{18... | collective-permute-start | bytes 18440 | tf_op jit(solution)/shard_map/ppermute | solution.py:520
  29.6 6.0 %copy-start.5 = (f32[18]{0:T(128)S(1)}, f32[18]{0:T(128)}, u32[]{:S(2)}) copy-start(f32[18]{0:T(128)} %param.15) | copy-start | bytes 220
  29.6 6.1 %copy-start.2 = (f32[4,40,384]{2,1,0:T(8,128)S(1)}, f32[4,40,384]{2,1,0:T(8,128)}, u32[]{:S(2)}) copy-start(f32[4,40,384]{2,1,0:T(8,128)} %share_ref.1) | copy-start | bytes 737284
  29.9 4.4 %collective-permute-start.6 = (f32[3,68,128]{2,1,0:T(8,128)S(1)}, f32[3,68,128]{2,1,0:T(8,128)S(1)}, u32[]{:S(2)}, u32[]{:S(2)}) collective-permute-start(f32[3,68,128]{2,1,0:T(8,128)S(1)} %get-tuple-element.58), channel_id=1, source_target_pairs={{0,8},{8,16},{16,24},{24,0},{1,9},{9,17},{17,25},{25,1},{2,10},{10... | collective-permute-start | bytes 313352 | tf_op jit(solution)/shard_map/ppermute | solution.py:520
  30.2 4.5 %collective-permute-start.7 = (f32[3,68,128]{2,1,0:T(8,128)S(1)}, f32[3,68,128]{2,1,0:T(8,128)S(1)}, u32[]{:S(2)}, u32[]{:S(2)}) collective-permute-start(f32[3,68,128]{2,1,0:T(8,128)S(1)} %get-tuple-element.59), channel_id=1, source_target_pairs={{8,0},{16,8},{24,16},{0,24},{9,1},{17,9},{25,17},{1,25},{10,2},{18... | collective-permute-start | bytes 313352 | tf_op jit(solution)/shard_map/ppermute | solution.py:520
  32.4 24.0 %copy-start.3 = (s32[4,3840]{1,0:T(4,128)S(1)}, s32[4,3840]{1,0:T(4,128)}, u32[]{:S(2)}) copy-start(s32[4,3840]{1,0:T(4,128)} %param.17) | copy-start | bytes 184324
  32.4 3.2 %collective-permute-start.8 = (f32[3,4,128]{2,1,0:T(4,128)S(1)}, f32[3,4,128]{2,1,0:T(4,128)S(1)}, u32[]{:S(2)}, u32[]{:S(2)}) collective-permute-start(f32[3,4,128]{2,1,0:T(4,128)S(1)} %get-tuple-element.60), channel_id=1, source_target_pairs={{0,8},{8,16},{16,24},{24,0},{1,9},{9,17},{17,25},{25,1},{2,10},{10... | collective-permute-start | bytes 18440 | tf_op jit(solution)/shard_map/ppermute | solution.py:520
  32.9 2.7 %collective-permute-start.9 = (f32[3,4,128]{2,1,0:T(4,128)S(1)}, f32[3,4,128]{2,1,0:T(4,128)S(1)}, u32[]{:S(2)}, u32[]{:S(2)}) collective-permute-start(f32[3,4,128]{2,1,0:T(4,128)S(1)} %get-tuple-element.61), channel_id=1, source_target_pairs={{8,0},{16,8},{24,16},{0,24},{9,1},{17,9},{25,17},{1,25},{10,2},{18... | collective-permute-start | bytes 18440 | tf_op jit(solution)/shard_map/ppermute | solution.py:520
  38.6 5.4 %collective-permute-start.10 = (f32[4,8,128]{2,1,0:T(8,128)S(1)}, f32[4,8,128]{2,1,0:T(8,128)S(1)}, u32[]{:S(2)}, u32[]{:S(2)}) collective-permute-start(f32[4,8,128]{2,1,0:T(8,128)S(1)} %get-tuple-element.69), channel_id=1, source_target_pairs={{0,2},{2,0},{4,6},{6,4},{1,3},{3,1},{5,7},{7,5},{8,10},{10,8},{12,... | collective-permute-start | bytes 49160 | tf_op jit(solution)/shard_map/ppermute | solution.py:482
  41.1 4.8 %collective-permute-start.11 = (f32[4,8,128]{2,1,0:T(8,128)S(1)}, f32[4,8,128]{2,1,0:T(8,128)S(1)}, u32[]{:S(2)}, u32[]{:S(2)}) collective-permute-start(f32[4,8,128]{2,1,0:T(8,128)S(1)} %get-tuple-element.70), channel_id=1, source_target_pairs={{0,4},{2,6},{4,0},{6,2},{1,5},{3,7},{5,1},{7,3},{8,12},{10,14},{12... | collective-permute-start | bytes 49160 | tf_op jit(solution)/shard_map/ppermute | solution.py:482
  44.0 5.6 %collective-permute-start.12 = (f32[4,8,128]{2,1,0:T(8,128)S(1)}, f32[4,8,128]{2,1,0:T(8,128)S(1)}, u32[]{:S(2)}, u32[]{:S(2)}) collective-permute-start(f32[4,8,128]{2,1,0:T(8,128)S(1)} %get-tuple-element.71), channel_id=1, source_target_pairs={{0,6},{2,4},{4,2},{6,0},{1,7},{3,5},{5,3},{7,1},{8,14},{10,12},{12... | collective-permute-start | bytes 49160 | tf_op jit(solution)/shard_map/ppermute | solution.py:482
  49.6 3.7 %collective-permute-start.13 = (f32[4,8,128]{2,1,0:T(8,128)S(1)}, f32[4,8,128]{2,1,0:T(8,128)S(1)}, u32[]{:S(2)}, u32[]{:S(2)}) collective-permute-start(f32[4,8,128]{2,1,0:T(8,128)S(1)} %add_add_fusion.mine_ref), channel_id=1, source_target_pairs={{0,1},{1,0},{2,3},{3,2},{4,5},{5,4},{6,7},{7,6},{8,9},{9,8},{10,11... | collective-permute-start | bytes 49160 | tf_op jit(solution)/shard_map/ppermute | solution.py:482
  53.4 3.1 %collective-permute-start.14 = (f32[8,128]{1,0:T(8,128)S(1)}, f32[8,128]{1,0:T(8,128)S(1)}, u32[]{:S(2)}, u32[]{:S(2)}) collective-permute-start(f32[8,128]{1,0:T(8,128)S(1)} %get-tuple-element.73), channel_id=1, source_target_pairs={{0,8},{8,16},{16,24},{24,0},{1,9},{9,17},{17,25},{25,1},{2,10},{10... | collective-permute-start | bytes 12296 | tf_op jit(solution)/shard_map/ppermute | solution.py:501
  53.5 3.7 %collective-permute-start.15 = (f32[8,128]{1,0:T(8,128)S(1)}, f32[8,128]{1,0:T(8,128)S(1)}, u32[]{:S(2)}, u32[]{:S(2)}) collective-permute-start(f32[8,128]{1,0:T(8,128)S(1)} %get-tuple-element.74), channel_id=1, source_target_pairs={{0,16},{8,24},{16,0},{24,8},{1,17},{9,25},{17,1},{25,9},{2,18},{10... | collective-permute-start | bytes 12296 | tf_op jit(solution)/shard_map/ppermute | solution.py:501
  55.1 2.7 %collective-permute-start.16 = (f32[8,128]{1,0:T(8,128)S(1)}, f32[8,128]{1,0:T(8,128)S(1)}, u32[]{:S(2)}, u32[]{:S(2)}) collective-permute-start(f32[8,128]{1,0:T(8,128)S(1)} %get-tuple-element.75), channel_id=1, source_target_pairs={{0,24},{8,0},{16,8},{24,16},{1,25},{9,1},{17,9},{25,17},{2,26},{10... | collective-permute-start | bytes 12296 | tf_op jit(solution)/shard_map/ppermute | solution.py:501
  57.8 4.4 %collective-permute-start.17 = (f32[4,8,128]{2,1,0:T(8,128)S(1)}, f32[4,8,128]{2,1,0:T(8,128)S(1)}, u32[]{:S(2)}, u32[]{:S(2)}) collective-permute-start(f32[4,8,128]{2,1,0:T(8,128)S(1)} %pad_maximum_fusion.refs_0_), channel_id=1, source_target_pairs={{0,2},{2,0},{4,6},{6,4},{1,3},{3,1},{5,7},{7,5},{8,10},{10,8},{12,... | collective-permute-start | bytes 49160 | tf_op jit(solution)/shard_map/ppermute | solution.py:482
  57.8 4.7 %collective-permute-start.18 = (f32[4,8,128]{2,1,0:T(8,128)S(1)}, f32[4,8,128]{2,1,0:T(8,128)S(1)}, u32[]{:S(2)}, u32[]{:S(2)}) collective-permute-start(f32[4,8,128]{2,1,0:T(8,128)S(1)} %pad_maximum_fusion.refs_0_), channel_id=1, source_target_pairs={{0,4},{2,6},{4,0},{6,2},{1,5},{3,7},{5,1},{7,3},{8,12},{10,14},{12... | collective-permute-start | bytes 49160 | tf_op jit(solution)/shard_map/ppermute | solution.py:482
  58.8 5.5 %collective-permute-start.19 = (f32[4,8,128]{2,1,0:T(8,128)S(1)}, f32[4,8,128]{2,1,0:T(8,128)S(1)}, u32[]{:S(2)}, u32[]{:S(2)}) collective-permute-start(f32[4,8,128]{2,1,0:T(8,128)S(1)} %pad_maximum_fusion.refs_0_), channel_id=1, source_target_pairs={{0,6},{2,4},{4,2},{6,0},{1,7},{3,5},{5,3},{7,1},{8,14},{10,12},{12... | collective-permute-start | bytes 49160 | tf_op jit(solution)/shard_map/ppermute | solution.py:482

commit v5 on v4

--- a/solution.py
+++ b/solution.py
@@ -122,7 +122,7 @@
 
 def flags(seam_ref):
     tile = lax.axis_index("tile")
-    return seam_ref[tile, 0:1, :] == 1, seam_ref[tile, 1:2, :] == 1
+    return seam_ref[0, pl.ds(tile, 1), :] == 1, seam_ref[1, pl.ds(tile, 1), :] == 1
 
 
 def start_kernel(f_hbm, out_ref, sem):
@@ -354,7 +354,7 @@
     cx_ref, code_ref, weight_ref, share_ref,
     out_hbm, *refs,
 ):
-    *piece_refs, lrow_ref, rrow_ref, ltop_ref, rtop_ref, out_ref, sens_ref, packed_ref, sems = refs
+    *piece_refs, lrow_ref, rrow_ref, ltop_ref, rtop_ref, out_ref, sens_ref, sems = refs
     below, sectors, tiles, padded, _ = v_ref.shape
     strips = (padded - 2 * ROWS) // ROWS
     flip_left, flip_right = flags(seam_ref)
@@ -414,12 +414,12 @@
         return 0
 
     lax.fori_loop(0, below, step, 0)
-    if len(piece_refs) == 1:
-        piece_refs[0][...] = sens_ref[...]
+    (piece_ref,) = piece_refs
+    if len(piece_ref.shape) == 2:
+        piece_ref[...] = sens_ref[...]
     else:
-        owners, group, depth, _ = packed_ref.shape
+        owners, group, copies, depth, _ = piece_ref.shape
         share = strips * ROWS * tiles // owners
-        rank = lax.axis_index("lev")
         for o in range(owners):
             for place in range(group * depth):
                 piece, line = divmod(place, depth)
@@ -428,9 +428,8 @@
                     row = sens_ref[x : x + 1, j * LANES : (j + 1) * LANES]
                 else:
                     row = jnp.zeros((1, LANES), jnp.float32)
-                packed_ref[o, piece, line : line + 1, :] = row
-        for apart, ref in enumerate(piece_refs):
-            ref[...] = packed_ref[:, jnp.bitwise_xor(rank, apart)]
+                for i in range(copies):
+                    piece_ref[o, piece, i, line : line + 1, :] = row
     for k in range(below + 2):
         send(k).wait()
 
@@ -439,7 +438,7 @@
     *value_refs, out_ref = refs
     rows, lanes = out_ref.shape
     group, owners, depth, _ = cells_ref.shape
-    tile, rank = lax.axis_index("tile"), lax.axis_index("lev")
+    rank = lax.axis_index("lev")
     high_iota = lax.broadcasted_iota(jnp.int32, (rows, lanes), 0)
     low_iota = lax.broadcasted_iota(jnp.int32, (lanes, lanes), 0)
     total = jnp.zeros((2 * rows, lanes), jnp.float32)
@@ -447,8 +446,7 @@
     for pair in range(0, len(lines), 2):
         lefts, rights = [], []
         for part, owner, line in lines[pair : pair + 2]:
-            source = lax.rem(tile + owners - owner, owners)
-            cells = cells_ref[jnp.bitwise_xor(rank, part), source, line : line + 1, :]
+            cells = cells_ref[jnp.bitwise_xor(rank, part), owner, line : line + 1, :]
             value = value_refs[part][owner, line : line + 1, :]
             coarse = value.astype(jnp.bfloat16).astype(jnp.float32)
             fine = value - coarse
@@ -469,14 +467,6 @@
     out_ref[...] = total[:rows] + total[rows:]
 
 
-def choose_kernel(mine_ref, other_ref, *out_refs):
-    owners = mine_ref.shape[0]
-    tile = lax.axis_index("tile")
-    for apart, ref in enumerate(out_refs):
-        owner = lax.rem(tile + apart, owners)
-        ref[...] = mine_ref[owner] + other_ref[owner]
-
-
 def exchanged(value, axis, apart):
     count = lax.axis_size(axis)
     return lax.ppermute(value, axis, [(i, i ^ apart) for i in range(count)])
@@ -484,26 +474,12 @@
 
 def remapped(pieces, flux_cell):
     owners, share = flux_cell.shape
-    group = lax.axis_size("lev")
-    depth = pieces[0].shape[1]
-    mine = pieces[0]
-    arrived = [exchanged(pieces[d], "lev", d) for d in range(1, group)]
-    for other in arrived:
-        mine = mine + other
-    other = exchanged(mine, "sec", 1)
-    if owners <= 8:
-        sent = call(
-            choose_kernel, (f32(depth, LANES),) * owners, [VM] * 2, [VM] * owners, (mine, other)
-        )
-        got = [sent[0]]
-        for d in range(1, owners):
-            hops = [(i, (i + d) % owners) for i in range(owners)]
-            got.append(lax.ppermute(sent[d], "tile", hops))
-        own = jnp.stack(got)
-    else:
-        own = lax.all_to_all(mine + other, "tile", split_axis=0, concat_axis=0, tiled=True)
-        order = jnp.remainder(lax.axis_index("tile") - jnp.arange(owners), owners)
-        own = jnp.take(own, order, axis=0)
+    _, group, copies, depth, _ = pieces.shape
+    sent = pieces.reshape(-1, depth, LANES)
+    arrived = lax.all_to_all(
+        sent, ("tile", "lev", "sec"), split_axis=0, concat_axis=0, tiled=True
+    )
+    own = jnp.sum(arrived.reshape(owners, group * copies, depth, LANES), axis=1)
     parts = [own] + [exchanged(own, "lev", d) for d in range(1, group)]
     cells = jnp.pad(flux_cell, ((0, 0), (0, group * depth * LANES - share)))
     cells = cells.reshape(owners, group, depth, LANES).transpose(1, 0, 2, 3)
@@ -539,7 +515,7 @@
     rim_next = kept(tiles, (below - 1) * sectors, LANES)
     rim_scratch = pltpu.VMEM((tiles, below * sectors, LANES), jnp.float32)
 
-    seam = jnp.broadcast_to(seam_code[:, :, None], (*seam_code.shape, LANES))
+    seam = jnp.broadcast_to(seam_code.T[:, :, None], (*seam_code.T.shape, LANES))
     weight = jnp.broadcast_to(level_weight[:, None], (levels, LANES))
 
     above = from_above(
@@ -609,15 +585,15 @@
     left_top, right_top = around(first_top, last_top)
 
     owners, share = flux_cell.shape
-    group = lax.axis_size("lev")
+    group, copies = lax.axis_size("lev"), lax.axis_size("sec")
     depth = -(-share // (group * LANES))
-    aligned = share % LANES == 0 and width % LANES == 0
-    pieces = (f32(owners, depth, LANES),) * group if aligned else (f32(columns, width),)
-    adjoint, *pieces = call(
+    aligned = share % LANES == 0
+    packed = (owners, group, copies, depth, LANES)
+    adjoint, pieces = call(
         final_kernel,
-        (f32(*forcing.shape), *pieces),
+        (f32(*forcing.shape), f32(*packed) if aligned else f32(columns, width)),
         [VM] * 12,
-        [HBM] + [VM] * len(pieces),
+        [HBM, VM],
         (
             v, vs, vt, left, right, left_top, right_top, seam,
             courant_x, limiter_code, weight, sector_share,
@@ -628,19 +604,14 @@
             pltpu.VMEM((tiles, sectors, LANES), jnp.float32),
             pltpu.VMEM((levels, sectors, columns, width), jnp.float32),
             pltpu.VMEM((columns, width), jnp.float32),
-            pltpu.VMEM((owners, group, depth, LANES), jnp.float32),
             pltpu.SemaphoreType.DMA((levels,)),
         ],
     )
     if not aligned:
-        packed = jnp.pad(
-            pieces[0].reshape(owners, share), ((0, 0), (0, group * depth * LANES - share))
-        ).reshape(owners, group, depth, LANES)
-        rank = lax.axis_index("lev")
-        pieces = [
-            lax.dynamic_index_in_dim(packed, jnp.bitwise_xor(rank, d), 1, keepdims=False)
-            for d in range(group)
-        ]
+        pieces = jnp.pad(
+            pieces.reshape(owners, share), ((0, 0), (0, group * depth * LANES - share))
+        ).reshape(owners, group, 1, depth, LANES)
+        pieces = jnp.broadcast_to(pieces, packed)
     flux_cell, pieces = lax.optimization_barrier((flux_cell, pieces))
     return (adjoint, remapped(pieces, flux_cell))
 

time: 68 us -> 58.7 us (0.86)
  local copies, waits for them, and re-layouts: 5.44 us -> 0.18 us
  starting transfers between devices: 25.1 us -> 22.9 us
  waiting for transfers between devices: 16.9 us -> 15.9 us
  Pallas kernels: 19.5 us -> 18.6 us
    all_to_all x0 -> x1, waiting for transfers between devices: none -> 7.71 us  [remapped(): lax.all_to_all(sent, ('tile', 'lev', 'sec'), split_axis=0, concat_axis=0,...]
    all_to_all x0 -> x1, starting transfers between devices: none -> 7.58 us  [remapped(): lax.all_to_all(sent, ('tile', 'lev', 'sec'), split_axis=0, concat_axis=0,...]
    ppermute x7 -> x3, waiting for transfers between devices: 10 us -> 3.05 us  [exchanged(): return lax.ppermute(value, axis, [(i, i ^ apart) for i in range(count)])]
    ppermute x7 -> x3, starting transfers between devices: 11.3 us -> 4.45 us  [exchanged(): return lax.ppermute(value, axis, [(i, i ^ apart) for i in range(count)])]
    unnamed x14 -> x9, local copies, waits for them, and re-layouts: 5.29 us -> 0.03 us
    ppermute x3 -> x0, starting transfers between devices: 3.05 us -> none  [remapped(): got.append(lax.ppermute(sent[d], 'tile', hops))]
    ppermute x3 -> x0, waiting for transfers between devices: 1.32 us -> none  [remapped(): got.append(lax.ppermute(sent[d], 'tile', hops))]
    pallas_call x9 -> x8, Pallas kernels: 19.5 us -> 18.6 us  [call(): pl.pallas_call(kernel, out_shape=out_shape, in_specs=in_specs, out_specs=...]
  transfers between devices with their start and end apart: 20 -> 14, of which waited for: 12 -> 8; matrix products, arithmetic and copies ran while one was open for 0% -> 0% of each run, Pallas kernels for 17% -> 18%
where the time goes in v5:
time: 58.7 us; the launch traced here: 58.4 us
  starting transfers between devices  22.9 us (39%)
  Pallas kernels  18.6 us (32%)
  waiting for transfers between devices  15.9 us (27%)
  between operations  0.79 us (1%)
    pallas_call x8, Pallas kernels, call(): pl.pallas_call(kernel, out_shape=out_shape, in_specs=in_specs, out_specs=...  18.6 us
    ppermute x8, starting transfers between devices, around(): return (lax.ppermute(last, 'tile', up), lax.ppermute(first, 'tile', down))  8.32 us
    all_to_all x1, waiting for transfers between devices, remapped(): lax.all_to_all(sent, ('tile', 'lev', 'sec'), split_axis=0, concat_axis=0,...  7.71 us
    all_to_all x1, starting transfers between devices, remapped(): lax.all_to_all(sent, ('tile', 'lev', 'sec'), split_axis=0, concat_axis=0,...  7.58 us
    ppermute x8, waiting for transfers between devices, around(): return (lax.ppermute(last, 'tile', up), lax.ppermute(first, 'tile', down))  4.75 us
    ppermute x3, starting transfers between devices, exchanged(): return lax.ppermute(value, axis, [(i, i ^ apart) for i in range(count)])  4.45 us
    ppermute x3, waiting for transfers between devices, exchanged(): return lax.ppermute(value, axis, [(i, i ^ apart) for i in range(count)])  3.05 us
    ppermute x2, starting transfers between devices, from_above(): return lax.ppermute(value, 'lev', [(i + 1, i) for i in range(count - 1)])  2.58 us
  transfers between devices with their start and end apart: 14, of which 8 were waited for; matrix products, arithmetic and copies ran while one was open for 0% of the time, Pallas kernels for 18%

profile of v5, /device:TPU:0, one launch (start us, length us, event | category | flops | bytes accessed | tf_op | source)
XLA Modules:
  0.0 58.4 jit_solution(816399269981849193)
XLA Ops:
  0.6 1.0 %shard_map.105 = f32[4,40,384]{2,1,0:T(8,128)S(1)} custom-call(f32[4,18,40,384]{3,2,1,0:T(8,128)} %f_hbm.3), custom_call_target="tpu_custom_call" | custom-call | flops 1 | bytes 1 | tf_op jit(solution)/shard_map/pallas_call | solution.py:19
  1.6 1.3 %collective-permute-start.2 = (f32[4,40,384]{2,1,0:T(8,128)S(1)}, f32[4,40,384]{2,1,0:T(8,128)S(1)}, u32[]{:S(2)}, u32[]{:S(2)}) collective-permute-start(f32[4,40,384]{2,1,0:T(8,128)S(1)} %shard_map.105), channel_id=1, source_target_pairs={{2,0},{4,2},{6,4},{3,1},{5,3},{7,5},{10,8},{12,10},{14,12},{11,9},... | collective-permute-start | bytes 737288 | tf_op jit(solution)/shard_map/ppermute | solution.py:501
  2.9 5.5 %shard_map.104 = (f32[17,4,3,56,128]{4,3,2,1,0:T(8,128)S(1)}, f32[3,68,128]{2,1,0:T(8,128)S(1)}, f32[3,68,128]{2,1,0:T(8,128)S(1)}, f32[4,40,384]{2,1,0:T(8,128)...) custom-call(f32[4,18,40,384]{3,2,1,0:T(8,128)} %f_hbm.3, ...), custom_call_target="tpu_custom_call" | custom-call | flops 1 | bytes 1 | tf_op jit(solution)/shard_map/pallas_call | solution.py:19
  8.4 0.5 collective-permute-start
  8.9 2.0 %collective-permute-start.1 = (f32[3,68,128]{2,1,0:T(8,128)S(1)}, f32[3,68,128]{2,1,0:T(8,128)S(1)}, u32[]{:S(2)}, u32[]{:S(2)}) collective-permute-start(f32[3,68,128]{2,1,0:T(8,128)S(1)} %get-tuple-element.31), channel_id=1, source_target_pairs={{8,0},{16,8},{24,16},{0,24},{9,1},{17,9},{25,17},{1,25},{10,2},{18... | collective-permute-start | bytes 313352 | tf_op jit(solution)/shard_map/ppermute | solution.py:496
  10.9 2.4 %collective-permute-done.left_ref = f32[3,68,128]{2,1,0:T(8,128)S(1)} collective-permute-done((f32[3,68,128]{2,1,0:T(8,128)S(1)}, f32[3,68,128]{2,1,0:T(8,128)S(1)}, u32[]{:S(2)}, u32[]{:S(2)}) %collective-permute-start) | collective-permute-done | bytes 104480 | tf_op jit(solution)/shard_map/ppermute | solution.py:496
  13.3 1.0 %collective-permute-done.1.right_ref = f32[3,68,128]{2,1,0:T(8,128)S(1)} collective-permute-done((f32[3,68,128]{2,1,0:T(8,128)S(1)}, f32[3,68,128]{2,1,0:T(8,128)S(1)}, u32[]{:S(2)}, u32[]{:S(2)}) %collective-permute-start.1) | collective-permute-done | bytes 104480 | tf_op jit(solution)/shard_map/ppermute | solution.py:496
  14.3 0.1 broadcast_in_dim.4.seam_ref
  14.3 0.3 shard_map.106
  14.6 1.3 %collective-permute-start.5 = (f32[4,40,384]{2,1,0:T(8,128)S(1)}, f32[4,40,384]{2,1,0:T(8,128)S(1)}, u32[]{:S(2)}, u32[]{:S(2)}) collective-permute-start(f32[4,40,384]{2,1,0:T(8,128)S(1)} %get-tuple-element.37.lowest_ref), channel_id=1, source_target_pairs={{2,0},{4,2},{6,4},{3,1},{5,3},{7,5},{10,8},{12,10},{14,12},{11,9},... | collective-permute-start | bytes 737288 | tf_op jit(solution)/shard_map/ppermute | solution.py:501
  15.9 1.5 %collective-permute-start.3 = (f32[3,4,128]{2,1,0:T(4,128)S(1)}, f32[3,4,128]{2,1,0:T(4,128)S(1)}, u32[]{:S(2)}, u32[]{:S(2)}) collective-permute-start(f32[3,4,128]{2,1,0:T(4,128)S(1)} %get-tuple-element.40), channel_id=1, source_target_pairs={{0,8},{8,16},{16,24},{24,0},{1,9},{9,17},{17,25},{25,1},{2,10},{10... | collective-permute-start | bytes 18440 | tf_op jit(solution)/shard_map/ppermute | solution.py:496
  17.4 0.8 %collective-permute-start.4 = (f32[3,4,128]{2,1,0:T(4,128)S(1)}, f32[3,4,128]{2,1,0:T(4,128)S(1)}, u32[]{:S(2)}, u32[]{:S(2)}) collective-permute-start(f32[3,4,128]{2,1,0:T(4,128)S(1)} %get-tuple-element.41), channel_id=1, source_target_pairs={{8,0},{16,8},{24,16},{0,24},{9,1},{17,9},{25,17},{1,25},{10,2},{18... | collective-permute-start | bytes 18440 | tf_op jit(solution)/shard_map/ppermute | solution.py:496
  18.1 4.6 %shard_map.107 = (f32[16,4,3,56,128]{4,3,2,1,0:T(8,128)S(1)}, f32[3,64,128]{2,1,0:T(8,128)S(1)}, f32[3,64,128]{2,1,0:T(8,128)S(1)}, f32[4,3,40,128]{3,2,1,0:T(8,128)S(1)}) custom-call(f32[17,4,3,56,128]{4,3,2,1,0:T(8,128)S(1)} %get-tuple-element.29.v_ref, f32[3,68,128]{2,1,0:T(8,128)S(1)} %collective-permute-done.left_ref, ...), custom_call_target="tpu_custom_call" | custom-call | flops 1 | bytes 1 | tf_op jit(solution)/shard_map/pallas_call | solution.py:19
  22.8 0.2 shard_map.108
  23.1 0.4 collective-permute-start.6
  23.5 1.4 %collective-permute-start.7 = (f32[3,68,128]{2,1,0:T(8,128)S(1)}, f32[3,68,128]{2,1,0:T(8,128)S(1)}, u32[]{:S(2)}, u32[]{:S(2)}) collective-permute-start(f32[3,68,128]{2,1,0:T(8,128)S(1)} %get-tuple-element.49), channel_id=1, source_target_pairs={{8,0},{16,8},{24,16},{0,24},{9,1},{17,9},{25,17},{1,25},{10,2},{18... | collective-permute-start | bytes 313352 | tf_op jit(solution)/shard_map/ppermute | solution.py:496
  24.9 0.4 collective-permute-done.5.above_ref
  25.3 0.2 shard_map.109
  25.5 0.6 collective-permute-start.8
  26.1 1.2 %collective-permute-start.9 = (f32[3,4,128]{2,1,0:T(4,128)S(1)}, f32[3,4,128]{2,1,0:T(4,128)S(1)}, u32[]{:S(2)}, u32[]{:S(2)}) collective-permute-start(f32[3,4,128]{2,1,0:T(4,128)S(1)} %get-tuple-element.51), channel_id=1, source_target_pairs={{8,0},{16,8},{24,16},{0,24},{9,1},{17,9},{25,17},{1,25},{10,2},{18... | collective-permute-start | bytes 18440 | tf_op jit(solution)/shard_map/ppermute | solution.py:496
  27.3 0.7 %collective-permute-done.7.right_ref = f32[3,68,128]{2,1,0:T(8,128)S(1)} collective-permute-done((f32[3,68,128]{2,1,0:T(8,128)S(1)}, f32[3,68,128]{2,1,0:T(8,128)S(1)}, u32[]{:S(2)}, u32[]{:S(2)}) %collective-permute-start.7) | collective-permute-done | bytes 104480 | tf_op jit(solution)/shard_map/ppermute | solution.py:496
  28.0 0.7 %collective-permute-done.8.left_top_ref = f32[3,4,128]{2,1,0:T(4,128)S(1)} collective-permute-done((f32[3,4,128]{2,1,0:T(4,128)S(1)}, f32[3,4,128]{2,1,0:T(4,128)S(1)}, u32[]{:S(2)}, u32[]{:S(2)}) %collective-permute-start.8) | collective-permute-done | bytes 6176 | tf_op jit(solution)/shard_map/ppermute | solution.py:496
  28.7 0.1 broadcast_in_dim.5.weight_ref
  28.8 3.5 %shard_map.110 = (f32[4,18,40,384]{3,2,1,0:T(8,128)}, f32[4,4,2,8,128]{4,3,2,1,0:T(8,128)}) custom-call(f32[16,4,3,56,128]{4,3,2,1,0:T(8,128)S(1)} %get-tuple-element.38.v_ref, f32[4,3,56,128]{3,2,1,0:T(8,128)S(1)} %get-tuple-element.45.vs_ref, f32[4,3,56,128]{3,2,1,0:T(8,128)S(1)} %get-tuple-element.47.vt_ref, ...), custom_call_target="tpu_custom_call" | custom-call | flops 1 | bytes 1 | tf_op jit(solution)/shard_map/pallas_call | solution.py:19
  32.3 7.6 %all-to-all-start = ((f32[32,8,128]{2,1,0:T(8,128)}), f32[32,8,128]{2,1,0:T(8,128)S(1)}, u32[]{:S(2)}, u32[]{:S(2)}) async-start(f32[32,8,128]{2,1,0:T(8,128)} %bitcast.2), calls=%async_computation | async-start | bytes 262144 | tf_op jit(solution)/shard_map/all_to_all | solution.py:479
  39.9 7.7 %all-to-all-done = f32[32,8,128]{2,1,0:T(8,128)S(1)} async-done(((f32[32,8,128]{2,1,0:T(8,128)}), f32[32,8,128]{2,1,0:T(8,128)S(1)}, u32[]{:S(2)}, u32[]{:S(2)}) %all-to-all-start) | async-done | bytes 131104 | tf_op jit(solution)/shard_map/all_to_all | solution.py:479
  47.6 1.1 %collective-permute-start.10 = (f32[4,8,128]{2,1,0:T(8,128)S(1)}, f32[4,8,128]{2,1,0:T(8,128)S(1)}, u32[]{:S(2)}, u32[]{:S(2)}) collective-permute-start(f32[4,8,128]{2,1,0:T(8,128)S(1)} %bitcast_reduce_fusion.refs_0_), channel_id=1, source_target_pairs={{0,2},{2,0},{4,6},{6,4},{1,3},{3,1},{5,7},{7,5},{8,10},{10,8},{12,... | collective-permute-start | bytes 49160 | tf_op jit(solution)/shard_map/ppermute | solution.py:472
  48.7 0.9 %collective-permute-start.11 = (f32[4,8,128]{2,1,0:T(8,128)S(1)}, f32[4,8,128]{2,1,0:T(8,128)S(1)}, u32[]{:S(2)}, u32[]{:S(2)}) collective-permute-start(f32[4,8,128]{2,1,0:T(8,128)S(1)} %bitcast_reduce_fusion.refs_0_), channel_id=1, source_target_pairs={{0,4},{2,6},{4,0},{6,2},{1,5},{3,7},{5,1},{7,3},{8,12},{10,14},{12... | collective-permute-start | bytes 49160 | tf_op jit(solution)/shard_map/ppermute | solution.py:472
  49.6 2.5 %collective-permute-start.12 = (f32[4,8,128]{2,1,0:T(8,128)S(1)}, f32[4,8,128]{2,1,0:T(8,128)S(1)}, u32[]{:S(2)}, u32[]{:S(2)}) collective-permute-start(f32[4,8,128]{2,1,0:T(8,128)S(1)} %bitcast_reduce_fusion.refs_0_), channel_id=1, source_target_pairs={{0,6},{2,4},{4,2},{6,0},{1,7},{3,5},{5,3},{7,1},{8,14},{10,12},{12... | collective-permute-start | bytes 49160 | tf_op jit(solution)/shard_map/ppermute | solution.py:472
  52.1 1.3 %collective-permute-done.11.refs_2_ = f32[4,8,128]{2,1,0:T(8,128)S(1)} collective-permute-done((f32[4,8,128]{2,1,0:T(8,128)S(1)}, f32[4,8,128]{2,1,0:T(8,128)S(1)}, u32[]{:S(2)}, u32[]{:S(2)}) %collective-permute-start.11) | collective-permute-done | bytes 16416 | tf_op jit(solution)/shard_map/ppermute | solution.py:472
  53.3 1.8 %collective-permute-done.12.refs_3_ = f32[4,8,128]{2,1,0:T(8,128)S(1)} collective-permute-done((f32[4,8,128]{2,1,0:T(8,128)S(1)}, f32[4,8,128]{2,1,0:T(8,128)S(1)}, u32[]{:S(2)}, u32[]{:S(2)}) %collective-permute-start.12) | collective-permute-done | bytes 16416 | tf_op jit(solution)/shard_map/ppermute | solution.py:472
  55.1 3.3 %shard_map.111 = f32[120,128]{1,0:T(8,128)} custom-call(s32[4,4,8,128]{3,2,1,0:T(8,128)S(1)} %copy_bitcast_fusion.1.cells_ref, f32[4,8,128]{2,1,0:T(8,128)S(1)} %bitcast_reduce_fusion.refs_0_, f32[4,8,128]{2,1,0:T(8,128)S(1)} %collective-permute-done.10.refs_1_, f32[4,8,128]{2,1,0:T(8,128)S(1)} %collective-permute-done.11.refs_2_, ...), custom_call_target="tpu_custom_call" | custom-call | flops 1 | bytes 1 | tf_op jit(solution)/shard_map/pallas_call | solution.py:19
  (17 shorter events, 0.1 us)
Async XLA Ops:
  1.6 12.7 %copy-start.2 = (s32[4,2]{0,1:T(2,128)S(1)}, s32[4,2]{0,1:T(2,128)}, u32[]{:S(2)}) copy-start(s32[4,2]{0,1:T(2,128)} %param.14) | copy-start | bytes 100
  1.6 12.7 %collective-permute-start.2 = (f32[4,40,384]{2,1,0:T(8,128)S(1)}, f32[4,40,384]{2,1,0:T(8,128)S(1)}, u32[]{:S(2)}, u32[]{:S(2)}) collective-permute-start(f32[4,40,384]{2,1,0:T(8,128)S(1)} %shard_map.105), channel_id=1, source_target_pairs={{2,0},{4,2},{6,4},{3,1},{5,3},{7,5},{10,8},{12,10},{14,12},{11,9},... | collective-permute-start | bytes 737288 | tf_op jit(solution)/shard_map/ppermute | solution.py:501
  8.4 4.9 %collective-permute-start = (f32[3,68,128]{2,1,0:T(8,128)S(1)}, f32[3,68,128]{2,1,0:T(8,128)S(1)}, u32[]{:S(2)}, u32[]{:S(2)}) collective-permute-start(f32[3,68,128]{2,1,0:T(8,128)S(1)} %get-tuple-element.30), channel_id=1, source_target_pairs={{0,8},{8,16},{16,24},{24,0},{1,9},{9,17},{17,25},{25,1},{2,10},{10... | collective-permute-start | bytes 313352 | tf_op jit(solution)/shard_map/ppermute | solution.py:496
  8.9 5.4 %collective-permute-start.1 = (f32[3,68,128]{2,1,0:T(8,128)S(1)}, f32[3,68,128]{2,1,0:T(8,128)S(1)}, u32[]{:S(2)}, u32[]{:S(2)}) collective-permute-start(f32[3,68,128]{2,1,0:T(8,128)S(1)} %get-tuple-element.31), channel_id=1, source_target_pairs={{8,0},{16,8},{24,16},{0,24},{9,1},{17,9},{25,17},{1,25},{10,2},{18... | collective-permute-start | bytes 313352 | tf_op jit(solution)/shard_map/ppermute | solution.py:496
  14.6 10.7 %collective-permute-start.5 = (f32[4,40,384]{2,1,0:T(8,128)S(1)}, f32[4,40,384]{2,1,0:T(8,128)S(1)}, u32[]{:S(2)}, u32[]{:S(2)}) collective-permute-start(f32[4,40,384]{2,1,0:T(8,128)S(1)} %get-tuple-element.37.lowest_ref), channel_id=1, source_target_pairs={{2,0},{4,2},{6,4},{3,1},{5,3},{7,5},{10,8},{12,10},{14,12},{11,9},... | collective-permute-start | bytes 737288 | tf_op jit(solution)/shard_map/ppermute | solution.py:501
  15.9 6.9 %collective-permute-start.3 = (f32[3,4,128]{2,1,0:T(4,128)S(1)}, f32[3,4,128]{2,1,0:T(4,128)S(1)}, u32[]{:S(2)}, u32[]{:S(2)}) collective-permute-start(f32[3,4,128]{2,1,0:T(4,128)S(1)} %get-tuple-element.40), channel_id=1, source_target_pairs={{0,8},{8,16},{16,24},{24,0},{1,9},{9,17},{17,25},{25,1},{2,10},{10... | collective-permute-start | bytes 18440 | tf_op jit(solution)/shard_map/ppermute | solution.py:496
  17.4 5.5 %collective-permute-start.4 = (f32[3,4,128]{2,1,0:T(4,128)S(1)}, f32[3,4,128]{2,1,0:T(4,128)S(1)}, u32[]{:S(2)}, u32[]{:S(2)}) collective-permute-start(f32[3,4,128]{2,1,0:T(4,128)S(1)} %get-tuple-element.41), channel_id=1, source_target_pairs={{8,0},{16,8},{24,16},{0,24},{9,1},{17,9},{25,17},{1,25},{10,2},{18... | collective-permute-start | bytes 18440 | tf_op jit(solution)/shard_map/ppermute | solution.py:496
  22.8 5.9 %copy-start.3 = (f32[18]{0:T(128)S(1)}, f32[18]{0:T(128)}, u32[]{:S(2)}) copy-start(f32[18]{0:T(128)} %param.15) | copy-start | bytes 220
  22.8 5.9 %copy-start = (f32[4,40,384]{2,1,0:T(8,128)S(1)}, f32[4,40,384]{2,1,0:T(8,128)}, u32[]{:S(2)}) copy-start(f32[4,40,384]{2,1,0:T(8,128)} %share_ref.1) | copy-start | bytes 737284
  23.1 4.2 %collective-permute-start.6 = (f32[3,68,128]{2,1,0:T(8,128)S(1)}, f32[3,68,128]{2,1,0:T(8,128)S(1)}, u32[]{:S(2)}, u32[]{:S(2)}) collective-permute-start(f32[3,68,128]{2,1,0:T(8,128)S(1)} %get-tuple-element.48), channel_id=1, source_target_pairs={{0,8},{8,16},{16,24},{24,0},{1,9},{9,17},{17,25},{25,1},{2,10},{10... | collective-permute-start | bytes 313352 | tf_op jit(solution)/shard_map/ppermute | solution.py:496
  23.5 4.5 %collective-permute-start.7 = (f32[3,68,128]{2,1,0:T(8,128)S(1)}, f32[3,68,128]{2,1,0:T(8,128)S(1)}, u32[]{:S(2)}, u32[]{:S(2)}) collective-permute-start(f32[3,68,128]{2,1,0:T(8,128)S(1)} %get-tuple-element.49), channel_id=1, source_target_pairs={{8,0},{16,8},{24,16},{0,24},{9,1},{17,9},{25,17},{1,25},{10,2},{18... | collective-permute-start | bytes 313352 | tf_op jit(solution)/shard_map/ppermute | solution.py:496
  25.5 14.4 %copy-start.1 = (s32[4,3840]{1,0:T(4,128)S(1)}, s32[4,3840]{1,0:T(4,128)}, u32[]{:S(2)}) copy-start(s32[4,3840]{1,0:T(4,128)} %param.17) | copy-start | bytes 184324
  25.5 3.2 %collective-permute-start.8 = (f32[3,4,128]{2,1,0:T(4,128)S(1)}, f32[3,4,128]{2,1,0:T(4,128)S(1)}, u32[]{:S(2)}, u32[]{:S(2)}) collective-permute-start(f32[3,4,128]{2,1,0:T(4,128)S(1)} %get-tuple-element.50), channel_id=1, source_target_pairs={{0,8},{8,16},{16,24},{24,0},{1,9},{9,17},{17,25},{25,1},{2,10},{10... | collective-permute-start | bytes 18440 | tf_op jit(solution)/shard_map/ppermute | solution.py:496
  26.1 2.6 %collective-permute-start.9 = (f32[3,4,128]{2,1,0:T(4,128)S(1)}, f32[3,4,128]{2,1,0:T(4,128)S(1)}, u32[]{:S(2)}, u32[]{:S(2)}) collective-permute-start(f32[3,4,128]{2,1,0:T(4,128)S(1)} %get-tuple-element.51), channel_id=1, source_target_pairs={{8,0},{16,8},{24,16},{0,24},{9,1},{17,9},{25,17},{1,25},{10,2},{18... | collective-permute-start | bytes 18440 | tf_op jit(solution)/shard_map/ppermute | solution.py:496
  32.3 15.3 %all-to-all-start = ((f32[32,8,128]{2,1,0:T(8,128)}), f32[32,8,128]{2,1,0:T(8,128)S(1)}, u32[]{:S(2)}, u32[]{:S(2)}) async-start(f32[32,8,128]{2,1,0:T(8,128)} %bitcast.2), calls=%async_computation | async-start | bytes 262144 | tf_op jit(solution)/shard_map/all_to_all | solution.py:479
  47.6 4.5 %collective-permute-start.10 = (f32[4,8,128]{2,1,0:T(8,128)S(1)}, f32[4,8,128]{2,1,0:T(8,128)S(1)}, u32[]{:S(2)}, u32[]{:S(2)}) collective-permute-start(f32[4,8,128]{2,1,0:T(8,128)S(1)} %bitcast_reduce_fusion.refs_0_), channel_id=1, source_target_pairs={{0,2},{2,0},{4,6},{6,4},{1,3},{3,1},{5,7},{7,5},{8,10},{10,8},{12,... | collective-permute-start | bytes 49160 | tf_op jit(solution)/shard_map/ppermute | solution.py:472
  48.7 4.6 %collective-permute-start.11 = (f32[4,8,128]{2,1,0:T(8,128)S(1)}, f32[4,8,128]{2,1,0:T(8,128)S(1)}, u32[]{:S(2)}, u32[]{:S(2)}) collective-permute-start(f32[4,8,128]{2,1,0:T(8,128)S(1)} %bitcast_reduce_fusion.refs_0_), channel_id=1, source_target_pairs={{0,4},{2,6},{4,0},{6,2},{1,5},{3,7},{5,1},{7,3},{8,12},{10,14},{12... | collective-permute-start | bytes 49160 | tf_op jit(solution)/shard_map/ppermute | solution.py:472
  49.6 5.5 %collective-permute-start.12 = (f32[4,8,128]{2,1,0:T(8,128)S(1)}, f32[4,8,128]{2,1,0:T(8,128)S(1)}, u32[]{:S(2)}, u32[]{:S(2)}) collective-permute-start(f32[4,8,128]{2,1,0:T(8,128)S(1)} %bitcast_reduce_fusion.refs_0_), channel_id=1, source_target_pairs={{0,6},{2,4},{4,2},{6,0},{1,7},{3,5},{5,3},{7,1},{8,14},{10,12},{12... | collective-permute-start | bytes 49160 | tf_op jit(solution)/shard_map/ppermute | solution.py:472

commit v6 on v5

--- a/solution.py
+++ b/solution.py
@@ -15,13 +15,14 @@
 HBM = pl.BlockSpec(memory_space=pltpu.HBM)
 
 
-def call(kernel, out_shape, in_specs, out_specs, operands, scratch=(), mib=16):
+def call(kernel, out_shape, in_specs, out_specs, operands, scratch=(), mib=16, aliases={}):
     return pl.pallas_call(
         kernel,
         out_shape=out_shape,
         in_specs=in_specs,
         out_specs=out_specs,
         scratch_shapes=list(scratch),
+        input_output_aliases=aliases,
         cost_estimate=pl.CostEstimate(flops=1, transcendentals=0, bytes_accessed=1),
         compiler_params=pltpu.CompilerParams(vmem_limit_bytes=mib * MIB),
     )(*operands)
@@ -199,7 +200,8 @@
 
 
 def ends_kernel(
-    v_ref, left_ref, right_ref, seam_ref, cx_ref, code_ref, here_ref, above_ref, mf_ref, cy_ref,
+    v_ref, inner_ref, left_ref, right_ref, seam_ref, cx_ref, code_ref, here_ref, above_ref,
+    mf_ref, cy_ref,
     out_ref, top_ref, first_ref, last_ref,
     lrow_ref, rrow_ref,
 ):
@@ -211,7 +213,11 @@
     turned(right_ref.at[:, :ROWS], flip_right, rrow_ref)
     cx = cx_ref[0].astype(jnp.float32)
     codes = code_ref[0]
-    for xt in range(strips):
+    for s in range(sectors):
+        for j in range(tiles):
+            lanes = slice(j * LANES, (j + 1) * LANES)
+            out_ref[s, ROWS : columns - ROWS, lanes] = inner_ref[s, j, ROWS : columns - ROWS]
+    for xt in (0, strips - 1):
         for j in range(tiles):
             factors = first_weights(cx, codes, 2, xt, j)
             for s in range(sectors):
@@ -243,19 +249,11 @@
                 store_rims(first_ref, last_ref, s, j, xt, strips - 1, value)
 
 
-def middle_kernel(
-    v_ref, left_ref, right_ref, lowest_ref, seam_ref, cx_ref, mf_ref, cy_ref, code_ref,
-    out_ref, first_ref, last_ref, top_ref,
-    lrow_ref, rrow_ref, a_ref,
+def middle_levels(
+    chosen, v_ref, lrow_ref, rrow_ref, cx_ref, mf_ref, cy_ref, code_ref, out_ref, a_ref, rims=None
 ):
     below, sectors, tiles, padded, _ = v_ref.shape
     strips = (padded - 2 * ROWS) // ROWS
-    flip_left, flip_right = flags(seam_ref)
-    turned(left_ref, flip_left, lrow_ref)
-    turned(right_ref, flip_right, rrow_ref)
-    for s in range(sectors):
-        for j in range(tiles):
-            a_ref[0, s, j] = lowest_ref[s, :, j * LANES : (j + 1) * LANES]
 
     def level(k, _):
         cx = cx_ref[k + 1].astype(jnp.float32)
@@ -264,7 +262,7 @@
         codes_x = code_ref[k + 1]
         codes_y = code_ref[k]
         slot = lax.rem(k, 2)
-        for xt in range(strips):
+        for xt in chosen:
             along = [first_weights(cx, codes_x, 2, xt, j) for j in range(tiles)]
             across = second_weights(cy, codes_y, 1, xt, tiles)
             rows = slice(xt * ROWS, (xt + 1) * ROWS)
@@ -282,11 +280,69 @@
                     parts.append(here + cut(mf, xt, j) * (upper - here))
                 for j, value in enumerate(second_sweep(parts, across)):
                     store_padded(out_ref, (k,), s, j, xt, value)
-                    store_rims(first_ref, last_ref, k * sectors + s, j, xt, strips - 1, value)
+                    if rims is not None:
+                        store_rims(*rims, k * sectors + s, j, xt, strips - 1, value)
         return 0
 
     lax.fori_loop(0, below - 1, level, 0)
-    top_ref[...] = a_ref[(below - 1) % 2]
+
+
+def inner_middle_kernel(
+    v_ref, cx_ref, mf_ref, cy_ref, code_ref, out_ref, lowest_ref, top_ref, a_ref
+):
+    below, sectors, tiles, padded, _ = v_ref.shape
+    strips = (padded - 2 * ROWS) // ROWS
+    cx = cx_ref[0].astype(jnp.float32)
+    for xt in range(1, strips - 1):
+        for j in range(tiles):
+            factors = first_weights(cx, code_ref[0], 2, xt, j)
+            for s in range(sectors):
+                value = first_sweep(
+                    lambda s, j, start: v_ref[0, s, j, start : start + ROWS, :],
+                    s, j, xt, strips - 1, factors, None, None,
+                )
+                a_ref[0, s, j, xt * ROWS : (xt + 1) * ROWS, :] = value
+                lowest_ref[s, j, xt * ROWS : (xt + 1) * ROWS, :] = value
+    middle_levels(
+        range(1, strips - 1), v_ref, None, None, cx_ref, mf_ref, cy_ref, code_ref, out_ref, a_ref
+    )
+    inner = slice(ROWS, (strips - 1) * ROWS)
+    top_ref[:, :, inner] = a_ref[(below - 1) % 2, :, :, inner]
+
+
+def outer_middle_kernel(
+    v_ref, inner_ref, inner_top_ref, left_ref, right_ref, lowest_ref, seam_ref,
+    cx_ref, mf_ref, cy_ref, code_ref,
+    out_ref, first_ref, last_ref, top_ref,
+    lrow_ref, rrow_ref, a_ref,
+):
+    below, sectors, tiles, padded, _ = v_ref.shape
+    strips = (padded - 2 * ROWS) // ROWS
+    ends = (0, strips - 1)
+    flip_left, flip_right = flags(seam_ref)
+    turned(left_ref, flip_left, lrow_ref)
+    turned(right_ref, flip_right, rrow_ref)
+    for s in range(sectors):
+        for j in range(tiles):
+            for xt in ends:
+                rows = slice(xt * ROWS, (xt + 1) * ROWS)
+                a_ref[0, s, j, rows] = lowest_ref[s, rows, j * LANES : (j + 1) * LANES]
+    middle_levels(
+        ends, v_ref, lrow_ref, rrow_ref, cx_ref, mf_ref, cy_ref, code_ref, out_ref, a_ref,
+        (first_ref, last_ref),
+    )
+    for xt in ends:
+        rows = slice(xt * ROWS, (xt + 1) * ROWS)
+        top_ref[:, :, rows] = a_ref[(below - 1) % 2, :, :, rows]
+    inner = slice(ROWS, (strips - 1) * ROWS)
+    top_ref[:, :, inner] = inner_top_ref[:, :, inner]
+    inner = slice(2 * ROWS, strips * ROWS)
+
+    def copy(k, _):
+        out_ref[k, :, :, inner] = inner_ref[k, :, :, inner]
+        return 0
+
+    lax.fori_loop(0, below - 1, copy, 0)
 
 
 def second_last_kernel(
@@ -349,89 +405,144 @@
                 store_rims(first_ref, last_ref, s, j, xt, strips - 1, value)
 
 
-def final_kernel(
+def final_level(
+    k, chosen, strips, field, left_row, right_row, refs, out_ref, sens_ref, start_sum
+):
+    cx_ref, code_ref, weight_ref, share_ref = refs
+    sectors, _, width = share_ref.shape
+    cx = cx_ref[k].astype(jnp.float32)
+    codes = code_ref[k]
+    factor = weight_ref[pl.ds(k, 1), :]
+    for xt in chosen:
+        rows = slice(xt * ROWS, (xt + 1) * ROWS)
+        for j in range(width // LANES):
+            lanes = slice(j * LANES, (j + 1) * LANES)
+            factors = first_weights(cx, codes, 0, xt, j)
+            total = 0.0
+            for s in range(sectors):
+                value = first_sweep(field, s, j, xt, strips - 1, factors, left_row, right_row)
+                out_ref[k, s, rows, lanes] = value
+                total = total + share_ref[s, rows, lanes] * value
+            if start_sum:
+                sens_ref[rows, lanes] = factor * total
+            else:
+                sens_ref[rows, lanes] += factor * total
+
+
+def inner_final_kernel(
+    v_ref, vs_ref, cx_ref, code_ref, weight_ref, share_ref, out_hbm, sens_ref, out_ref, sems
+):
+    below, _, _, padded, _ = v_ref.shape
+    strips = (padded - 2 * ROWS) // ROWS
+    refs = (cx_ref, code_ref, weight_ref, share_ref)
+    inner = pl.ds(ROWS, (strips - 2) * ROWS)
+
+    def send(k):
+        return pltpu.make_async_copy(out_ref.at[k, :, inner], out_hbm.at[:, k, inner], sems.at[k])
+
+    final_level(
+        below, range(1, strips - 1), strips,
+        lambda s, j, start: vs_ref[s, j, start : start + ROWS, :],
+        None, None, refs, out_ref, sens_ref, True,
+    )
+    send(below).start()
+
+    def step(k, _):
+        final_level(
+            k, range(1, strips - 1), strips,
+            lambda s, j, start: v_ref[k, s, j, start : start + ROWS, :],
+            None, None, refs, out_ref, sens_ref, False,
+        )
+        send(k).start()
+        return 0
+
+    lax.fori_loop(0, below, step, 0)
+    for k in range(below + 1):
+        send(k).wait()
+
+
+def outer_final_kernel(
     v_ref, vs_ref, vt_ref, left_ref, right_ref, left_top_ref, right_top_ref, seam_ref,
-    cx_ref, code_ref, weight_ref, share_ref,
-    out_hbm, *refs,
-):
-    *piece_refs, lrow_ref, rrow_ref, ltop_ref, rtop_ref, out_ref, sens_ref, sems = refs
+    cx_ref, code_ref, weight_ref, share_ref, inner_ref, done_hbm,
+    out_hbm, piece_ref,
+    lrow_ref, rrow_ref, ltop_ref, rtop_ref, out_ref, sens_ref, flat_ref, sems,
+):
     below, sectors, tiles, padded, _ = v_ref.shape
     strips = (padded - 2 * ROWS) // ROWS
+    ends = (0, strips - 1)
+    refs = (cx_ref, code_ref, weight_ref, share_ref)
     flip_left, flip_right = flags(seam_ref)
     turned(left_ref, flip_left, lrow_ref)
     turned(right_ref, flip_right, rrow_ref)
     turned(left_top_ref, flip_left, ltop_ref)
     turned(right_top_ref, flip_right, rtop_ref)
 
-    def send(k):
-        return pltpu.make_async_copy(out_ref.at[k], out_hbm.at[:, k], sems.at[k])
-
-    def level(k, field, left_row, right_row, start_sum):
-        cx = cx_ref[k].astype(jnp.float32)
-        codes = code_ref[k]
-        factor = weight_ref[pl.ds(k, 1), :]
-        for xt in range(strips):
-            rows = slice(xt * ROWS, (xt + 1) * ROWS)
-            for j in range(tiles):
-                lanes = slice(j * LANES, (j + 1) * LANES)
-                factors = first_weights(cx, codes, 0, xt, j)
-                total = 0.0
-                for s in range(sectors):
-                    value = first_sweep(
-                        field, s, j, xt, strips - 1, factors, left_row, right_row
-                    )
-                    out_ref[k, s, rows, lanes] = value
-                    total = total + share_ref[s, rows, lanes] * value
-                if start_sum:
-                    sens_ref[rows, lanes] = factor * total
-                else:
-                    sens_ref[rows, lanes] += factor * total
-        send(k).start()
-
-    level(
-        below + 1,
+    def send(k, i):
+        rows = pl.ds(ends[i] * ROWS, ROWS)
+        return pltpu.make_async_copy(out_ref.at[k, :, rows], out_hbm.at[:, k, rows], sems.at[i, k])
+
+    send_top = pltpu.make_async_copy(
+        out_ref.at[below + 1], out_hbm.at[:, below + 1], sems.at[0, below + 1]
+    )
+    final_level(
+        below + 1, range(strips), strips,
         lambda s, j, start: vt_ref[s, j, start : start + ROWS, :],
         lambda s, j: ltop_ref[j, s : s + 1, :],
         lambda s, j: rtop_ref[j, s : s + 1, :],
-        True,
-    )
-    level(
-        below,
+        refs, out_ref, sens_ref, True,
+    )
+    send_top.start()
+    final_level(
+        below, ends, strips,
         lambda s, j, start: vs_ref[s, j, start : start + ROWS, :],
         lambda s, j: lrow_ref[j, below * sectors + s : below * sectors + s + 1, :],
         lambda s, j: rrow_ref[j, below * sectors + s : below * sectors + s + 1, :],
-        False,
-    )
+        refs, out_ref, sens_ref, False,
+    )
+    for i in range(2):
+        send(below, i).start()
 
     def step(k, _):
-        level(
-            k,
+        final_level(
+            k, ends, strips,
             lambda s, j, start: v_ref[k, s, j, start : start + ROWS, :],
             lambda s, j: lrow_ref[j, pl.ds(k * sectors + s, 1), :],
             lambda s, j: rrow_ref[j, pl.ds(k * sectors + s, 1), :],
-            False,
+            refs, out_ref, sens_ref, False,
         )
+        for i in range(2):
+            send(k, i).start()
         return 0
 
     lax.fori_loop(0, below, step, 0)
-    (piece_ref,) = piece_refs
+    inner = slice(ROWS, (strips - 1) * ROWS)
+    sens_ref[inner] += inner_ref[inner]
     if len(piece_ref.shape) == 2:
         piece_ref[...] = sens_ref[...]
     else:
         owners, group, copies, depth, _ = piece_ref.shape
         share = strips * ROWS * tiles // owners
+        for xt in range(strips):
+            for j in range(tiles):
+                value = sens_ref[xt * ROWS : (xt + 1) * ROWS, j * LANES : (j + 1) * LANES]
+                flat_ref[pl.ds(xt * ROWS * tiles + j, ROWS, stride=tiles), :] = value
         for o in range(owners):
-            for place in range(group * depth):
-                piece, line = divmod(place, depth)
-                if place < share:
-                    x, j = divmod(o * share + place, tiles)
-                    row = sens_ref[x : x + 1, j * LANES : (j + 1) * LANES]
-                else:
-                    row = jnp.zeros((1, LANES), jnp.float32)
+            for piece in range(group):
+                start = piece * depth
+                used = max(0, min(depth, share - start))
+                value = jnp.zeros((depth, LANES), jnp.float32)
+                if used:
+                    start += o * share
+                    value = flat_ref[start : start + depth, :]
+                    if used < depth:
+                        line = lax.broadcasted_iota(jnp.int32, (depth, LANES), 0)
+                        value = jnp.where(line < used, value, 0.0)
                 for i in range(copies):
-                    piece_ref[o, piece, i, line : line + 1, :] = row
-    for k in range(below + 2):
-        send(k).wait()
+                    piece_ref[o, piece, i] = value
+    send_top.wait()
+    for k in range(below + 1):
+        for i in range(2):
+            send(k, i).wait()
 
 
 def scatter_kernel(cells_ref, *refs):
@@ -537,13 +648,25 @@
         ],
     )
     left, right = around(first, last)
+    lines = kept(sectors, tiles, columns, LANES)
+    inner_field = kept(below - 1, sectors, tiles, padded, LANES)
+    a_scratch = pltpu.VMEM((2, sectors, tiles, columns, LANES), jnp.float32)
+    inner, inner_lowest, inner_top = call(
+        inner_middle_kernel,
+        (inner_field, lines, lines),
+        [VM] * 5,
+        [VM] * 3,
+        (v, courant_x, mass_flux, courant_y, limiter_code),
+        [a_scratch],
+    )
     lowest, vt, first_top, last_top = call(
         ends_kernel,
         (plane, field_top, rim_top, rim_top),
-        [VM] * 10,
+        [VM] * 11,
         [VM] * 4,
         (
-            v, left, right, seam, courant_x, limiter_code, top, above, mass_flux, courant_y,
+            v, inner_lowest, left, right, seam, courant_x, limiter_code, top, above,
+            mass_flux, courant_y,
         ),
         [pltpu.VMEM((tiles, ROWS, LANES), jnp.float32)] * 2,
     )
@@ -551,17 +674,15 @@
     left_top, right_top = around(first_top, last_top)
 
     v, first, last, top = call(
-        middle_kernel,
+        outer_middle_kernel,
+        (inner_field, rim_next, rim_next, lines),
+        [VM] * 11,
+        [VM] * 4,
         (
-            kept(below - 1, sectors, tiles, padded, LANES),
-            rim_next,
-            rim_next,
-            kept(sectors, tiles, columns, LANES),
+            v, inner, inner_top, left, right, lowest, seam,
+            courant_x, mass_flux, courant_y, limiter_code,
         ),
-        [VM] * 9,
-        [VM] * 4,
-        (v, left, right, lowest, seam, courant_x, mass_flux, courant_y, limiter_code),
-        [rim_scratch, rim_scratch, pltpu.VMEM((2, sectors, tiles, columns, LANES), jnp.float32)],
+        [rim_scratch, rim_scratch, a_scratch],
     )
     vs, first, last, top = call(
         second_last_kernel,
@@ -589,23 +710,34 @@
     depth = -(-share // (group * LANES))
     aligned = share % LANES == 0
     packed = (owners, group, copies, depth, LANES)
+    stage = pltpu.VMEM((levels, sectors, columns, width), jnp.float32)
+    adjoint, inner = call(
+        inner_final_kernel,
+        (f32(*forcing.shape), kept(columns, width)),
+        [VM] * 6,
+        [HBM, VM],
+        (v, vs, courant_x, limiter_code, weight, sector_share),
+        [stage, pltpu.SemaphoreType.DMA((levels,))],
+    )
     adjoint, pieces = call(
-        final_kernel,
+        outer_final_kernel,
         (f32(*forcing.shape), f32(*packed) if aligned else f32(columns, width)),
-        [VM] * 12,
+        [VM] * 13 + [HBM],
         [HBM, VM],
         (
             v, vs, vt, left, right, left_top, right_top, seam,
-            courant_x, limiter_code, weight, sector_share,
+            courant_x, limiter_code, weight, sector_share, inner, adjoint,
         ),
         [
             rim_scratch, rim_scratch,
             pltpu.VMEM((tiles, sectors, LANES), jnp.float32),
             pltpu.VMEM((tiles, sectors, LANES), jnp.float32),
-            pltpu.VMEM((levels, sectors, columns, width), jnp.float32),
+            stage,
             pltpu.VMEM((columns, width), jnp.float32),
-            pltpu.SemaphoreType.DMA((levels,)),
+            pltpu.VMEM((columns * tiles + ROWS, LANES), jnp.float32),
+            pltpu.SemaphoreType.DMA((2, levels)),
         ],
+        aliases={13: 0},
     )
     if not aligned:
         pieces = jnp.pad(

time: 58.7 us -> 56.8 us (0.968)
  waiting for transfers between devices: 15.9 us -> 13.2 us
  Pallas kernels: 18.6 us -> 21.1 us
  starting transfers between devices: 22.9 us -> 21.3 us
    ppermute x8, waiting for transfers between devices: 4.75 us -> 0.25 us  [around(): return (lax.ppermute(last, 'tile', up), lax.ppermute(first, 'tile', down))]
    pallas_call x8 -> x10, Pallas kernels: 18.6 us -> 21.1 us  [call(): pl.pallas_call(kernel, out_shape=out_shape, in_specs=in_specs, out_specs=...]
    ppermute x2, waiting for transfers between devices: 0.4 us -> 2.14 us  [from_above(): return lax.ppermute(value, 'lev', [(i + 1, i) for i in range(count - 1)])]
    all_to_all x1, starting transfers between devices: 7.58 us -> 5.97 us  [remapped(): lax.all_to_all(sent, ('tile', 'lev', 'sec'), split_axis=0, concat_axis=0,...]
  transfers between devices with their start and end apart: 14 -> 14, of which waited for: 8 -> 5; matrix products, arithmetic and copies ran while one was open for 0% -> 0% of each run, Pallas kernels for 18% -> 25%
where the time goes in v6:
time: 56.8 us; the launch traced here: 56.6 us
  starting transfers between devices  21.3 us (38%)
  Pallas kernels  21.1 us (37%)
  waiting for transfers between devices  13.2 us (23%)
  between operations  0.84 us (1%)
    pallas_call x10, Pallas kernels, call(): pl.pallas_call(kernel, out_shape=out_shape, in_specs=in_specs, out_specs=...  21.1 us
    ppermute x8, starting transfers between devices, around(): return (lax.ppermute(last, 'tile', up), lax.ppermute(first, 'tile', down))  8.32 us
    all_to_all x1, waiting for transfers between devices, remapped(): lax.all_to_all(sent, ('tile', 'lev', 'sec'), split_axis=0, concat_axis=0,...  7.71 us
    all_to_all x1, starting transfers between devices, remapped(): lax.all_to_all(sent, ('tile', 'lev', 'sec'), split_axis=0, concat_axis=0,...  5.97 us
    ppermute x3, starting transfers between devices, exchanged(): return lax.ppermute(value, axis, [(i, i ^ apart) for i in range(count)])  4.45 us
    ppermute x3, waiting for transfers between devices, exchanged(): return lax.ppermute(value, axis, [(i, i ^ apart) for i in range(count)])  3.05 us
    ppermute x2, starting transfers between devices, from_above(): return lax.ppermute(value, 'lev', [(i + 1, i) for i in range(count - 1)])  2.58 us
    ppermute x2, waiting for transfers between devices, from_above(): return lax.ppermute(value, 'lev', [(i + 1, i) for i in range(count - 1)])  2.14 us
  transfers between devices with their start and end apart: 14, of which 5 were waited for; matrix products, arithmetic and copies ran while one was open for 0% of the time, Pallas kernels for 25%

profile of v6, /device:TPU:0, one launch (start us, length us, event | category | flops | bytes accessed | tf_op | source)
XLA Modules:
  0.0 56.6 jit_solution(18202161594412854631)
XLA Ops:
  0.6 1.0 %shard_map.106 = f32[4,40,384]{2,1,0:T(8,128)S(1)} custom-call(f32[4,18,40,384]{3,2,1,0:T(8,128)} %f_hbm.3), custom_call_target="tpu_custom_call" | custom-call | flops 1 | bytes 1 | tf_op jit(solution)/shard_map/pallas_call | solution.py:19
  1.6 1.3 %collective-permute-start.2 = (f32[4,40,384]{2,1,0:T(8,128)S(1)}, f32[4,40,384]{2,1,0:T(8,128)S(1)}, u32[]{:S(2)}, u32[]{:S(2)}) collective-permute-start(f32[4,40,384]{2,1,0:T(8,128)S(1)} %shard_map.106), channel_id=1, source_target_pairs={{2,0},{4,2},{6,4},{3,1},{5,3},{7,5},{10,8},{12,10},{14,12},{11,9},... | collective-permute-start | bytes 737288 | tf_op jit(solution)/shard_map/ppermute | solution.py:612
  2.9 5.5 %shard_map.104 = (f32[17,4,3,56,128]{4,3,2,1,0:T(8,128)S(1)}, f32[3,68,128]{2,1,0:T(8,128)S(1)}, f32[3,68,128]{2,1,0:T(8,128)S(1)}, f32[4,40,384]{2,1,0:T(8,128)...) custom-call(f32[4,18,40,384]{3,2,1,0:T(8,128)} %f_hbm.3, ...), custom_call_target="tpu_custom_call" | custom-call | flops 1 | bytes 1 | tf_op jit(solution)/shard_map/pallas_call | solution.py:19
  8.4 0.5 collective-permute-start
  8.9 2.0 %collective-permute-start.1 = (f32[3,68,128]{2,1,0:T(8,128)S(1)}, f32[3,68,128]{2,1,0:T(8,128)S(1)}, u32[]{:S(2)}, u32[]{:S(2)}) collective-permute-start(f32[3,68,128]{2,1,0:T(8,128)S(1)} %get-tuple-element.42), channel_id=1, source_target_pairs={{8,0},{16,8},{24,16},{0,24},{9,1},{17,9},{25,17},{1,25},{10,2},{18... | collective-permute-start | bytes 313352 | tf_op jit(solution)/shard_map/ppermute | solution.py:607
  10.9 3.1 %shard_map.105 = (f32[16,4,3,56,128]{4,3,2,1,0:T(8,128)S(1)}, f32[4,3,40,128]{3,2,1,0:T(8,128)S(1)}, f32[4,3,40,128]{3,2,1,0:T(8,128)S(1)}) custom-call(f32[17,4,3,56,128]{4,3,2,1,0:T(8,128)S(1)} %get-tuple-element.34.v_ref, bf16[18,40,384]{2,1,0:T(8,128)(2,1)S(1)} %get-tuple-element.35.cx_ref, bf16[18,40,384]{2,1,0:T(8,128)(2,1)S(1)} %get-tuple-element.36.mf_ref, ...), custom_call_target="tpu_custom_call" | custom-call | flops 1 | bytes 1 | tf_op jit(solution)/shard_map/pallas_call | solution.py:19
  14.0 0.2 collective-permute-done.1.right_ref
  14.3 0.1 broadcast_in_dim.4.seam_ref
  14.3 0.2 shard_map.107
  14.6 1.3 %collective-permute-start.5 = (f32[4,40,384]{2,1,0:T(8,128)S(1)}, f32[4,40,384]{2,1,0:T(8,128)S(1)}, u32[]{:S(2)}, u32[]{:S(2)}) collective-permute-start(f32[4,40,384]{2,1,0:T(8,128)S(1)} %get-tuple-element.45.lowest_ref), channel_id=1, source_target_pairs={{2,0},{4,2},{6,4},{3,1},{5,3},{7,5},{10,8},{12,10},{14,12},{11,9},... | collective-permute-start | bytes 737288 | tf_op jit(solution)/shard_map/ppermute | solution.py:612
  15.9 1.5 %collective-permute-start.3 = (f32[3,4,128]{2,1,0:T(4,128)S(1)}, f32[3,4,128]{2,1,0:T(4,128)S(1)}, u32[]{:S(2)}, u32[]{:S(2)}) collective-permute-start(f32[3,4,128]{2,1,0:T(4,128)S(1)} %get-tuple-element.48), channel_id=1, source_target_pairs={{0,8},{8,16},{16,24},{24,0},{1,9},{9,17},{17,25},{25,1},{2,10},{10... | collective-permute-start | bytes 18440 | tf_op jit(solution)/shard_map/ppermute | solution.py:607
  17.4 0.8 %collective-permute-start.4 = (f32[3,4,128]{2,1,0:T(4,128)S(1)}, f32[3,4,128]{2,1,0:T(4,128)S(1)}, u32[]{:S(2)}, u32[]{:S(2)}) collective-permute-start(f32[3,4,128]{2,1,0:T(4,128)S(1)} %get-tuple-element.49), channel_id=1, source_target_pairs={{8,0},{16,8},{24,16},{0,24},{9,1},{17,9},{25,17},{1,25},{10,2},{18... | collective-permute-start | bytes 18440 | tf_op jit(solution)/shard_map/ppermute | solution.py:607
  18.1 3.1 %shard_map.108 = (f32[16,4,3,56,128]{4,3,2,1,0:T(8,128)S(1)}, f32[3,64,128]{2,1,0:T(8,128)S(1)}, f32[3,64,128]{2,1,0:T(8,128)S(1)}, f32[4,3,40,128]{3,2,1,0:T(8,128)S(1)}) custom-call(f32[17,4,3,56,128]{4,3,2,1,0:T(8,128)S(1)} %get-tuple-element.34.v_ref, f32[16,4,3,56,128]{4,3,2,1,0:T(8,128)S(1)} %get-tuple-element.39.inner_ref, ...), custom_call_target="tpu_custom_call" | custom-call | flops 1 | bytes 1 | tf_op jit(solution)/shard_map/pallas_call | solution.py:19
  21.2 0.0 copy-start.3
  21.3 0.2 shard_map.109
  21.5 0.6 %collective-permute-start.6 = (f32[3,68,128]{2,1,0:T(8,128)S(1)}, f32[3,68,128]{2,1,0:T(8,128)S(1)}, u32[]{:S(2)}, u32[]{:S(2)}) collective-permute-start(f32[3,68,128]{2,1,0:T(8,128)S(1)} %get-tuple-element.56), channel_id=1, source_target_pairs={{0,8},{8,16},{16,24},{24,0},{1,9},{9,17},{17,25},{25,1},{2,10},{10... | collective-permute-start | bytes 313352 | tf_op jit(solution)/shard_map/ppermute | solution.py:607
  22.1 1.2 %collective-permute-start.7 = (f32[3,68,128]{2,1,0:T(8,128)S(1)}, f32[3,68,128]{2,1,0:T(8,128)S(1)}, u32[]{:S(2)}, u32[]{:S(2)}) collective-permute-start(f32[3,68,128]{2,1,0:T(8,128)S(1)} %get-tuple-element.57), channel_id=1, source_target_pairs={{8,0},{16,8},{24,16},{0,24},{9,1},{17,9},{25,17},{1,25},{10,2},{18... | collective-permute-start | bytes 313352 | tf_op jit(solution)/shard_map/ppermute | solution.py:607
  23.3 2.1 %collective-permute-done.5.above_ref = f32[4,40,384]{2,1,0:T(8,128)S(1)} collective-permute-done((f32[4,40,384]{2,1,0:T(8,128)S(1)}, f32[4,40,384]{2,1,0:T(8,128)S(1)}, u32[]{:S(2)}, u32[]{:S(2)}) %collective-permute-start.5) | collective-permute-done | bytes 245792 | tf_op jit(solution)/shard_map/ppermute | solution.py:612
  25.5 0.2 shard_map.110
  25.7 0.5 collective-permute-start.8
  26.1 1.3 %collective-permute-start.9 = (f32[3,4,128]{2,1,0:T(4,128)S(1)}, f32[3,4,128]{2,1,0:T(4,128)S(1)}, u32[]{:S(2)}, u32[]{:S(2)}) collective-permute-start(f32[3,4,128]{2,1,0:T(4,128)S(1)} %get-tuple-element.59), channel_id=1, source_target_pairs={{8,0},{16,8},{24,16},{0,24},{9,1},{17,9},{25,17},{1,25},{10,2},{18... | collective-permute-start | bytes 18440 | tf_op jit(solution)/shard_map/ppermute | solution.py:607
  27.5 0.1 broadcast_in_dim.5.weight_ref
  27.6 1.8 %shard_map.111 = (f32[4,18,40,384]{3,2,1,0:T(8,128)}, f32[40,384]{1,0:T(8,128)S(1)}) custom-call(f32[16,4,3,56,128]{4,3,2,1,0:T(8,128)S(1)} %get-tuple-element.46.v_ref, f32[4,3,56,128]{3,2,1,0:T(8,128)S(1)} %get-tuple-element.53.vs_ref, bf16[18,40,384]{2,1,0:T(8,128)(2,1)S(1)} %get-tuple-element.35.cx_ref, s32[18,40,384]{2,1,0:T(8,128)S(1)} %get-tuple-element.38.code_ref, ...), custom_call_target="tpu_custom_call" | custom-call | flops 1 | bytes 1 | tf_op jit(solution)/shard_map/pallas_call | solution.py:19
  29.4 2.6 %shard_map.112 = (f32[4,18,40,384]{3,2,1,0:T(8,128)}, f32[4,4,2,8,128]{4,3,2,1,0:T(8,128)}) custom-call(f32[16,4,3,56,128]{4,3,2,1,0:T(8,128)S(1)} %get-tuple-element.46.v_ref, f32[4,3,56,128]{3,2,1,0:T(8,128)S(1)} %get-tuple-element.53.vs_ref, f32[4,3,56,128]{3,2,1,0:T(8,128)S(1)} %get-tuple-element.55.vt_ref, ...), custom_call_target="tpu_custom_call", output_to_operand_aliasing={{0}: (13, {})} | custom-call | flops 1 | bytes 1 | tf_op jit(solution)/shard_map/pallas_call | solution.py:19
  32.1 6.0 %all-to-all-start = ((f32[32,8,128]{2,1,0:T(8,128)}), f32[32,8,128]{2,1,0:T(8,128)S(1)}, u32[]{:S(2)}, u32[]{:S(2)}) async-start(f32[32,8,128]{2,1,0:T(8,128)} %bitcast.2), calls=%async_computation | async-start | bytes 262144 | tf_op jit(solution)/shard_map/all_to_all | solution.py:590
  38.1 7.7 %all-to-all-done = f32[32,8,128]{2,1,0:T(8,128)S(1)} async-done(((f32[32,8,128]{2,1,0:T(8,128)}), f32[32,8,128]{2,1,0:T(8,128)S(1)}, u32[]{:S(2)}, u32[]{:S(2)}) %all-to-all-start) | async-done | bytes 131104 | tf_op jit(solution)/shard_map/all_to_all | solution.py:590
  45.8 1.1 %collective-permute-start.10 = (f32[4,8,128]{2,1,0:T(8,128)S(1)}, f32[4,8,128]{2,1,0:T(8,128)S(1)}, u32[]{:S(2)}, u32[]{:S(2)}) collective-permute-start(f32[4,8,128]{2,1,0:T(8,128)S(1)} %bitcast_reduce_fusion.refs_0_), channel_id=1, source_target_pairs={{0,2},{2,0},{4,6},{6,4},{1,3},{3,1},{5,7},{7,5},{8,10},{10,8},{12,... | collective-permute-start | bytes 49160 | tf_op jit(solution)/shard_map/ppermute | solution.py:583
  46.9 0.9 %collective-permute-start.11 = (f32[4,8,128]{2,1,0:T(8,128)S(1)}, f32[4,8,128]{2,1,0:T(8,128)S(1)}, u32[]{:S(2)}, u32[]{:S(2)}) collective-permute-start(f32[4,8,128]{2,1,0:T(8,128)S(1)} %bitcast_reduce_fusion.refs_0_), channel_id=1, source_target_pairs={{0,4},{2,6},{4,0},{6,2},{1,5},{3,7},{5,1},{7,3},{8,12},{10,14},{12... | collective-permute-start | bytes 49160 | tf_op jit(solution)/shard_map/ppermute | solution.py:583
  47.8 2.5 %collective-permute-start.12 = (f32[4,8,128]{2,1,0:T(8,128)S(1)}, f32[4,8,128]{2,1,0:T(8,128)S(1)}, u32[]{:S(2)}, u32[]{:S(2)}) collective-permute-start(f32[4,8,128]{2,1,0:T(8,128)S(1)} %bitcast_reduce_fusion.refs_0_), channel_id=1, source_target_pairs={{0,6},{2,4},{4,2},{6,0},{1,7},{3,5},{5,3},{7,1},{8,14},{10,12},{12... | collective-permute-start | bytes 49160 | tf_op jit(solution)/shard_map/ppermute | solution.py:583
  50.3 1.3 %collective-permute-done.11.refs_2_ = f32[4,8,128]{2,1,0:T(8,128)S(1)} collective-permute-done((f32[4,8,128]{2,1,0:T(8,128)S(1)}, f32[4,8,128]{2,1,0:T(8,128)S(1)}, u32[]{:S(2)}, u32[]{:S(2)}) %collective-permute-start.11) | collective-permute-done | bytes 16416 | tf_op jit(solution)/shard_map/ppermute | solution.py:583
  51.5 1.8 %collective-permute-done.12.refs_3_ = f32[4,8,128]{2,1,0:T(8,128)S(1)} collective-permute-done((f32[4,8,128]{2,1,0:T(8,128)S(1)}, f32[4,8,128]{2,1,0:T(8,128)S(1)}, u32[]{:S(2)}, u32[]{:S(2)}) %collective-permute-start.12) | collective-permute-done | bytes 16416 | tf_op jit(solution)/shard_map/ppermute | solution.py:583
  53.3 3.3 %shard_map.113 = f32[120,128]{1,0:T(8,128)} custom-call(s32[4,4,8,128]{3,2,1,0:T(8,128)S(1)} %copy_bitcast_fusion.1.cells_ref, f32[4,8,128]{2,1,0:T(8,128)S(1)} %bitcast_reduce_fusion.refs_0_, f32[4,8,128]{2,1,0:T(8,128)S(1)} %collective-permute-done.10.refs_1_, f32[4,8,128]{2,1,0:T(8,128)S(1)} %collective-permute-done.11.refs_2_, ...), custom_call_target="tpu_custom_call" | custom-call | flops 1 | bytes 1 | tf_op jit(solution)/shard_map/pallas_call | solution.py:19
  (19 shorter events, 0.1 us)
Async XLA Ops:
  1.6 12.7 %collective-permute-start.2 = (f32[4,40,384]{2,1,0:T(8,128)S(1)}, f32[4,40,384]{2,1,0:T(8,128)S(1)}, u32[]{:S(2)}, u32[]{:S(2)}) collective-permute-start(f32[4,40,384]{2,1,0:T(8,128)S(1)} %shard_map.106), channel_id=1, source_target_pairs={{2,0},{4,2},{6,4},{3,1},{5,3},{7,5},{10,8},{12,10},{14,12},{11,9},... | collective-permute-start | bytes 737288 | tf_op jit(solution)/shard_map/ppermute | solution.py:612
  8.4 5.9 %copy-start.2 = (s32[4,2]{0,1:T(2,128)S(1)}, s32[4,2]{0,1:T(2,128)}, u32[]{:S(2)}) copy-start(s32[4,2]{0,1:T(2,128)} %param.14) | copy-start | bytes 100
  8.4 5.6 %collective-permute-start = (f32[3,68,128]{2,1,0:T(8,128)S(1)}, f32[3,68,128]{2,1,0:T(8,128)S(1)}, u32[]{:S(2)}, u32[]{:S(2)}) collective-permute-start(f32[3,68,128]{2,1,0:T(8,128)S(1)} %get-tuple-element.41), channel_id=1, source_target_pairs={{0,8},{8,16},{16,24},{24,0},{1,9},{9,17},{17,25},{25,1},{2,10},{10... | collective-permute-start | bytes 313352 | tf_op jit(solution)/shard_map/ppermute | solution.py:607
  8.9 5.4 %collective-permute-start.1 = (f32[3,68,128]{2,1,0:T(8,128)S(1)}, f32[3,68,128]{2,1,0:T(8,128)S(1)}, u32[]{:S(2)}, u32[]{:S(2)}) collective-permute-start(f32[3,68,128]{2,1,0:T(8,128)S(1)} %get-tuple-element.42), channel_id=1, source_target_pairs={{8,0},{16,8},{24,16},{0,24},{9,1},{17,9},{25,17},{1,25},{10,2},{18... | collective-permute-start | bytes 313352 | tf_op jit(solution)/shard_map/ppermute | solution.py:607
  14.6 10.9 %collective-permute-start.5 = (f32[4,40,384]{2,1,0:T(8,128)S(1)}, f32[4,40,384]{2,1,0:T(8,128)S(1)}, u32[]{:S(2)}, u32[]{:S(2)}) collective-permute-start(f32[4,40,384]{2,1,0:T(8,128)S(1)} %get-tuple-element.45.lowest_ref), channel_id=1, source_target_pairs={{2,0},{4,2},{6,4},{3,1},{5,3},{7,5},{10,8},{12,10},{14,12},{11,9},... | collective-permute-start | bytes 737288 | tf_op jit(solution)/shard_map/ppermute | solution.py:612
  15.9 5.4 %collective-permute-start.3 = (f32[3,4,128]{2,1,0:T(4,128)S(1)}, f32[3,4,128]{2,1,0:T(4,128)S(1)}, u32[]{:S(2)}, u32[]{:S(2)}) collective-permute-start(f32[3,4,128]{2,1,0:T(4,128)S(1)} %get-tuple-element.48), channel_id=1, source_target_pairs={{0,8},{8,16},{16,24},{24,0},{1,9},{9,17},{17,25},{25,1},{2,10},{10... | collective-permute-start | bytes 18440 | tf_op jit(solution)/shard_map/ppermute | solution.py:607
  17.4 3.9 %collective-permute-start.4 = (f32[3,4,128]{2,1,0:T(4,128)S(1)}, f32[3,4,128]{2,1,0:T(4,128)S(1)}, u32[]{:S(2)}, u32[]{:S(2)}) collective-permute-start(f32[3,4,128]{2,1,0:T(4,128)S(1)} %get-tuple-element.49), channel_id=1, source_target_pairs={{8,0},{16,8},{24,16},{0,24},{9,1},{17,9},{25,17},{1,25},{10,2},{18... | collective-permute-start | bytes 18440 | tf_op jit(solution)/shard_map/ppermute | solution.py:607
  21.2 6.2 %copy-start.3 = (f32[18]{0:T(128)S(1)}, f32[18]{0:T(128)}, u32[]{:S(2)}) copy-start(f32[18]{0:T(128)} %param.15) | copy-start | bytes 220
  21.3 6.3 %copy-start = (f32[4,40,384]{2,1,0:T(8,128)S(1)}, f32[4,40,384]{2,1,0:T(8,128)}, u32[]{:S(2)}) copy-start(f32[4,40,384]{2,1,0:T(8,128)} %share_ref.3) | copy-start | bytes 737284
  21.5 7.9 %collective-permute-start.6 = (f32[3,68,128]{2,1,0:T(8,128)S(1)}, f32[3,68,128]{2,1,0:T(8,128)S(1)}, u32[]{:S(2)}, u32[]{:S(2)}) collective-permute-start(f32[3,68,128]{2,1,0:T(8,128)S(1)} %get-tuple-element.56), channel_id=1, source_target_pairs={{0,8},{8,16},{16,24},{24,0},{1,9},{9,17},{17,25},{25,1},{2,10},{10... | collective-permute-start | bytes 313352 | tf_op jit(solution)/shard_map/ppermute | solution.py:607
  22.1 7.3 %collective-permute-start.7 = (f32[3,68,128]{2,1,0:T(8,128)S(1)}, f32[3,68,128]{2,1,0:T(8,128)S(1)}, u32[]{:S(2)}, u32[]{:S(2)}) collective-permute-start(f32[3,68,128]{2,1,0:T(8,128)S(1)} %get-tuple-element.57), channel_id=1, source_target_pairs={{8,0},{16,8},{24,16},{0,24},{9,1},{17,9},{25,17},{1,25},{10,2},{18... | collective-permute-start | bytes 313352 | tf_op jit(solution)/shard_map/ppermute | solution.py:607
  25.7 3.7 %collective-permute-start.8 = (f32[3,4,128]{2,1,0:T(4,128)S(1)}, f32[3,4,128]{2,1,0:T(4,128)S(1)}, u32[]{:S(2)}, u32[]{:S(2)}) collective-permute-start(f32[3,4,128]{2,1,0:T(4,128)S(1)} %get-tuple-element.58), channel_id=1, source_target_pairs={{0,8},{8,16},{16,24},{24,0},{1,9},{9,17},{17,25},{25,1},{2,10},{10... | collective-permute-start | bytes 18440 | tf_op jit(solution)/shard_map/ppermute | solution.py:607
  26.1 3.3 %collective-permute-start.9 = (f32[3,4,128]{2,1,0:T(4,128)S(1)}, f32[3,4,128]{2,1,0:T(4,128)S(1)}, u32[]{:S(2)}, u32[]{:S(2)}) collective-permute-start(f32[3,4,128]{2,1,0:T(4,128)S(1)} %get-tuple-element.59), channel_id=1, source_target_pairs={{8,0},{16,8},{24,16},{0,24},{9,1},{17,9},{25,17},{1,25},{10,2},{18... | collective-permute-start | bytes 18440 | tf_op jit(solution)/shard_map/ppermute | solution.py:607
  29.4 8.6 %copy-start.1 = (s32[4,3840]{1,0:T(4,128)S(1)}, s32[4,3840]{1,0:T(4,128)}, u32[]{:S(2)}) copy-start(s32[4,3840]{1,0:T(4,128)} %param.17) | copy-start | bytes 184324
  32.1 13.7 %all-to-all-start = ((f32[32,8,128]{2,1,0:T(8,128)}), f32[32,8,128]{2,1,0:T(8,128)S(1)}, u32[]{:S(2)}, u32[]{:S(2)}) async-start(f32[32,8,128]{2,1,0:T(8,128)} %bitcast.2), calls=%async_computation | async-start | bytes 262144 | tf_op jit(solution)/shard_map/all_to_all | solution.py:590
  45.8 4.5 %collective-permute-start.10 = (f32[4,8,128]{2,1,0:T(8,128)S(1)}, f32[4,8,128]{2,1,0:T(8,128)S(1)}, u32[]{:S(2)}, u32[]{:S(2)}) collective-permute-start(f32[4,8,128]{2,1,0:T(8,128)S(1)} %bitcast_reduce_fusion.refs_0_), channel_id=1, source_target_pairs={{0,2},{2,0},{4,6},{6,4},{1,3},{3,1},{5,7},{7,5},{8,10},{10,8},{12,... | collective-permute-start | bytes 49160 | tf_op jit(solution)/shard_map/ppermute | solution.py:583
  46.9 4.6 %collective-permute-start.11 = (f32[4,8,128]{2,1,0:T(8,128)S(1)}, f32[4,8,128]{2,1,0:T(8,128)S(1)}, u32[]{:S(2)}, u32[]{:S(2)}) collective-permute-start(f32[4,8,128]{2,1,0:T(8,128)S(1)} %bitcast_reduce_fusion.refs_0_), channel_id=1, source_target_pairs={{0,4},{2,6},{4,0},{6,2},{1,5},{3,7},{5,1},{7,3},{8,12},{10,14},{12... | collective-permute-start | bytes 49160 | tf_op jit(solution)/shard_map/ppermute | solution.py:583
  47.8 5.5 %collective-permute-start.12 = (f32[4,8,128]{2,1,0:T(8,128)S(1)}, f32[4,8,128]{2,1,0:T(8,128)S(1)}, u32[]{:S(2)}, u32[]{:S(2)}) collective-permute-start(f32[4,8,128]{2,1,0:T(8,128)S(1)} %bitcast_reduce_fusion.refs_0_), channel_id=1, source_target_pairs={{0,6},{2,4},{4,2},{6,0},{1,7},{3,5},{5,3},{7,1},{8,14},{10,12},{12... | collective-permute-start | bytes 49160 | tf_op jit(solution)/shard_map/ppermute | solution.py:583

commit v7 on v6

--- a/solution.py
+++ b/solution.py
@@ -133,15 +133,12 @@
 
 
 def lower_kernel(
-    f_hbm, mf_hbm, cy_hbm, code_hbm, cx_hbm,
+    f_ref, mf_hbm, cy_hbm, code_hbm, cx_hbm,
     v_ref, first_ref, last_ref, top_ref, mf_ref, cy_ref, code_ref, cx_ref,
-    f_ref, sems,
-):
-    sectors, levels, columns, width = f_hbm.shape
+    sems,
+):
+    sectors, levels, columns, width = f_ref.shape
     tiles, strips = width // LANES, columns // ROWS
-
-    def fetch(k):
-        return pltpu.make_async_copy(f_hbm.at[:, k], f_ref.at[k], sems.at[0, k])
 
     def fetch_code(k):
         return pltpu.make_async_copy(code_hbm.at[k], code_ref.at[k], sems.at[1, k])
@@ -153,21 +150,16 @@
         return pltpu.make_async_copy(cy_hbm.at[k], cy_ref.at[k], sems.at[3, k])
 
     fetch_cx = pltpu.make_async_copy(cx_hbm, cx_ref, sems.at[4, 0])
-    fetch(0).start()
     for k in range(levels):
         fetch_mf(k).start()
         fetch_cy(k).start()
         fetch_code(k).start()
-        if k < levels - 1:
-            fetch(k + 1).start()
     fetch_cx.start()
-    fetch(0).wait()
 
     def level(k, _):
         fetch_mf(k).wait()
         fetch_cy(k).wait()
         fetch_code(k).wait()
-        fetch(k + 1).wait()
         mf = mf_ref[k].astype(jnp.float32)
         cy = cy_ref[k].astype(jnp.float32)
         codes = code_ref[k]
@@ -178,8 +170,8 @@
                 parts = []
                 for j in range(tiles):
                     lanes = slice(j * LANES, (j + 1) * LANES)
-                    here = f_ref[k, s, rows, lanes]
-                    upper = f_ref[k + 1, s, rows, lanes]
+                    here = f_ref[s, k, rows, lanes]
+                    upper = f_ref[s, k + 1, rows, lanes]
                     parts.append(here + cut(mf, xt, j) * (upper - here))
                 for j, value in enumerate(second_sweep(parts, factors)):
                     store_padded(v_ref, (k,), s, j, xt, value)
@@ -187,7 +179,7 @@
         return 0
 
     lax.fori_loop(0, levels - 1, level, 0)
-    top_ref[...] = f_ref[levels - 1]
+    top_ref[...] = f_ref[:, levels - 1]
     fetch_mf(levels - 1).wait()
     fetch_cy(levels - 1).wait()
     fetch_code(levels - 1).wait()
@@ -463,9 +455,9 @@
 
 def outer_final_kernel(
     v_ref, vs_ref, vt_ref, left_ref, right_ref, left_top_ref, right_top_ref, seam_ref,
-    cx_ref, code_ref, weight_ref, share_ref, inner_ref, done_hbm,
-    out_hbm, piece_ref,
-    lrow_ref, rrow_ref, ltop_ref, rtop_ref, out_ref, sens_ref, flat_ref, sems,
+    cx_ref, code_ref, weight_ref, share_ref, inner_ref,
+    out_ref, piece_ref,
+    lrow_ref, rrow_ref, ltop_ref, rtop_ref, sens_ref, flat_ref,
 ):
     below, sectors, tiles, padded, _ = v_ref.shape
     strips = (padded - 2 * ROWS) // ROWS
@@ -477,13 +469,6 @@
     turned(left_top_ref, flip_left, ltop_ref)
     turned(right_top_ref, flip_right, rtop_ref)
 
-    def send(k, i):
-        rows = pl.ds(ends[i] * ROWS, ROWS)
-        return pltpu.make_async_copy(out_ref.at[k, :, rows], out_hbm.at[:, k, rows], sems.at[i, k])
-
-    send_top = pltpu.make_async_copy(
-        out_ref.at[below + 1], out_hbm.at[:, below + 1], sems.at[0, below + 1]
-    )
     final_level(
         below + 1, range(strips), strips,
         lambda s, j, start: vt_ref[s, j, start : start + ROWS, :],
@@ -491,7 +476,6 @@
         lambda s, j: rtop_ref[j, s : s + 1, :],
         refs, out_ref, sens_ref, True,
     )
-    send_top.start()
     final_level(
         below, ends, strips,
         lambda s, j, start: vs_ref[s, j, start : start + ROWS, :],
@@ -499,8 +483,6 @@
         lambda s, j: rrow_ref[j, below * sectors + s : below * sectors + s + 1, :],
         refs, out_ref, sens_ref, False,
     )
-    for i in range(2):
-        send(below, i).start()
 
     def step(k, _):
         final_level(
@@ -510,8 +492,6 @@
             lambda s, j: rrow_ref[j, pl.ds(k * sectors + s, 1), :],
             refs, out_ref, sens_ref, False,
         )
-        for i in range(2):
-            send(k, i).start()
         return 0
 
     lax.fori_loop(0, below, step, 0)
@@ -539,43 +519,85 @@
                         value = jnp.where(line < used, value, 0.0)
                 for i in range(copies):
                     piece_ref[o, piece, i] = value
+
+
+def write_kernel(part_ref, done_hbm, out_hbm, sems):
+    levels, _, columns, _ = part_ref.shape
+
+    def send(k, i):
+        rows = pl.ds(i * (columns - ROWS), ROWS)
+        return pltpu.make_async_copy(part_ref.at[k, :, rows], out_hbm.at[:, k, rows], sems.at[i, k])
+
+    top = levels - 1
+    send_top = pltpu.make_async_copy(part_ref.at[top], out_hbm.at[:, top], sems.at[0, top])
+    send_top.start()
+    for k in range(top):
+        for i in range(2):
+            send(k, i).start()
     send_top.wait()
-    for k in range(below + 1):
+    for k in range(top):
         for i in range(2):
             send(k, i).wait()
 
 
-def scatter_kernel(cells_ref, *refs):
+def mark_kernel(cells_ref, high_ref, low_ref):
+    pairs, tall, _ = low_ref.shape
+    short = high_ref.shape[1]
+    high_iota = lax.broadcasted_iota(jnp.int32, (short, LANES), 0)
+    low_iota = lax.broadcasted_iota(jnp.int32, (tall, LANES), 0)
+
+    def step(pair, _):
+        for i in range(2):
+            cells = cells_ref[pl.ds(2 * pair + i, 1), :]
+            high = jnp.right_shift(cells, 8) == high_iota
+            low = jnp.bitwise_and(cells, 255) == low_iota
+            lanes = slice(i * LANES, (i + 1) * LANES)
+            high_ref[pair, :, lanes] = jnp.where(high, 1.0, 0.0).astype(jnp.bfloat16)
+            low_ref[pair, :, lanes] = jnp.where(low, 1.0, 0.0).astype(jnp.bfloat16)
+        return 0
+
+    lax.fori_loop(0, pairs, step, 0)
+
+
+def total_kernel(arrived_ref, *refs):
+    out_ref = refs[-1]
+    owners, senders, _, _ = arrived_ref.shape
+    for o in range(owners):
+        total = arrived_ref[o, 0]
+        for i in range(1, senders):
+            total = total + arrived_ref[o, i]
+        out_ref[o] = total
+
+
+def scatter_kernel(high_ref, low_ref, *refs):
     *value_refs, out_ref = refs
-    rows, lanes = out_ref.shape
-    group, owners, depth, _ = cells_ref.shape
+    group = len(value_refs)
+    pairs, short, _ = high_ref.shape
+    each = pairs // group
     rank = lax.axis_index("lev")
-    high_iota = lax.broadcasted_iota(jnp.int32, (rows, lanes), 0)
-    low_iota = lax.broadcasted_iota(jnp.int32, (lanes, lanes), 0)
-    total = jnp.zeros((2 * rows, lanes), jnp.float32)
-    lines = [(i, o, r) for i in range(group) for o in range(owners) for r in range(depth)]
-    for pair in range(0, len(lines), 2):
-        lefts, rights = [], []
-        for part, owner, line in lines[pair : pair + 2]:
-            cells = cells_ref[jnp.bitwise_xor(rank, part), owner, line : line + 1, :]
-            value = value_refs[part][owner, line : line + 1, :]
-            coarse = value.astype(jnp.bfloat16).astype(jnp.float32)
-            fine = value - coarse
-            here = jnp.right_shift(cells, 7) == high_iota
-            lefts.append(
-                jnp.concatenate(
-                    [jnp.where(here, coarse, 0.0), jnp.where(here, fine, 0.0)], axis=0
-                ).astype(jnp.bfloat16)
+    total = jnp.zeros((2 * short, low_ref.shape[1]), jnp.float32)
+    for part, value_ref in enumerate(value_refs):
+        base = jnp.bitwise_xor(rank, part) * each
+        for pair in range(each):
+            high = high_ref[base + pair]
+            scaled = []
+            value = jnp.concatenate(
+                [value_ref[2 * pair + i : 2 * pair + i + 1, :] for i in range(2)], axis=1
             )
-            match = jnp.bitwise_and(cells, 127) == low_iota
-            rights.append(jnp.where(match, 1.0, 0.0).astype(jnp.bfloat16))
-        total += lax.dot_general(
-            jnp.concatenate(lefts, axis=1),
-            jnp.concatenate(rights, axis=1),
-            (((1,), (1,)), ((), ())),
-            preferred_element_type=jnp.float32,
-        )
-    out_ref[...] = total[:rows] + total[rows:]
+            coarse = value.astype(jnp.bfloat16)
+            fine = (value - coarse.astype(jnp.float32)).astype(jnp.bfloat16)
+            for bits in (coarse, fine):
+                scaled.append(high * jnp.broadcast_to(bits, high.shape))
+            total += lax.dot_general(
+                jnp.concatenate(scaled, axis=0),
+                low_ref[base + pair],
+                (((1,), (1,)), ((), ())),
+                preferred_element_type=jnp.float32,
+            )
+    total = total[:short] + total[short:]
+    rows = out_ref.shape[0] // 2
+    for i in range(2):
+        out_ref[pl.ds(i, rows, stride=2), :] = total[:rows, i * LANES : (i + 1) * LANES]
 
 
 def exchanged(value, axis, apart):
@@ -583,19 +605,36 @@
     return lax.ppermute(value, axis, [(i, i ^ apart) for i in range(count)])
 
 
-def remapped(pieces, flux_cell):
+def remapped(pieces, flux_cell, adjoint):
     owners, share = flux_cell.shape
     _, group, copies, depth, _ = pieces.shape
     sent = pieces.reshape(-1, depth, LANES)
     arrived = lax.all_to_all(
         sent, ("tile", "lev", "sec"), split_axis=0, concat_axis=0, tiled=True
     )
-    own = jnp.sum(arrived.reshape(owners, group * copies, depth, LANES), axis=1)
+    cells = jnp.pad(flux_cell, ((0, 0), (0, group * depth * LANES - share)))
+    cells = cells.reshape(owners, group, depth, LANES).transpose(1, 0, 2, 3).reshape(-1, LANES)
+    pairs = cells.shape[0] // 2
+    high, low = call(
+        mark_kernel,
+        (
+            pltpu.VMEM((pairs, FL_DEV // 256 + 4, 256), jnp.bfloat16),
+            pltpu.VMEM((pairs, 256, 256), jnp.bfloat16),
+        ),
+        [VM],
+        [VM] * 2,
+        (cells,),
+    )
+    own = call(
+        total_kernel,
+        f32(owners, depth, LANES),
+        [VM, VM, VM, HBM],
+        VM,
+        (arrived.reshape(owners, group * copies, depth, LANES), high, low, *in_hbm(adjoint)),
+    ).reshape(owners * depth, LANES)
     parts = [own] + [exchanged(own, "lev", d) for d in range(1, group)]
-    cells = jnp.pad(flux_cell, ((0, 0), (0, group * depth * LANES - share)))
-    cells = cells.reshape(owners, group, depth, LANES).transpose(1, 0, 2, 3)
     out = call(
-        scatter_kernel, f32(FL_DEV // LANES, LANES), [VM] * (group + 1), VM, (cells, *parts)
+        scatter_kernel, f32(FL_DEV // LANES, LANES), [VM] * (group + 2), VM, (high, low, *parts)
     )
     return out.reshape(-1)
 
@@ -639,13 +678,10 @@
             field, rim, rim, plane,
             narrow, narrow, pltpu.VMEM((levels, columns, width), jnp.int32), narrow,
         ),
-        [HBM] * 5,
+        [VM] + [HBM] * 4,
         [VM] * 8,
-        in_hbm(forcing, mass_flux, courant_y, limiter_code, courant_x),
-        [
-            pltpu.VMEM((levels, sectors, columns, width), jnp.float32),
-            pltpu.SemaphoreType.DMA((5, levels)),
-        ],
+        (forcing, *in_hbm(mass_flux, courant_y, limiter_code, courant_x)),
+        [pltpu.SemaphoreType.DMA((5, levels))],
     )
     left, right = around(first, last)
     lines = kept(sectors, tiles, columns, LANES)
@@ -719,25 +755,34 @@
         (v, vs, courant_x, limiter_code, weight, sector_share),
         [stage, pltpu.SemaphoreType.DMA((levels,))],
     )
-    adjoint, pieces = call(
+    part, pieces = call(
         outer_final_kernel,
-        (f32(*forcing.shape), f32(*packed) if aligned else f32(columns, width)),
-        [VM] * 13 + [HBM],
-        [HBM, VM],
+        (
+            kept(levels, sectors, columns, width),
+            f32(*packed) if aligned else f32(columns, width),
+        ),
+        [VM] * 13,
+        [VM, VM],
         (
             v, vs, vt, left, right, left_top, right_top, seam,
-            courant_x, limiter_code, weight, sector_share, inner, adjoint,
+            courant_x, limiter_code, weight, sector_share, inner,
         ),
         [
             rim_scratch, rim_scratch,
             pltpu.VMEM((tiles, sectors, LANES), jnp.float32),
             pltpu.VMEM((tiles, sectors, LANES), jnp.float32),
-            stage,
             pltpu.VMEM((columns, width), jnp.float32),
             pltpu.VMEM((columns * tiles + ROWS, LANES), jnp.float32),
-            pltpu.SemaphoreType.DMA((2, levels)),
         ],
-        aliases={13: 0},
+    )
+    adjoint = call(
+        write_kernel,
+        f32(*forcing.shape),
+        [VM, HBM],
+        HBM,
+        (part, adjoint),
+        [pltpu.SemaphoreType.DMA((2, levels))],
+        aliases={1: 0},
     )
     if not aligned:
         pieces = jnp.pad(
@@ -745,7 +790,7 @@
         ).reshape(owners, group, 1, depth, LANES)
         pieces = jnp.broadcast_to(pieces, packed)
     flux_cell, pieces = lax.optimization_barrier((flux_cell, pieces))
-    return (adjoint, remapped(pieces, flux_cell))
+    return (adjoint, remapped(pieces, flux_cell, adjoint))
 
 
 def solution(mesh):

time: 56.8 us -> 65.8 us (1.16)
  local copies, waits for them, and re-layouts: 0.18 us -> 11.2 us
  waiting for transfers between devices: 13.2 us -> 7.72 us
  Pallas kernels: 21.1 us -> 24.2 us
    unnamed x9 -> x20, local copies, waits for them, and re-layouts: 0.03 us -> 11 us
    all_to_all x1, waiting for transfers between devices: 7.71 us -> 0.01 us  [remapped(): lax.all_to_all(sent, ('tile', 'lev', 'sec'), split_axis=0, concat_axis=0,...]
    pallas_call x10 -> x13, Pallas kernels: 21.1 us -> 24.2 us  [call(): pl.pallas_call(kernel, out_shape=out_shape, in_specs=in_specs, out_specs=...]
    ppermute x3, waiting for transfers between devices: 3.05 us -> 5.33 us  [exchanged(): return lax.ppermute(value, axis, [(i, i ^ apart) for i in range(count)])]
  transfers between devices with their start and end apart: 14 -> 14, of which waited for: 5 -> 4; matrix products, arithmetic and copies ran while one was open for 0% -> 0% of each run, Pallas kernels for 25% -> 27%
where the time goes in v7:
time: 65.8 us; the launch traced here: 65.5 us
  Pallas kernels  24.2 us (37%)
  starting transfers between devices  21.5 us (33%)
  local copies, waits for them, and re-layouts  11.2 us (17%)
  waiting for transfers between devices  7.72 us (12%)
  between operations  0.9 us (1%)
    pallas_call x13, Pallas kernels, call(): pl.pallas_call(kernel, out_shape=out_shape, in_specs=in_specs, out_specs=...  24.2 us
    unnamed x20, local copies, waits for them, and re-layouts  11 us
    ppermute x8, starting transfers between devices, around(): return (lax.ppermute(last, 'tile', up), lax.ppermute(first, 'tile', down))  8.32 us
    all_to_all x1, starting transfers between devices, remapped(): lax.all_to_all(sent, ('tile', 'lev', 'sec'), split_axis=0, concat_axis=0,...  5.97 us
    ppermute x3, waiting for transfers between devices, exchanged(): return lax.ppermute(value, axis, [(i, i ^ apart) for i in range(count)])  5.33 us
    ppermute x3, starting transfers between devices, exchanged(): return lax.ppermute(value, axis, [(i, i ^ apart) for i in range(count)])  4.45 us
    ppermute x2, starting transfers between devices, from_above(): return lax.ppermute(value, 'lev', [(i + 1, i) for i in range(count - 1)])  2.72 us
    ppermute x2, waiting for transfers between devices, from_above(): return lax.ppermute(value, 'lev', [(i + 1, i) for i in range(count - 1)])  2.12 us
  transfers between devices with their start and end apart: 14, of which 4 were waited for; matrix products, arithmetic and copies ran while one was open for 0% of the time, Pallas kernels for 27%

profile of v7, /device:TPU:0, one launch (start us, length us, event | category | flops | bytes accessed | tf_op | source)
XLA Modules:
  0.0 65.5 jit_solution(7539877808709420872)
XLA Ops:
  0.6 1.1 %shard_map.106 = f32[4,40,384]{2,1,0:T(8,128)S(1)} custom-call(f32[4,18,40,384]{3,2,1,0:T(8,128)} %f_hbm.1), custom_call_target="tpu_custom_call" | custom-call | flops 1 | bytes 1 | tf_op jit(solution)/shard_map/pallas_call | solution.py:19
  1.8 1.4 %collective-permute-start.2 = (f32[4,40,384]{2,1,0:T(8,128)S(1)}, f32[4,40,384]{2,1,0:T(8,128)S(1)}, u32[]{:S(2)}, u32[]{:S(2)}) collective-permute-start(f32[4,40,384]{2,1,0:T(8,128)S(1)} %shard_map.106), channel_id=1, source_target_pairs={{2,0},{4,2},{6,4},{3,1},{5,3},{7,5},{10,8},{12,10},{14,12},{11,9},... | collective-permute-start | bytes 737288 | tf_op jit(solution)/shard_map/ppermute | solution.py:651
  3.2 5.2 %shard_map.104 = (f32[17,4,3,56,128]{4,3,2,1,0:T(8,128)S(1)}, f32[3,68,128]{2,1,0:T(8,128)S(1)}, f32[3,68,128]{2,1,0:T(8,128)S(1)}, f32[4,40,384]{2,1,0:T(8,128)...) custom-call(f32[4,18,40,384]{3,2,1,0:T(8,128)S(1)} %copy-done.2, ...), custom_call_target="tpu_custom_call" | custom-call | flops 1 | bytes 1 | tf_op jit(solution)/shard_map/pallas_call | solution.py:19
  8.4 0.5 collective-permute-start
  8.9 2.0 %collective-permute-start.1 = (f32[3,68,128]{2,1,0:T(8,128)S(1)}, f32[3,68,128]{2,1,0:T(8,128)S(1)}, u32[]{:S(2)}, u32[]{:S(2)}) collective-permute-start(f32[3,68,128]{2,1,0:T(8,128)S(1)} %get-tuple-element.44), channel_id=1, source_target_pairs={{8,0},{16,8},{24,16},{0,24},{9,1},{17,9},{25,17},{1,25},{10,2},{18... | collective-permute-start | bytes 313352 | tf_op jit(solution)/shard_map/ppermute | solution.py:646
  10.9 3.1 %shard_map.105 = (f32[16,4,3,56,128]{4,3,2,1,0:T(8,128)S(1)}, f32[4,3,40,128]{3,2,1,0:T(8,128)S(1)}, f32[4,3,40,128]{3,2,1,0:T(8,128)S(1)}) custom-call(f32[17,4,3,56,128]{4,3,2,1,0:T(8,128)S(1)} %get-tuple-element.36.v_ref, bf16[18,40,384]{2,1,0:T(8,128)(2,1)S(1)} %get-tuple-element.37.cx_ref, bf16[18,40,384]{2,1,0:T(8,128)(2,1)S(1)} %get-tuple-element.38.mf_ref, ...), custom_call_target="tpu_custom_call" | custom-call | flops 1 | bytes 1 | tf_op jit(solution)/shard_map/pallas_call | solution.py:19
  14.1 0.2 collective-permute-done.1.right_ref
  14.4 0.2 shard_map.107
  14.6 1.3 %collective-permute-start.5 = (f32[4,40,384]{2,1,0:T(8,128)S(1)}, f32[4,40,384]{2,1,0:T(8,128)S(1)}, u32[]{:S(2)}, u32[]{:S(2)}) collective-permute-start(f32[4,40,384]{2,1,0:T(8,128)S(1)} %get-tuple-element.47.lowest_ref), channel_id=1, source_target_pairs={{2,0},{4,2},{6,4},{3,1},{5,3},{7,5},{10,8},{12,10},{14,12},{11,9},... | collective-permute-start | bytes 737288 | tf_op jit(solution)/shard_map/ppermute | solution.py:651
  15.9 1.5 %collective-permute-start.3 = (f32[3,4,128]{2,1,0:T(4,128)S(1)}, f32[3,4,128]{2,1,0:T(4,128)S(1)}, u32[]{:S(2)}, u32[]{:S(2)}) collective-permute-start(f32[3,4,128]{2,1,0:T(4,128)S(1)} %get-tuple-element.50), channel_id=1, source_target_pairs={{0,8},{8,16},{16,24},{24,0},{1,9},{9,17},{17,25},{25,1},{2,10},{10... | collective-permute-start | bytes 18440 | tf_op jit(solution)/shard_map/ppermute | solution.py:646
  17.4 0.8 %collective-permute-start.4 = (f32[3,4,128]{2,1,0:T(4,128)S(1)}, f32[3,4,128]{2,1,0:T(4,128)S(1)}, u32[]{:S(2)}, u32[]{:S(2)}) collective-permute-start(f32[3,4,128]{2,1,0:T(4,128)S(1)} %get-tuple-element.51), channel_id=1, source_target_pairs={{8,0},{16,8},{24,16},{0,24},{9,1},{17,9},{25,17},{1,25},{10,2},{18... | collective-permute-start | bytes 18440 | tf_op jit(solution)/shard_map/ppermute | solution.py:646
  18.2 3.1 %shard_map.108 = (f32[16,4,3,56,128]{4,3,2,1,0:T(8,128)S(1)}, f32[3,64,128]{2,1,0:T(8,128)S(1)}, f32[3,64,128]{2,1,0:T(8,128)S(1)}, f32[4,3,40,128]{3,2,1,0:T(8,128)S(1)}) custom-call(f32[17,4,3,56,128]{4,3,2,1,0:T(8,128)S(1)} %get-tuple-element.36.v_ref, f32[16,4,3,56,128]{4,3,2,1,0:T(8,128)S(1)} %get-tuple-element.41.inner_ref, ...), custom_call_target="tpu_custom_call" | custom-call | flops 1 | bytes 1 | tf_op jit(solution)/shard_map/pallas_call | solution.py:19
  21.3 0.2 shard_map.109
  21.6 0.6 collective-permute-start.6
  22.1 1.2 %collective-permute-start.7 = (f32[3,68,128]{2,1,0:T(8,128)S(1)}, f32[3,68,128]{2,1,0:T(8,128)S(1)}, u32[]{:S(2)}, u32[]{:S(2)}) collective-permute-start(f32[3,68,128]{2,1,0:T(8,128)S(1)} %get-tuple-element.59), channel_id=1, source_target_pairs={{8,0},{16,8},{24,16},{0,24},{9,1},{17,9},{25,17},{1,25},{10,2},{18... | collective-permute-start | bytes 313352 | tf_op jit(solution)/shard_map/ppermute | solution.py:646
  23.4 2.1 %collective-permute-done.5.above_ref = f32[4,40,384]{2,1,0:T(8,128)S(1)} collective-permute-done((f32[4,40,384]{2,1,0:T(8,128)S(1)}, f32[4,40,384]{2,1,0:T(8,128)S(1)}, u32[]{:S(2)}, u32[]{:S(2)}) %collective-permute-start.5) | collective-permute-done | bytes 245792 | tf_op jit(solution)/shard_map/ppermute | solution.py:651
  25.7 0.5 collective-permute-start.8
  26.2 1.3 %collective-permute-start.9 = (f32[3,4,128]{2,1,0:T(4,128)S(1)}, f32[3,4,128]{2,1,0:T(4,128)S(1)}, u32[]{:S(2)}, u32[]{:S(2)}) collective-permute-start(f32[3,4,128]{2,1,0:T(4,128)S(1)} %get-tuple-element.61), channel_id=1, source_target_pairs={{8,0},{16,8},{24,16},{0,24},{9,1},{17,9},{25,17},{1,25},{10,2},{18... | collective-permute-start | bytes 18440 | tf_op jit(solution)/shard_map/ppermute | solution.py:646
  27.6 1.8 %shard_map.111 = (f32[4,18,40,384]{3,2,1,0:T(8,128)}, f32[40,384]{1,0:T(8,128)S(1)}) custom-call(f32[16,4,3,56,128]{4,3,2,1,0:T(8,128)S(1)} %get-tuple-element.48.v_ref, f32[4,3,56,128]{3,2,1,0:T(8,128)S(1)} %get-tuple-element.55.vs_ref, bf16[18,40,384]{2,1,0:T(8,128)(2,1)S(1)} %get-tuple-element.37.cx_ref, s32[18,40,384]{2,1,0:T(8,128)S(1)} %get-tuple-element.40.code_ref, ...), custom_call_target="tpu_custom_call" | custom-call | flops 1 | bytes 1 | tf_op jit(solution)/shard_map/pallas_call | solution.py:19
  29.5 1.8 %shard_map.112 = (f32[18,4,40,384]{3,2,1,0:T(8,128)S(1)}, f32[4,4,2,8,128]{4,3,2,1,0:T(8,128)}) custom-call(f32[16,4,3,56,128]{4,3,2,1,0:T(8,128)S(1)} %get-tuple-element.48.v_ref, f32[4,3,56,128]{3,2,1,0:T(8,128)S(1)} %get-tuple-element.55.vs_ref, f32[4,3,56,128]{3,2,1,0:T(8,128)S(1)} %get-tuple-element.57.vt_ref, ...), custom_call_target="tpu_custom_call" | custom-call | flops 1 | bytes 1 | tf_op jit(solution)/shard_map/pallas_call | solution.py:19
  31.2 2.1 %copy-done.3 = f32[18,4,40,384]{3,2,1,0:T(8,128)} copy-done((f32[18,4,40,384]{3,2,1,0:T(8,128)}, f32[18,4,40,384]{3,2,1,0:T(8,128)S(1)}, u32[]{:S(2)}) %copy-start.3) | copy-done | bytes 4423704
  33.3 6.0 %all-to-all-start = ((f32[32,8,128]{2,1,0:T(8,128)}), f32[32,8,128]{2,1,0:T(8,128)S(1)}, u32[]{:S(2)}, u32[]{:S(2)}) async-start(f32[32,8,128]{2,1,0:T(8,128)} %bitcast.3), calls=%async_computation | async-start | bytes 262144 | tf_op jit(solution)/shard_map/all_to_all | solution.py:612
  39.4 2.4 %shard_map.114 = (bf16[64,64,256]{2,1,0:T(8,128)(2,1)S(1)}, bf16[64,256,256]{2,1,0:T(8,128)(2,1)S(1)}) custom-call(s32[128,128]{1,0:T(8,128)S(1)} %bitcast.15), custom_call_target="tpu_custom_call" | custom-call | flops 1 | bytes 1 | tf_op jit(solution)/shard_map/pallas_call | solution.py:19
  41.8 3.3 %copy-done = bf16[64,256,256]{2,1,0:T(8,128)(2,1)} copy-done((bf16[64,256,256]{2,1,0:T(8,128)(2,1)}, bf16[64,256,256]{2,1,0:T(8,128)(2,1)S(1)}, u32[]{:S(2)}) %copy-start) | copy-done | bytes 8388632
  45.0 2.3 %copy-done.4 = f32[18,4,40,384]{3,2,1,0:T(8,128)S(1)} copy-done((f32[18,4,40,384]{3,2,1,0:T(8,128)S(1)}, f32[18,4,40,384]{3,2,1,0:T(8,128)}, u32[]{:S(2)}) %copy-start.4) | copy-done | bytes 4423704
  47.3 1.5 %shard_map.113.refs_2_ = f32[4,18,40,384]{3,2,1,0:T(8,128)} custom-call(f32[18,4,40,384]{3,2,1,0:T(8,128)S(1)} %copy-done.4, f32[4,18,40,384]{3,2,1,0:T(8,128)} %get-tuple-element.64.done_hbm), custom_call_target="tpu_custom_call", output_to_operand_aliasing={{}: (1, {})} | custom-call | flops 1 | bytes 1 | tf_op jit(solution)/shard_map/pallas_call | solution.py:19
  48.8 3.4 %copy-done.1 = bf16[64,256,256]{2,1,0:T(8,128)(2,1)S(1)} copy-done((bf16[64,256,256]{2,1,0:T(8,128)(2,1)S(1)}, bf16[64,256,256]{2,1,0:T(8,128)(2,1)}, u32[]{:S(2)}) %copy-start.1) | copy-done | bytes 8388632
  52.2 1.8 %collective-permute-start.10 = (f32[32,128]{1,0:T(8,128)S(1)}, f32[32,128]{1,0:T(8,128)S(1)}, u32[]{:S(2)}, u32[]{:S(2)}) collective-permute-start(f32[32,128]{1,0:T(8,128)S(1)} %bitcast.16), channel_id=1, source_target_pairs={{0,2},{2,0},{4,6},{6,4},{1,3},{3,1},{5,7},{7,5},{8,10},{10,8},{12,... | collective-permute-start | bytes 49160 | tf_op jit(solution)/shard_map/ppermute | solution.py:605
  54.1 2.4 %collective-permute-start.11 = (f32[32,128]{1,0:T(8,128)S(1)}, f32[32,128]{1,0:T(8,128)S(1)}, u32[]{:S(2)}, u32[]{:S(2)}) collective-permute-start(f32[32,128]{1,0:T(8,128)S(1)} %bitcast.17), channel_id=1, source_target_pairs={{0,4},{2,6},{4,0},{6,2},{1,5},{3,7},{5,1},{7,3},{8,12},{10,14},{12... | collective-permute-start | bytes 49160 | tf_op jit(solution)/shard_map/ppermute | solution.py:605
  56.7 2.1 %collective-permute-done.11.refs_2_ = f32[32,128]{1,0:T(8,128)S(1)} collective-permute-done((f32[32,128]{1,0:T(8,128)S(1)}, f32[32,128]{1,0:T(8,128)S(1)}, u32[]{:S(2)}, u32[]{:S(2)}) %collective-permute-start.11) | collective-permute-done | bytes 16416 | tf_op jit(solution)/shard_map/ppermute | solution.py:605
  58.8 3.2 %collective-permute-done.12.refs_3_ = f32[32,128]{1,0:T(8,128)S(1)} collective-permute-done((f32[32,128]{1,0:T(8,128)S(1)}, f32[32,128]{1,0:T(8,128)S(1)}, u32[]{:S(2)}, u32[]{:S(2)}) %collective-permute-start.12) | collective-permute-done | bytes 16416 | tf_op jit(solution)/shard_map/ppermute | solution.py:605
  62.0 3.5 %shard_map.116 = f32[120,128]{1,0:T(8,128)} custom-call(bf16[64,64,256]{2,1,0:T(8,128)(2,1)S(1)} %get-tuple-element.67.refs_0_.high_ref, bf16[64,256,256]{2,1,0:T(8,128)(2,1)S(1)} %copy-done.1, f32[32,128]{1,0:T(8,128)S(1)} %bitcast.19, f32[32,128]{1,0:T(8,128)S(1)} %collective-permute-done.10.refs_1_, f32[32,128]{1,0:T(8,128)S(1)} %collective-permute-done.11.refs_2_, ...), custom_call_target="tpu_custom_call" | custom-call | flops 1 | bytes 1 | tf_op jit(solution)/shard_map/pallas_call | solution.py:19
  (32 shorter events, 0.6 us)
Async XLA Ops:
  0.6 2.6 %copy-start.2 = (f32[4,18,40,384]{3,2,1,0:T(8,128)S(1)}, f32[4,18,40,384]{3,2,1,0:T(8,128)}, u32[]{:S(2)}) copy-start(f32[4,18,40,384]{3,2,1,0:T(8,128)} %f_hbm.1) | copy-start | bytes 13271044
  1.8 12.6 %collective-permute-start.2 = (f32[4,40,384]{2,1,0:T(8,128)S(1)}, f32[4,40,384]{2,1,0:T(8,128)S(1)}, u32[]{:S(2)}, u32[]{:S(2)}) collective-permute-start(f32[4,40,384]{2,1,0:T(8,128)S(1)} %shard_map.106), channel_id=1, source_target_pairs={{2,0},{4,2},{6,4},{3,1},{5,3},{7,5},{10,8},{12,10},{14,12},{11,9},... | collective-permute-start | bytes 737288 | tf_op jit(solution)/shard_map/ppermute | solution.py:651
  8.4 5.9 %copy-start.7 = (s32[4,2]{0,1:T(2,128)S(1)}, s32[4,2]{0,1:T(2,128)}, u32[]{:S(2)}) copy-start(s32[4,2]{0,1:T(2,128)} %param.14) | copy-start | bytes 100
  8.4 5.6 %collective-permute-start = (f32[3,68,128]{2,1,0:T(8,128)S(1)}, f32[3,68,128]{2,1,0:T(8,128)S(1)}, u32[]{:S(2)}, u32[]{:S(2)}) collective-permute-start(f32[3,68,128]{2,1,0:T(8,128)S(1)} %get-tuple-element.43), channel_id=1, source_target_pairs={{0,8},{8,16},{16,24},{24,0},{1,9},{9,17},{17,25},{25,1},{2,10},{10... | collective-permute-start | bytes 313352 | tf_op jit(solution)/shard_map/ppermute | solution.py:646
  8.9 5.4 %collective-permute-start.1 = (f32[3,68,128]{2,1,0:T(8,128)S(1)}, f32[3,68,128]{2,1,0:T(8,128)S(1)}, u32[]{:S(2)}, u32[]{:S(2)}) collective-permute-start(f32[3,68,128]{2,1,0:T(8,128)S(1)} %get-tuple-element.44), channel_id=1, source_target_pairs={{8,0},{16,8},{24,16},{0,24},{9,1},{17,9},{25,17},{1,25},{10,2},{18... | collective-permute-start | bytes 313352 | tf_op jit(solution)/shard_map/ppermute | solution.py:646
  14.6 10.9 %collective-permute-start.5 = (f32[4,40,384]{2,1,0:T(8,128)S(1)}, f32[4,40,384]{2,1,0:T(8,128)S(1)}, u32[]{:S(2)}, u32[]{:S(2)}) collective-permute-start(f32[4,40,384]{2,1,0:T(8,128)S(1)} %get-tuple-element.47.lowest_ref), channel_id=1, source_target_pairs={{2,0},{4,2},{6,4},{3,1},{5,3},{7,5},{10,8},{12,10},{14,12},{11,9},... | collective-permute-start | bytes 737288 | tf_op jit(solution)/shard_map/ppermute | solution.py:651
  15.9 5.4 %collective-permute-start.3 = (f32[3,4,128]{2,1,0:T(4,128)S(1)}, f32[3,4,128]{2,1,0:T(4,128)S(1)}, u32[]{:S(2)}, u32[]{:S(2)}) collective-permute-start(f32[3,4,128]{2,1,0:T(4,128)S(1)} %get-tuple-element.50), channel_id=1, source_target_pairs={{0,8},{8,16},{16,24},{24,0},{1,9},{9,17},{17,25},{25,1},{2,10},{10... | collective-permute-start | bytes 18440 | tf_op jit(solution)/shard_map/ppermute | solution.py:646
  17.4 3.9 %collective-permute-start.4 = (f32[3,4,128]{2,1,0:T(4,128)S(1)}, f32[3,4,128]{2,1,0:T(4,128)S(1)}, u32[]{:S(2)}, u32[]{:S(2)}) collective-permute-start(f32[3,4,128]{2,1,0:T(4,128)S(1)} %get-tuple-element.51), channel_id=1, source_target_pairs={{8,0},{16,8},{24,16},{0,24},{9,1},{17,9},{25,17},{1,25},{10,2},{18... | collective-permute-start | bytes 18440 | tf_op jit(solution)/shard_map/ppermute | solution.py:646
  21.3 6.2 %copy-start.8 = (f32[18]{0:T(128)S(1)}, f32[18]{0:T(128)}, u32[]{:S(2)}) copy-start(f32[18]{0:T(128)} %param.15) | copy-start | bytes 220
  21.3 6.3 %copy-start.5 = (f32[4,40,384]{2,1,0:T(8,128)S(1)}, f32[4,40,384]{2,1,0:T(8,128)}, u32[]{:S(2)}) copy-start(f32[4,40,384]{2,1,0:T(8,128)} %share_ref.3) | copy-start | bytes 737284
  21.6 7.9 %collective-permute-start.6 = (f32[3,68,128]{2,1,0:T(8,128)S(1)}, f32[3,68,128]{2,1,0:T(8,128)S(1)}, u32[]{:S(2)}, u32[]{:S(2)}) collective-permute-start(f32[3,68,128]{2,1,0:T(8,128)S(1)} %get-tuple-element.58), channel_id=1, source_target_pairs={{0,8},{8,16},{16,24},{24,0},{1,9},{9,17},{17,25},{25,1},{2,10},{10... | collective-permute-start | bytes 313352 | tf_op jit(solution)/shard_map/ppermute | solution.py:646
  22.1 7.3 %collective-permute-start.7 = (f32[3,68,128]{2,1,0:T(8,128)S(1)}, f32[3,68,128]{2,1,0:T(8,128)S(1)}, u32[]{:S(2)}, u32[]{:S(2)}) collective-permute-start(f32[3,68,128]{2,1,0:T(8,128)S(1)} %get-tuple-element.59), channel_id=1, source_target_pairs={{8,0},{16,8},{24,16},{0,24},{9,1},{17,9},{25,17},{1,25},{10,2},{18... | collective-permute-start | bytes 313352 | tf_op jit(solution)/shard_map/ppermute | solution.py:646
  25.7 3.7 %collective-permute-start.8 = (f32[3,4,128]{2,1,0:T(4,128)S(1)}, f32[3,4,128]{2,1,0:T(4,128)S(1)}, u32[]{:S(2)}, u32[]{:S(2)}) collective-permute-start(f32[3,4,128]{2,1,0:T(4,128)S(1)} %get-tuple-element.60), channel_id=1, source_target_pairs={{0,8},{8,16},{16,24},{24,0},{1,9},{9,17},{17,25},{25,1},{2,10},{10... | collective-permute-start | bytes 18440 | tf_op jit(solution)/shard_map/ppermute | solution.py:646
  26.2 3.3 %collective-permute-start.9 = (f32[3,4,128]{2,1,0:T(4,128)S(1)}, f32[3,4,128]{2,1,0:T(4,128)S(1)}, u32[]{:S(2)}, u32[]{:S(2)}) collective-permute-start(f32[3,4,128]{2,1,0:T(4,128)S(1)} %get-tuple-element.61), channel_id=1, source_target_pairs={{8,0},{16,8},{24,16},{0,24},{9,1},{17,9},{25,17},{1,25},{10,2},{18... | collective-permute-start | bytes 18440 | tf_op jit(solution)/shard_map/ppermute | solution.py:646
  29.4 9.9 %copy-start.6 = (s32[4,3840]{1,0:T(4,128)S(1)}, s32[4,3840]{1,0:T(4,128)}, u32[]{:S(2)}) copy-start(s32[4,3840]{1,0:T(4,128)} %param.17) | copy-start | bytes 184324
  31.2 2.1 %copy-start.3 = (f32[18,4,40,384]{3,2,1,0:T(8,128)}, f32[18,4,40,384]{3,2,1,0:T(8,128)S(1)}, u32[]{:S(2)}) copy-start(f32[18,4,40,384]{3,2,1,0:T(8,128)S(1)} %get-tuple-element.63.part_ref) | copy-start | bytes 13271044
  33.3 15.5 %all-to-all-start = ((f32[32,8,128]{2,1,0:T(8,128)}), f32[32,8,128]{2,1,0:T(8,128)S(1)}, u32[]{:S(2)}, u32[]{:S(2)}) async-start(f32[32,8,128]{2,1,0:T(8,128)} %bitcast.3), calls=%async_computation | async-start | bytes 262144 | tf_op jit(solution)/shard_map/all_to_all | solution.py:612
  41.7 3.3 %copy-start = (bf16[64,256,256]{2,1,0:T(8,128)(2,1)}, bf16[64,256,256]{2,1,0:T(8,128)(2,1)S(1)}, u32[]{:S(2)}) copy-start(bf16[64,256,256]{2,1,0:T(8,128)(2,1)S(1)} %get-tuple-element.68.refs_1_.low_ref) | copy-start | bytes 25165828
  45.0 2.3 %copy-start.4 = (f32[18,4,40,384]{3,2,1,0:T(8,128)S(1)}, f32[18,4,40,384]{3,2,1,0:T(8,128)}, u32[]{:S(2)}) copy-start(f32[18,4,40,384]{3,2,1,0:T(8,128)} %copy-done.3) | copy-start | bytes 13271044
  48.8 3.4 %copy-start.1 = (bf16[64,256,256]{2,1,0:T(8,128)(2,1)S(1)}, bf16[64,256,256]{2,1,0:T(8,128)(2,1)}, u32[]{:S(2)}) copy-start(bf16[64,256,256]{2,1,0:T(8,128)(2,1)} %copy-done) | copy-start | bytes 25165828
  52.2 4.5 %collective-permute-start.10 = (f32[32,128]{1,0:T(8,128)S(1)}, f32[32,128]{1,0:T(8,128)S(1)}, u32[]{:S(2)}, u32[]{:S(2)}) collective-permute-start(f32[32,128]{1,0:T(8,128)S(1)} %bitcast.16), channel_id=1, source_target_pairs={{0,2},{2,0},{4,6},{6,4},{1,3},{3,1},{5,7},{7,5},{8,10},{10,8},{12,... | collective-permute-start | bytes 49160 | tf_op jit(solution)/shard_map/ppermute | solution.py:605
  54.1 4.7 %collective-permute-start.11 = (f32[32,128]{1,0:T(8,128)S(1)}, f32[32,128]{1,0:T(8,128)S(1)}, u32[]{:S(2)}, u32[]{:S(2)}) collective-permute-start(f32[32,128]{1,0:T(8,128)S(1)} %bitcast.17), channel_id=1, source_target_pairs={{0,4},{2,6},{4,0},{6,2},{1,5},{3,7},{5,1},{7,3},{8,12},{10,14},{12... | collective-permute-start | bytes 49160 | tf_op jit(solution)/shard_map/ppermute | solution.py:605
  56.5 5.5 %collective-permute-start.12 = (f32[32,128]{1,0:T(8,128)S(1)}, f32[32,128]{1,0:T(8,128)S(1)}, u32[]{:S(2)}, u32[]{:S(2)}) collective-permute-start(f32[32,128]{1,0:T(8,128)S(1)} %bitcast.18), channel_id=1, source_target_pairs={{0,6},{2,4},{4,2},{6,0},{1,7},{3,5},{5,3},{7,1},{8,14},{10,12},{12... | collective-permute-start | bytes 49160 | tf_op jit(solution)/shard_map/ppermute | solution.py:605

commit v8 on v6

--- a/solution.py
+++ b/solution.py
@@ -126,48 +126,30 @@
     return seam_ref[0, pl.ds(tile, 1), :] == 1, seam_ref[1, pl.ds(tile, 1), :] == 1
 
 
-def start_kernel(f_hbm, out_ref, sem):
-    copy = pltpu.make_async_copy(f_hbm.at[:, 0], out_ref, sem)
-    copy.start()
-    copy.wait()
-
-
-def lower_kernel(
-    f_hbm, mf_hbm, cy_hbm, code_hbm, cx_hbm,
-    v_ref, first_ref, last_ref, top_ref, mf_ref, cy_ref, code_ref, cx_ref,
-    f_ref, sems,
-):
-    sectors, levels, columns, width = f_hbm.shape
+def start_kernel(f_hbm, mf_hbm, cy_hbm, code_hbm, cx_hbm, out_ref, mf_ref, cy_ref, code_ref, cx_ref, sems):
+    copies = [
+        pltpu.make_async_copy(source, target, sems.at[i])
+        for i, (source, target) in enumerate(
+            (
+                (f_hbm.at[:, 0], out_ref),
+                (mf_hbm, mf_ref),
+                (cy_hbm, cy_ref),
+                (code_hbm, code_ref),
+                (cx_hbm, cx_ref),
+            )
+        )
+    ]
+    for copy in copies:
+        copy.start()
+    for copy in copies:
+        copy.wait()
+
+
+def lower_kernel(f_ref, mf_ref, cy_ref, code_ref, v_ref, first_ref, last_ref, top_ref):
+    sectors, levels, columns, width = f_ref.shape
     tiles, strips = width // LANES, columns // ROWS
 
-    def fetch(k):
-        return pltpu.make_async_copy(f_hbm.at[:, k], f_ref.at[k], sems.at[0, k])
-
-    def fetch_code(k):
-        return pltpu.make_async_copy(code_hbm.at[k], code_ref.at[k], sems.at[1, k])
-
-    def fetch_mf(k):
-        return pltpu.make_async_copy(mf_hbm.at[k], mf_ref.at[k], sems.at[2, k])
-
-    def fetch_cy(k):
-        return pltpu.make_async_copy(cy_hbm.at[k], cy_ref.at[k], sems.at[3, k])
-
-    fetch_cx = pltpu.make_async_copy(cx_hbm, cx_ref, sems.at[4, 0])
-    fetch(0).start()
-    for k in range(levels):
-        fetch_mf(k).start()
-        fetch_cy(k).start()
-        fetch_code(k).start()
-        if k < levels - 1:
-            fetch(k + 1).start()
-    fetch_cx.start()
-    fetch(0).wait()
-
     def level(k, _):
-        fetch_mf(k).wait()
-        fetch_cy(k).wait()
-        fetch_code(k).wait()
-        fetch(k + 1).wait()
         mf = mf_ref[k].astype(jnp.float32)
         cy = cy_ref[k].astype(jnp.float32)
         codes = code_ref[k]
@@ -178,8 +160,8 @@
                 parts = []
                 for j in range(tiles):
                     lanes = slice(j * LANES, (j + 1) * LANES)
-                    here = f_ref[k, s, rows, lanes]
-                    upper = f_ref[k + 1, s, rows, lanes]
+                    here = f_ref[s, k, rows, lanes]
+                    upper = f_ref[s, k + 1, rows, lanes]
                     parts.append(here + cut(mf, xt, j) * (upper - here))
                 for j, value in enumerate(second_sweep(parts, factors)):
                     store_padded(v_ref, (k,), s, j, xt, value)
@@ -187,11 +169,7 @@
         return 0
 
     lax.fori_loop(0, levels - 1, level, 0)
-    top_ref[...] = f_ref[levels - 1]
-    fetch_mf(levels - 1).wait()
-    fetch_cy(levels - 1).wait()
-    fetch_code(levels - 1).wait()
-    fetch_cx.wait()
+    top_ref[...] = f_ref[:, levels - 1]
 
 
 def first_weights(cx, codes, bit, xt, j):
@@ -550,32 +528,41 @@
     rows, lanes = out_ref.shape
     group, owners, depth, _ = cells_ref.shape
     rank = lax.axis_index("lev")
-    high_iota = lax.broadcasted_iota(jnp.int32, (rows, lanes), 0)
-    low_iota = lax.broadcasted_iota(jnp.int32, (lanes, lanes), 0)
-    total = jnp.zeros((2 * rows, lanes), jnp.float32)
+    half = jnp.bfloat16
+    zero, one = jnp.zeros((), half), jnp.ones((), half)
+    iota = lax.broadcasted_iota(jnp.int32, (lanes, lanes), 0).astype(jnp.float32).astype(half)
+    total = jnp.zeros((2 * lanes, lanes), jnp.float32)
     lines = [(i, o, r) for i in range(group) for o in range(owners) for r in range(depth)]
-    for pair in range(0, len(lines), 2):
+    wide = 8
+
+    def spread(row):
+        return jnp.broadcast_to(row, (lanes, lanes)).astype(half)
+
+    for start in range(0, len(lines), wide):
         lefts, rights = [], []
-        for part, owner, line in lines[pair : pair + 2]:
+        for part, owner, line in lines[start : start + wide]:
             cells = cells_ref[jnp.bitwise_xor(rank, part), owner, line : line + 1, :]
             value = value_refs[part][owner, line : line + 1, :]
-            coarse = value.astype(jnp.bfloat16).astype(jnp.float32)
-            fine = value - coarse
-            here = jnp.right_shift(cells, 7) == high_iota
+            coarse = value.astype(half).astype(jnp.float32)
+            high = spread(jnp.right_shift(cells, 7).astype(jnp.float32)) == iota
+            low = spread(jnp.bitwise_and(cells, 127).astype(jnp.float32)) == iota
             lefts.append(
                 jnp.concatenate(
-                    [jnp.where(here, coarse, 0.0), jnp.where(here, fine, 0.0)], axis=0
-                ).astype(jnp.bfloat16)
+                    [
+                        jnp.where(high, spread(coarse), zero),
+                        jnp.where(high, spread(value - coarse), zero),
+                    ],
+                    axis=0,
+                )
             )
-            match = jnp.bitwise_and(cells, 127) == low_iota
-            rights.append(jnp.where(match, 1.0, 0.0).astype(jnp.bfloat16))
+            rights.append(jnp.where(low, one, zero))
         total += lax.dot_general(
             jnp.concatenate(lefts, axis=1),
             jnp.concatenate(rights, axis=1),
             (((1,), (1,)), ((), ())),
             preferred_element_type=jnp.float32,
         )
-    out_ref[...] = total[:rows] + total[rows:]
+    out_ref[...] = total[:rows] + total[lanes : lanes + rows]
 
 
 def exchanged(value, axis, apart):
@@ -629,23 +616,22 @@
     seam = jnp.broadcast_to(seam_code.T[:, :, None], (*seam_code.T.shape, LANES))
     weight = jnp.broadcast_to(level_weight[:, None], (levels, LANES))
 
-    above = from_above(
-        call(start_kernel, plane, [HBM], VM, in_hbm(forcing), [pltpu.SemaphoreType.DMA])
-    )
     narrow = pltpu.VMEM((levels, columns, width), jnp.bfloat16)
-    v, first, last, top, mass_flux, courant_y, limiter_code, courant_x = call(
+    lowest, mass_flux, courant_y, limiter_code, courant_x = call(
+        start_kernel,
+        (plane, narrow, narrow, pltpu.VMEM((levels, columns, width), jnp.int32), narrow),
+        [HBM] * 5,
+        [VM] * 5,
+        in_hbm(forcing, mass_flux, courant_y, limiter_code, courant_x),
+        [pltpu.SemaphoreType.DMA((5,))],
+    )
+    above = from_above(lowest)
+    v, first, last, top = call(
         lower_kernel,
-        (
-            field, rim, rim, plane,
-            narrow, narrow, pltpu.VMEM((levels, columns, width), jnp.int32), narrow,
-        ),
-        [HBM] * 5,
-        [VM] * 8,
-        in_hbm(forcing, mass_flux, courant_y, limiter_code, courant_x),
-        [
-            pltpu.VMEM((levels, sectors, columns, width), jnp.float32),
-            pltpu.SemaphoreType.DMA((5, levels)),
-        ],
+        (field, rim, rim, plane),
+        [VM] * 4,
+        [VM] * 4,
+        (forcing, mass_flux, courant_y, limiter_code),
     )
     left, right = around(first, last)
     lines = kept(sectors, tiles, columns, LANES)

time: 56.8 us -> 55.7 us (0.981)
  Pallas kernels: 21.1 us -> 19.8 us
    pallas_call x10, Pallas kernels: 21.1 us -> 19.8 us  [call(): pl.pallas_call(kernel, out_shape=out_shape, in_specs=in_specs, out_specs=...]
  transfers between devices with their start and end apart: 14 -> 14, of which waited for: 5 -> 6; matrix products, arithmetic and copies ran while one was open for 0% -> 0% of each run, Pallas kernels for 25% -> 22%
where the time goes in v8:
time: 55.7 us; the launch traced here: 55.5 us
  starting transfers between devices  21.3 us (38%)
  Pallas kernels  19.8 us (36%)
  waiting for transfers between devices  13.4 us (24%)
  between operations  0.85 us (2%)
    pallas_call x10, Pallas kernels, call(): pl.pallas_call(kernel, out_shape=out_shape, in_specs=in_specs, out_specs=...  19.8 us
    ppermute x8, starting transfers between devices, around(): return (lax.ppermute(last, 'tile', up), lax.ppermute(first, 'tile', down))  8.1 us
    all_to_all x1, waiting for transfers between devices, remapped(): lax.all_to_all(sent, ('tile', 'lev', 'sec'), split_axis=0, concat_axis=0,...  7.71 us
    all_to_all x1, starting transfers between devices, remapped(): lax.all_to_all(sent, ('tile', 'lev', 'sec'), split_axis=0, concat_axis=0,...  5.98 us
    ppermute x3, starting transfers between devices, exchanged(): return lax.ppermute(value, axis, [(i, i ^ apart) for i in range(count)])  4.45 us
    ppermute x3, waiting for transfers between devices, exchanged(): return lax.ppermute(value, axis, [(i, i ^ apart) for i in range(count)])  3.05 us
    ppermute x2, starting transfers between devices, from_above(): return lax.ppermute(value, 'lev', [(i + 1, i) for i in range(count - 1)])  2.72 us
    ppermute x2, waiting for transfers between devices, from_above(): return lax.ppermute(value, 'lev', [(i + 1, i) for i in range(count - 1)])  2.34 us
  transfers between devices with their start and end apart: 14, of which 6 were waited for; matrix products, arithmetic and copies ran while one was open for 0% of the time, Pallas kernels for 22%

profile of v8, /device:TPU:0, one launch (start us, length us, event | category | flops | bytes accessed | tf_op | source)
XLA Modules:
  0.0 55.5 jit_solution(1238547731653353687)
XLA Ops:
  0.6 2.0 %shard_map.104 = (f32[4,40,384]{2,1,0:T(8,128)S(1)}, bf16[18,40,384]{2,1,0:T(8,128)(2,1)S(1)}, bf16[18,40,384]{2,1,0:T(8,128)(2,1)S(1)}, s32[18,40,384]{2,1,0:T(8,128)S(1)}, bf16[18,40,384]{2,1,0:T(8,128)(2,1)S(1)}) custom-call(f32[4,18,40,384]{3,2,1,0:T(8,128)} %f_ref.1, bf16[18,40,384]{2,1,0:T(8,128)(2,1)} %mf_hbm.1, bf16[18,40,384]{2,1,0:T(8,128)(2,1)} %cy_hbm.1, ...), custom_call_target="tpu_custom_call" | custom-call | flops 1 | bytes 1 | tf_op jit(solution)/shard_map/pallas_call | solution.py:19
  2.7 1.4 %collective-permute-start.2 = (f32[4,40,384]{2,1,0:T(8,128)S(1)}, f32[4,40,384]{2,1,0:T(8,128)S(1)}, u32[]{:S(2)}, u32[]{:S(2)}) collective-permute-start(f32[4,40,384]{2,1,0:T(8,128)S(1)} %get-tuple-element.46), channel_id=1, source_target_pairs={{2,0},{4,2},{6,4},{3,1},{5,3},{7,5},{10,8},{12,10},{14,12},{11,9},... | collective-permute-start | bytes 737288 | tf_op jit(solution)/shard_map/ppermute | solution.py:599
  4.1 3.5 %shard_map.105 = (f32[17,4,3,56,128]{4,3,2,1,0:T(8,128)S(1)}, f32[3,68,128]{2,1,0:T(8,128)S(1)}, f32[3,68,128]{2,1,0:T(8,128)S(1)}, f32[4,40,384]{2,1,0:T(8,128)S(1)}) custom-call(f32[4,18,40,384]{3,2,1,0:T(8,128)S(1)} %copy-done, bf16[18,40,384]{2,1,0:T(8,128)(2,1)S(1)} %get-tuple-element.35.mf_ref, bf16[18,40,384]{2,1,0:T(8,128)(2,1)S(1)} %get-tuple-element.36.cy_ref, ...), custom_call_target="tpu_custom_call" | custom-call | flops 1 | bytes 1 | tf_op jit(solution)/shard_map/pallas_call | solution.py:19
  7.6 0.5 collective-permute-start
  8.1 2.0 %collective-permute-start.1 = (f32[3,68,128]{2,1,0:T(8,128)S(1)}, f32[3,68,128]{2,1,0:T(8,128)S(1)}, u32[]{:S(2)}, u32[]{:S(2)}) collective-permute-start(f32[3,68,128]{2,1,0:T(8,128)S(1)} %get-tuple-element.43), channel_id=1, source_target_pairs={{8,0},{16,8},{24,16},{0,24},{9,1},{17,9},{25,17},{1,25},{10,2},{18... | collective-permute-start | bytes 313352 | tf_op jit(solution)/shard_map/ppermute | solution.py:594
  10.1 3.1 %shard_map.106 = (f32[16,4,3,56,128]{4,3,2,1,0:T(8,128)S(1)}, f32[4,3,40,128]{3,2,1,0:T(8,128)S(1)}, f32[4,3,40,128]{3,2,1,0:T(8,128)S(1)}) custom-call(f32[17,4,3,56,128]{4,3,2,1,0:T(8,128)S(1)} %get-tuple-element.38.v_ref, bf16[18,40,384]{2,1,0:T(8,128)(2,1)S(1)} %get-tuple-element.39.cx_ref, bf16[18,40,384]{2,1,0:T(8,128)(2,1)S(1)} %get-tuple-element.35.mf_ref, ...), custom_call_target="tpu_custom_call" | custom-call | flops 1 | bytes 1 | tf_op jit(solution)/shard_map/pallas_call | solution.py:19
  13.2 0.2 collective-permute-done.1.right_ref
  13.5 0.2 collective-permute-done.2.above_ref
  13.7 0.1 broadcast_in_dim.4.seam_ref
  13.8 0.2 shard_map.107
  14.0 1.3 %collective-permute-start.5 = (f32[4,40,384]{2,1,0:T(8,128)S(1)}, f32[4,40,384]{2,1,0:T(8,128)S(1)}, u32[]{:S(2)}, u32[]{:S(2)}) collective-permute-start(f32[4,40,384]{2,1,0:T(8,128)S(1)} %get-tuple-element.47.lowest_ref), channel_id=1, source_target_pairs={{2,0},{4,2},{6,4},{3,1},{5,3},{7,5},{10,8},{12,10},{14,12},{11,9},... | collective-permute-start | bytes 737288 | tf_op jit(solution)/shard_map/ppermute | solution.py:599
  15.3 1.2 %collective-permute-start.3 = (f32[3,4,128]{2,1,0:T(4,128)S(1)}, f32[3,4,128]{2,1,0:T(4,128)S(1)}, u32[]{:S(2)}, u32[]{:S(2)}) collective-permute-start(f32[3,4,128]{2,1,0:T(4,128)S(1)} %get-tuple-element.50), channel_id=1, source_target_pairs={{0,8},{8,16},{16,24},{24,0},{1,9},{9,17},{17,25},{25,1},{2,10},{10... | collective-permute-start | bytes 18440 | tf_op jit(solution)/shard_map/ppermute | solution.py:594
  16.5 0.8 %collective-permute-start.4 = (f32[3,4,128]{2,1,0:T(4,128)S(1)}, f32[3,4,128]{2,1,0:T(4,128)S(1)}, u32[]{:S(2)}, u32[]{:S(2)}) collective-permute-start(f32[3,4,128]{2,1,0:T(4,128)S(1)} %get-tuple-element.51), channel_id=1, source_target_pairs={{8,0},{16,8},{24,16},{0,24},{9,1},{17,9},{25,17},{1,25},{10,2},{18... | collective-permute-start | bytes 18440 | tf_op jit(solution)/shard_map/ppermute | solution.py:594
  17.3 3.1 %shard_map.108 = (f32[16,4,3,56,128]{4,3,2,1,0:T(8,128)S(1)}, f32[3,64,128]{2,1,0:T(8,128)S(1)}, f32[3,64,128]{2,1,0:T(8,128)S(1)}, f32[4,3,40,128]{3,2,1,0:T(8,128)S(1)}) custom-call(f32[17,4,3,56,128]{4,3,2,1,0:T(8,128)S(1)} %get-tuple-element.38.v_ref, f32[16,4,3,56,128]{4,3,2,1,0:T(8,128)S(1)} %get-tuple-element.40.inner_ref, ...), custom_call_target="tpu_custom_call" | custom-call | flops 1 | bytes 1 | tf_op jit(solution)/shard_map/pallas_call | solution.py:19
  20.5 0.2 shard_map.109
  20.7 0.6 %collective-permute-start.6 = (f32[3,68,128]{2,1,0:T(8,128)S(1)}, f32[3,68,128]{2,1,0:T(8,128)S(1)}, u32[]{:S(2)}, u32[]{:S(2)}) collective-permute-start(f32[3,68,128]{2,1,0:T(8,128)S(1)} %get-tuple-element.58), channel_id=1, source_target_pairs={{0,8},{8,16},{16,24},{24,0},{1,9},{9,17},{17,25},{25,1},{2,10},{10... | collective-permute-start | bytes 313352 | tf_op jit(solution)/shard_map/ppermute | solution.py:594
  21.3 1.2 %collective-permute-start.7 = (f32[3,68,128]{2,1,0:T(8,128)S(1)}, f32[3,68,128]{2,1,0:T(8,128)S(1)}, u32[]{:S(2)}, u32[]{:S(2)}) collective-permute-start(f32[3,68,128]{2,1,0:T(8,128)S(1)} %get-tuple-element.59), channel_id=1, source_target_pairs={{8,0},{16,8},{24,16},{0,24},{9,1},{17,9},{25,17},{1,25},{10,2},{18... | collective-permute-start | bytes 313352 | tf_op jit(solution)/shard_map/ppermute | solution.py:594
  22.5 2.1 %collective-permute-done.5.above_ref = f32[4,40,384]{2,1,0:T(8,128)S(1)} collective-permute-done((f32[4,40,384]{2,1,0:T(8,128)S(1)}, f32[4,40,384]{2,1,0:T(8,128)S(1)}, u32[]{:S(2)}, u32[]{:S(2)}) %collective-permute-start.5) | collective-permute-done | bytes 245792 | tf_op jit(solution)/shard_map/ppermute | solution.py:599
  24.6 0.2 shard_map.110
  24.9 0.5 collective-permute-start.8
  25.3 1.3 %collective-permute-start.9 = (f32[3,4,128]{2,1,0:T(4,128)S(1)}, f32[3,4,128]{2,1,0:T(4,128)S(1)}, u32[]{:S(2)}, u32[]{:S(2)}) collective-permute-start(f32[3,4,128]{2,1,0:T(4,128)S(1)} %get-tuple-element.61), channel_id=1, source_target_pairs={{8,0},{16,8},{24,16},{0,24},{9,1},{17,9},{25,17},{1,25},{10,2},{18... | collective-permute-start | bytes 18440 | tf_op jit(solution)/shard_map/ppermute | solution.py:594
  26.7 0.1 broadcast_in_dim.5.weight_ref
  26.7 1.8 %shard_map.111 = (f32[4,18,40,384]{3,2,1,0:T(8,128)}, f32[40,384]{1,0:T(8,128)S(1)}) custom-call(f32[16,4,3,56,128]{4,3,2,1,0:T(8,128)S(1)} %get-tuple-element.48.v_ref, f32[4,3,56,128]{3,2,1,0:T(8,128)S(1)} %get-tuple-element.55.vs_ref, bf16[18,40,384]{2,1,0:T(8,128)(2,1)S(1)} %get-tuple-element.39.cx_ref, s32[18,40,384]{2,1,0:T(8,128)S(1)} %get-tuple-element.37.code_ref, ...), custom_call_target="tpu_custom_call" | custom-call | flops 1 | bytes 1 | tf_op jit(solution)/shard_map/pallas_call | solution.py:19
  28.6 2.6 %shard_map.112 = (f32[4,18,40,384]{3,2,1,0:T(8,128)}, f32[4,4,2,8,128]{4,3,2,1,0:T(8,128)}) custom-call(f32[16,4,3,56,128]{4,3,2,1,0:T(8,128)S(1)} %get-tuple-element.48.v_ref, f32[4,3,56,128]{3,2,1,0:T(8,128)S(1)} %get-tuple-element.55.vs_ref, f32[4,3,56,128]{3,2,1,0:T(8,128)S(1)} %get-tuple-element.57.vt_ref, ...), custom_call_target="tpu_custom_call", output_to_operand_aliasing={{0}: (13, {})} | custom-call | flops 1 | bytes 1 | tf_op jit(solution)/shard_map/pallas_call | solution.py:19
  31.3 6.0 %all-to-all-start = ((f32[32,8,128]{2,1,0:T(8,128)}), f32[32,8,128]{2,1,0:T(8,128)S(1)}, u32[]{:S(2)}, u32[]{:S(2)}) async-start(f32[32,8,128]{2,1,0:T(8,128)} %bitcast.2), calls=%async_computation | async-start | bytes 262144 | tf_op jit(solution)/shard_map/all_to_all | solution.py:577
  37.3 7.7 %all-to-all-done = f32[32,8,128]{2,1,0:T(8,128)S(1)} async-done(((f32[32,8,128]{2,1,0:T(8,128)}), f32[32,8,128]{2,1,0:T(8,128)S(1)}, u32[]{:S(2)}, u32[]{:S(2)}) %all-to-all-start) | async-done | bytes 131104 | tf_op jit(solution)/shard_map/all_to_all | solution.py:577
  45.0 1.1 %collective-permute-start.10 = (f32[4,8,128]{2,1,0:T(8,128)S(1)}, f32[4,8,128]{2,1,0:T(8,128)S(1)}, u32[]{:S(2)}, u32[]{:S(2)}) collective-permute-start(f32[4,8,128]{2,1,0:T(8,128)S(1)} %bitcast_reduce_fusion.refs_0_), channel_id=1, source_target_pairs={{0,2},{2,0},{4,6},{6,4},{1,3},{3,1},{5,7},{7,5},{8,10},{10,8},{12,... | collective-permute-start | bytes 49160 | tf_op jit(solution)/shard_map/ppermute | solution.py:570
  46.1 0.9 %collective-permute-start.11 = (f32[4,8,128]{2,1,0:T(8,128)S(1)}, f32[4,8,128]{2,1,0:T(8,128)S(1)}, u32[]{:S(2)}, u32[]{:S(2)}) collective-permute-start(f32[4,8,128]{2,1,0:T(8,128)S(1)} %bitcast_reduce_fusion.refs_0_), channel_id=1, source_target_pairs={{0,4},{2,6},{4,0},{6,2},{1,5},{3,7},{5,1},{7,3},{8,12},{10,14},{12... | collective-permute-start | bytes 49160 | tf_op jit(solution)/shard_map/ppermute | solution.py:570
  47.0 2.5 %collective-permute-start.12 = (f32[4,8,128]{2,1,0:T(8,128)S(1)}, f32[4,8,128]{2,1,0:T(8,128)S(1)}, u32[]{:S(2)}, u32[]{:S(2)}) collective-permute-start(f32[4,8,128]{2,1,0:T(8,128)S(1)} %bitcast_reduce_fusion.refs_0_), channel_id=1, source_target_pairs={{0,6},{2,4},{4,2},{6,0},{1,7},{3,5},{5,3},{7,1},{8,14},{10,12},{12... | collective-permute-start | bytes 49160 | tf_op jit(solution)/shard_map/ppermute | solution.py:570
  49.5 1.3 %collective-permute-done.11.refs_2_ = f32[4,8,128]{2,1,0:T(8,128)S(1)} collective-permute-done((f32[4,8,128]{2,1,0:T(8,128)S(1)}, f32[4,8,128]{2,1,0:T(8,128)S(1)}, u32[]{:S(2)}, u32[]{:S(2)}) %collective-permute-start.11) | collective-permute-done | bytes 16416 | tf_op jit(solution)/shard_map/ppermute | solution.py:570
  50.8 1.8 %collective-permute-done.12.refs_3_ = f32[4,8,128]{2,1,0:T(8,128)S(1)} collective-permute-done((f32[4,8,128]{2,1,0:T(8,128)S(1)}, f32[4,8,128]{2,1,0:T(8,128)S(1)}, u32[]{:S(2)}, u32[]{:S(2)}) %collective-permute-start.12) | collective-permute-done | bytes 16416 | tf_op jit(solution)/shard_map/ppermute | solution.py:570
  52.5 3.0 %shard_map.113 = f32[120,128]{1,0:T(8,128)} custom-call(s32[4,4,8,128]{3,2,1,0:T(8,128)S(1)} %copy_bitcast_fusion.1.cells_ref, f32[4,8,128]{2,1,0:T(8,128)S(1)} %bitcast_reduce_fusion.refs_0_, f32[4,8,128]{2,1,0:T(8,128)S(1)} %collective-permute-done.10.refs_1_, f32[4,8,128]{2,1,0:T(8,128)S(1)} %collective-permute-done.11.refs_2_, ...), custom_call_target="tpu_custom_call" | custom-call | flops 1 | bytes 1 | tf_op jit(solution)/shard_map/pallas_call | solution.py:19
  (21 shorter events, 0.1 us)
Async XLA Ops:
  0.6 3.5 %copy-start = (f32[4,18,40,384]{3,2,1,0:T(8,128)S(1)}, f32[4,18,40,384]{3,2,1,0:T(8,128)}, u32[]{:S(2)}) copy-start(f32[4,18,40,384]{3,2,1,0:T(8,128)} %f_ref.1) | copy-start | bytes 13271044
  2.7 11.0 %collective-permute-start.2 = (f32[4,40,384]{2,1,0:T(8,128)S(1)}, f32[4,40,384]{2,1,0:T(8,128)S(1)}, u32[]{:S(2)}, u32[]{:S(2)}) collective-permute-start(f32[4,40,384]{2,1,0:T(8,128)S(1)} %get-tuple-element.46), channel_id=1, source_target_pairs={{2,0},{4,2},{6,4},{3,1},{5,3},{7,5},{10,8},{12,10},{14,12},{11,9},... | collective-permute-start | bytes 737288 | tf_op jit(solution)/shard_map/ppermute | solution.py:599
  7.6 6.1 %copy-start.3 = (s32[4,2]{0,1:T(2,128)S(1)}, s32[4,2]{0,1:T(2,128)}, u32[]{:S(2)}) copy-start(s32[4,2]{0,1:T(2,128)} %param.14) | copy-start | bytes 100
  7.6 5.6 %collective-permute-start = (f32[3,68,128]{2,1,0:T(8,128)S(1)}, f32[3,68,128]{2,1,0:T(8,128)S(1)}, u32[]{:S(2)}, u32[]{:S(2)}) collective-permute-start(f32[3,68,128]{2,1,0:T(8,128)S(1)} %get-tuple-element.42), channel_id=1, source_target_pairs={{0,8},{8,16},{16,24},{24,0},{1,9},{9,17},{17,25},{25,1},{2,10},{10... | collective-permute-start | bytes 313352 | tf_op jit(solution)/shard_map/ppermute | solution.py:594
  8.1 5.4 %collective-permute-start.1 = (f32[3,68,128]{2,1,0:T(8,128)S(1)}, f32[3,68,128]{2,1,0:T(8,128)S(1)}, u32[]{:S(2)}, u32[]{:S(2)}) collective-permute-start(f32[3,68,128]{2,1,0:T(8,128)S(1)} %get-tuple-element.43), channel_id=1, source_target_pairs={{8,0},{16,8},{24,16},{0,24},{9,1},{17,9},{25,17},{1,25},{10,2},{18... | collective-permute-start | bytes 313352 | tf_op jit(solution)/shard_map/ppermute | solution.py:594
  14.0 10.7 %collective-permute-start.5 = (f32[4,40,384]{2,1,0:T(8,128)S(1)}, f32[4,40,384]{2,1,0:T(8,128)S(1)}, u32[]{:S(2)}, u32[]{:S(2)}) collective-permute-start(f32[4,40,384]{2,1,0:T(8,128)S(1)} %get-tuple-element.47.lowest_ref), channel_id=1, source_target_pairs={{2,0},{4,2},{6,4},{3,1},{5,3},{7,5},{10,8},{12,10},{14,12},{11,9},... | collective-permute-start | bytes 737288 | tf_op jit(solution)/shard_map/ppermute | solution.py:599
  15.3 5.2 %collective-permute-start.3 = (f32[3,4,128]{2,1,0:T(4,128)S(1)}, f32[3,4,128]{2,1,0:T(4,128)S(1)}, u32[]{:S(2)}, u32[]{:S(2)}) collective-permute-start(f32[3,4,128]{2,1,0:T(4,128)S(1)} %get-tuple-element.50), channel_id=1, source_target_pairs={{0,8},{8,16},{16,24},{24,0},{1,9},{9,17},{17,25},{25,1},{2,10},{10... | collective-permute-start | bytes 18440 | tf_op jit(solution)/shard_map/ppermute | solution.py:594
  16.5 3.9 %collective-permute-start.4 = (f32[3,4,128]{2,1,0:T(4,128)S(1)}, f32[3,4,128]{2,1,0:T(4,128)S(1)}, u32[]{:S(2)}, u32[]{:S(2)}) collective-permute-start(f32[3,4,128]{2,1,0:T(4,128)S(1)} %get-tuple-element.51), channel_id=1, source_target_pairs={{8,0},{16,8},{24,16},{0,24},{9,1},{17,9},{25,17},{1,25},{10,2},{18... | collective-permute-start | bytes 18440 | tf_op jit(solution)/shard_map/ppermute | solution.py:594
  20.4 6.2 %copy-start.4 = (f32[18]{0:T(128)S(1)}, f32[18]{0:T(128)}, u32[]{:S(2)}) copy-start(f32[18]{0:T(128)} %param.15) | copy-start | bytes 220
  20.4 6.3 %copy-start.1 = (f32[4,40,384]{2,1,0:T(8,128)S(1)}, f32[4,40,384]{2,1,0:T(8,128)}, u32[]{:S(2)}) copy-start(f32[4,40,384]{2,1,0:T(8,128)} %share_ref.3) | copy-start | bytes 737284
  20.7 7.9 %collective-permute-start.6 = (f32[3,68,128]{2,1,0:T(8,128)S(1)}, f32[3,68,128]{2,1,0:T(8,128)S(1)}, u32[]{:S(2)}, u32[]{:S(2)}) collective-permute-start(f32[3,68,128]{2,1,0:T(8,128)S(1)} %get-tuple-element.58), channel_id=1, source_target_pairs={{0,8},{8,16},{16,24},{24,0},{1,9},{9,17},{17,25},{25,1},{2,10},{10... | collective-permute-start | bytes 313352 | tf_op jit(solution)/shard_map/ppermute | solution.py:594
  21.3 7.3 %collective-permute-start.7 = (f32[3,68,128]{2,1,0:T(8,128)S(1)}, f32[3,68,128]{2,1,0:T(8,128)S(1)}, u32[]{:S(2)}, u32[]{:S(2)}) collective-permute-start(f32[3,68,128]{2,1,0:T(8,128)S(1)} %get-tuple-element.59), channel_id=1, source_target_pairs={{8,0},{16,8},{24,16},{0,24},{9,1},{17,9},{25,17},{1,25},{10,2},{18... | collective-permute-start | bytes 313352 | tf_op jit(solution)/shard_map/ppermute | solution.py:594
  24.9 3.7 %collective-permute-start.8 = (f32[3,4,128]{2,1,0:T(4,128)S(1)}, f32[3,4,128]{2,1,0:T(4,128)S(1)}, u32[]{:S(2)}, u32[]{:S(2)}) collective-permute-start(f32[3,4,128]{2,1,0:T(4,128)S(1)} %get-tuple-element.60), channel_id=1, source_target_pairs={{0,8},{8,16},{16,24},{24,0},{1,9},{9,17},{17,25},{25,1},{2,10},{10... | collective-permute-start | bytes 18440 | tf_op jit(solution)/shard_map/ppermute | solution.py:594
  25.3 3.3 %collective-permute-start.9 = (f32[3,4,128]{2,1,0:T(4,128)S(1)}, f32[3,4,128]{2,1,0:T(4,128)S(1)}, u32[]{:S(2)}, u32[]{:S(2)}) collective-permute-start(f32[3,4,128]{2,1,0:T(4,128)S(1)} %get-tuple-element.61), channel_id=1, source_target_pairs={{8,0},{16,8},{24,16},{0,24},{9,1},{17,9},{25,17},{1,25},{10,2},{18... | collective-permute-start | bytes 18440 | tf_op jit(solution)/shard_map/ppermute | solution.py:594
  28.6 8.7 %copy-start.2 = (s32[4,3840]{1,0:T(4,128)S(1)}, s32[4,3840]{1,0:T(4,128)}, u32[]{:S(2)}) copy-start(s32[4,3840]{1,0:T(4,128)} %param.17) | copy-start | bytes 184324
  31.3 13.7 %all-to-all-start = ((f32[32,8,128]{2,1,0:T(8,128)}), f32[32,8,128]{2,1,0:T(8,128)S(1)}, u32[]{:S(2)}, u32[]{:S(2)}) async-start(f32[32,8,128]{2,1,0:T(8,128)} %bitcast.2), calls=%async_computation | async-start | bytes 262144 | tf_op jit(solution)/shard_map/all_to_all | solution.py:577
  45.0 4.5 %collective-permute-start.10 = (f32[4,8,128]{2,1,0:T(8,128)S(1)}, f32[4,8,128]{2,1,0:T(8,128)S(1)}, u32[]{:S(2)}, u32[]{:S(2)}) collective-permute-start(f32[4,8,128]{2,1,0:T(8,128)S(1)} %bitcast_reduce_fusion.refs_0_), channel_id=1, source_target_pairs={{0,2},{2,0},{4,6},{6,4},{1,3},{3,1},{5,7},{7,5},{8,10},{10,8},{12,... | collective-permute-start | bytes 49160 | tf_op jit(solution)/shard_map/ppermute | solution.py:570
  46.1 4.6 %collective-permute-start.11 = (f32[4,8,128]{2,1,0:T(8,128)S(1)}, f32[4,8,128]{2,1,0:T(8,128)S(1)}, u32[]{:S(2)}, u32[]{:S(2)}) collective-permute-start(f32[4,8,128]{2,1,0:T(8,128)S(1)} %bitcast_reduce_fusion.refs_0_), channel_id=1, source_target_pairs={{0,4},{2,6},{4,0},{6,2},{1,5},{3,7},{5,1},{7,3},{8,12},{10,14},{12... | collective-permute-start | bytes 49160 | tf_op jit(solution)/shard_map/ppermute | solution.py:570
  47.0 5.5 %collective-permute-start.12 = (f32[4,8,128]{2,1,0:T(8,128)S(1)}, f32[4,8,128]{2,1,0:T(8,128)S(1)}, u32[]{:S(2)}, u32[]{:S(2)}) collective-permute-start(f32[4,8,128]{2,1,0:T(8,128)S(1)} %bitcast_reduce_fusion.refs_0_), channel_id=1, source_target_pairs={{0,6},{2,4},{4,2},{6,0},{1,7},{3,5},{5,3},{7,1},{8,14},{10,12},{12... | collective-permute-start | bytes 49160 | tf_op jit(solution)/shard_map/ppermute | solution.py:570

commit v9 on v8

--- a/solution.py
+++ b/solution.py
@@ -16,13 +16,18 @@
 
 
 def call(kernel, out_shape, in_specs, out_specs, operands, scratch=(), mib=16, aliases={}):
+    if isinstance(out_shape, tuple):
+        out_specs = tuple(
+            tuple(spec for _ in part) if isinstance(part, tuple) else spec
+            for spec, part in zip(out_specs, out_shape)
+        )
     return pl.pallas_call(
         kernel,
         out_shape=out_shape,
-        in_specs=in_specs,
+        in_specs=[jax.tree.map(lambda _: spec, part) for spec, part in zip(in_specs, operands)],
         out_specs=out_specs,
         scratch_shapes=list(scratch),
-        input_output_aliases=aliases,
+        input_output_aliases={len(jax.tree.leaves(operands[:i])): o for i, o in aliases.items()},
         cost_estimate=pl.CostEstimate(flops=1, transcendentals=0, bytes_accessed=1),
         compiler_params=pltpu.CompilerParams(vmem_limit_bytes=mib * MIB),
     )(*operands)
@@ -38,6 +43,11 @@
 
 def f32(*shape):
     return jax.ShapeDtypeStruct(shape, jnp.float32)
+
+
+def half_of(halves, s):
+    count = halves[0].shape[0]
+    return halves[s // count], s % count
 
 
 def cut(value, xt, j):
@@ -131,7 +141,8 @@
         pltpu.make_async_copy(source, target, sems.at[i])
         for i, (source, target) in enumerate(
             (
-                (f_hbm.at[:, 0], out_ref),
+                (f_hbm.at[: f_hbm.shape[0] // 2, 0], out_ref[0]),
+                (f_hbm.at[f_hbm.shape[0] // 2 :, 0], out_ref[1]),
                 (mf_hbm, mf_ref),
                 (cy_hbm, cy_ref),
                 (code_hbm, code_ref),
@@ -184,7 +195,7 @@
     lrow_ref, rrow_ref,
 ):
     _, sectors, tiles, _, _ = v_ref.shape
-    columns = out_ref.shape[1]
+    columns = here_ref.shape[1]
     strips = columns // ROWS
     flip_left, flip_right = flags(seam_ref)
     turned(left_ref.at[:, :ROWS], flip_left, lrow_ref)
@@ -194,7 +205,8 @@
     for s in range(sectors):
         for j in range(tiles):
             lanes = slice(j * LANES, (j + 1) * LANES)
-            out_ref[s, ROWS : columns - ROWS, lanes] = inner_ref[s, j, ROWS : columns - ROWS]
+            half, at = half_of(out_ref, s)
+            half[at, ROWS : columns - ROWS, lanes] = inner_ref[s, j, ROWS : columns - ROWS]
     for xt in (0, strips - 1):
         for j in range(tiles):
             factors = first_weights(cx, codes, 2, xt, j)
@@ -205,7 +217,8 @@
                     lambda s, j: lrow_ref[j, s : s + 1, :],
                     lambda s, j: rrow_ref[j, s : s + 1, :],
                 )
-                out_ref[s, xt * ROWS : (xt + 1) * ROWS, j * LANES : (j + 1) * LANES] = value
+                half, at = half_of(out_ref, s)
+                half[at, xt * ROWS : (xt + 1) * ROWS, j * LANES : (j + 1) * LANES] = value
 
     level = mf_ref.shape[0] - 1
     at_top = lax.axis_index("lev") == lax.axis_size("lev") - 1
@@ -220,7 +233,8 @@
             for j in range(tiles):
                 lanes = slice(j * LANES, (j + 1) * LANES)
                 here = here_ref[s, rows, lanes]
-                upper = jnp.where(at_top, here, above_ref[s, rows, lanes])
+                half, at = half_of(above_ref, s)
+                upper = jnp.where(at_top, here, half[at, rows, lanes])
                 parts.append(here + cut(mf, xt, j) * (upper - here))
             for j, value in enumerate(second_sweep(parts, factors)):
                 store_padded(top_ref, (), s, j, xt, value)
@@ -304,7 +318,8 @@
         for j in range(tiles):
             for xt in ends:
                 rows = slice(xt * ROWS, (xt + 1) * ROWS)
-                a_ref[0, s, j, rows] = lowest_ref[s, rows, j * LANES : (j + 1) * LANES]
+                half, at = half_of(lowest_ref, s)
+                a_ref[0, s, j, rows] = half[at, rows, j * LANES : (j + 1) * LANES]
     middle_levels(
         ends, v_ref, lrow_ref, rrow_ref, cx_ref, mf_ref, cy_ref, code_ref, out_ref, a_ref,
         (first_ref, last_ref),
@@ -375,7 +390,8 @@
             parts = []
             for j in range(tiles):
                 here = here_ref[s, j, rows, :]
-                upper = above_ref[s, rows, j * LANES : (j + 1) * LANES]
+                half, at = half_of(above_ref, s)
+                upper = half[at, rows, j * LANES : (j + 1) * LANES]
                 upper = jnp.where(at_top, here, upper)
                 parts.append(here + cut(mf, xt, j) * (upper - here))
             for j, value in enumerate(second_sweep(parts, across)):
@@ -594,9 +610,9 @@
     return lax.ppermute(last, "tile", up), lax.ppermute(first, "tile", down)
 
 
-def from_above(value):
+def from_above(halves):
     count = lax.axis_size("lev")
-    return lax.ppermute(value, "lev", [(i + 1, i) for i in range(count - 1)])
+    return tuple(lax.ppermute(half, "lev", [(i + 1, i) for i in range(count - 1)]) for half in halves)
 
 
 def shards(
@@ -608,6 +624,7 @@
     field = kept(below, sectors, tiles, padded, LANES)
     field_top = kept(sectors, tiles, padded, LANES)
     plane = kept(sectors, columns, width)
+    halves = (kept(sectors // 2, columns, width),) * 2
     rim = kept(tiles, below * sectors, LANES)
     rim_top = kept(tiles, sectors, LANES)
     rim_next = kept(tiles, (below - 1) * sectors, LANES)
@@ -619,11 +636,11 @@
     narrow = pltpu.VMEM((levels, columns, width), jnp.bfloat16)
     lowest, mass_flux, courant_y, limiter_code, courant_x = call(
         start_kernel,
-        (plane, narrow, narrow, pltpu.VMEM((levels, columns, width), jnp.int32), narrow),
+        (halves, narrow, narrow, pltpu.VMEM((levels, columns, width), jnp.int32), narrow),
         [HBM] * 5,
         [VM] * 5,
         in_hbm(forcing, mass_flux, courant_y, limiter_code, courant_x),
-        [pltpu.SemaphoreType.DMA((5,))],
+        [pltpu.SemaphoreType.DMA((6,))],
     )
     above = from_above(lowest)
     v, first, last, top = call(
@@ -647,7 +664,7 @@
     )
     lowest, vt, first_top, last_top = call(
         ends_kernel,
-        (plane, field_top, rim_top, rim_top),
+        (halves, field_top, rim_top, rim_top),
         [VM] * 11,
         [VM] * 4,
         (

time: 55.7 us -> 60.1 us (1.079)
  starting transfers between devices: 21.3 us -> 26.4 us
  waiting for transfers between devices: 13.4 us -> 12.5 us
    ppermute x2 -> x4, starting transfers between devices: 2.72 us -> 5.3 us  [from_above(): lax.ppermute(half, 'lev', [(i + 1, i) for i in range(count - 1)])]
    all_to_all x1, starting transfers between devices: 5.98 us -> 8.34 us  [remapped(): lax.all_to_all(sent, ('tile', 'lev', 'sec'), split_axis=0, concat_axis=0,...]
    ppermute x2 -> x4, waiting for transfers between devices: 2.34 us -> 1.46 us  [from_above(): lax.ppermute(half, 'lev', [(i + 1, i) for i in range(count - 1)])]
  transfers between devices with their start and end apart: 14 -> 16, of which waited for: 6 -> 5; matrix products, arithmetic and copies ran while one was open for 0% -> 0% of each run, Pallas kernels for 22% -> 20%
where the time goes in v9:
time: 60.1 us; the launch traced here: 59.8 us
  starting transfers between devices  26.4 us (44%)
  Pallas kernels  19.9 us (33%)
  waiting for transfers between devices  12.5 us (21%)
  between operations  0.87 us (1%)
    pallas_call x10, Pallas kernels, call(): pl.pallas_call(kernel, out_shape=out_shape, in_specs=[jax.tree.map(lambda...  19.9 us
    all_to_all x1, starting transfers between devices, remapped(): lax.all_to_all(sent, ('tile', 'lev', 'sec'), split_axis=0, concat_axis=0,...  8.34 us
    ppermute x8, starting transfers between devices, around(): return (lax.ppermute(last, 'tile', up), lax.ppermute(first, 'tile', down))  8.32 us
    all_to_all x1, waiting for transfers between devices, remapped(): lax.all_to_all(sent, ('tile', 'lev', 'sec'), split_axis=0, concat_axis=0,...  7.71 us
    ppermute x4, starting transfers between devices, from_above(): lax.ppermute(half, 'lev', [(i + 1, i) for i in range(count - 1)])  5.3 us
    ppermute x3, starting transfers between devices, exchanged(): return lax.ppermute(value, axis, [(i, i ^ apart) for i in range(count)])  4.45 us
    ppermute x3, waiting for transfers between devices, exchanged(): return lax.ppermute(value, axis, [(i, i ^ apart) for i in range(count)])  3.05 us
    ppermute x4, waiting for transfers between devices, from_above(): lax.ppermute(half, 'lev', [(i + 1, i) for i in range(count - 1)])  1.46 us
  transfers between devices with their start and end apart: 16, of which 5 were waited for; matrix products, arithmetic and copies ran while one was open for 0% of the time, Pallas kernels for 20%

profile of v9, /device:TPU:0, one launch (start us, length us, event | category | flops | bytes accessed | tf_op | source)
XLA Modules:
  0.0 59.8 jit_solution(16328272047041028156)
XLA Ops:
  0.6 2.0 %shard_map.104 = (f32[2,40,384]{2,1,0:T(8,128)S(1)}, f32[2,40,384]{2,1,0:T(8,128)S(1)}, bf16[18,40,384]{2,1,0:T(8,128)(2,1)S(1)}, bf16[18,40,384]{2,1,0:T(8,128)...) custom-call(f32[4,18,40,384]{3,2,1,0:T(8,128)} %f_ref.1, bf16[18,40,384]{2,1,0:T(8,128)(2,1)} %mf_hbm.1, ...), custom_call_target="tpu_custom_call" | custom-call | flops 1 | bytes 1 | tf_op jit(solution)/shard_map/pallas_call | solution.py:24
  2.7 1.4 %collective-permute-start.2 = (f32[2,40,384]{2,1,0:T(8,128)S(1)}, f32[2,40,384]{2,1,0:T(8,128)S(1)}, u32[]{:S(2)}, u32[]{:S(2)}) collective-permute-start(f32[2,40,384]{2,1,0:T(8,128)S(1)} %get-tuple-element.48), channel_id=1, source_target_pairs={{2,0},{4,2},{6,4},{3,1},{5,3},{7,5},{10,8},{12,10},{14,12},{11,9},... | collective-permute-start | bytes 368648 | tf_op jit(solution)/shard_map/ppermute | solution.py:615
  4.1 1.3 %collective-permute-start.3 = (f32[2,40,384]{2,1,0:T(8,128)S(1)}, f32[2,40,384]{2,1,0:T(8,128)S(1)}, u32[]{:S(2)}, u32[]{:S(2)}) collective-permute-start(f32[2,40,384]{2,1,0:T(8,128)S(1)} %get-tuple-element.49), channel_id=1, source_target_pairs={{2,0},{4,2},{6,4},{3,1},{5,3},{7,5},{10,8},{12,10},{14,12},{11,9},... | collective-permute-start | bytes 368648 | tf_op jit(solution)/shard_map/ppermute | solution.py:615
  5.4 3.5 %shard_map.105 = (f32[17,4,3,56,128]{4,3,2,1,0:T(8,128)S(1)}, f32[3,68,128]{2,1,0:T(8,128)S(1)}, f32[3,68,128]{2,1,0:T(8,128)S(1)}, f32[4,40,384]{2,1,0:T(8,128)S(1)}) custom-call(f32[4,18,40,384]{3,2,1,0:T(8,128)S(1)} %copy-done, bf16[18,40,384]{2,1,0:T(8,128)(2,1)S(1)} %get-tuple-element.37.mf_ref, bf16[18,40,384]{2,1,0:T(8,128)(2,1)S(1)} %get-tuple-element.38.cy_ref, ...), custom_call_target="tpu_custom_call" | custom-call | flops 1 | bytes 1 | tf_op jit(solution)/shard_map/pallas_call | solution.py:24
  8.9 0.5 collective-permute-start
  9.4 2.0 %collective-permute-start.1 = (f32[3,68,128]{2,1,0:T(8,128)S(1)}, f32[3,68,128]{2,1,0:T(8,128)S(1)}, u32[]{:S(2)}, u32[]{:S(2)}) collective-permute-start(f32[3,68,128]{2,1,0:T(8,128)S(1)} %get-tuple-element.45), channel_id=1, source_target_pairs={{8,0},{16,8},{24,16},{0,24},{9,1},{17,9},{25,17},{1,25},{10,2},{18... | collective-permute-start | bytes 313352 | tf_op jit(solution)/shard_map/ppermute | solution.py:610
  11.4 3.1 %shard_map.106 = (f32[16,4,3,56,128]{4,3,2,1,0:T(8,128)S(1)}, f32[4,3,40,128]{3,2,1,0:T(8,128)S(1)}, f32[4,3,40,128]{3,2,1,0:T(8,128)S(1)}) custom-call(f32[17,4,3,56,128]{4,3,2,1,0:T(8,128)S(1)} %get-tuple-element.40.v_ref, bf16[18,40,384]{2,1,0:T(8,128)(2,1)S(1)} %get-tuple-element.41.cx_ref, bf16[18,40,384]{2,1,0:T(8,128)(2,1)S(1)} %get-tuple-element.37.mf_ref, ...), custom_call_target="tpu_custom_call" | custom-call | flops 1 | bytes 1 | tf_op jit(solution)/shard_map/pallas_call | solution.py:24
  14.5 0.2 collective-permute-done.1.right_ref
  14.8 0.1 broadcast_in_dim.4.seam_ref
  14.9 0.2 shard_map.107
  15.1 1.3 %collective-permute-start.6 = (f32[2,40,384]{2,1,0:T(8,128)S(1)}, f32[2,40,384]{2,1,0:T(8,128)S(1)}, u32[]{:S(2)}, u32[]{:S(2)}) collective-permute-start(f32[2,40,384]{2,1,0:T(8,128)S(1)} %get-tuple-element.50.lowest_ref_0_), channel_id=1, source_target_pairs={{2,0},{4,2},{6,4},{3,1},{5,3},{7,5},{10,8},{12,10},{14,12},{11,9},... | collective-permute-start | bytes 368648 | tf_op jit(solution)/shard_map/ppermute | solution.py:615
  16.4 1.3 %collective-permute-start.7 = (f32[2,40,384]{2,1,0:T(8,128)S(1)}, f32[2,40,384]{2,1,0:T(8,128)S(1)}, u32[]{:S(2)}, u32[]{:S(2)}) collective-permute-start(f32[2,40,384]{2,1,0:T(8,128)S(1)} %get-tuple-element.51.lowest_ref_1_), channel_id=1, source_target_pairs={{2,0},{4,2},{6,4},{3,1},{5,3},{7,5},{10,8},{12,10},{14,12},{11,9},... | collective-permute-start | bytes 368648 | tf_op jit(solution)/shard_map/ppermute | solution.py:615
  17.7 1.5 %collective-permute-start.4 = (f32[3,4,128]{2,1,0:T(4,128)S(1)}, f32[3,4,128]{2,1,0:T(4,128)S(1)}, u32[]{:S(2)}, u32[]{:S(2)}) collective-permute-start(f32[3,4,128]{2,1,0:T(4,128)S(1)} %get-tuple-element.54), channel_id=1, source_target_pairs={{0,8},{8,16},{16,24},{24,0},{1,9},{9,17},{17,25},{25,1},{2,10},{10... | collective-permute-start | bytes 18440 | tf_op jit(solution)/shard_map/ppermute | solution.py:610
  19.2 0.8 %collective-permute-start.5 = (f32[3,4,128]{2,1,0:T(4,128)S(1)}, f32[3,4,128]{2,1,0:T(4,128)S(1)}, u32[]{:S(2)}, u32[]{:S(2)}) collective-permute-start(f32[3,4,128]{2,1,0:T(4,128)S(1)} %get-tuple-element.55), channel_id=1, source_target_pairs={{8,0},{16,8},{24,16},{0,24},{9,1},{17,9},{25,17},{1,25},{10,2},{18... | collective-permute-start | bytes 18440 | tf_op jit(solution)/shard_map/ppermute | solution.py:610
  19.9 3.1 %shard_map.108 = (f32[16,4,3,56,128]{4,3,2,1,0:T(8,128)S(1)}, f32[3,64,128]{2,1,0:T(8,128)S(1)}, f32[3,64,128]{2,1,0:T(8,128)S(1)}, f32[4,3,40,128]{3,2,1,0:T(8,128)S(1)}) custom-call(f32[17,4,3,56,128]{4,3,2,1,0:T(8,128)S(1)} %get-tuple-element.40.v_ref, f32[16,4,3,56,128]{4,3,2,1,0:T(8,128)S(1)} %get-tuple-element.42.inner_ref, ...), custom_call_target="tpu_custom_call" | custom-call | flops 1 | bytes 1 | tf_op jit(solution)/shard_map/pallas_call | solution.py:24
  23.1 0.2 shard_map.109
  23.3 0.6 collective-permute-start.8
  23.9 1.2 %collective-permute-start.9 = (f32[3,68,128]{2,1,0:T(8,128)S(1)}, f32[3,68,128]{2,1,0:T(8,128)S(1)}, u32[]{:S(2)}, u32[]{:S(2)}) collective-permute-start(f32[3,68,128]{2,1,0:T(8,128)S(1)} %get-tuple-element.63), channel_id=1, source_target_pairs={{8,0},{16,8},{24,16},{0,24},{9,1},{17,9},{25,17},{1,25},{10,2},{18... | collective-permute-start | bytes 313352 | tf_op jit(solution)/shard_map/ppermute | solution.py:610
  25.1 1.5 %collective-permute-done.7.above_ref_1_ = f32[2,40,384]{2,1,0:T(8,128)S(1)} collective-permute-done((f32[2,40,384]{2,1,0:T(8,128)S(1)}, f32[2,40,384]{2,1,0:T(8,128)S(1)}, u32[]{:S(2)}, u32[]{:S(2)}) %collective-permute-start.7) | collective-permute-done | bytes 122912 | tf_op jit(solution)/shard_map/ppermute | solution.py:615
  26.6 0.2 shard_map.110
  26.8 0.7 %collective-permute-start.10 = (f32[3,4,128]{2,1,0:T(4,128)S(1)}, f32[3,4,128]{2,1,0:T(4,128)S(1)}, u32[]{:S(2)}, u32[]{:S(2)}) collective-permute-start(f32[3,4,128]{2,1,0:T(4,128)S(1)} %get-tuple-element.64), channel_id=1, source_target_pairs={{0,8},{8,16},{16,24},{24,0},{1,9},{9,17},{17,25},{25,1},{2,10},{10... | collective-permute-start | bytes 18440 | tf_op jit(solution)/shard_map/ppermute | solution.py:610
  27.6 1.1 %collective-permute-start.11 = (f32[3,4,128]{2,1,0:T(4,128)S(1)}, f32[3,4,128]{2,1,0:T(4,128)S(1)}, u32[]{:S(2)}, u32[]{:S(2)}) collective-permute-start(f32[3,4,128]{2,1,0:T(4,128)S(1)} %get-tuple-element.65), channel_id=1, source_target_pairs={{8,0},{16,8},{24,16},{0,24},{9,1},{17,9},{25,17},{1,25},{10,2},{18... | collective-permute-start | bytes 18440 | tf_op jit(solution)/shard_map/ppermute | solution.py:610
  28.7 1.8 %shard_map.111 = (f32[4,18,40,384]{3,2,1,0:T(8,128)}, f32[40,384]{1,0:T(8,128)S(1)}) custom-call(f32[16,4,3,56,128]{4,3,2,1,0:T(8,128)S(1)} %get-tuple-element.52.v_ref, f32[4,3,56,128]{3,2,1,0:T(8,128)S(1)} %get-tuple-element.59.vs_ref, bf16[18,40,384]{2,1,0:T(8,128)(2,1)S(1)} %get-tuple-element.41.cx_ref, s32[18,40,384]{2,1,0:T(8,128)S(1)} %get-tuple-element.39.code_ref, ...), custom_call_target="tpu_custom_call" | custom-call | flops 1 | bytes 1 | tf_op jit(solution)/shard_map/pallas_call | solution.py:24
  30.6 2.7 %shard_map.112 = (f32[4,18,40,384]{3,2,1,0:T(8,128)}, f32[4,4,2,8,128]{4,3,2,1,0:T(8,128)}) custom-call(f32[16,4,3,56,128]{4,3,2,1,0:T(8,128)S(1)} %get-tuple-element.52.v_ref, f32[4,3,56,128]{3,2,1,0:T(8,128)S(1)} %get-tuple-element.59.vs_ref, f32[4,3,56,128]{3,2,1,0:T(8,128)S(1)} %get-tuple-element.61.vt_ref, ...), custom_call_target="tpu_custom_call", output_to_operand_aliasing={{0}: (13, {})} | custom-call | flops 1 | bytes 1 | tf_op jit(solution)/shard_map/pallas_call | solution.py:24
  33.3 8.3 %all-to-all-start = ((f32[32,8,128]{2,1,0:T(8,128)}), f32[32,8,128]{2,1,0:T(8,128)S(1)}, u32[]{:S(2)}, u32[]{:S(2)}) async-start(f32[32,8,128]{2,1,0:T(8,128)} %bitcast.2), calls=%async_computation | async-start | bytes 262144 | tf_op jit(solution)/shard_map/all_to_all | solution.py:593
  41.6 7.7 %all-to-all-done = f32[32,8,128]{2,1,0:T(8,128)S(1)} async-done(((f32[32,8,128]{2,1,0:T(8,128)}), f32[32,8,128]{2,1,0:T(8,128)S(1)}, u32[]{:S(2)}, u32[]{:S(2)}) %all-to-all-start) | async-done | bytes 131104 | tf_op jit(solution)/shard_map/all_to_all | solution.py:593
  49.4 1.1 %collective-permute-start.12 = (f32[4,8,128]{2,1,0:T(8,128)S(1)}, f32[4,8,128]{2,1,0:T(8,128)S(1)}, u32[]{:S(2)}, u32[]{:S(2)}) collective-permute-start(f32[4,8,128]{2,1,0:T(8,128)S(1)} %bitcast_reduce_fusion.refs_0_), channel_id=1, source_target_pairs={{0,2},{2,0},{4,6},{6,4},{1,3},{3,1},{5,7},{7,5},{8,10},{10,8},{12,... | collective-permute-start | bytes 49160 | tf_op jit(solution)/shard_map/ppermute | solution.py:586
  50.4 0.9 %collective-permute-start.13 = (f32[4,8,128]{2,1,0:T(8,128)S(1)}, f32[4,8,128]{2,1,0:T(8,128)S(1)}, u32[]{:S(2)}, u32[]{:S(2)}) collective-permute-start(f32[4,8,128]{2,1,0:T(8,128)S(1)} %bitcast_reduce_fusion.refs_0_), channel_id=1, source_target_pairs={{0,4},{2,6},{4,0},{6,2},{1,5},{3,7},{5,1},{7,3},{8,12},{10,14},{12... | collective-permute-start | bytes 49160 | tf_op jit(solution)/shard_map/ppermute | solution.py:586
  51.3 2.5 %collective-permute-start.14 = (f32[4,8,128]{2,1,0:T(8,128)S(1)}, f32[4,8,128]{2,1,0:T(8,128)S(1)}, u32[]{:S(2)}, u32[]{:S(2)}) collective-permute-start(f32[4,8,128]{2,1,0:T(8,128)S(1)} %bitcast_reduce_fusion.refs_0_), channel_id=1, source_target_pairs={{0,6},{2,4},{4,2},{6,0},{1,7},{3,5},{5,3},{7,1},{8,14},{10,12},{12... | collective-permute-start | bytes 49160 | tf_op jit(solution)/shard_map/ppermute | solution.py:586
  53.8 1.3 %collective-permute-done.13.refs_2_ = f32[4,8,128]{2,1,0:T(8,128)S(1)} collective-permute-done((f32[4,8,128]{2,1,0:T(8,128)S(1)}, f32[4,8,128]{2,1,0:T(8,128)S(1)}, u32[]{:S(2)}, u32[]{:S(2)}) %collective-permute-start.13) | collective-permute-done | bytes 16416 | tf_op jit(solution)/shard_map/ppermute | solution.py:586
  55.1 1.8 %collective-permute-done.14.refs_3_ = f32[4,8,128]{2,1,0:T(8,128)S(1)} collective-permute-done((f32[4,8,128]{2,1,0:T(8,128)S(1)}, f32[4,8,128]{2,1,0:T(8,128)S(1)}, u32[]{:S(2)}, u32[]{:S(2)}) %collective-permute-start.14) | collective-permute-done | bytes 16416 | tf_op jit(solution)/shard_map/ppermute | solution.py:586
  56.9 3.0 %shard_map.113 = f32[120,128]{1,0:T(8,128)} custom-call(s32[4,4,8,128]{3,2,1,0:T(8,128)S(1)} %copy_bitcast_fusion.1.cells_ref, f32[4,8,128]{2,1,0:T(8,128)S(1)} %bitcast_reduce_fusion.refs_0_, f32[4,8,128]{2,1,0:T(8,128)S(1)} %collective-permute-done.12.refs_1_, f32[4,8,128]{2,1,0:T(8,128)S(1)} %collective-permute-done.13.refs_2_, ...), custom_call_target="tpu_custom_call" | custom-call | flops 1 | bytes 1 | tf_op jit(solution)/shard_map/pallas_call | solution.py:24
  (25 shorter events, 0.1 us)
Async XLA Ops:
  0.6 4.8 %copy-start = (f32[4,18,40,384]{3,2,1,0:T(8,128)S(1)}, f32[4,18,40,384]{3,2,1,0:T(8,128)}, u32[]{:S(2)}) copy-start(f32[4,18,40,384]{3,2,1,0:T(8,128)} %f_ref.1) | copy-start | bytes 13271044
  2.7 12.1 %collective-permute-start.2 = (f32[2,40,384]{2,1,0:T(8,128)S(1)}, f32[2,40,384]{2,1,0:T(8,128)S(1)}, u32[]{:S(2)}, u32[]{:S(2)}) collective-permute-start(f32[2,40,384]{2,1,0:T(8,128)S(1)} %get-tuple-element.48), channel_id=1, source_target_pairs={{2,0},{4,2},{6,4},{3,1},{5,3},{7,5},{10,8},{12,10},{14,12},{11,9},... | collective-permute-start | bytes 368648 | tf_op jit(solution)/shard_map/ppermute | solution.py:615
  4.1 10.7 %collective-permute-start.3 = (f32[2,40,384]{2,1,0:T(8,128)S(1)}, f32[2,40,384]{2,1,0:T(8,128)S(1)}, u32[]{:S(2)}, u32[]{:S(2)}) collective-permute-start(f32[2,40,384]{2,1,0:T(8,128)S(1)} %get-tuple-element.49), channel_id=1, source_target_pairs={{2,0},{4,2},{6,4},{3,1},{5,3},{7,5},{10,8},{12,10},{14,12},{11,9},... | collective-permute-start | bytes 368648 | tf_op jit(solution)/shard_map/ppermute | solution.py:615
  8.9 5.9 %copy-start.3 = (s32[4,2]{0,1:T(2,128)S(1)}, s32[4,2]{0,1:T(2,128)}, u32[]{:S(2)}) copy-start(s32[4,2]{0,1:T(2,128)} %param.14) | copy-start | bytes 100
  8.9 5.6 %collective-permute-start = (f32[3,68,128]{2,1,0:T(8,128)S(1)}, f32[3,68,128]{2,1,0:T(8,128)S(1)}, u32[]{:S(2)}, u32[]{:S(2)}) collective-permute-start(f32[3,68,128]{2,1,0:T(8,128)S(1)} %get-tuple-element.44), channel_id=1, source_target_pairs={{0,8},{8,16},{16,24},{24,0},{1,9},{9,17},{17,25},{25,1},{2,10},{10... | collective-permute-start | bytes 313352 | tf_op jit(solution)/shard_map/ppermute | solution.py:610
  9.4 5.4 %collective-permute-start.1 = (f32[3,68,128]{2,1,0:T(8,128)S(1)}, f32[3,68,128]{2,1,0:T(8,128)S(1)}, u32[]{:S(2)}, u32[]{:S(2)}) collective-permute-start(f32[3,68,128]{2,1,0:T(8,128)S(1)} %get-tuple-element.45), channel_id=1, source_target_pairs={{8,0},{16,8},{24,16},{0,24},{9,1},{17,9},{25,17},{1,25},{10,2},{18... | collective-permute-start | bytes 313352 | tf_op jit(solution)/shard_map/ppermute | solution.py:610
  15.1 10.1 %collective-permute-start.6 = (f32[2,40,384]{2,1,0:T(8,128)S(1)}, f32[2,40,384]{2,1,0:T(8,128)S(1)}, u32[]{:S(2)}, u32[]{:S(2)}) collective-permute-start(f32[2,40,384]{2,1,0:T(8,128)S(1)} %get-tuple-element.50.lowest_ref_0_), channel_id=1, source_target_pairs={{2,0},{4,2},{6,4},{3,1},{5,3},{7,5},{10,8},{12,10},{14,12},{11,9},... | collective-permute-start | bytes 368648 | tf_op jit(solution)/shard_map/ppermute | solution.py:615
  16.4 10.2 %collective-permute-start.7 = (f32[2,40,384]{2,1,0:T(8,128)S(1)}, f32[2,40,384]{2,1,0:T(8,128)S(1)}, u32[]{:S(2)}, u32[]{:S(2)}) collective-permute-start(f32[2,40,384]{2,1,0:T(8,128)S(1)} %get-tuple-element.51.lowest_ref_1_), channel_id=1, source_target_pairs={{2,0},{4,2},{6,4},{3,1},{5,3},{7,5},{10,8},{12,10},{14,12},{11,9},... | collective-permute-start | bytes 368648 | tf_op jit(solution)/shard_map/ppermute | solution.py:615
  17.7 5.4 %collective-permute-start.4 = (f32[3,4,128]{2,1,0:T(4,128)S(1)}, f32[3,4,128]{2,1,0:T(4,128)S(1)}, u32[]{:S(2)}, u32[]{:S(2)}) collective-permute-start(f32[3,4,128]{2,1,0:T(4,128)S(1)} %get-tuple-element.54), channel_id=1, source_target_pairs={{0,8},{8,16},{16,24},{24,0},{1,9},{9,17},{17,25},{25,1},{2,10},{10... | collective-permute-start | bytes 18440 | tf_op jit(solution)/shard_map/ppermute | solution.py:610
  19.2 3.9 %collective-permute-start.5 = (f32[3,4,128]{2,1,0:T(4,128)S(1)}, f32[3,4,128]{2,1,0:T(4,128)S(1)}, u32[]{:S(2)}, u32[]{:S(2)}) collective-permute-start(f32[3,4,128]{2,1,0:T(4,128)S(1)} %get-tuple-element.55), channel_id=1, source_target_pairs={{8,0},{16,8},{24,16},{0,24},{9,1},{17,9},{25,17},{1,25},{10,2},{18... | collective-permute-start | bytes 18440 | tf_op jit(solution)/shard_map/ppermute | solution.py:610
  23.1 5.6 %copy-start.4 = (f32[18]{0:T(128)S(1)}, f32[18]{0:T(128)}, u32[]{:S(2)}) copy-start(f32[18]{0:T(128)} %param.15) | copy-start | bytes 220
  23.1 5.6 %copy-start.1 = (f32[4,40,384]{2,1,0:T(8,128)S(1)}, f32[4,40,384]{2,1,0:T(8,128)}, u32[]{:S(2)}) copy-start(f32[4,40,384]{2,1,0:T(8,128)} %share_ref.3) | copy-start | bytes 737284
  23.3 7.2 %collective-permute-start.8 = (f32[3,68,128]{2,1,0:T(8,128)S(1)}, f32[3,68,128]{2,1,0:T(8,128)S(1)}, u32[]{:S(2)}, u32[]{:S(2)}) collective-permute-start(f32[3,68,128]{2,1,0:T(8,128)S(1)} %get-tuple-element.62), channel_id=1, source_target_pairs={{0,8},{8,16},{16,24},{24,0},{1,9},{9,17},{17,25},{25,1},{2,10},{10... | collective-permute-start | bytes 313352 | tf_op jit(solution)/shard_map/ppermute | solution.py:610
  23.9 6.6 %collective-permute-start.9 = (f32[3,68,128]{2,1,0:T(8,128)S(1)}, f32[3,68,128]{2,1,0:T(8,128)S(1)}, u32[]{:S(2)}, u32[]{:S(2)}) collective-permute-start(f32[3,68,128]{2,1,0:T(8,128)S(1)} %get-tuple-element.63), channel_id=1, source_target_pairs={{8,0},{16,8},{24,16},{0,24},{9,1},{17,9},{25,17},{1,25},{10,2},{18... | collective-permute-start | bytes 313352 | tf_op jit(solution)/shard_map/ppermute | solution.py:610
  26.8 3.7 %collective-permute-start.10 = (f32[3,4,128]{2,1,0:T(4,128)S(1)}, f32[3,4,128]{2,1,0:T(4,128)S(1)}, u32[]{:S(2)}, u32[]{:S(2)}) collective-permute-start(f32[3,4,128]{2,1,0:T(4,128)S(1)} %get-tuple-element.64), channel_id=1, source_target_pairs={{0,8},{8,16},{16,24},{24,0},{1,9},{9,17},{17,25},{25,1},{2,10},{10... | collective-permute-start | bytes 18440 | tf_op jit(solution)/shard_map/ppermute | solution.py:610
  27.6 3.0 %collective-permute-start.11 = (f32[3,4,128]{2,1,0:T(4,128)S(1)}, f32[3,4,128]{2,1,0:T(4,128)S(1)}, u32[]{:S(2)}, u32[]{:S(2)}) collective-permute-start(f32[3,4,128]{2,1,0:T(4,128)S(1)} %get-tuple-element.65), channel_id=1, source_target_pairs={{8,0},{16,8},{24,16},{0,24},{9,1},{17,9},{25,17},{1,25},{10,2},{18... | collective-permute-start | bytes 18440 | tf_op jit(solution)/shard_map/ppermute | solution.py:610
  30.6 11.0 %copy-start.2 = (s32[4,3840]{1,0:T(4,128)S(1)}, s32[4,3840]{1,0:T(4,128)}, u32[]{:S(2)}) copy-start(s32[4,3840]{1,0:T(4,128)} %param.17) | copy-start | bytes 184324
  33.3 16.1 %all-to-all-start = ((f32[32,8,128]{2,1,0:T(8,128)}), f32[32,8,128]{2,1,0:T(8,128)S(1)}, u32[]{:S(2)}, u32[]{:S(2)}) async-start(f32[32,8,128]{2,1,0:T(8,128)} %bitcast.2), calls=%async_computation | async-start | bytes 262144 | tf_op jit(solution)/shard_map/all_to_all | solution.py:593
  49.4 4.5 %collective-permute-start.12 = (f32[4,8,128]{2,1,0:T(8,128)S(1)}, f32[4,8,128]{2,1,0:T(8,128)S(1)}, u32[]{:S(2)}, u32[]{:S(2)}) collective-permute-start(f32[4,8,128]{2,1,0:T(8,128)S(1)} %bitcast_reduce_fusion.refs_0_), channel_id=1, source_target_pairs={{0,2},{2,0},{4,6},{6,4},{1,3},{3,1},{5,7},{7,5},{8,10},{10,8},{12,... | collective-permute-start | bytes 49160 | tf_op jit(solution)/shard_map/ppermute | solution.py:586
  50.4 4.6 %collective-permute-start.13 = (f32[4,8,128]{2,1,0:T(8,128)S(1)}, f32[4,8,128]{2,1,0:T(8,128)S(1)}, u32[]{:S(2)}, u32[]{:S(2)}) collective-permute-start(f32[4,8,128]{2,1,0:T(8,128)S(1)} %bitcast_reduce_fusion.refs_0_), channel_id=1, source_target_pairs={{0,4},{2,6},{4,0},{6,2},{1,5},{3,7},{5,1},{7,3},{8,12},{10,14},{12... | collective-permute-start | bytes 49160 | tf_op jit(solution)/shard_map/ppermute | solution.py:586
  51.3 5.5 %collective-permute-start.14 = (f32[4,8,128]{2,1,0:T(8,128)S(1)}, f32[4,8,128]{2,1,0:T(8,128)S(1)}, u32[]{:S(2)}, u32[]{:S(2)}) collective-permute-start(f32[4,8,128]{2,1,0:T(8,128)S(1)} %bitcast_reduce_fusion.refs_0_), channel_id=1, source_target_pairs={{0,6},{2,4},{4,2},{6,0},{1,7},{3,5},{5,3},{7,1},{8,14},{10,12},{12... | collective-permute-start | bytes 49160 | tf_op jit(solution)/shard_map/ppermute | solution.py:586

commit v10 on v8

--- a/solution.py
+++ b/solution.py
@@ -83,18 +83,22 @@
     return out
 
 
-def first_sweep(field, s, j, xt, last, factors, left_row, right_row):
+def first_sweep(field, s, j, xt, factors, before=None, after=None):
     start = ROWS * (xt + 1)
     sub = lax.broadcasted_iota(jnp.int32, (ROWS, LANES), 0)
     own_value = field(s, j, start)
     following = field(s, j, start + 1)
     previous = field(s, j, start - 1)
-    if xt == 0:
-        previous = jnp.where(sub == 0, left_row(s, j), previous)
-    if xt == last:
-        following = jnp.where(sub == ROWS - 1, right_row(s, j), following)
+    if before is not None:
+        previous = jnp.where(sub == 0, before(s, j), previous)
+    if after is not None:
+        following = jnp.where(sub == ROWS - 1, after(s, j), following)
     ahead, back, own = factors
     return own * own_value + ahead * following + back * previous
+
+
+def rim_rows(xt, last, left_row, right_row):
+    return (left_row if xt == 0 else None, right_row if xt == last else None)
 
 
 def turned(source_ref, flag, target_ref):
@@ -201,9 +205,12 @@
             for s in range(sectors):
                 value = first_sweep(
                     lambda s, j, start: v_ref[0, s, j, start : start + ROWS, :],
-                    s, j, xt, strips - 1, factors,
-                    lambda s, j: lrow_ref[j, s : s + 1, :],
-                    lambda s, j: rrow_ref[j, s : s + 1, :],
+                    s, j, xt, factors,
+                    *rim_rows(
+                        xt, strips - 1,
+                        lambda s, j: lrow_ref[j, s : s + 1, :],
+                        lambda s, j: rrow_ref[j, s : s + 1, :],
+                    ),
                 )
                 out_ref[s, xt * ROWS : (xt + 1) * ROWS, j * LANES : (j + 1) * LANES] = value
 
@@ -249,9 +256,12 @@
                 for j in range(tiles):
                     upper = first_sweep(
                         lambda s, j, start: v_ref[k + 1, s, j, start : start + ROWS, :],
-                        s, j, xt, strips - 1, along[j],
-                        lambda s, j: lrow_ref[j, pl.ds((k + 1) * sectors + s, 1), :],
-                        lambda s, j: rrow_ref[j, pl.ds((k + 1) * sectors + s, 1), :],
+                        s, j, xt, along[j],
+                        *rim_rows(
+                            xt, strips - 1,
+                            lambda s, j: lrow_ref[j, pl.ds((k + 1) * sectors + s, 1), :],
+                            lambda s, j: rrow_ref[j, pl.ds((k + 1) * sectors + s, 1), :],
+                        ),
                     )
                     here = a_ref[slot, s, j, rows, :]
                     a_ref[1 - slot, s, j, rows, :] = upper
@@ -277,7 +287,7 @@
             for s in range(sectors):
                 value = first_sweep(
                     lambda s, j, start: v_ref[0, s, j, start : start + ROWS, :],
-                    s, j, xt, strips - 1, factors, None, None,
+                    s, j, xt, factors,
                 )
                 a_ref[0, s, j, xt * ROWS : (xt + 1) * ROWS, :] = value
                 lowest_ref[s, j, xt * ROWS : (xt + 1) * ROWS, :] = value
@@ -289,7 +299,7 @@
 
 
 def outer_middle_kernel(
-    v_ref, inner_ref, inner_top_ref, left_ref, right_ref, lowest_ref, seam_ref,
+    v_ref, inner_top_ref, left_ref, right_ref, lowest_ref, seam_ref,
     cx_ref, mf_ref, cy_ref, code_ref,
     out_ref, first_ref, last_ref, top_ref,
     lrow_ref, rrow_ref, a_ref,
@@ -314,13 +324,6 @@
         top_ref[:, :, rows] = a_ref[(below - 1) % 2, :, :, rows]
     inner = slice(ROWS, (strips - 1) * ROWS)
     top_ref[:, :, inner] = inner_top_ref[:, :, inner]
-    inner = slice(2 * ROWS, strips * ROWS)
-
-    def copy(k, _):
-        out_ref[k, :, :, inner] = inner_ref[k, :, :, inner]
-        return 0
-
-    lax.fori_loop(0, below - 1, copy, 0)
 
 
 def second_last_kernel(
@@ -349,9 +352,12 @@
             for j in range(tiles):
                 upper = first_sweep(
                     lambda s, j, start: vt_ref[s, j, start : start + ROWS, :],
-                    s, j, xt, strips - 1, along[j],
-                    lambda s, j: lrow_ref[j, s : s + 1, :],
-                    lambda s, j: rrow_ref[j, s : s + 1, :],
+                    s, j, xt, along[j],
+                    *rim_rows(
+                        xt, strips - 1,
+                        lambda s, j: lrow_ref[j, s : s + 1, :],
+                        lambda s, j: rrow_ref[j, s : s + 1, :],
+                    ),
                 )
                 top_ref[s, j, rows, :] = upper
                 here = lower_ref[s, j, rows, :]
@@ -361,7 +367,9 @@
                 store_rims(first_ref, last_ref, done + s, j, xt, strips - 1, value)
 
 
-def highest_kernel(here_ref, above_ref, mf_ref, cy_ref, code_ref, out_ref, first_ref, last_ref):
+def highest_kernel(
+    here_ref, above_ref, mf_ref, cy_ref, code_ref, done_ref, out_ref, first_ref, last_ref
+):
     sectors, tiles, columns, _ = here_ref.shape
     strips = columns // ROWS
     top = mf_ref.shape[0] - 1
@@ -383,9 +391,7 @@
                 store_rims(first_ref, last_ref, s, j, xt, strips - 1, value)
 
 
-def final_level(
-    k, chosen, strips, field, left_row, right_row, refs, out_ref, sens_ref, start_sum
-):
+def final_level(k, chosen, field, rows_at, refs, out_ref, sens_ref=None, start_sum=False):
     cx_ref, code_ref, weight_ref, share_ref = refs
     sectors, _, width = share_ref.shape
     cx = cx_ref[k].astype(jnp.float32)
@@ -398,9 +404,12 @@
             factors = first_weights(cx, codes, 0, xt, j)
             total = 0.0
             for s in range(sectors):
-                value = first_sweep(field, s, j, xt, strips - 1, factors, left_row, right_row)
+                value = first_sweep(field, s, j, xt, factors, *rows_at(xt))
                 out_ref[k, s, rows, lanes] = value
-                total = total + share_ref[s, rows, lanes] * value
+                if sens_ref is not None:
+                    total = total + share_ref[s, rows, lanes] * value
+            if sens_ref is None:
+                continue
             if start_sum:
                 sens_ref[rows, lanes] = factor * total
             else:
@@ -408,28 +417,36 @@
 
 
 def inner_final_kernel(
-    v_ref, vs_ref, cx_ref, code_ref, weight_ref, share_ref, out_hbm, sens_ref, out_ref, sems
+    inner_ref, outer_ref, vs_ref, cx_ref, code_ref, weight_ref, share_ref,
+    out_hbm, sens_ref, out_ref, sems,
 ):
-    below, _, _, padded, _ = v_ref.shape
+    below, _, _, padded, _ = inner_ref.shape
     strips = (padded - 2 * ROWS) // ROWS
     refs = (cx_ref, code_ref, weight_ref, share_ref)
     inner = pl.ds(ROWS, (strips - 2) * ROWS)
+    chosen = range(1, strips - 1)
 
     def send(k):
         return pltpu.make_async_copy(out_ref.at[k, :, inner], out_hbm.at[:, k, inner], sems.at[k])
 
     final_level(
-        below, range(1, strips - 1), strips,
-        lambda s, j, start: vs_ref[s, j, start : start + ROWS, :],
-        None, None, refs, out_ref, sens_ref, True,
+        below, chosen, lambda s, j, start: vs_ref[s, j, start : start + ROWS, :],
+        lambda xt: (None, None), refs, out_ref, sens_ref, True,
     )
     send(below).start()
 
     def step(k, _):
+        low, high = 2 * ROWS - 1, strips * ROWS
+
+        def rows_at(xt):
+            return (
+                (lambda s, j: outer_ref[k, s, j, low : low + 1, :]) if xt == 1 else None,
+                (lambda s, j: outer_ref[k, s, j, high : high + 1, :]) if xt == strips - 2 else None,
+            )
+
         final_level(
-            k, range(1, strips - 1), strips,
-            lambda s, j, start: v_ref[k, s, j, start : start + ROWS, :],
-            None, None, refs, out_ref, sens_ref, False,
+            k, chosen, lambda s, j, start: inner_ref[k, s, j, start : start + ROWS, :],
+            rows_at, refs, out_ref, sens_ref,
         )
         send(k).start()
         return 0
@@ -440,12 +457,12 @@
 
 
 def outer_final_kernel(
-    v_ref, vs_ref, vt_ref, left_ref, right_ref, left_top_ref, right_top_ref, seam_ref,
-    cx_ref, code_ref, weight_ref, share_ref, inner_ref, done_hbm,
+    inner_ref, outer_ref, vs_ref, vt_ref, left_ref, right_ref, left_top_ref, right_top_ref, seam_ref,
+    cx_ref, code_ref, weight_ref, share_ref, inner_sens_ref, done_hbm,
     out_hbm, piece_ref,
     lrow_ref, rrow_ref, ltop_ref, rtop_ref, out_ref, sens_ref, flat_ref, sems,
 ):
-    below, sectors, tiles, padded, _ = v_ref.shape
+    below, sectors, tiles, padded, _ = outer_ref.shape
     strips = (padded - 2 * ROWS) // ROWS
     ends = (0, strips - 1)
     refs = (cx_ref, code_ref, weight_ref, share_ref)
@@ -463,38 +480,73 @@
         out_ref.at[below + 1], out_hbm.at[:, below + 1], sems.at[0, below + 1]
     )
     final_level(
-        below + 1, range(strips), strips,
-        lambda s, j, start: vt_ref[s, j, start : start + ROWS, :],
-        lambda s, j: ltop_ref[j, s : s + 1, :],
-        lambda s, j: rtop_ref[j, s : s + 1, :],
+        below + 1, range(strips), lambda s, j, start: vt_ref[s, j, start : start + ROWS, :],
+        lambda xt: rim_rows(
+            xt, strips - 1,
+            lambda s, j: ltop_ref[j, s : s + 1, :],
+            lambda s, j: rtop_ref[j, s : s + 1, :],
+        ),
         refs, out_ref, sens_ref, True,
     )
     send_top.start()
+    edge = below * sectors
     final_level(
-        below, ends, strips,
-        lambda s, j, start: vs_ref[s, j, start : start + ROWS, :],
-        lambda s, j: lrow_ref[j, below * sectors + s : below * sectors + s + 1, :],
-        lambda s, j: rrow_ref[j, below * sectors + s : below * sectors + s + 1, :],
-        refs, out_ref, sens_ref, False,
+        below, ends, lambda s, j, start: vs_ref[s, j, start : start + ROWS, :],
+        lambda xt: rim_rows(
+            xt, strips - 1,
+            lambda s, j: lrow_ref[j, edge + s : edge + s + 1, :],
+            lambda s, j: rrow_ref[j, edge + s : edge + s + 1, :],
+        ),
+        refs, out_ref,
     )
     for i in range(2):
         send(below, i).start()
 
     def step(k, _):
+        low, high = 2 * ROWS, strips * ROWS - 1
+
+        def rows_at(xt):
+            if xt == 0:
+                return (
+                    lambda s, j: lrow_ref[j, pl.ds(k * sectors + s, 1), :],
+                    lambda s, j: inner_ref[k, s, j, low : low + 1, :],
+                )
+            return (
+                lambda s, j: inner_ref[k, s, j, high : high + 1, :],
+                lambda s, j: rrow_ref[j, pl.ds(k * sectors + s, 1), :],
+            )
+
         final_level(
-            k, ends, strips,
-            lambda s, j, start: v_ref[k, s, j, start : start + ROWS, :],
-            lambda s, j: lrow_ref[j, pl.ds(k * sectors + s, 1), :],
-            lambda s, j: rrow_ref[j, pl.ds(k * sectors + s, 1), :],
-            refs, out_ref, sens_ref, False,
+            k, ends, lambda s, j, start: outer_ref[k, s, j, start : start + ROWS, :],
+            rows_at, refs, out_ref,
         )
         for i in range(2):
             send(k, i).start()
         return 0
 
     lax.fori_loop(0, below, step, 0)
+
+    places = [
+        (slice(xt * ROWS, (xt + 1) * ROWS), slice(j * LANES, (j + 1) * LANES))
+        for xt in ends
+        for j in range(tiles)
+    ]
+
+    def add(k, sums):
+        factor = weight_ref[pl.ds(k, 1), :]
+        out = []
+        for total, place in zip(sums, places):
+            part = share_ref[(0, *place)] * out_ref[(k, 0, *place)]
+            for s in range(1, sectors):
+                part = part + share_ref[(s, *place)] * out_ref[(k, s, *place)]
+            out.append(total + factor * part)
+        return tuple(out)
+
+    sums = lax.fori_loop(0, below + 1, add, tuple(sens_ref[place] for place in places))
+    for total, place in zip(sums, places):
+        sens_ref[place] = total
     inner = slice(ROWS, (strips - 1) * ROWS)
-    sens_ref[inner] += inner_ref[inner]
+    sens_ref[inner] += inner_sens_ref[inner]
     if len(piece_ref.shape) == 2:
         piece_ref[...] = sens_ref[...]
     else:
@@ -530,13 +582,14 @@
     rank = lax.axis_index("lev")
     half = jnp.bfloat16
     zero, one = jnp.zeros((), half), jnp.ones((), half)
-    iota = lax.broadcasted_iota(jnp.int32, (lanes, lanes), 0).astype(jnp.float32).astype(half)
-    total = jnp.zeros((2 * lanes, lanes), jnp.float32)
+    tall, short = 2 * lanes, lanes // 2
+    iota = lax.broadcasted_iota(jnp.int32, (tall, lanes), 0).astype(jnp.float32).astype(half)
+    total = jnp.zeros((2 * short, tall), jnp.float32)
     lines = [(i, o, r) for i in range(group) for o in range(owners) for r in range(depth)]
-    wide = 8
-
-    def spread(row):
-        return jnp.broadcast_to(row, (lanes, lanes)).astype(half)
+    wide = 4
+
+    def spread(row, count):
+        return jnp.broadcast_to(row, (count, lanes)).astype(half)
 
     for start in range(0, len(lines), wide):
         lefts, rights = [], []
@@ -544,25 +597,28 @@
             cells = cells_ref[jnp.bitwise_xor(rank, part), owner, line : line + 1, :]
             value = value_refs[part][owner, line : line + 1, :]
             coarse = value.astype(half).astype(jnp.float32)
-            high = spread(jnp.right_shift(cells, 7).astype(jnp.float32)) == iota
-            low = spread(jnp.bitwise_and(cells, 127).astype(jnp.float32)) == iota
+            high = jnp.right_shift(cells, 8).astype(jnp.float32)
+            low = jnp.bitwise_and(cells, 255).astype(jnp.float32)
+            high = spread(high, short) == iota[:short]
             lefts.append(
                 jnp.concatenate(
                     [
-                        jnp.where(high, spread(coarse), zero),
-                        jnp.where(high, spread(value - coarse), zero),
+                        jnp.where(high, spread(coarse, short), zero),
+                        jnp.where(high, spread(value - coarse, short), zero),
                     ],
                     axis=0,
                 )
             )
-            rights.append(jnp.where(low, one, zero))
+            rights.append(jnp.where(spread(low, tall) == iota, one, zero))
         total += lax.dot_general(
             jnp.concatenate(lefts, axis=1),
             jnp.concatenate(rights, axis=1),
             (((1,), (1,)), ((), ())),
             preferred_element_type=jnp.float32,
         )
-    out_ref[...] = total[:rows] + total[lanes : lanes + rows]
+    total = total[:short] + total[short:]
+    for i in range(2):
+        out_ref[pl.ds(i, rows // 2, stride=2), :] = total[: rows // 2, i * lanes : (i + 1) * lanes]
 
 
 def exchanged(value, axis, apart):
@@ -659,13 +715,13 @@
     above = from_above(lowest)
     left_top, right_top = around(first_top, last_top)
 
-    v, first, last, top = call(
+    outer, first, last, top = call(
         outer_middle_kernel,
         (inner_field, rim_next, rim_next, lines),
-        [VM] * 11,
+        [VM] * 10,
         [VM] * 4,
         (
-            v, inner, inner_top, left, right, lowest, seam,
+            v, inner_top, left, right, lowest, seam,
             courant_x, mass_flux, courant_y, limiter_code,
         ),
         [rim_scratch, rim_scratch, a_scratch],
@@ -682,37 +738,37 @@
         [pltpu.VMEM((tiles, sectors, LANES), jnp.float32)] * 2,
     )
     left, right = around(first, last)
-    vt, first_top, last_top = call(
-        highest_kernel,
-        (field_top, rim_top, rim_top),
-        [VM] * 5,
-        [VM] * 3,
-        (top, above, mass_flux, courant_y, limiter_code),
-    )
-    left_top, right_top = around(first_top, last_top)
-
     owners, share = flux_cell.shape
     group, copies = lax.axis_size("lev"), lax.axis_size("sec")
     depth = -(-share // (group * LANES))
     aligned = share % LANES == 0
     packed = (owners, group, copies, depth, LANES)
     stage = pltpu.VMEM((levels, sectors, columns, width), jnp.float32)
-    adjoint, inner = call(
+    adjoint, inner_sens = call(
         inner_final_kernel,
         (f32(*forcing.shape), kept(columns, width)),
+        [VM] * 7,
+        [HBM, VM],
+        (inner, outer, vs, courant_x, limiter_code, weight, sector_share),
+        [stage, pltpu.SemaphoreType.DMA((levels,))],
+    )
+    vt, first_top, last_top = call(
+        highest_kernel,
+        (field_top, rim_top, rim_top),
         [VM] * 6,
-        [HBM, VM],
-        (v, vs, courant_x, limiter_code, weight, sector_share),
-        [stage, pltpu.SemaphoreType.DMA((levels,))],
-    )
+        [VM] * 3,
+        (top, above, mass_flux, courant_y, limiter_code, inner_sens),
+    )
+    left_top, right_top = around(first_top, last_top)
+
     adjoint, pieces = call(
         outer_final_kernel,
         (f32(*forcing.shape), f32(*packed) if aligned else f32(columns, width)),
-        [VM] * 13 + [HBM],
+        [VM] * 14 + [HBM],
         [HBM, VM],
         (
-            v, vs, vt, left, right, left_top, right_top, seam,
-            courant_x, limiter_code, weight, sector_share, inner, adjoint,
+            inner, outer, vs, vt, left, right, left_top, right_top, seam,
+            courant_x, limiter_code, weight, sector_share, inner_sens, adjoint,
         ),
         [
             rim_scratch, rim_scratch,
@@ -723,7 +779,7 @@
             pltpu.VMEM((columns * tiles + ROWS, LANES), jnp.float32),
             pltpu.SemaphoreType.DMA((2, levels)),
         ],
-        aliases={13: 0},
+        aliases={14: 0},
     )
     if not aligned:
         pieces = jnp.pad(

time: 55.7 us -> 56.5 us (1.014)
  starting transfers between devices: 21.3 us -> 23.4 us
  waiting for transfers between devices: 13.4 us -> 11.7 us
    all_to_all x1, starting transfers between devices: 5.98 us -> 8.12 us  [remapped(): lax.all_to_all(sent, ('tile', 'lev', 'sec'), split_axis=0, concat_axis=0,...]
    ppermute x2, waiting for transfers between devices: 2.34 us -> 0.46 us  [from_above(): return lax.ppermute(value, 'lev', [(i + 1, i) for i in range(count - 1)])]
    ppermute x8, waiting for transfers between devices: 0.26 us -> 1.6 us  [around(): return (lax.ppermute(last, 'tile', up), lax.ppermute(first, 'tile', down))]
    ppermute x3, waiting for transfers between devices: 3.05 us -> 1.88 us  [exchanged(): return lax.ppermute(value, axis, [(i, i ^ apart) for i in range(count)])]
  transfers between devices with their start and end apart: 14 -> 14, of which waited for: 6 -> 7; matrix products, arithmetic and copies ran while one was open for 0% -> 0% of each run, Pallas kernels for 22% -> 21%
where the time goes in v10:
time: 56.5 us; the launch traced here: 56.3 us
  starting transfers between devices  23.4 us (41%)
  Pallas kernels  20.3 us (36%)
  waiting for transfers between devices  11.7 us (21%)
  between operations  0.8 us (1%)
    pallas_call x10, Pallas kernels, call(): pl.pallas_call(kernel, out_shape=out_shape, in_specs=in_specs, out_specs=...  20.3 us
    all_to_all x1, starting transfers between devices, remapped(): lax.all_to_all(sent, ('tile', 'lev', 'sec'), split_axis=0, concat_axis=0,...  8.12 us
    ppermute x8, starting transfers between devices, around(): return (lax.ppermute(last, 'tile', up), lax.ppermute(first, 'tile', down))  8.1 us
    all_to_all x1, waiting for transfers between devices, remapped(): lax.all_to_all(sent, ('tile', 'lev', 'sec'), split_axis=0, concat_axis=0,...  7.71 us
    ppermute x3, starting transfers between devices, exchanged(): return lax.ppermute(value, axis, [(i, i ^ apart) for i in range(count)])  4.45 us
    ppermute x2, starting transfers between devices, from_above(): return lax.ppermute(value, 'lev', [(i + 1, i) for i in range(count - 1)])  2.72 us
    ppermute x3, waiting for transfers between devices, exchanged(): return lax.ppermute(value, axis, [(i, i ^ apart) for i in range(count)])  1.88 us
    ppermute x8, waiting for transfers between devices, around(): return (lax.ppermute(last, 'tile', up), lax.ppermute(first, 'tile', down))  1.6 us
  transfers between devices with their start and end apart: 14, of which 7 were waited for; matrix products, arithmetic and copies ran while one was open for 0% of the time, Pallas kernels for 21%

profile of v10, /device:TPU:0, one launch (start us, length us, event | category | flops | bytes accessed | tf_op | source)
XLA Modules:
  0.0 56.3 jit_solution(2408220304575881861)
XLA Ops:
  0.6 2.0 %shard_map.104 = (f32[4,40,384]{2,1,0:T(8,128)S(1)}, bf16[18,40,384]{2,1,0:T(8,128)(2,1)S(1)}, bf16[18,40,384]{2,1,0:T(8,128)(2,1)S(1)}, s32[18,40,384]{2,1,0:T(8,128)S(1)}, bf16[18,40,384]{2,1,0:T(8,128)(2,1)S(1)}) custom-call(f32[4,18,40,384]{3,2,1,0:T(8,128)} %f_ref.1, bf16[18,40,384]{2,1,0:T(8,128)(2,1)} %mf_hbm.1, bf16[18,40,384]{2,1,0:T(8,128)(2,1)} %cy_hbm.1, ...), custom_call_target="tpu_custom_call" | custom-call | flops 1 | bytes 1 | tf_op jit(solution)/shard_map/pallas_call | solution.py:19
  2.7 1.4 %collective-permute-start.2 = (f32[4,40,384]{2,1,0:T(8,128)S(1)}, f32[4,40,384]{2,1,0:T(8,128)S(1)}, u32[]{:S(2)}, u32[]{:S(2)}) collective-permute-start(f32[4,40,384]{2,1,0:T(8,128)S(1)} %get-tuple-element.46), channel_id=1, source_target_pairs={{2,0},{4,2},{6,4},{3,1},{5,3},{7,5},{10,8},{12,10},{14,12},{11,9},... | collective-permute-start | bytes 737288 | tf_op jit(solution)/shard_map/ppermute | solution.py:655
  4.1 3.5 %shard_map.105 = (f32[17,4,3,56,128]{4,3,2,1,0:T(8,128)S(1)}, f32[3,68,128]{2,1,0:T(8,128)S(1)}, f32[3,68,128]{2,1,0:T(8,128)S(1)}, f32[4,40,384]{2,1,0:T(8,128)S(1)}) custom-call(f32[4,18,40,384]{3,2,1,0:T(8,128)S(1)} %copy-done, bf16[18,40,384]{2,1,0:T(8,128)(2,1)S(1)} %get-tuple-element.35.mf_ref, bf16[18,40,384]{2,1,0:T(8,128)(2,1)S(1)} %get-tuple-element.36.cy_ref, ...), custom_call_target="tpu_custom_call" | custom-call | flops 1 | bytes 1 | tf_op jit(solution)/shard_map/pallas_call | solution.py:19
  7.6 0.5 collective-permute-start
  8.1 2.0 %collective-permute-start.1 = (f32[3,68,128]{2,1,0:T(8,128)S(1)}, f32[3,68,128]{2,1,0:T(8,128)S(1)}, u32[]{:S(2)}, u32[]{:S(2)}) collective-permute-start(f32[3,68,128]{2,1,0:T(8,128)S(1)} %get-tuple-element.43), channel_id=1, source_target_pairs={{8,0},{16,8},{24,16},{0,24},{9,1},{17,9},{25,17},{1,25},{10,2},{18... | collective-permute-start | bytes 313352 | tf_op jit(solution)/shard_map/ppermute | solution.py:650
  10.1 3.1 %shard_map.106 = (f32[16,4,3,56,128]{4,3,2,1,0:T(8,128)S(1)}, f32[4,3,40,128]{3,2,1,0:T(8,128)S(1)}, f32[4,3,40,128]{3,2,1,0:T(8,128)S(1)}) custom-call(f32[17,4,3,56,128]{4,3,2,1,0:T(8,128)S(1)} %get-tuple-element.38.v_ref, bf16[18,40,384]{2,1,0:T(8,128)(2,1)S(1)} %get-tuple-element.39.cx_ref, bf16[18,40,384]{2,1,0:T(8,128)(2,1)S(1)} %get-tuple-element.35.mf_ref, ...), custom_call_target="tpu_custom_call" | custom-call | flops 1 | bytes 1 | tf_op jit(solution)/shard_map/pallas_call | solution.py:19
  13.2 0.2 collective-permute-done.1.right_ref
  13.5 0.2 collective-permute-done.2.above_ref
  13.7 0.1 broadcast_in_dim.4.seam_ref
  13.8 0.2 shard_map.107
  14.0 1.3 %collective-permute-start.5 = (f32[4,40,384]{2,1,0:T(8,128)S(1)}, f32[4,40,384]{2,1,0:T(8,128)S(1)}, u32[]{:S(2)}, u32[]{:S(2)}) collective-permute-start(f32[4,40,384]{2,1,0:T(8,128)S(1)} %get-tuple-element.47.lowest_ref), channel_id=1, source_target_pairs={{2,0},{4,2},{6,4},{3,1},{5,3},{7,5},{10,8},{12,10},{14,12},{11,9},... | collective-permute-start | bytes 737288 | tf_op jit(solution)/shard_map/ppermute | solution.py:655
  15.3 1.2 %collective-permute-start.3 = (f32[3,4,128]{2,1,0:T(4,128)S(1)}, f32[3,4,128]{2,1,0:T(4,128)S(1)}, u32[]{:S(2)}, u32[]{:S(2)}) collective-permute-start(f32[3,4,128]{2,1,0:T(4,128)S(1)} %get-tuple-element.50), channel_id=1, source_target_pairs={{0,8},{8,16},{16,24},{24,0},{1,9},{9,17},{17,25},{25,1},{2,10},{10... | collective-permute-start | bytes 18440 | tf_op jit(solution)/shard_map/ppermute | solution.py:650
  16.5 0.8 %collective-permute-start.4 = (f32[3,4,128]{2,1,0:T(4,128)S(1)}, f32[3,4,128]{2,1,0:T(4,128)S(1)}, u32[]{:S(2)}, u32[]{:S(2)}) collective-permute-start(f32[3,4,128]{2,1,0:T(4,128)S(1)} %get-tuple-element.51), channel_id=1, source_target_pairs={{8,0},{16,8},{24,16},{0,24},{9,1},{17,9},{25,17},{1,25},{10,2},{18... | collective-permute-start | bytes 18440 | tf_op jit(solution)/shard_map/ppermute | solution.py:650
  17.3 2.9 %shard_map.108 = (f32[16,4,3,56,128]{4,3,2,1,0:T(8,128)S(1)}, f32[3,64,128]{2,1,0:T(8,128)S(1)}, f32[3,64,128]{2,1,0:T(8,128)S(1)}, f32[4,3,40,128]{3,2,1,0:T(8,128)S(1)}) custom-call(f32[17,4,3,56,128]{4,3,2,1,0:T(8,128)S(1)} %get-tuple-element.38.v_ref, f32[4,3,40,128]{3,2,1,0:T(8,128)S(1)} %get-tuple-element.41.inner_top_ref, ...), custom_call_target="tpu_custom_call" | custom-call | flops 1 | bytes 1 | tf_op jit(solution)/shard_map/pallas_call | solution.py:19
  20.3 0.2 shard_map.109
  20.5 0.8 %collective-permute-start.6 = (f32[3,68,128]{2,1,0:T(8,128)S(1)}, f32[3,68,128]{2,1,0:T(8,128)S(1)}, u32[]{:S(2)}, u32[]{:S(2)}) collective-permute-start(f32[3,68,128]{2,1,0:T(8,128)S(1)} %get-tuple-element.59), channel_id=1, source_target_pairs={{0,8},{8,16},{16,24},{24,0},{1,9},{9,17},{17,25},{25,1},{2,10},{10... | collective-permute-start | bytes 313352 | tf_op jit(solution)/shard_map/ppermute | solution.py:650
  21.3 1.0 %collective-permute-start.7 = (f32[3,68,128]{2,1,0:T(8,128)S(1)}, f32[3,68,128]{2,1,0:T(8,128)S(1)}, u32[]{:S(2)}, u32[]{:S(2)}) collective-permute-start(f32[3,68,128]{2,1,0:T(8,128)S(1)} %get-tuple-element.60), channel_id=1, source_target_pairs={{8,0},{16,8},{24,16},{0,24},{9,1},{17,9},{25,17},{1,25},{10,2},{18... | collective-permute-start | bytes 313352 | tf_op jit(solution)/shard_map/ppermute | solution.py:650
  22.4 2.0 %shard_map.110 = (f32[4,18,40,384]{3,2,1,0:T(8,128)}, f32[40,384]{1,0:T(8,128)S(1)}) custom-call(f32[16,4,3,56,128]{4,3,2,1,0:T(8,128)S(1)} %get-tuple-element.40.inner_ref, f32[16,4,3,56,128]{4,3,2,1,0:T(8,128)S(1)} %get-tuple-element.48.outer_ref, f32[4,3,56,128]{3,2,1,0:T(8,128)S(1)} %get-tuple-element.55.vs_ref, ...), custom_call_target="tpu_custom_call" | custom-call | flops 1 | bytes 1 | tf_op jit(solution)/shard_map/pallas_call | solution.py:19
  24.4 0.2 collective-permute-done.5.above_ref
  24.7 0.2 shard_map.111
  24.9 0.4 collective-permute-start.8
  25.3 1.3 %collective-permute-start.9 = (f32[3,4,128]{2,1,0:T(4,128)S(1)}, f32[3,4,128]{2,1,0:T(4,128)S(1)}, u32[]{:S(2)}, u32[]{:S(2)}) collective-permute-start(f32[3,4,128]{2,1,0:T(4,128)S(1)} %get-tuple-element.62), channel_id=1, source_target_pairs={{8,0},{16,8},{24,16},{0,24},{9,1},{17,9},{25,17},{1,25},{10,2},{18... | collective-permute-start | bytes 18440 | tf_op jit(solution)/shard_map/ppermute | solution.py:650
  26.7 1.3 %collective-permute-done.8.left_top_ref = f32[3,4,128]{2,1,0:T(4,128)S(1)} collective-permute-done((f32[3,4,128]{2,1,0:T(4,128)S(1)}, f32[3,4,128]{2,1,0:T(4,128)S(1)}, u32[]{:S(2)}, u32[]{:S(2)}) %collective-permute-start.8) | collective-permute-done | bytes 6176 | tf_op jit(solution)/shard_map/ppermute | solution.py:650
  28.0 2.5 %shard_map.112 = (f32[4,18,40,384]{3,2,1,0:T(8,128)}, f32[4,4,2,8,128]{4,3,2,1,0:T(8,128)}) custom-call(f32[16,4,3,56,128]{4,3,2,1,0:T(8,128)S(1)} %get-tuple-element.40.inner_ref, f32[16,4,3,56,128]{4,3,2,1,0:T(8,128)S(1)} %get-tuple-element.48.outer_ref, f32[4,3,56,128]{3,2,1,0:T(8,128)S(1)} %get-tuple-element.55.vs_ref, ...), custom_call_target="tpu_custom_call", output_to_operand_aliasing={{0}: (14, {})} | custom-call | flops 1 | bytes 1 | tf_op jit(solution)/shard_map/pallas_call | solution.py:19
  30.6 8.1 %all-to-all-start = ((f32[32,8,128]{2,1,0:T(8,128)}), f32[32,8,128]{2,1,0:T(8,128)S(1)}, u32[]{:S(2)}, u32[]{:S(2)}) async-start(f32[32,8,128]{2,1,0:T(8,128)} %bitcast.2), calls=%async_computation | async-start | bytes 262144 | tf_op jit(solution)/shard_map/all_to_all | solution.py:633
  38.7 7.7 %all-to-all-done = f32[32,8,128]{2,1,0:T(8,128)S(1)} async-done(((f32[32,8,128]{2,1,0:T(8,128)}), f32[32,8,128]{2,1,0:T(8,128)S(1)}, u32[]{:S(2)}, u32[]{:S(2)}) %all-to-all-start) | async-done | bytes 131104 | tf_op jit(solution)/shard_map/all_to_all | solution.py:633
  46.4 1.4 %collective-permute-start.12 = (f32[4,8,128]{2,1,0:T(8,128)S(1)}, f32[4,8,128]{2,1,0:T(8,128)S(1)}, u32[]{:S(2)}, u32[]{:S(2)}) collective-permute-start(f32[4,8,128]{2,1,0:T(8,128)S(1)} %bitcast_reduce_fusion.refs_0_), channel_id=1, source_target_pairs={{0,6},{2,4},{4,2},{6,0},{1,7},{3,5},{5,3},{7,1},{8,14},{10,12},{12... | collective-permute-start | bytes 49160 | tf_op jit(solution)/shard_map/ppermute | solution.py:626
  47.9 1.1 %collective-permute-start.11 = (f32[4,8,128]{2,1,0:T(8,128)S(1)}, f32[4,8,128]{2,1,0:T(8,128)S(1)}, u32[]{:S(2)}, u32[]{:S(2)}) collective-permute-start(f32[4,8,128]{2,1,0:T(8,128)S(1)} %bitcast_reduce_fusion.refs_0_), channel_id=1, source_target_pairs={{0,4},{2,6},{4,0},{6,2},{1,5},{3,7},{5,1},{7,3},{8,12},{10,14},{12... | collective-permute-start | bytes 49160 | tf_op jit(solution)/shard_map/ppermute | solution.py:626
  49.0 1.9 %collective-permute-start.10 = (f32[4,8,128]{2,1,0:T(8,128)S(1)}, f32[4,8,128]{2,1,0:T(8,128)S(1)}, u32[]{:S(2)}, u32[]{:S(2)}) collective-permute-start(f32[4,8,128]{2,1,0:T(8,128)S(1)} %bitcast_reduce_fusion.refs_0_), channel_id=1, source_target_pairs={{0,2},{2,0},{4,6},{6,4},{1,3},{3,1},{5,7},{7,5},{8,10},{10,8},{12,... | collective-permute-start | bytes 49160 | tf_op jit(solution)/shard_map/ppermute | solution.py:626
  50.9 1.1 %collective-permute-done.12.refs_3_ = f32[4,8,128]{2,1,0:T(8,128)S(1)} collective-permute-done((f32[4,8,128]{2,1,0:T(8,128)S(1)}, f32[4,8,128]{2,1,0:T(8,128)S(1)}, u32[]{:S(2)}, u32[]{:S(2)}) %collective-permute-start.12) | collective-permute-done | bytes 16416 | tf_op jit(solution)/shard_map/ppermute | solution.py:626
  52.0 0.7 %collective-permute-done.11.refs_2_ = f32[4,8,128]{2,1,0:T(8,128)S(1)} collective-permute-done((f32[4,8,128]{2,1,0:T(8,128)S(1)}, f32[4,8,128]{2,1,0:T(8,128)S(1)}, u32[]{:S(2)}, u32[]{:S(2)}) %collective-permute-start.11) | collective-permute-done | bytes 16416 | tf_op jit(solution)/shard_map/ppermute | solution.py:626
  52.8 3.5 %shard_map.113 = f32[120,128]{1,0:T(8,128)} custom-call(s32[4,4,8,128]{3,2,1,0:T(8,128)S(1)} %copy_bitcast_fusion.1.cells_ref, f32[4,8,128]{2,1,0:T(8,128)S(1)} %bitcast_reduce_fusion.refs_0_, f32[4,8,128]{2,1,0:T(8,128)S(1)} %collective-permute-done.10.refs_1_, f32[4,8,128]{2,1,0:T(8,128)S(1)} %collective-permute-done.11.refs_2_, ...), custom_call_target="tpu_custom_call" | custom-call | flops 1 | bytes 1 | tf_op jit(solution)/shard_map/pallas_call | solution.py:19
  (21 shorter events, 0.2 us)
Async XLA Ops:
  0.6 3.5 %copy-start = (f32[4,18,40,384]{3,2,1,0:T(8,128)S(1)}, f32[4,18,40,384]{3,2,1,0:T(8,128)}, u32[]{:S(2)}) copy-start(f32[4,18,40,384]{3,2,1,0:T(8,128)} %f_ref.1) | copy-start | bytes 13271044
  2.7 11.0 %collective-permute-start.2 = (f32[4,40,384]{2,1,0:T(8,128)S(1)}, f32[4,40,384]{2,1,0:T(8,128)S(1)}, u32[]{:S(2)}, u32[]{:S(2)}) collective-permute-start(f32[4,40,384]{2,1,0:T(8,128)S(1)} %get-tuple-element.46), channel_id=1, source_target_pairs={{2,0},{4,2},{6,4},{3,1},{5,3},{7,5},{10,8},{12,10},{14,12},{11,9},... | collective-permute-start | bytes 737288 | tf_op jit(solution)/shard_map/ppermute | solution.py:655
  7.6 6.1 %copy-start.3 = (s32[4,2]{0,1:T(2,128)S(1)}, s32[4,2]{0,1:T(2,128)}, u32[]{:S(2)}) copy-start(s32[4,2]{0,1:T(2,128)} %param.14) | copy-start | bytes 100
  7.6 5.6 %collective-permute-start = (f32[3,68,128]{2,1,0:T(8,128)S(1)}, f32[3,68,128]{2,1,0:T(8,128)S(1)}, u32[]{:S(2)}, u32[]{:S(2)}) collective-permute-start(f32[3,68,128]{2,1,0:T(8,128)S(1)} %get-tuple-element.42), channel_id=1, source_target_pairs={{0,8},{8,16},{16,24},{24,0},{1,9},{9,17},{17,25},{25,1},{2,10},{10... | collective-permute-start | bytes 313352 | tf_op jit(solution)/shard_map/ppermute | solution.py:650
  8.1 5.4 %collective-permute-start.1 = (f32[3,68,128]{2,1,0:T(8,128)S(1)}, f32[3,68,128]{2,1,0:T(8,128)S(1)}, u32[]{:S(2)}, u32[]{:S(2)}) collective-permute-start(f32[3,68,128]{2,1,0:T(8,128)S(1)} %get-tuple-element.43), channel_id=1, source_target_pairs={{8,0},{16,8},{24,16},{0,24},{9,1},{17,9},{25,17},{1,25},{10,2},{18... | collective-permute-start | bytes 313352 | tf_op jit(solution)/shard_map/ppermute | solution.py:650
  14.0 10.7 %collective-permute-start.5 = (f32[4,40,384]{2,1,0:T(8,128)S(1)}, f32[4,40,384]{2,1,0:T(8,128)S(1)}, u32[]{:S(2)}, u32[]{:S(2)}) collective-permute-start(f32[4,40,384]{2,1,0:T(8,128)S(1)} %get-tuple-element.47.lowest_ref), channel_id=1, source_target_pairs={{2,0},{4,2},{6,4},{3,1},{5,3},{7,5},{10,8},{12,10},{14,12},{11,9},... | collective-permute-start | bytes 737288 | tf_op jit(solution)/shard_map/ppermute | solution.py:655
  15.3 5.0 %collective-permute-start.3 = (f32[3,4,128]{2,1,0:T(4,128)S(1)}, f32[3,4,128]{2,1,0:T(4,128)S(1)}, u32[]{:S(2)}, u32[]{:S(2)}) collective-permute-start(f32[3,4,128]{2,1,0:T(4,128)S(1)} %get-tuple-element.50), channel_id=1, source_target_pairs={{0,8},{8,16},{16,24},{24,0},{1,9},{9,17},{17,25},{25,1},{2,10},{10... | collective-permute-start | bytes 18440 | tf_op jit(solution)/shard_map/ppermute | solution.py:650
  16.5 3.7 %collective-permute-start.4 = (f32[3,4,128]{2,1,0:T(4,128)S(1)}, f32[3,4,128]{2,1,0:T(4,128)S(1)}, u32[]{:S(2)}, u32[]{:S(2)}) collective-permute-start(f32[3,4,128]{2,1,0:T(4,128)S(1)} %get-tuple-element.51), channel_id=1, source_target_pairs={{8,0},{16,8},{24,16},{0,24},{9,1},{17,9},{25,17},{1,25},{10,2},{18... | collective-permute-start | bytes 18440 | tf_op jit(solution)/shard_map/ppermute | solution.py:650
  17.3 5.0 %copy-start.4 = (f32[18]{0:T(128)S(1)}, f32[18]{0:T(128)}, u32[]{:S(2)}) copy-start(f32[18]{0:T(128)} %param.15) | copy-start | bytes 220
  17.3 5.1 %copy-start.1 = (f32[4,40,384]{2,1,0:T(8,128)S(1)}, f32[4,40,384]{2,1,0:T(8,128)}, u32[]{:S(2)}) copy-start(f32[4,40,384]{2,1,0:T(8,128)} %share_ref.3) | copy-start | bytes 737284
  20.5 6.1 %collective-permute-start.6 = (f32[3,68,128]{2,1,0:T(8,128)S(1)}, f32[3,68,128]{2,1,0:T(8,128)S(1)}, u32[]{:S(2)}, u32[]{:S(2)}) collective-permute-start(f32[3,68,128]{2,1,0:T(8,128)S(1)} %get-tuple-element.59), channel_id=1, source_target_pairs={{0,8},{8,16},{16,24},{24,0},{1,9},{9,17},{17,25},{25,1},{2,10},{10... | collective-permute-start | bytes 313352 | tf_op jit(solution)/shard_map/ppermute | solution.py:650
  21.3 5.4 %collective-permute-start.7 = (f32[3,68,128]{2,1,0:T(8,128)S(1)}, f32[3,68,128]{2,1,0:T(8,128)S(1)}, u32[]{:S(2)}, u32[]{:S(2)}) collective-permute-start(f32[3,68,128]{2,1,0:T(8,128)S(1)} %get-tuple-element.60), channel_id=1, source_target_pairs={{8,0},{16,8},{24,16},{0,24},{9,1},{17,9},{25,17},{1,25},{10,2},{18... | collective-permute-start | bytes 313352 | tf_op jit(solution)/shard_map/ppermute | solution.py:650
  24.9 3.1 %collective-permute-start.8 = (f32[3,4,128]{2,1,0:T(4,128)S(1)}, f32[3,4,128]{2,1,0:T(4,128)S(1)}, u32[]{:S(2)}, u32[]{:S(2)}) collective-permute-start(f32[3,4,128]{2,1,0:T(4,128)S(1)} %get-tuple-element.61), channel_id=1, source_target_pairs={{0,8},{8,16},{16,24},{24,0},{1,9},{9,17},{17,25},{25,1},{2,10},{10... | collective-permute-start | bytes 18440 | tf_op jit(solution)/shard_map/ppermute | solution.py:650
  25.3 2.7 %collective-permute-start.9 = (f32[3,4,128]{2,1,0:T(4,128)S(1)}, f32[3,4,128]{2,1,0:T(4,128)S(1)}, u32[]{:S(2)}, u32[]{:S(2)}) collective-permute-start(f32[3,4,128]{2,1,0:T(4,128)S(1)} %get-tuple-element.62), channel_id=1, source_target_pairs={{8,0},{16,8},{24,16},{0,24},{9,1},{17,9},{25,17},{1,25},{10,2},{18... | collective-permute-start | bytes 18440 | tf_op jit(solution)/shard_map/ppermute | solution.py:650
  28.0 10.7 %copy-start.2 = (s32[4,3840]{1,0:T(4,128)S(1)}, s32[4,3840]{1,0:T(4,128)}, u32[]{:S(2)}) copy-start(s32[4,3840]{1,0:T(4,128)} %param.17) | copy-start | bytes 184324
  30.6 15.9 %all-to-all-start = ((f32[32,8,128]{2,1,0:T(8,128)}), f32[32,8,128]{2,1,0:T(8,128)S(1)}, u32[]{:S(2)}, u32[]{:S(2)}) async-start(f32[32,8,128]{2,1,0:T(8,128)} %bitcast.2), calls=%async_computation | async-start | bytes 262144 | tf_op jit(solution)/shard_map/all_to_all | solution.py:633
  46.4 5.6 %collective-permute-start.12 = (f32[4,8,128]{2,1,0:T(8,128)S(1)}, f32[4,8,128]{2,1,0:T(8,128)S(1)}, u32[]{:S(2)}, u32[]{:S(2)}) collective-permute-start(f32[4,8,128]{2,1,0:T(8,128)S(1)} %bitcast_reduce_fusion.refs_0_), channel_id=1, source_target_pairs={{0,6},{2,4},{4,2},{6,0},{1,7},{3,5},{5,3},{7,1},{8,14},{10,12},{12... | collective-permute-start | bytes 49160 | tf_op jit(solution)/shard_map/ppermute | solution.py:626
  47.9 4.9 %collective-permute-start.11 = (f32[4,8,128]{2,1,0:T(8,128)S(1)}, f32[4,8,128]{2,1,0:T(8,128)S(1)}, u32[]{:S(2)}, u32[]{:S(2)}) collective-permute-start(f32[4,8,128]{2,1,0:T(8,128)S(1)} %bitcast_reduce_fusion.refs_0_), channel_id=1, source_target_pairs={{0,4},{2,6},{4,0},{6,2},{1,5},{3,7},{5,1},{7,3},{8,12},{10,14},{12... | collective-permute-start | bytes 49160 | tf_op jit(solution)/shard_map/ppermute | solution.py:626
  49.0 3.8 %collective-permute-start.10 = (f32[4,8,128]{2,1,0:T(8,128)S(1)}, f32[4,8,128]{2,1,0:T(8,128)S(1)}, u32[]{:S(2)}, u32[]{:S(2)}) collective-permute-start(f32[4,8,128]{2,1,0:T(8,128)S(1)} %bitcast_reduce_fusion.refs_0_), channel_id=1, source_target_pairs={{0,2},{2,0},{4,6},{6,4},{1,3},{3,1},{5,7},{7,5},{8,10},{10,8},{12,... | collective-permute-start | bytes 49160 | tf_op jit(solution)/shard_map/ppermute | solution.py:626

commit v11 on v10

--- a/solution.py
+++ b/solution.py
@@ -367,9 +367,7 @@
                 store_rims(first_ref, last_ref, done + s, j, xt, strips - 1, value)
 
 
-def highest_kernel(
-    here_ref, above_ref, mf_ref, cy_ref, code_ref, done_ref, out_ref, first_ref, last_ref
-):
+def highest_kernel(here_ref, above_ref, mf_ref, cy_ref, code_ref, out_ref, first_ref, last_ref):
     sectors, tiles, columns, _ = here_ref.shape
     strips = columns // ROWS
     top = mf_ref.shape[0] - 1
@@ -575,50 +573,53 @@
             send(k, i).wait()
 
 
-def scatter_kernel(cells_ref, *refs):
+def low_kernel(turned_ref, low_ref):
+    count = low_ref.shape[0]
+    iota = lax.broadcasted_iota(jnp.int32, (LANES, LANES), 1)
+    for line in range(count):
+        low = jnp.bitwise_and(turned_ref[:, line : line + 1], LANES - 1)
+        low_ref[line] = jnp.where(low == iota, 1.0, 0.0).astype(jnp.bfloat16)
+
+
+def scatter_kernel(cells_ref, low_ref, *refs):
     *value_refs, out_ref = refs
     rows, lanes = out_ref.shape
     group, owners, depth, _ = cells_ref.shape
+    each = owners * depth
     rank = lax.axis_index("lev")
     half = jnp.bfloat16
-    zero, one = jnp.zeros((), half), jnp.ones((), half)
-    tall, short = 2 * lanes, lanes // 2
-    iota = lax.broadcasted_iota(jnp.int32, (tall, lanes), 0).astype(jnp.float32).astype(half)
-    total = jnp.zeros((2 * short, tall), jnp.float32)
-    lines = [(i, o, r) for i in range(group) for o in range(owners) for r in range(depth)]
-    wide = 4
-
-    def spread(row, count):
-        return jnp.broadcast_to(row, (count, lanes)).astype(half)
-
-    for start in range(0, len(lines), wide):
-        lefts, rights = [], []
-        for part, owner, line in lines[start : start + wide]:
-            cells = cells_ref[jnp.bitwise_xor(rank, part), owner, line : line + 1, :]
-            value = value_refs[part][owner, line : line + 1, :]
-            coarse = value.astype(half).astype(jnp.float32)
-            high = jnp.right_shift(cells, 8).astype(jnp.float32)
-            low = jnp.bitwise_and(cells, 255).astype(jnp.float32)
-            high = spread(high, short) == iota[:short]
-            lefts.append(
-                jnp.concatenate(
-                    [
-                        jnp.where(high, spread(coarse, short), zero),
-                        jnp.where(high, spread(value - coarse, short), zero),
-                    ],
-                    axis=0,
+    zero = jnp.zeros((), half)
+    iota = lax.broadcasted_iota(jnp.int32, (lanes, lanes), 0).astype(jnp.float32).astype(half)
+    total = jnp.zeros((2 * lanes, lanes), jnp.float32)
+    wide = 8
+
+    def spread(row):
+        return jnp.broadcast_to(row, (lanes, lanes)).astype(half)
+
+    for part in range(group):
+        piece = jnp.bitwise_xor(rank, part)
+        for start in range(0, each, wide):
+            lefts = []
+            for place in range(start, start + wide):
+                owner, line = divmod(place, depth)
+                cells = cells_ref[piece, owner, line : line + 1, :]
+                value = value_refs[part][owner, line : line + 1, :]
+                coarse = value.astype(half).astype(jnp.float32)
+                high = spread(jnp.right_shift(cells, 7).astype(jnp.float32)) == iota
+                lefts.append(
+                    jnp.concatenate(
+                        [
+                            jnp.where(high, spread(coarse), zero),
+                            jnp.where(high, spread(value - coarse), zero),
+                        ],
+                        axis=0,
+                    )
                 )
+            low = low_ref[pl.ds(piece * each + start, wide)].reshape(wide * lanes, lanes)
+            total += jnp.dot(
+                jnp.concatenate(lefts, axis=1), low, preferred_element_type=jnp.float32
             )
-            rights.append(jnp.where(spread(low, tall) == iota, one, zero))
-        total += lax.dot_general(
-            jnp.concatenate(lefts, axis=1),
-            jnp.concatenate(rights, axis=1),
-            (((1,), (1,)), ((), ())),
-            preferred_element_type=jnp.float32,
-        )
-    total = total[:short] + total[short:]
-    for i in range(2):
-        out_ref[pl.ds(i, rows // 2, stride=2), :] = total[: rows // 2, i * lanes : (i + 1) * lanes]
+    out_ref[...] = total[:rows] + total[lanes : lanes + rows]
 
 
 def exchanged(value, axis, apart):
@@ -634,11 +635,20 @@
         sent, ("tile", "lev", "sec"), split_axis=0, concat_axis=0, tiled=True
     )
     own = jnp.sum(arrived.reshape(owners, group * copies, depth, LANES), axis=1)
-    parts = [own] + [exchanged(own, "lev", d) for d in range(1, group)]
+    arrived = [exchanged(own, "lev", d) for d in range(group - 1, 0, -1)]
+    parts = [own, *reversed(arrived)]
     cells = jnp.pad(flux_cell, ((0, 0), (0, group * depth * LANES - share)))
     cells = cells.reshape(owners, group, depth, LANES).transpose(1, 0, 2, 3)
+    lines = cells.size // LANES
+    low = call(
+        low_kernel,
+        pltpu.VMEM((lines, LANES, LANES), jnp.bfloat16),
+        [VM],
+        VM,
+        (cells.reshape(lines, LANES).T,),
+    )
     out = call(
-        scatter_kernel, f32(FL_DEV // LANES, LANES), [VM] * (group + 1), VM, (cells, *parts)
+        scatter_kernel, f32(FL_DEV // LANES, LANES), [VM] * (group + 2), VM, (cells, low, *parts)
     )
     return out.reshape(-1)
 
@@ -738,6 +748,15 @@
         [pltpu.VMEM((tiles, sectors, LANES), jnp.float32)] * 2,
     )
     left, right = around(first, last)
+    vt, first_top, last_top = call(
+        highest_kernel,
+        (field_top, rim_top, rim_top),
+        [VM] * 5,
+        [VM] * 3,
+        (top, above, mass_flux, courant_y, limiter_code),
+    )
+    left_top, right_top = around(first_top, last_top)
+
     owners, share = flux_cell.shape
     group, copies = lax.axis_size("lev"), lax.axis_size("sec")
     depth = -(-share // (group * LANES))
@@ -752,15 +771,6 @@
         (inner, outer, vs, courant_x, limiter_code, weight, sector_share),
         [stage, pltpu.SemaphoreType.DMA((levels,))],
     )
-    vt, first_top, last_top = call(
-        highest_kernel,
-        (field_top, rim_top, rim_top),
-        [VM] * 6,
-        [VM] * 3,
-        (top, above, mass_flux, courant_y, limiter_code, inner_sens),
-    )
-    left_top, right_top = around(first_top, last_top)
-
     adjoint, pieces = call(
         outer_final_kernel,
         (f32(*forcing.shape), f32(*packed) if aligned else f32(columns, width)),

time: 56.5 us -> 55.1 us (0.975)
  starting transfers between devices: 23.4 us -> 21.1 us
  Pallas kernels: 20.3 us -> 22.2 us
  waiting for transfers between devices: 11.7 us -> 10.5 us
    all_to_all x1, starting transfers between devices: 8.12 us -> 5.79 us  [remapped(): lax.all_to_all(sent, ('tile', 'lev', 'sec'), split_axis=0, concat_axis=0,...]
    ppermute x2, waiting for transfers between devices: 0.46 us -> 2.52 us  [from_above(): return lax.ppermute(value, 'lev', [(i + 1, i) for i in range(count - 1)])]
    pallas_call x10 -> x11, Pallas kernels: 20.3 us -> 22.2 us  [call(): pl.pallas_call(kernel, out_shape=out_shape, in_specs=in_specs, out_specs=...]
    ppermute x3, waiting for transfers between devices: 1.88 us -> 0.01 us  [exchanged(): return lax.ppermute(value, axis, [(i, i ^ apart) for i in range(count)])]
    ppermute x8, waiting for transfers between devices: 1.6 us -> 0.26 us  [around(): return (lax.ppermute(last, 'tile', up), lax.ppermute(first, 'tile', down))]
  transfers between devices with their start and end apart: 14 -> 14, of which waited for: 7 -> 4; matrix products, arithmetic and copies ran while one was open for 0% -> 0% of each run, Pallas kernels for 21% -> 26%
where the time goes in v11:
time: 55.1 us; the launch traced here: 54.9 us
  Pallas kernels  22.2 us (40%)
  starting transfers between devices  21.1 us (38%)
  waiting for transfers between devices  10.5 us (19%)
  between operations  0.89 us (2%)
    pallas_call x11, Pallas kernels, call(): pl.pallas_call(kernel, out_shape=out_shape, in_specs=in_specs, out_specs=...  22.2 us
    ppermute x8, starting transfers between devices, around(): return (lax.ppermute(last, 'tile', up), lax.ppermute(first, 'tile', down))  8.11 us
    all_to_all x1, waiting for transfers between devices, remapped(): lax.all_to_all(sent, ('tile', 'lev', 'sec'), split_axis=0, concat_axis=0,...  7.71 us
    all_to_all x1, starting transfers between devices, remapped(): lax.all_to_all(sent, ('tile', 'lev', 'sec'), split_axis=0, concat_axis=0,...  5.79 us
    ppermute x3, starting transfers between devices, exchanged(): return lax.ppermute(value, axis, [(i, i ^ apart) for i in range(count)])  4.45 us
    ppermute x2, starting transfers between devices, from_above(): return lax.ppermute(value, 'lev', [(i + 1, i) for i in range(count - 1)])  2.72 us
    ppermute x2, waiting for transfers between devices, from_above(): return lax.ppermute(value, 'lev', [(i + 1, i) for i in range(count - 1)])  2.52 us
  transfers between devices with their start and end apart: 14, of which 4 were waited for; matrix products, arithmetic and copies ran while one was open for 0% of the time, Pallas kernels for 26%

profile of v11, /device:TPU:0, one launch (start us, length us, event | category | flops | bytes accessed | tf_op | source)
XLA Modules:
  0.0 54.9 jit_solution(12534158445404025253)
XLA Ops:
  0.6 2.0 %shard_map.104 = (f32[4,40,384]{2,1,0:T(8,128)S(1)}, bf16[18,40,384]{2,1,0:T(8,128)(2,1)S(1)}, bf16[18,40,384]{2,1,0:T(8,128)(2,1)S(1)}, s32[18,40,384]{2,1,0:T(8,128)S(1)}, bf16[18,40,384]{2,1,0:T(8,128)(2,1)S(1)}) custom-call(f32[4,18,40,384]{3,2,1,0:T(8,128)} %f_ref.1, bf16[18,40,384]{2,1,0:T(8,128)(2,1)} %mf_hbm.1, bf16[18,40,384]{2,1,0:T(8,128)(2,1)} %cy_hbm.1, ...), custom_call_target="tpu_custom_call" | custom-call | flops 1 | bytes 1 | tf_op jit(solution)/shard_map/pallas_call | solution.py:19
  2.7 1.4 %collective-permute-start.2 = (f32[4,40,384]{2,1,0:T(8,128)S(1)}, f32[4,40,384]{2,1,0:T(8,128)S(1)}, u32[]{:S(2)}, u32[]{:S(2)}) collective-permute-start(f32[4,40,384]{2,1,0:T(8,128)S(1)} %get-tuple-element.46), channel_id=1, source_target_pairs={{2,0},{4,2},{6,4},{3,1},{5,3},{7,5},{10,8},{12,10},{14,12},{11,9},... | collective-permute-start | bytes 737288 | tf_op jit(solution)/shard_map/ppermute | solution.py:665
  4.1 3.5 %shard_map.105 = (f32[17,4,3,56,128]{4,3,2,1,0:T(8,128)S(1)}, f32[3,68,128]{2,1,0:T(8,128)S(1)}, f32[3,68,128]{2,1,0:T(8,128)S(1)}, f32[4,40,384]{2,1,0:T(8,128)S(1)}) custom-call(f32[4,18,40,384]{3,2,1,0:T(8,128)S(1)} %copy-done, bf16[18,40,384]{2,1,0:T(8,128)(2,1)S(1)} %get-tuple-element.35.mf_ref, bf16[18,40,384]{2,1,0:T(8,128)(2,1)S(1)} %get-tuple-element.36.cy_ref, ...), custom_call_target="tpu_custom_call" | custom-call | flops 1 | bytes 1 | tf_op jit(solution)/shard_map/pallas_call | solution.py:19
  7.6 0.5 collective-permute-start
  8.1 2.0 %collective-permute-start.1 = (f32[3,68,128]{2,1,0:T(8,128)S(1)}, f32[3,68,128]{2,1,0:T(8,128)S(1)}, u32[]{:S(2)}, u32[]{:S(2)}) collective-permute-start(f32[3,68,128]{2,1,0:T(8,128)S(1)} %get-tuple-element.43), channel_id=1, source_target_pairs={{8,0},{16,8},{24,16},{0,24},{9,1},{17,9},{25,17},{1,25},{10,2},{18... | collective-permute-start | bytes 313352 | tf_op jit(solution)/shard_map/ppermute | solution.py:660
  10.1 3.1 %shard_map.106 = (f32[16,4,3,56,128]{4,3,2,1,0:T(8,128)S(1)}, f32[4,3,40,128]{3,2,1,0:T(8,128)S(1)}, f32[4,3,40,128]{3,2,1,0:T(8,128)S(1)}) custom-call(f32[17,4,3,56,128]{4,3,2,1,0:T(8,128)S(1)} %get-tuple-element.38.v_ref, bf16[18,40,384]{2,1,0:T(8,128)(2,1)S(1)} %get-tuple-element.39.cx_ref, bf16[18,40,384]{2,1,0:T(8,128)(2,1)S(1)} %get-tuple-element.35.mf_ref, ...), custom_call_target="tpu_custom_call" | custom-call | flops 1 | bytes 1 | tf_op jit(solution)/shard_map/pallas_call | solution.py:19
  13.2 0.2 collective-permute-done.1.right_ref
  13.5 0.2 collective-permute-done.2.above_ref
  13.7 0.1 broadcast_in_dim.4.seam_ref
  13.8 0.2 shard_map.107
  14.0 1.3 %collective-permute-start.5 = (f32[4,40,384]{2,1,0:T(8,128)S(1)}, f32[4,40,384]{2,1,0:T(8,128)S(1)}, u32[]{:S(2)}, u32[]{:S(2)}) collective-permute-start(f32[4,40,384]{2,1,0:T(8,128)S(1)} %get-tuple-element.47.lowest_ref), channel_id=1, source_target_pairs={{2,0},{4,2},{6,4},{3,1},{5,3},{7,5},{10,8},{12,10},{14,12},{11,9},... | collective-permute-start | bytes 737288 | tf_op jit(solution)/shard_map/ppermute | solution.py:665
  15.3 1.3 %collective-permute-start.3 = (f32[3,4,128]{2,1,0:T(4,128)S(1)}, f32[3,4,128]{2,1,0:T(4,128)S(1)}, u32[]{:S(2)}, u32[]{:S(2)}) collective-permute-start(f32[3,4,128]{2,1,0:T(4,128)S(1)} %get-tuple-element.50), channel_id=1, source_target_pairs={{0,8},{8,16},{16,24},{24,0},{1,9},{9,17},{17,25},{25,1},{2,10},{10... | collective-permute-start | bytes 18440 | tf_op jit(solution)/shard_map/ppermute | solution.py:660
  16.6 0.8 %collective-permute-start.4 = (f32[3,4,128]{2,1,0:T(4,128)S(1)}, f32[3,4,128]{2,1,0:T(4,128)S(1)}, u32[]{:S(2)}, u32[]{:S(2)}) collective-permute-start(f32[3,4,128]{2,1,0:T(4,128)S(1)} %get-tuple-element.51), channel_id=1, source_target_pairs={{8,0},{16,8},{24,16},{0,24},{9,1},{17,9},{25,17},{1,25},{10,2},{18... | collective-permute-start | bytes 18440 | tf_op jit(solution)/shard_map/ppermute | solution.py:660
  17.3 2.9 %shard_map.108 = (f32[16,4,3,56,128]{4,3,2,1,0:T(8,128)S(1)}, f32[3,64,128]{2,1,0:T(8,128)S(1)}, f32[3,64,128]{2,1,0:T(8,128)S(1)}, f32[4,3,40,128]{3,2,1,0:T(8,128)S(1)}) custom-call(f32[17,4,3,56,128]{4,3,2,1,0:T(8,128)S(1)} %get-tuple-element.38.v_ref, f32[4,3,40,128]{3,2,1,0:T(8,128)S(1)} %get-tuple-element.41.inner_top_ref, ...), custom_call_target="tpu_custom_call" | custom-call | flops 1 | bytes 1 | tf_op jit(solution)/shard_map/pallas_call | solution.py:19
  20.3 0.2 shard_map.109
  20.6 0.8 %collective-permute-start.6 = (f32[3,68,128]{2,1,0:T(8,128)S(1)}, f32[3,68,128]{2,1,0:T(8,128)S(1)}, u32[]{:S(2)}, u32[]{:S(2)}) collective-permute-start(f32[3,68,128]{2,1,0:T(8,128)S(1)} %get-tuple-element.58), channel_id=1, source_target_pairs={{0,8},{8,16},{16,24},{24,0},{1,9},{9,17},{17,25},{25,1},{2,10},{10... | collective-permute-start | bytes 313352 | tf_op jit(solution)/shard_map/ppermute | solution.py:660
  21.3 1.0 %collective-permute-start.7 = (f32[3,68,128]{2,1,0:T(8,128)S(1)}, f32[3,68,128]{2,1,0:T(8,128)S(1)}, u32[]{:S(2)}, u32[]{:S(2)}) collective-permute-start(f32[3,68,128]{2,1,0:T(8,128)S(1)} %get-tuple-element.59), channel_id=1, source_target_pairs={{8,0},{16,8},{24,16},{0,24},{9,1},{17,9},{25,17},{1,25},{10,2},{18... | collective-permute-start | bytes 313352 | tf_op jit(solution)/shard_map/ppermute | solution.py:660
  22.4 2.3 %collective-permute-done.5.above_ref = f32[4,40,384]{2,1,0:T(8,128)S(1)} collective-permute-done((f32[4,40,384]{2,1,0:T(8,128)S(1)}, f32[4,40,384]{2,1,0:T(8,128)S(1)}, u32[]{:S(2)}, u32[]{:S(2)}) %collective-permute-start.5) | collective-permute-done | bytes 245792 | tf_op jit(solution)/shard_map/ppermute | solution.py:665
  24.7 0.2 shard_map.110
  24.9 0.4 collective-permute-start.8
  25.3 1.3 %collective-permute-start.9 = (f32[3,4,128]{2,1,0:T(4,128)S(1)}, f32[3,4,128]{2,1,0:T(4,128)S(1)}, u32[]{:S(2)}, u32[]{:S(2)}) collective-permute-start(f32[3,4,128]{2,1,0:T(4,128)S(1)} %get-tuple-element.61), channel_id=1, source_target_pairs={{8,0},{16,8},{24,16},{0,24},{9,1},{17,9},{25,17},{1,25},{10,2},{18... | collective-permute-start | bytes 18440 | tf_op jit(solution)/shard_map/ppermute | solution.py:660
  26.7 0.1 broadcast_in_dim.5.weight_ref
  26.7 2.0 %shard_map.111 = (f32[4,18,40,384]{3,2,1,0:T(8,128)}, f32[40,384]{1,0:T(8,128)S(1)}) custom-call(f32[16,4,3,56,128]{4,3,2,1,0:T(8,128)S(1)} %get-tuple-element.40.inner_ref, f32[16,4,3,56,128]{4,3,2,1,0:T(8,128)S(1)} %get-tuple-element.48.outer_ref, f32[4,3,56,128]{3,2,1,0:T(8,128)S(1)} %get-tuple-element.55.vs_ref, ...), custom_call_target="tpu_custom_call" | custom-call | flops 1 | bytes 1 | tf_op jit(solution)/shard_map/pallas_call | solution.py:19
  28.8 2.5 %shard_map.112 = (f32[4,18,40,384]{3,2,1,0:T(8,128)}, f32[4,4,2,8,128]{4,3,2,1,0:T(8,128)}) custom-call(f32[16,4,3,56,128]{4,3,2,1,0:T(8,128)S(1)} %get-tuple-element.40.inner_ref, f32[16,4,3,56,128]{4,3,2,1,0:T(8,128)S(1)} %get-tuple-element.48.outer_ref, f32[4,3,56,128]{3,2,1,0:T(8,128)S(1)} %get-tuple-element.55.vs_ref, ...), custom_call_target="tpu_custom_call", output_to_operand_aliasing={{0}: (14, {})} | custom-call | flops 1 | bytes 1 | tf_op jit(solution)/shard_map/pallas_call | solution.py:19
  31.4 5.8 %all-to-all-start = ((f32[32,8,128]{2,1,0:T(8,128)}), f32[32,8,128]{2,1,0:T(8,128)S(1)}, u32[]{:S(2)}, u32[]{:S(2)}) async-start(f32[32,8,128]{2,1,0:T(8,128)} %bitcast.4), calls=%async_computation | async-start | bytes 262144 | tf_op jit(solution)/shard_map/all_to_all | solution.py:634
  37.2 7.7 %all-to-all-done = f32[32,8,128]{2,1,0:T(8,128)S(1)} async-done(((f32[32,8,128]{2,1,0:T(8,128)}), f32[32,8,128]{2,1,0:T(8,128)S(1)}, u32[]{:S(2)}, u32[]{:S(2)}) %all-to-all-start) | async-done | bytes 131104 | tf_op jit(solution)/shard_map/all_to_all | solution.py:634
  44.9 1.4 %collective-permute-start.12 = (f32[4,8,128]{2,1,0:T(8,128)S(1)}, f32[4,8,128]{2,1,0:T(8,128)S(1)}, u32[]{:S(2)}, u32[]{:S(2)}) collective-permute-start(f32[4,8,128]{2,1,0:T(8,128)S(1)} %bitcast_reduce_fusion.refs_0_), channel_id=1, source_target_pairs={{0,6},{2,4},{4,2},{6,0},{1,7},{3,5},{5,3},{7,1},{8,14},{10,12},{12... | collective-permute-start | bytes 49160 | tf_op jit(solution)/shard_map/ppermute | solution.py:627
  46.3 1.1 %collective-permute-start.11 = (f32[4,8,128]{2,1,0:T(8,128)S(1)}, f32[4,8,128]{2,1,0:T(8,128)S(1)}, u32[]{:S(2)}, u32[]{:S(2)}) collective-permute-start(f32[4,8,128]{2,1,0:T(8,128)S(1)} %bitcast_reduce_fusion.refs_0_), channel_id=1, source_target_pairs={{0,4},{2,6},{4,0},{6,2},{1,5},{3,7},{5,1},{7,3},{8,12},{10,14},{12... | collective-permute-start | bytes 49160 | tf_op jit(solution)/shard_map/ppermute | solution.py:627
  47.5 1.9 %collective-permute-start.10 = (f32[4,8,128]{2,1,0:T(8,128)S(1)}, f32[4,8,128]{2,1,0:T(8,128)S(1)}, u32[]{:S(2)}, u32[]{:S(2)}) collective-permute-start(f32[4,8,128]{2,1,0:T(8,128)S(1)} %bitcast_reduce_fusion.refs_0_), channel_id=1, source_target_pairs={{0,2},{2,0},{4,6},{6,4},{1,3},{3,1},{5,7},{7,5},{8,10},{10,8},{12,... | collective-permute-start | bytes 49160 | tf_op jit(solution)/shard_map/ppermute | solution.py:627
  49.4 0.1 copy.14
  49.5 2.4 %shard_map.113.low_ref = bf16[128,128,128]{2,1,0:T(8,128)(2,1)S(1)} custom-call(s32[128,128]{1,0:T(8,128)S(1)} %bitcast.16), custom_call_target="tpu_custom_call" | custom-call | flops 1 | bytes 1 | tf_op jit(solution)/shard_map/pallas_call | solution.py:19
  51.9 3.0 %shard_map.114 = f32[120,128]{1,0:T(8,128)} custom-call(s32[4,4,8,128]{3,2,1,0:T(8,128)S(1)} %get-tuple-element.69.cells_ref, bf16[128,128,128]{2,1,0:T(8,128)(2,1)S(1)} %shard_map.113.low_ref, f32[4,8,128]{2,1,0:T(8,128)S(1)} %bitcast_reduce_fusion.refs_0_, f32[4,8,128]{2,1,0:T(8,128)S(1)} %collective-permute-done.10.refs_1_, ...), custom_call_target="tpu_custom_call" | custom-call | flops 1 | bytes 1 | tf_op jit(solution)/shard_map/pallas_call | solution.py:19
  (23 shorter events, 0.1 us)
Async XLA Ops:
  0.6 3.5 %copy-start = (f32[4,18,40,384]{3,2,1,0:T(8,128)S(1)}, f32[4,18,40,384]{3,2,1,0:T(8,128)}, u32[]{:S(2)}) copy-start(f32[4,18,40,384]{3,2,1,0:T(8,128)} %f_ref.1) | copy-start | bytes 13271044
  2.7 11.0 %collective-permute-start.2 = (f32[4,40,384]{2,1,0:T(8,128)S(1)}, f32[4,40,384]{2,1,0:T(8,128)S(1)}, u32[]{:S(2)}, u32[]{:S(2)}) collective-permute-start(f32[4,40,384]{2,1,0:T(8,128)S(1)} %get-tuple-element.46), channel_id=1, source_target_pairs={{2,0},{4,2},{6,4},{3,1},{5,3},{7,5},{10,8},{12,10},{14,12},{11,9},... | collective-permute-start | bytes 737288 | tf_op jit(solution)/shard_map/ppermute | solution.py:665
  7.6 6.1 %copy-start.3 = (s32[4,2]{0,1:T(2,128)S(1)}, s32[4,2]{0,1:T(2,128)}, u32[]{:S(2)}) copy-start(s32[4,2]{0,1:T(2,128)} %param.14) | copy-start | bytes 100
  7.6 5.6 %collective-permute-start = (f32[3,68,128]{2,1,0:T(8,128)S(1)}, f32[3,68,128]{2,1,0:T(8,128)S(1)}, u32[]{:S(2)}, u32[]{:S(2)}) collective-permute-start(f32[3,68,128]{2,1,0:T(8,128)S(1)} %get-tuple-element.42), channel_id=1, source_target_pairs={{0,8},{8,16},{16,24},{24,0},{1,9},{9,17},{17,25},{25,1},{2,10},{10... | collective-permute-start | bytes 313352 | tf_op jit(solution)/shard_map/ppermute | solution.py:660
  8.1 5.4 %collective-permute-start.1 = (f32[3,68,128]{2,1,0:T(8,128)S(1)}, f32[3,68,128]{2,1,0:T(8,128)S(1)}, u32[]{:S(2)}, u32[]{:S(2)}) collective-permute-start(f32[3,68,128]{2,1,0:T(8,128)S(1)} %get-tuple-element.43), channel_id=1, source_target_pairs={{8,0},{16,8},{24,16},{0,24},{9,1},{17,9},{25,17},{1,25},{10,2},{18... | collective-permute-start | bytes 313352 | tf_op jit(solution)/shard_map/ppermute | solution.py:660
  14.0 10.7 %collective-permute-start.5 = (f32[4,40,384]{2,1,0:T(8,128)S(1)}, f32[4,40,384]{2,1,0:T(8,128)S(1)}, u32[]{:S(2)}, u32[]{:S(2)}) collective-permute-start(f32[4,40,384]{2,1,0:T(8,128)S(1)} %get-tuple-element.47.lowest_ref), channel_id=1, source_target_pairs={{2,0},{4,2},{6,4},{3,1},{5,3},{7,5},{10,8},{12,10},{14,12},{11,9},... | collective-permute-start | bytes 737288 | tf_op jit(solution)/shard_map/ppermute | solution.py:665
  15.3 5.0 %collective-permute-start.3 = (f32[3,4,128]{2,1,0:T(4,128)S(1)}, f32[3,4,128]{2,1,0:T(4,128)S(1)}, u32[]{:S(2)}, u32[]{:S(2)}) collective-permute-start(f32[3,4,128]{2,1,0:T(4,128)S(1)} %get-tuple-element.50), channel_id=1, source_target_pairs={{0,8},{8,16},{16,24},{24,0},{1,9},{9,17},{17,25},{25,1},{2,10},{10... | collective-permute-start | bytes 18440 | tf_op jit(solution)/shard_map/ppermute | solution.py:660
  16.6 3.7 %collective-permute-start.4 = (f32[3,4,128]{2,1,0:T(4,128)S(1)}, f32[3,4,128]{2,1,0:T(4,128)S(1)}, u32[]{:S(2)}, u32[]{:S(2)}) collective-permute-start(f32[3,4,128]{2,1,0:T(4,128)S(1)} %get-tuple-element.51), channel_id=1, source_target_pairs={{8,0},{16,8},{24,16},{0,24},{9,1},{17,9},{25,17},{1,25},{10,2},{18... | collective-permute-start | bytes 18440 | tf_op jit(solution)/shard_map/ppermute | solution.py:660
  20.3 6.4 %copy-start.4 = (f32[18]{0:T(128)S(1)}, f32[18]{0:T(128)}, u32[]{:S(2)}) copy-start(f32[18]{0:T(128)} %param.15) | copy-start | bytes 220
  20.3 6.5 %copy-start.1 = (f32[4,40,384]{2,1,0:T(8,128)S(1)}, f32[4,40,384]{2,1,0:T(8,128)}, u32[]{:S(2)}) copy-start(f32[4,40,384]{2,1,0:T(8,128)} %share_ref.3) | copy-start | bytes 737284
  20.6 8.2 %collective-permute-start.6 = (f32[3,68,128]{2,1,0:T(8,128)S(1)}, f32[3,68,128]{2,1,0:T(8,128)S(1)}, u32[]{:S(2)}, u32[]{:S(2)}) collective-permute-start(f32[3,68,128]{2,1,0:T(8,128)S(1)} %get-tuple-element.58), channel_id=1, source_target_pairs={{0,8},{8,16},{16,24},{24,0},{1,9},{9,17},{17,25},{25,1},{2,10},{10... | collective-permute-start | bytes 313352 | tf_op jit(solution)/shard_map/ppermute | solution.py:660
  21.3 7.5 %collective-permute-start.7 = (f32[3,68,128]{2,1,0:T(8,128)S(1)}, f32[3,68,128]{2,1,0:T(8,128)S(1)}, u32[]{:S(2)}, u32[]{:S(2)}) collective-permute-start(f32[3,68,128]{2,1,0:T(8,128)S(1)} %get-tuple-element.59), channel_id=1, source_target_pairs={{8,0},{16,8},{24,16},{0,24},{9,1},{17,9},{25,17},{1,25},{10,2},{18... | collective-permute-start | bytes 313352 | tf_op jit(solution)/shard_map/ppermute | solution.py:660
  24.9 3.9 %collective-permute-start.8 = (f32[3,4,128]{2,1,0:T(4,128)S(1)}, f32[3,4,128]{2,1,0:T(4,128)S(1)}, u32[]{:S(2)}, u32[]{:S(2)}) collective-permute-start(f32[3,4,128]{2,1,0:T(4,128)S(1)} %get-tuple-element.60), channel_id=1, source_target_pairs={{0,8},{8,16},{16,24},{24,0},{1,9},{9,17},{17,25},{25,1},{2,10},{10... | collective-permute-start | bytes 18440 | tf_op jit(solution)/shard_map/ppermute | solution.py:660
  25.3 3.5 %collective-permute-start.9 = (f32[3,4,128]{2,1,0:T(4,128)S(1)}, f32[3,4,128]{2,1,0:T(4,128)S(1)}, u32[]{:S(2)}, u32[]{:S(2)}) collective-permute-start(f32[3,4,128]{2,1,0:T(4,128)S(1)} %get-tuple-element.61), channel_id=1, source_target_pairs={{8,0},{16,8},{24,16},{0,24},{9,1},{17,9},{25,17},{1,25},{10,2},{18... | collective-permute-start | bytes 18440 | tf_op jit(solution)/shard_map/ppermute | solution.py:660
  28.8 8.4 %copy-start.2 = (s32[4,3840]{1,0:T(4,128)S(1)}, s32[4,3840]{1,0:T(4,128)}, u32[]{:S(2)}) copy-start(s32[4,3840]{1,0:T(4,128)} %param.17) | copy-start | bytes 184324
  31.4 13.5 %all-to-all-start = ((f32[32,8,128]{2,1,0:T(8,128)}), f32[32,8,128]{2,1,0:T(8,128)S(1)}, u32[]{:S(2)}, u32[]{:S(2)}) async-start(f32[32,8,128]{2,1,0:T(8,128)} %bitcast.4), calls=%async_computation | async-start | bytes 262144 | tf_op jit(solution)/shard_map/all_to_all | solution.py:634
  44.9 7.0 %collective-permute-start.12 = (f32[4,8,128]{2,1,0:T(8,128)S(1)}, f32[4,8,128]{2,1,0:T(8,128)S(1)}, u32[]{:S(2)}, u32[]{:S(2)}) collective-permute-start(f32[4,8,128]{2,1,0:T(8,128)S(1)} %bitcast_reduce_fusion.refs_0_), channel_id=1, source_target_pairs={{0,6},{2,4},{4,2},{6,0},{1,7},{3,5},{5,3},{7,1},{8,14},{10,12},{12... | collective-permute-start | bytes 49160 | tf_op jit(solution)/shard_map/ppermute | solution.py:627
  46.3 5.6 %collective-permute-start.11 = (f32[4,8,128]{2,1,0:T(8,128)S(1)}, f32[4,8,128]{2,1,0:T(8,128)S(1)}, u32[]{:S(2)}, u32[]{:S(2)}) collective-permute-start(f32[4,8,128]{2,1,0:T(8,128)S(1)} %bitcast_reduce_fusion.refs_0_), channel_id=1, source_target_pairs={{0,4},{2,6},{4,0},{6,2},{1,5},{3,7},{5,1},{7,3},{8,12},{10,14},{12... | collective-permute-start | bytes 49160 | tf_op jit(solution)/shard_map/ppermute | solution.py:627
  47.5 4.5 %collective-permute-start.10 = (f32[4,8,128]{2,1,0:T(8,128)S(1)}, f32[4,8,128]{2,1,0:T(8,128)S(1)}, u32[]{:S(2)}, u32[]{:S(2)}) collective-permute-start(f32[4,8,128]{2,1,0:T(8,128)S(1)} %bitcast_reduce_fusion.refs_0_), channel_id=1, source_target_pairs={{0,2},{2,0},{4,6},{6,4},{1,3},{3,1},{5,7},{7,5},{8,10},{10,8},{12,... | collective-permute-start | bytes 49160 | tf_op jit(solution)/shard_map/ppermute | solution.py:627

commit v12 on v10

--- a/solution.py
+++ b/solution.py
@@ -367,9 +367,7 @@
                 store_rims(first_ref, last_ref, done + s, j, xt, strips - 1, value)
 
 
-def highest_kernel(
-    here_ref, above_ref, mf_ref, cy_ref, code_ref, done_ref, out_ref, first_ref, last_ref
-):
+def highest_kernel(here_ref, above_ref, mf_ref, cy_ref, code_ref, out_ref, first_ref, last_ref):
     sectors, tiles, columns, _ = here_ref.shape
     strips = columns // ROWS
     top = mf_ref.shape[0] - 1
@@ -582,43 +580,40 @@
     rank = lax.axis_index("lev")
     half = jnp.bfloat16
     zero, one = jnp.zeros((), half), jnp.ones((), half)
-    tall, short = 2 * lanes, lanes // 2
-    iota = lax.broadcasted_iota(jnp.int32, (tall, lanes), 0).astype(jnp.float32).astype(half)
-    total = jnp.zeros((2 * short, tall), jnp.float32)
+    iota = lax.broadcasted_iota(jnp.int32, (lanes, lanes), 0).astype(jnp.float32).astype(half)
+    total = jnp.zeros((2 * lanes, lanes), jnp.float32)
     lines = [(i, o, r) for i in range(group) for o in range(owners) for r in range(depth)]
-    wide = 4
-
-    def spread(row, count):
-        return jnp.broadcast_to(row, (count, lanes)).astype(half)
+    wide = 8
+
+    def spread(row):
+        return jnp.broadcast_to(row, (lanes, lanes)).astype(half)
 
     for start in range(0, len(lines), wide):
         lefts, rights = [], []
         for part, owner, line in lines[start : start + wide]:
-            cells = cells_ref[jnp.bitwise_xor(rank, part), owner, line : line + 1, :]
+            piece = jnp.bitwise_xor(rank, (group - part) % group)
+            cells = cells_ref[piece, owner, line : line + 1, :]
             value = value_refs[part][owner, line : line + 1, :]
             coarse = value.astype(half).astype(jnp.float32)
-            high = jnp.right_shift(cells, 8).astype(jnp.float32)
-            low = jnp.bitwise_and(cells, 255).astype(jnp.float32)
-            high = spread(high, short) == iota[:short]
+            high = spread(jnp.right_shift(cells, 7).astype(jnp.float32)) == iota
+            low = spread(jnp.bitwise_and(cells, 127).astype(jnp.float32)) == iota
             lefts.append(
                 jnp.concatenate(
                     [
-                        jnp.where(high, spread(coarse, short), zero),
-                        jnp.where(high, spread(value - coarse, short), zero),
+                        jnp.where(high, spread(coarse), zero),
+                        jnp.where(high, spread(value - coarse), zero),
                     ],
                     axis=0,
                 )
             )
-            rights.append(jnp.where(spread(low, tall) == iota, one, zero))
+            rights.append(jnp.where(low, one, zero))
         total += lax.dot_general(
             jnp.concatenate(lefts, axis=1),
             jnp.concatenate(rights, axis=1),
             (((1,), (1,)), ((), ())),
             preferred_element_type=jnp.float32,
         )
-    total = total[:short] + total[short:]
-    for i in range(2):
-        out_ref[pl.ds(i, rows // 2, stride=2), :] = total[: rows // 2, i * lanes : (i + 1) * lanes]
+    out_ref[...] = total[:rows] + total[lanes : lanes + rows]
 
 
 def exchanged(value, axis, apart):
@@ -634,7 +629,7 @@
         sent, ("tile", "lev", "sec"), split_axis=0, concat_axis=0, tiled=True
     )
     own = jnp.sum(arrived.reshape(owners, group * copies, depth, LANES), axis=1)
-    parts = [own] + [exchanged(own, "lev", d) for d in range(1, group)]
+    parts = [own] + [exchanged(own, "lev", group - d) for d in range(1, group)]
     cells = jnp.pad(flux_cell, ((0, 0), (0, group * depth * LANES - share)))
     cells = cells.reshape(owners, group, depth, LANES).transpose(1, 0, 2, 3)
     out = call(
@@ -738,6 +733,15 @@
         [pltpu.VMEM((tiles, sectors, LANES), jnp.float32)] * 2,
     )
     left, right = around(first, last)
+    vt, first_top, last_top = call(
+        highest_kernel,
+        (field_top, rim_top, rim_top),
+        [VM] * 5,
+        [VM] * 3,
+        (top, above, mass_flux, courant_y, limiter_code),
+    )
+    left_top, right_top = around(first_top, last_top)
+
     owners, share = flux_cell.shape
     group, copies = lax.axis_size("lev"), lax.axis_size("sec")
     depth = -(-share // (group * LANES))
@@ -752,15 +756,6 @@
         (inner, outer, vs, courant_x, limiter_code, weight, sector_share),
         [stage, pltpu.SemaphoreType.DMA((levels,))],
     )
-    vt, first_top, last_top = call(
-        highest_kernel,
-        (field_top, rim_top, rim_top),
-        [VM] * 6,
-        [VM] * 3,
-        (top, above, mass_flux, courant_y, limiter_code, inner_sens),
-    )
-    left_top, right_top = around(first_top, last_top)
-
     adjoint, pieces = call(
         outer_final_kernel,
         (f32(*forcing.shape), f32(*packed) if aligned else f32(columns, width)),

time: 56.5 us -> 55.6 us (0.984)
  starting transfers between devices: 23.4 us -> 21.1 us
  waiting for transfers between devices: 11.7 us -> 13.5 us
  Pallas kernels: 20.3 us -> 19.7 us
    all_to_all x1, starting transfers between devices: 8.12 us -> 5.79 us  [remapped(): lax.all_to_all(sent, ('tile', 'lev', 'sec'), split_axis=0, concat_axis=0,...]
    ppermute x2, waiting for transfers between devices: 0.46 us -> 2.52 us  [from_above(): return lax.ppermute(value, 'lev', [(i + 1, i) for i in range(count - 1)])]
    ppermute x8, waiting for transfers between devices: 1.6 us -> 0.26 us  [around(): return (lax.ppermute(last, 'tile', up), lax.ppermute(first, 'tile', down))]
    ppermute x3, waiting for transfers between devices: 1.88 us -> 3.05 us  [exchanged(): return lax.ppermute(value, axis, [(i, i ^ apart) for i in range(count)])]
  transfers between devices with their start and end apart: 14 -> 14, of which waited for: 7 -> 6; matrix products, arithmetic and copies ran while one was open for 0% -> 0% of each run, Pallas kernels for 21% -> 22%
where the time goes in v12:
time: 55.6 us; the launch traced here: 55.4 us
  starting transfers between devices  21.1 us (38%)
  Pallas kernels  19.7 us (35%)
  waiting for transfers between devices  13.5 us (24%)
  between operations  0.85 us (2%)
    pallas_call x10, Pallas kernels, call(): pl.pallas_call(kernel, out_shape=out_shape, in_specs=in_specs, out_specs=...  19.7 us
    ppermute x8, starting transfers between devices, around(): return (lax.ppermute(last, 'tile', up), lax.ppermute(first, 'tile', down))  8.11 us
    all_to_all x1, waiting for transfers between devices, remapped(): lax.all_to_all(sent, ('tile', 'lev', 'sec'), split_axis=0, concat_axis=0,...  7.71 us
    all_to_all x1, starting transfers between devices, remapped(): lax.all_to_all(sent, ('tile', 'lev', 'sec'), split_axis=0, concat_axis=0,...  5.79 us
    ppermute x3, starting transfers between devices, exchanged(): return lax.ppermute(value, axis, [(i, i ^ apart) for i in range(count)])  4.45 us
    ppermute x3, waiting for transfers between devices, exchanged(): return lax.ppermute(value, axis, [(i, i ^ apart) for i in range(count)])  3.05 us
    ppermute x2, starting transfers between devices, from_above(): return lax.ppermute(value, 'lev', [(i + 1, i) for i in range(count - 1)])  2.72 us
    ppermute x2, waiting for transfers between devices, from_above(): return lax.ppermute(value, 'lev', [(i + 1, i) for i in range(count - 1)])  2.52 us
  transfers between devices with their start and end apart: 14, of which 6 were waited for; matrix products, arithmetic and copies ran while one was open for 0% of the time, Pallas kernels for 22%

profile of v12, /device:TPU:0, one launch (start us, length us, event | category | flops | bytes accessed | tf_op | source)
XLA Modules:
  0.0 55.4 jit_solution(4656101476887893542)
XLA Ops:
  0.6 2.0 %shard_map.104 = (f32[4,40,384]{2,1,0:T(8,128)S(1)}, bf16[18,40,384]{2,1,0:T(8,128)(2,1)S(1)}, bf16[18,40,384]{2,1,0:T(8,128)(2,1)S(1)}, s32[18,40,384]{2,1,0:T(8,128)S(1)}, bf16[18,40,384]{2,1,0:T(8,128)(2,1)S(1)}) custom-call(f32[4,18,40,384]{3,2,1,0:T(8,128)} %f_ref.1, bf16[18,40,384]{2,1,0:T(8,128)(2,1)} %mf_hbm.1, bf16[18,40,384]{2,1,0:T(8,128)(2,1)} %cy_hbm.1, ...), custom_call_target="tpu_custom_call" | custom-call | flops 1 | bytes 1 | tf_op jit(solution)/shard_map/pallas_call | solution.py:19
  2.7 1.4 %collective-permute-start.2 = (f32[4,40,384]{2,1,0:T(8,128)S(1)}, f32[4,40,384]{2,1,0:T(8,128)S(1)}, u32[]{:S(2)}, u32[]{:S(2)}) collective-permute-start(f32[4,40,384]{2,1,0:T(8,128)S(1)} %get-tuple-element.46), channel_id=1, source_target_pairs={{2,0},{4,2},{6,4},{3,1},{5,3},{7,5},{10,8},{12,10},{14,12},{11,9},... | collective-permute-start | bytes 737288 | tf_op jit(solution)/shard_map/ppermute | solution.py:650
  4.1 3.5 %shard_map.105 = (f32[17,4,3,56,128]{4,3,2,1,0:T(8,128)S(1)}, f32[3,68,128]{2,1,0:T(8,128)S(1)}, f32[3,68,128]{2,1,0:T(8,128)S(1)}, f32[4,40,384]{2,1,0:T(8,128)S(1)}) custom-call(f32[4,18,40,384]{3,2,1,0:T(8,128)S(1)} %copy-done, bf16[18,40,384]{2,1,0:T(8,128)(2,1)S(1)} %get-tuple-element.35.mf_ref, bf16[18,40,384]{2,1,0:T(8,128)(2,1)S(1)} %get-tuple-element.36.cy_ref, ...), custom_call_target="tpu_custom_call" | custom-call | flops 1 | bytes 1 | tf_op jit(solution)/shard_map/pallas_call | solution.py:19
  7.6 0.5 collective-permute-start
  8.1 2.0 %collective-permute-start.1 = (f32[3,68,128]{2,1,0:T(8,128)S(1)}, f32[3,68,128]{2,1,0:T(8,128)S(1)}, u32[]{:S(2)}, u32[]{:S(2)}) collective-permute-start(f32[3,68,128]{2,1,0:T(8,128)S(1)} %get-tuple-element.43), channel_id=1, source_target_pairs={{8,0},{16,8},{24,16},{0,24},{9,1},{17,9},{25,17},{1,25},{10,2},{18... | collective-permute-start | bytes 313352 | tf_op jit(solution)/shard_map/ppermute | solution.py:645
  10.1 3.1 %shard_map.106 = (f32[16,4,3,56,128]{4,3,2,1,0:T(8,128)S(1)}, f32[4,3,40,128]{3,2,1,0:T(8,128)S(1)}, f32[4,3,40,128]{3,2,1,0:T(8,128)S(1)}) custom-call(f32[17,4,3,56,128]{4,3,2,1,0:T(8,128)S(1)} %get-tuple-element.38.v_ref, bf16[18,40,384]{2,1,0:T(8,128)(2,1)S(1)} %get-tuple-element.39.cx_ref, bf16[18,40,384]{2,1,0:T(8,128)(2,1)S(1)} %get-tuple-element.35.mf_ref, ...), custom_call_target="tpu_custom_call" | custom-call | flops 1 | bytes 1 | tf_op jit(solution)/shard_map/pallas_call | solution.py:19
  13.2 0.2 collective-permute-done.1.right_ref
  13.5 0.2 collective-permute-done.2.above_ref
  13.7 0.1 broadcast_in_dim.4.seam_ref
  13.8 0.2 shard_map.107
  14.0 1.3 %collective-permute-start.5 = (f32[4,40,384]{2,1,0:T(8,128)S(1)}, f32[4,40,384]{2,1,0:T(8,128)S(1)}, u32[]{:S(2)}, u32[]{:S(2)}) collective-permute-start(f32[4,40,384]{2,1,0:T(8,128)S(1)} %get-tuple-element.47.lowest_ref), channel_id=1, source_target_pairs={{2,0},{4,2},{6,4},{3,1},{5,3},{7,5},{10,8},{12,10},{14,12},{11,9},... | collective-permute-start | bytes 737288 | tf_op jit(solution)/shard_map/ppermute | solution.py:650
  15.3 1.3 %collective-permute-start.3 = (f32[3,4,128]{2,1,0:T(4,128)S(1)}, f32[3,4,128]{2,1,0:T(4,128)S(1)}, u32[]{:S(2)}, u32[]{:S(2)}) collective-permute-start(f32[3,4,128]{2,1,0:T(4,128)S(1)} %get-tuple-element.50), channel_id=1, source_target_pairs={{0,8},{8,16},{16,24},{24,0},{1,9},{9,17},{17,25},{25,1},{2,10},{10... | collective-permute-start | bytes 18440 | tf_op jit(solution)/shard_map/ppermute | solution.py:645
  16.6 0.8 %collective-permute-start.4 = (f32[3,4,128]{2,1,0:T(4,128)S(1)}, f32[3,4,128]{2,1,0:T(4,128)S(1)}, u32[]{:S(2)}, u32[]{:S(2)}) collective-permute-start(f32[3,4,128]{2,1,0:T(4,128)S(1)} %get-tuple-element.51), channel_id=1, source_target_pairs={{8,0},{16,8},{24,16},{0,24},{9,1},{17,9},{25,17},{1,25},{10,2},{18... | collective-permute-start | bytes 18440 | tf_op jit(solution)/shard_map/ppermute | solution.py:645
  17.3 2.9 %shard_map.108 = (f32[16,4,3,56,128]{4,3,2,1,0:T(8,128)S(1)}, f32[3,64,128]{2,1,0:T(8,128)S(1)}, f32[3,64,128]{2,1,0:T(8,128)S(1)}, f32[4,3,40,128]{3,2,1,0:T(8,128)S(1)}) custom-call(f32[17,4,3,56,128]{4,3,2,1,0:T(8,128)S(1)} %get-tuple-element.38.v_ref, f32[4,3,40,128]{3,2,1,0:T(8,128)S(1)} %get-tuple-element.41.inner_top_ref, ...), custom_call_target="tpu_custom_call" | custom-call | flops 1 | bytes 1 | tf_op jit(solution)/shard_map/pallas_call | solution.py:19
  20.3 0.2 shard_map.109
  20.6 0.8 %collective-permute-start.6 = (f32[3,68,128]{2,1,0:T(8,128)S(1)}, f32[3,68,128]{2,1,0:T(8,128)S(1)}, u32[]{:S(2)}, u32[]{:S(2)}) collective-permute-start(f32[3,68,128]{2,1,0:T(8,128)S(1)} %get-tuple-element.58), channel_id=1, source_target_pairs={{0,8},{8,16},{16,24},{24,0},{1,9},{9,17},{17,25},{25,1},{2,10},{10... | collective-permute-start | bytes 313352 | tf_op jit(solution)/shard_map/ppermute | solution.py:645
  21.3 1.0 %collective-permute-start.7 = (f32[3,68,128]{2,1,0:T(8,128)S(1)}, f32[3,68,128]{2,1,0:T(8,128)S(1)}, u32[]{:S(2)}, u32[]{:S(2)}) collective-permute-start(f32[3,68,128]{2,1,0:T(8,128)S(1)} %get-tuple-element.59), channel_id=1, source_target_pairs={{8,0},{16,8},{24,16},{0,24},{9,1},{17,9},{25,17},{1,25},{10,2},{18... | collective-permute-start | bytes 313352 | tf_op jit(solution)/shard_map/ppermute | solution.py:645
  22.4 2.3 %collective-permute-done.5.above_ref = f32[4,40,384]{2,1,0:T(8,128)S(1)} collective-permute-done((f32[4,40,384]{2,1,0:T(8,128)S(1)}, f32[4,40,384]{2,1,0:T(8,128)S(1)}, u32[]{:S(2)}, u32[]{:S(2)}) %collective-permute-start.5) | collective-permute-done | bytes 245792 | tf_op jit(solution)/shard_map/ppermute | solution.py:650
  24.7 0.2 shard_map.110
  24.9 0.4 collective-permute-start.8
  25.3 1.3 %collective-permute-start.9 = (f32[3,4,128]{2,1,0:T(4,128)S(1)}, f32[3,4,128]{2,1,0:T(4,128)S(1)}, u32[]{:S(2)}, u32[]{:S(2)}) collective-permute-start(f32[3,4,128]{2,1,0:T(4,128)S(1)} %get-tuple-element.61), channel_id=1, source_target_pairs={{8,0},{16,8},{24,16},{0,24},{9,1},{17,9},{25,17},{1,25},{10,2},{18... | collective-permute-start | bytes 18440 | tf_op jit(solution)/shard_map/ppermute | solution.py:645
  26.7 0.1 broadcast_in_dim.5.weight_ref
  26.7 2.0 %shard_map.111 = (f32[4,18,40,384]{3,2,1,0:T(8,128)}, f32[40,384]{1,0:T(8,128)S(1)}) custom-call(f32[16,4,3,56,128]{4,3,2,1,0:T(8,128)S(1)} %get-tuple-element.40.inner_ref, f32[16,4,3,56,128]{4,3,2,1,0:T(8,128)S(1)} %get-tuple-element.48.outer_ref, f32[4,3,56,128]{3,2,1,0:T(8,128)S(1)} %get-tuple-element.55.vs_ref, ...), custom_call_target="tpu_custom_call" | custom-call | flops 1 | bytes 1 | tf_op jit(solution)/shard_map/pallas_call | solution.py:19
  28.8 2.5 %shard_map.112 = (f32[4,18,40,384]{3,2,1,0:T(8,128)}, f32[4,4,2,8,128]{4,3,2,1,0:T(8,128)}) custom-call(f32[16,4,3,56,128]{4,3,2,1,0:T(8,128)S(1)} %get-tuple-element.40.inner_ref, f32[16,4,3,56,128]{4,3,2,1,0:T(8,128)S(1)} %get-tuple-element.48.outer_ref, f32[4,3,56,128]{3,2,1,0:T(8,128)S(1)} %get-tuple-element.55.vs_ref, ...), custom_call_target="tpu_custom_call", output_to_operand_aliasing={{0}: (14, {})} | custom-call | flops 1 | bytes 1 | tf_op jit(solution)/shard_map/pallas_call | solution.py:19
  31.4 5.8 %all-to-all-start = ((f32[32,8,128]{2,1,0:T(8,128)}), f32[32,8,128]{2,1,0:T(8,128)S(1)}, u32[]{:S(2)}, u32[]{:S(2)}) async-start(f32[32,8,128]{2,1,0:T(8,128)} %bitcast.2), calls=%async_computation | async-start | bytes 262144 | tf_op jit(solution)/shard_map/all_to_all | solution.py:628
  37.2 7.7 %all-to-all-done = f32[32,8,128]{2,1,0:T(8,128)S(1)} async-done(((f32[32,8,128]{2,1,0:T(8,128)}), f32[32,8,128]{2,1,0:T(8,128)S(1)}, u32[]{:S(2)}, u32[]{:S(2)}) %all-to-all-start) | async-done | bytes 131104 | tf_op jit(solution)/shard_map/all_to_all | solution.py:628
  44.9 1.1 %collective-permute-start.12 = (f32[4,8,128]{2,1,0:T(8,128)S(1)}, f32[4,8,128]{2,1,0:T(8,128)S(1)}, u32[]{:S(2)}, u32[]{:S(2)}) collective-permute-start(f32[4,8,128]{2,1,0:T(8,128)S(1)} %bitcast_reduce_fusion.refs_0_), channel_id=1, source_target_pairs={{0,2},{2,0},{4,6},{6,4},{1,3},{3,1},{5,7},{7,5},{8,10},{10,8},{12,... | collective-permute-start | bytes 49160 | tf_op jit(solution)/shard_map/ppermute | solution.py:621
  46.0 0.9 %collective-permute-start.11 = (f32[4,8,128]{2,1,0:T(8,128)S(1)}, f32[4,8,128]{2,1,0:T(8,128)S(1)}, u32[]{:S(2)}, u32[]{:S(2)}) collective-permute-start(f32[4,8,128]{2,1,0:T(8,128)S(1)} %bitcast_reduce_fusion.refs_0_), channel_id=1, source_target_pairs={{0,4},{2,6},{4,0},{6,2},{1,5},{3,7},{5,1},{7,3},{8,12},{10,14},{12... | collective-permute-start | bytes 49160 | tf_op jit(solution)/shard_map/ppermute | solution.py:621
  46.9 2.5 %collective-permute-start.10 = (f32[4,8,128]{2,1,0:T(8,128)S(1)}, f32[4,8,128]{2,1,0:T(8,128)S(1)}, u32[]{:S(2)}, u32[]{:S(2)}) collective-permute-start(f32[4,8,128]{2,1,0:T(8,128)S(1)} %bitcast_reduce_fusion.refs_0_), channel_id=1, source_target_pairs={{0,6},{2,4},{4,2},{6,0},{1,7},{3,5},{5,3},{7,1},{8,14},{10,12},{12... | collective-permute-start | bytes 49160 | tf_op jit(solution)/shard_map/ppermute | solution.py:621
  49.4 1.3 %collective-permute-done.11.refs_2_ = f32[4,8,128]{2,1,0:T(8,128)S(1)} collective-permute-done((f32[4,8,128]{2,1,0:T(8,128)S(1)}, f32[4,8,128]{2,1,0:T(8,128)S(1)}, u32[]{:S(2)}, u32[]{:S(2)}) %collective-permute-start.11) | collective-permute-done | bytes 16416 | tf_op jit(solution)/shard_map/ppermute | solution.py:621
  50.6 1.8 %collective-permute-done.10.refs_1_ = f32[4,8,128]{2,1,0:T(8,128)S(1)} collective-permute-done((f32[4,8,128]{2,1,0:T(8,128)S(1)}, f32[4,8,128]{2,1,0:T(8,128)S(1)}, u32[]{:S(2)}, u32[]{:S(2)}) %collective-permute-start.10) | collective-permute-done | bytes 16416 | tf_op jit(solution)/shard_map/ppermute | solution.py:621
  52.4 3.0 %shard_map.113 = f32[120,128]{1,0:T(8,128)} custom-call(s32[4,4,8,128]{3,2,1,0:T(8,128)S(1)} %copy_bitcast_fusion.1.cells_ref, f32[4,8,128]{2,1,0:T(8,128)S(1)} %bitcast_reduce_fusion.refs_0_, f32[4,8,128]{2,1,0:T(8,128)S(1)} %collective-permute-done.10.refs_1_, f32[4,8,128]{2,1,0:T(8,128)S(1)} %collective-permute-done.11.refs_2_, ...), custom_call_target="tpu_custom_call" | custom-call | flops 1 | bytes 1 | tf_op jit(solution)/shard_map/pallas_call | solution.py:19
  (21 shorter events, 0.1 us)
Async XLA Ops:
  0.6 3.5 %copy-start = (f32[4,18,40,384]{3,2,1,0:T(8,128)S(1)}, f32[4,18,40,384]{3,2,1,0:T(8,128)}, u32[]{:S(2)}) copy-start(f32[4,18,40,384]{3,2,1,0:T(8,128)} %f_ref.1) | copy-start | bytes 13271044
  2.7 11.0 %collective-permute-start.2 = (f32[4,40,384]{2,1,0:T(8,128)S(1)}, f32[4,40,384]{2,1,0:T(8,128)S(1)}, u32[]{:S(2)}, u32[]{:S(2)}) collective-permute-start(f32[4,40,384]{2,1,0:T(8,128)S(1)} %get-tuple-element.46), channel_id=1, source_target_pairs={{2,0},{4,2},{6,4},{3,1},{5,3},{7,5},{10,8},{12,10},{14,12},{11,9},... | collective-permute-start | bytes 737288 | tf_op jit(solution)/shard_map/ppermute | solution.py:650
  7.6 6.1 %copy-start.3 = (s32[4,2]{0,1:T(2,128)S(1)}, s32[4,2]{0,1:T(2,128)}, u32[]{:S(2)}) copy-start(s32[4,2]{0,1:T(2,128)} %param.14) | copy-start | bytes 100
  7.6 5.6 %collective-permute-start = (f32[3,68,128]{2,1,0:T(8,128)S(1)}, f32[3,68,128]{2,1,0:T(8,128)S(1)}, u32[]{:S(2)}, u32[]{:S(2)}) collective-permute-start(f32[3,68,128]{2,1,0:T(8,128)S(1)} %get-tuple-element.42), channel_id=1, source_target_pairs={{0,8},{8,16},{16,24},{24,0},{1,9},{9,17},{17,25},{25,1},{2,10},{10... | collective-permute-start | bytes 313352 | tf_op jit(solution)/shard_map/ppermute | solution.py:645
  8.1 5.4 %collective-permute-start.1 = (f32[3,68,128]{2,1,0:T(8,128)S(1)}, f32[3,68,128]{2,1,0:T(8,128)S(1)}, u32[]{:S(2)}, u32[]{:S(2)}) collective-permute-start(f32[3,68,128]{2,1,0:T(8,128)S(1)} %get-tuple-element.43), channel_id=1, source_target_pairs={{8,0},{16,8},{24,16},{0,24},{9,1},{17,9},{25,17},{1,25},{10,2},{18... | collective-permute-start | bytes 313352 | tf_op jit(solution)/shard_map/ppermute | solution.py:645
  14.0 10.7 %collective-permute-start.5 = (f32[4,40,384]{2,1,0:T(8,128)S(1)}, f32[4,40,384]{2,1,0:T(8,128)S(1)}, u32[]{:S(2)}, u32[]{:S(2)}) collective-permute-start(f32[4,40,384]{2,1,0:T(8,128)S(1)} %get-tuple-element.47.lowest_ref), channel_id=1, source_target_pairs={{2,0},{4,2},{6,4},{3,1},{5,3},{7,5},{10,8},{12,10},{14,12},{11,9},... | collective-permute-start | bytes 737288 | tf_op jit(solution)/shard_map/ppermute | solution.py:650
  15.3 5.0 %collective-permute-start.3 = (f32[3,4,128]{2,1,0:T(4,128)S(1)}, f32[3,4,128]{2,1,0:T(4,128)S(1)}, u32[]{:S(2)}, u32[]{:S(2)}) collective-permute-start(f32[3,4,128]{2,1,0:T(4,128)S(1)} %get-tuple-element.50), channel_id=1, source_target_pairs={{0,8},{8,16},{16,24},{24,0},{1,9},{9,17},{17,25},{25,1},{2,10},{10... | collective-permute-start | bytes 18440 | tf_op jit(solution)/shard_map/ppermute | solution.py:645
  16.6 3.7 %collective-permute-start.4 = (f32[3,4,128]{2,1,0:T(4,128)S(1)}, f32[3,4,128]{2,1,0:T(4,128)S(1)}, u32[]{:S(2)}, u32[]{:S(2)}) collective-permute-start(f32[3,4,128]{2,1,0:T(4,128)S(1)} %get-tuple-element.51), channel_id=1, source_target_pairs={{8,0},{16,8},{24,16},{0,24},{9,1},{17,9},{25,17},{1,25},{10,2},{18... | collective-permute-start | bytes 18440 | tf_op jit(solution)/shard_map/ppermute | solution.py:645
  20.3 6.4 %copy-start.4 = (f32[18]{0:T(128)S(1)}, f32[18]{0:T(128)}, u32[]{:S(2)}) copy-start(f32[18]{0:T(128)} %param.15) | copy-start | bytes 220
  20.3 6.5 %copy-start.1 = (f32[4,40,384]{2,1,0:T(8,128)S(1)}, f32[4,40,384]{2,1,0:T(8,128)}, u32[]{:S(2)}) copy-start(f32[4,40,384]{2,1,0:T(8,128)} %share_ref.3) | copy-start | bytes 737284
  20.6 8.2 %collective-permute-start.6 = (f32[3,68,128]{2,1,0:T(8,128)S(1)}, f32[3,68,128]{2,1,0:T(8,128)S(1)}, u32[]{:S(2)}, u32[]{:S(2)}) collective-permute-start(f32[3,68,128]{2,1,0:T(8,128)S(1)} %get-tuple-element.58), channel_id=1, source_target_pairs={{0,8},{8,16},{16,24},{24,0},{1,9},{9,17},{17,25},{25,1},{2,10},{10... | collective-permute-start | bytes 313352 | tf_op jit(solution)/shard_map/ppermute | solution.py:645
  21.3 7.5 %collective-permute-start.7 = (f32[3,68,128]{2,1,0:T(8,128)S(1)}, f32[3,68,128]{2,1,0:T(8,128)S(1)}, u32[]{:S(2)}, u32[]{:S(2)}) collective-permute-start(f32[3,68,128]{2,1,0:T(8,128)S(1)} %get-tuple-element.59), channel_id=1, source_target_pairs={{8,0},{16,8},{24,16},{0,24},{9,1},{17,9},{25,17},{1,25},{10,2},{18... | collective-permute-start | bytes 313352 | tf_op jit(solution)/shard_map/ppermute | solution.py:645
  24.9 3.9 %collective-permute-start.8 = (f32[3,4,128]{2,1,0:T(4,128)S(1)}, f32[3,4,128]{2,1,0:T(4,128)S(1)}, u32[]{:S(2)}, u32[]{:S(2)}) collective-permute-start(f32[3,4,128]{2,1,0:T(4,128)S(1)} %get-tuple-element.60), channel_id=1, source_target_pairs={{0,8},{8,16},{16,24},{24,0},{1,9},{9,17},{17,25},{25,1},{2,10},{10... | collective-permute-start | bytes 18440 | tf_op jit(solution)/shard_map/ppermute | solution.py:645
  25.3 3.5 %collective-permute-start.9 = (f32[3,4,128]{2,1,0:T(4,128)S(1)}, f32[3,4,128]{2,1,0:T(4,128)S(1)}, u32[]{:S(2)}, u32[]{:S(2)}) collective-permute-start(f32[3,4,128]{2,1,0:T(4,128)S(1)} %get-tuple-element.61), channel_id=1, source_target_pairs={{8,0},{16,8},{24,16},{0,24},{9,1},{17,9},{25,17},{1,25},{10,2},{18... | collective-permute-start | bytes 18440 | tf_op jit(solution)/shard_map/ppermute | solution.py:645
  28.8 8.4 %copy-start.2 = (s32[4,3840]{1,0:T(4,128)S(1)}, s32[4,3840]{1,0:T(4,128)}, u32[]{:S(2)}) copy-start(s32[4,3840]{1,0:T(4,128)} %param.17) | copy-start | bytes 184324
  31.4 13.5 %all-to-all-start = ((f32[32,8,128]{2,1,0:T(8,128)}), f32[32,8,128]{2,1,0:T(8,128)S(1)}, u32[]{:S(2)}, u32[]{:S(2)}) async-start(f32[32,8,128]{2,1,0:T(8,128)} %bitcast.2), calls=%async_computation | async-start | bytes 262144 | tf_op jit(solution)/shard_map/all_to_all | solution.py:628
  44.9 4.5 %collective-permute-start.12 = (f32[4,8,128]{2,1,0:T(8,128)S(1)}, f32[4,8,128]{2,1,0:T(8,128)S(1)}, u32[]{:S(2)}, u32[]{:S(2)}) collective-permute-start(f32[4,8,128]{2,1,0:T(8,128)S(1)} %bitcast_reduce_fusion.refs_0_), channel_id=1, source_target_pairs={{0,2},{2,0},{4,6},{6,4},{1,3},{3,1},{5,7},{7,5},{8,10},{10,8},{12,... | collective-permute-start | bytes 49160 | tf_op jit(solution)/shard_map/ppermute | solution.py:621
  46.0 4.6 %collective-permute-start.11 = (f32[4,8,128]{2,1,0:T(8,128)S(1)}, f32[4,8,128]{2,1,0:T(8,128)S(1)}, u32[]{:S(2)}, u32[]{:S(2)}) collective-permute-start(f32[4,8,128]{2,1,0:T(8,128)S(1)} %bitcast_reduce_fusion.refs_0_), channel_id=1, source_target_pairs={{0,4},{2,6},{4,0},{6,2},{1,5},{3,7},{5,1},{7,3},{8,12},{10,14},{12... | collective-permute-start | bytes 49160 | tf_op jit(solution)/shard_map/ppermute | solution.py:621
  46.9 5.5 %collective-permute-start.10 = (f32[4,8,128]{2,1,0:T(8,128)S(1)}, f32[4,8,128]{2,1,0:T(8,128)S(1)}, u32[]{:S(2)}, u32[]{:S(2)}) collective-permute-start(f32[4,8,128]{2,1,0:T(8,128)S(1)} %bitcast_reduce_fusion.refs_0_), channel_id=1, source_target_pairs={{0,6},{2,4},{4,2},{6,0},{1,7},{3,5},{5,3},{7,1},{8,14},{10,12},{12... | collective-permute-start | bytes 49160 | tf_op jit(solution)/shard_map/ppermute | solution.py:621

commit v13 on v12

--- a/solution.py
+++ b/solution.py
@@ -99,6 +99,18 @@
 
 def rim_rows(xt, last, left_row, right_row):
     return (left_row if xt == 0 else None, right_row if xt == last else None)
+
+
+def near_rows(other_ref, k, xt, strips, left_row, right_row):
+    def row(place):
+        return lambda s, j: other_ref[k, s, j, place : place + 1, :]
+
+    first, last = ROWS * (xt + 1), ROWS * (xt + 2)
+    if xt == 0:
+        return left_row, row(last)
+    if xt == strips - 1:
+        return row(first - 1), right_row
+    return (row(first - 1) if xt == 1 else None, row(last) if xt == strips - 2 else None)
 
 
 def turned(source_ref, flag, target_ref):
@@ -149,7 +161,7 @@
         copy.wait()
 
 
-def lower_kernel(f_ref, mf_ref, cy_ref, code_ref, v_ref, first_ref, last_ref, top_ref):
+def lower_levels(chosen, f_ref, mf_ref, cy_ref, code_ref, v_ref, rims=None):
     sectors, levels, columns, width = f_ref.shape
     tiles, strips = width // LANES, columns // ROWS
 
@@ -157,7 +169,7 @@
         mf = mf_ref[k].astype(jnp.float32)
         cy = cy_ref[k].astype(jnp.float32)
         codes = code_ref[k]
-        for xt in range(strips):
+        for xt in chosen:
             factors = second_weights(cy, codes, 3, xt, tiles)
             rows = slice(xt * ROWS, (xt + 1) * ROWS)
             for s in range(sectors):
@@ -169,11 +181,23 @@
                     parts.append(here + cut(mf, xt, j) * (upper - here))
                 for j, value in enumerate(second_sweep(parts, factors)):
                     store_padded(v_ref, (k,), s, j, xt, value)
-                    store_rims(first_ref, last_ref, k * sectors + s, j, xt, strips - 1, value)
+                    if rims is not None:
+                        store_rims(*rims, k * sectors + s, j, xt, strips - 1, value)
         return 0
 
     lax.fori_loop(0, levels - 1, level, 0)
-    top_ref[...] = f_ref[:, levels - 1]
+
+
+def outer_lower_kernel(f_ref, mf_ref, cy_ref, code_ref, v_ref, first_ref, last_ref):
+    strips = f_ref.shape[2] // ROWS
+    rims = (first_ref, last_ref)
+    lower_levels((0, strips - 1), f_ref, mf_ref, cy_ref, code_ref, v_ref, rims)
+
+
+def inner_lower_kernel(f_ref, mf_ref, cy_ref, code_ref, v_ref, top_ref):
+    strips = f_ref.shape[2] // ROWS
+    lower_levels(range(1, strips - 1), f_ref, mf_ref, cy_ref, code_ref, v_ref)
+    top_ref[...] = f_ref[:, f_ref.shape[1] - 1]
 
 
 def first_weights(cx, codes, bit, xt, j):
@@ -182,8 +206,8 @@
 
 
 def ends_kernel(
-    v_ref, inner_ref, left_ref, right_ref, seam_ref, cx_ref, code_ref, here_ref, above_ref,
-    mf_ref, cy_ref,
+    v_ref, next_ref, inner_ref, left_ref, right_ref, seam_ref, cx_ref, code_ref,
+    here_ref, above_ref, mf_ref, cy_ref,
     out_ref, top_ref, first_ref, last_ref,
     lrow_ref, rrow_ref,
 ):
@@ -206,8 +230,8 @@
                 value = first_sweep(
                     lambda s, j, start: v_ref[0, s, j, start : start + ROWS, :],
                     s, j, xt, factors,
-                    *rim_rows(
-                        xt, strips - 1,
+                    *near_rows(
+                        next_ref, 0, xt, strips,
                         lambda s, j: lrow_ref[j, s : s + 1, :],
                         lambda s, j: rrow_ref[j, s : s + 1, :],
                     ),
@@ -235,7 +259,8 @@
 
 
 def middle_levels(
-    chosen, v_ref, lrow_ref, rrow_ref, cx_ref, mf_ref, cy_ref, code_ref, out_ref, a_ref, rims=None
+    chosen, v_ref, next_ref, lrow_ref, rrow_ref, cx_ref, mf_ref, cy_ref, code_ref, out_ref, a_ref,
+    rims=None,
 ):
     below, sectors, tiles, padded, _ = v_ref.shape
     strips = (padded - 2 * ROWS) // ROWS
@@ -257,8 +282,8 @@
                     upper = first_sweep(
                         lambda s, j, start: v_ref[k + 1, s, j, start : start + ROWS, :],
                         s, j, xt, along[j],
-                        *rim_rows(
-                            xt, strips - 1,
+                        *near_rows(
+                            next_ref, k + 1, xt, strips,
                             lambda s, j: lrow_ref[j, pl.ds((k + 1) * sectors + s, 1), :],
                             lambda s, j: rrow_ref[j, pl.ds((k + 1) * sectors + s, 1), :],
                         ),
@@ -276,7 +301,7 @@
 
 
 def inner_middle_kernel(
-    v_ref, cx_ref, mf_ref, cy_ref, code_ref, out_ref, lowest_ref, top_ref, a_ref
+    v_ref, next_ref, cx_ref, mf_ref, cy_ref, code_ref, out_ref, lowest_ref, top_ref, a_ref
 ):
     below, sectors, tiles, padded, _ = v_ref.shape
     strips = (padded - 2 * ROWS) // ROWS
@@ -287,19 +312,20 @@
             for s in range(sectors):
                 value = first_sweep(
                     lambda s, j, start: v_ref[0, s, j, start : start + ROWS, :],
-                    s, j, xt, factors,
+                    s, j, xt, factors, *near_rows(next_ref, 0, xt, strips, None, None),
                 )
                 a_ref[0, s, j, xt * ROWS : (xt + 1) * ROWS, :] = value
                 lowest_ref[s, j, xt * ROWS : (xt + 1) * ROWS, :] = value
     middle_levels(
-        range(1, strips - 1), v_ref, None, None, cx_ref, mf_ref, cy_ref, code_ref, out_ref, a_ref
+        range(1, strips - 1), v_ref, next_ref, None, None, cx_ref, mf_ref, cy_ref, code_ref,
+        out_ref, a_ref,
     )
     inner = slice(ROWS, (strips - 1) * ROWS)
     top_ref[:, :, inner] = a_ref[(below - 1) % 2, :, :, inner]
 
 
 def outer_middle_kernel(
-    v_ref, inner_top_ref, left_ref, right_ref, lowest_ref, seam_ref,
+    v_ref, next_ref, inner_top_ref, left_ref, right_ref, lowest_ref, seam_ref,
     cx_ref, mf_ref, cy_ref, code_ref,
     out_ref, first_ref, last_ref, top_ref,
     lrow_ref, rrow_ref, a_ref,
@@ -316,7 +342,7 @@
                 rows = slice(xt * ROWS, (xt + 1) * ROWS)
                 a_ref[0, s, j, rows] = lowest_ref[s, rows, j * LANES : (j + 1) * LANES]
     middle_levels(
-        ends, v_ref, lrow_ref, rrow_ref, cx_ref, mf_ref, cy_ref, code_ref, out_ref, a_ref,
+        ends, v_ref, next_ref, lrow_ref, rrow_ref, cx_ref, mf_ref, cy_ref, code_ref, out_ref, a_ref,
         (first_ref, last_ref),
     )
     for xt in ends:
@@ -591,8 +617,7 @@
     for start in range(0, len(lines), wide):
         lefts, rights = [], []
         for part, owner, line in lines[start : start + wide]:
-            piece = jnp.bitwise_xor(rank, (group - part) % group)
-            cells = cells_ref[piece, owner, line : line + 1, :]
+            cells = cells_ref[jnp.bitwise_xor(rank, part), owner, line : line + 1, :]
             value = value_refs[part][owner, line : line + 1, :]
             coarse = value.astype(half).astype(jnp.float32)
             high = spread(jnp.right_shift(cells, 7).astype(jnp.float32)) == iota
@@ -629,7 +654,7 @@
         sent, ("tile", "lev", "sec"), split_axis=0, concat_axis=0, tiled=True
     )
     own = jnp.sum(arrived.reshape(owners, group * copies, depth, LANES), axis=1)
-    parts = [own] + [exchanged(own, "lev", group - d) for d in range(1, group)]
+    parts = [own] + [exchanged(own, "lev", d) for d in range(1, group)]
     cells = jnp.pad(flux_cell, ((0, 0), (0, group * depth * LANES - share)))
     cells = cells.reshape(owners, group, depth, LANES).transpose(1, 0, 2, 3)
     out = call(
@@ -677,11 +702,18 @@
         [pltpu.SemaphoreType.DMA((5,))],
     )
     above = from_above(lowest)
-    v, first, last, top = call(
-        lower_kernel,
-        (field, rim, rim, plane),
+    v, first, last = call(
+        outer_lower_kernel,
+        (field, rim, rim),
         [VM] * 4,
+        [VM] * 3,
+        (forcing, mass_flux, courant_y, limiter_code),
+    )
+    v_inner, top = call(
+        inner_lower_kernel,
+        (field, plane),
         [VM] * 4,
+        [VM] * 2,
         (forcing, mass_flux, courant_y, limiter_code),
     )
     left, right = around(first, last)
@@ -691,32 +723,32 @@
     inner, inner_lowest, inner_top = call(
         inner_middle_kernel,
         (inner_field, lines, lines),
-        [VM] * 5,
+        [VM] * 6,
         [VM] * 3,
-        (v, courant_x, mass_flux, courant_y, limiter_code),
+        (v_inner, v, courant_x, mass_flux, courant_y, limiter_code),
         [a_scratch],
     )
     lowest, vt, first_top, last_top = call(
         ends_kernel,
         (plane, field_top, rim_top, rim_top),
+        [VM] * 12,
+        [VM] * 4,
+        (
+            v, v_inner, inner_lowest, left, right, seam, courant_x, limiter_code, top, above,
+            mass_flux, courant_y,
+        ),
+        [pltpu.VMEM((tiles, ROWS, LANES), jnp.float32)] * 2,
+    )
+    above = from_above(lowest)
+    left_top, right_top = around(first_top, last_top)
+
+    outer, first, last, top = call(
+        outer_middle_kernel,
+        (inner_field, rim_next, rim_next, lines),
         [VM] * 11,
         [VM] * 4,
         (
-            v, inner_lowest, left, right, seam, courant_x, limiter_code, top, above,
-            mass_flux, courant_y,
-        ),
-        [pltpu.VMEM((tiles, ROWS, LANES), jnp.float32)] * 2,
-    )
-    above = from_above(lowest)
-    left_top, right_top = around(first_top, last_top)
-
-    outer, first, last, top = call(
-        outer_middle_kernel,
-        (inner_field, rim_next, rim_next, lines),
-        [VM] * 10,
-        [VM] * 4,
-        (
-            v, inner_top, left, right, lowest, seam,
+            v, v_inner, inner_top, left, right, lowest, seam,
             courant_x, mass_flux, courant_y, limiter_code,
         ),
         [rim_scratch, rim_scratch, a_scratch],

time: 55.6 us -> 57.1 us (1.027)
  Pallas kernels: 19.7 us -> 21.2 us
    pallas_call x10 -> x11, Pallas kernels: 19.7 us -> 21.2 us  [call(): pl.pallas_call(kernel, out_shape=out_shape, in_specs=in_specs, out_specs=...]
    ppermute x2, waiting for transfers between devices: 2.52 us -> 3.2 us  [from_above(): return lax.ppermute(value, 'lev', [(i + 1, i) for i in range(count - 1)])]
  transfers between devices with their start and end apart: 14 -> 14, of which waited for: 6 -> 4; matrix products, arithmetic and copies ran while one was open for 0% -> 0% of each run, Pallas kernels for 22% -> 23%
where the time goes in v13:
time: 57.1 us; the launch traced here: 56.9 us
  Pallas kernels  21.2 us (37%)
  starting transfers between devices  20.6 us (36%)
  waiting for transfers between devices  14 us (25%)
  between operations  0.9 us (2%)
    pallas_call x11, Pallas kernels, call(): pl.pallas_call(kernel, out_shape=out_shape, in_specs=in_specs, out_specs=...  21.2 us
    ppermute x8, starting transfers between devices, around(): return (lax.ppermute(last, 'tile', up), lax.ppermute(first, 'tile', down))  7.88 us
    all_to_all x1, waiting for transfers between devices, remapped(): lax.all_to_all(sent, ('tile', 'lev', 'sec'), split_axis=0, concat_axis=0,...  7.71 us
    all_to_all x1, starting transfers between devices, remapped(): lax.all_to_all(sent, ('tile', 'lev', 'sec'), split_axis=0, concat_axis=0,...  5.56 us
    ppermute x3, starting transfers between devices, exchanged(): return lax.ppermute(value, axis, [(i, i ^ apart) for i in range(count)])  4.45 us
    ppermute x2, waiting for transfers between devices, from_above(): return lax.ppermute(value, 'lev', [(i + 1, i) for i in range(count - 1)])  3.2 us
    ppermute x3, waiting for transfers between devices, exchanged(): return lax.ppermute(value, axis, [(i, i ^ apart) for i in range(count)])  3.05 us
    ppermute x2, starting transfers between devices, from_above(): return lax.ppermute(value, 'lev', [(i + 1, i) for i in range(count - 1)])  2.72 us
  transfers between devices with their start and end apart: 14, of which 4 were waited for; matrix products, arithmetic and copies ran while one was open for 0% of the time, Pallas kernels for 23%

profile of v13, /device:TPU:0, one launch (start us, length us, event | category | flops | bytes accessed | tf_op | source)
XLA Modules:
  0.0 56.9 jit_solution(15985160938195107694)
XLA Ops:
  0.6 2.0 %shard_map.104 = (f32[4,40,384]{2,1,0:T(8,128)S(1)}, bf16[18,40,384]{2,1,0:T(8,128)(2,1)S(1)}, bf16[18,40,384]{2,1,0:T(8,128)(2,1)S(1)}, s32[18,40,384]{2,1,0:T(8,128)S(1)}, bf16[18,40,384]{2,1,0:T(8,128)(2,1)S(1)}) custom-call(f32[4,18,40,384]{3,2,1,0:T(8,128)} %f_ref.3, bf16[18,40,384]{2,1,0:T(8,128)(2,1)} %mf_hbm.1, bf16[18,40,384]{2,1,0:T(8,128)(2,1)} %cy_hbm.1, ...), custom_call_target="tpu_custom_call" | custom-call | flops 1 | bytes 1 | tf_op jit(solution)/shard_map/pallas_call | solution.py:19
  2.7 1.4 %collective-permute-start.2 = (f32[4,40,384]{2,1,0:T(8,128)S(1)}, f32[4,40,384]{2,1,0:T(8,128)S(1)}, u32[]{:S(2)}, u32[]{:S(2)}) collective-permute-start(f32[4,40,384]{2,1,0:T(8,128)S(1)} %get-tuple-element.48), channel_id=1, source_target_pairs={{2,0},{4,2},{6,4},{3,1},{5,3},{7,5},{10,8},{12,10},{14,12},{11,9},... | collective-permute-start | bytes 737288 | tf_op jit(solution)/shard_map/ppermute | solution.py:675
  4.1 2.1 %shard_map.106 = (f32[17,4,3,56,128]{4,3,2,1,0:T(8,128)S(1)}, f32[3,68,128]{2,1,0:T(8,128)S(1)}, f32[3,68,128]{2,1,0:T(8,128)S(1)}) custom-call(f32[4,18,40,384]{3,2,1,0:T(8,128)S(1)} %copy-done, bf16[18,40,384]{2,1,0:T(8,128)(2,1)S(1)} %get-tuple-element.36.mf_ref, bf16[18,40,384]{2,1,0:T(8,128)(2,1)S(1)} %get-tuple-element.37.cy_ref, ...), custom_call_target="tpu_custom_call" | custom-call | flops 1 | bytes 1 | tf_op jit(solution)/shard_map/pallas_call | solution.py:19
  6.3 0.5 collective-permute-start
  6.8 2.0 %collective-permute-start.1 = (f32[3,68,128]{2,1,0:T(8,128)S(1)}, f32[3,68,128]{2,1,0:T(8,128)S(1)}, u32[]{:S(2)}, u32[]{:S(2)}) collective-permute-start(f32[3,68,128]{2,1,0:T(8,128)S(1)} %get-tuple-element.45), channel_id=1, source_target_pairs={{8,0},{16,8},{24,16},{0,24},{9,1},{17,9},{25,17},{1,25},{10,2},{18... | collective-permute-start | bytes 313352 | tf_op jit(solution)/shard_map/ppermute | solution.py:670
  8.8 2.6 %shard_map.105 = (f32[17,4,3,56,128]{4,3,2,1,0:T(8,128)S(1)}, f32[4,40,384]{2,1,0:T(8,128)S(1)}) custom-call(f32[4,18,40,384]{3,2,1,0:T(8,128)S(1)} %copy-done, bf16[18,40,384]{2,1,0:T(8,128)(2,1)S(1)} %get-tuple-element.36.mf_ref, bf16[18,40,384]{2,1,0:T(8,128)(2,1)S(1)} %get-tuple-element.37.cy_ref, s32[18,40,384]{2,1,0:T(8,128)S(1)} %get-tuple-element.38.code_ref), custom_call_target="tpu_custom_call" | custom-call | flops 1 | bytes 1 | tf_op jit(solution)/shard_map/pallas_call | solution.py:19
  11.3 3.3 %shard_map.107 = (f32[16,4,3,56,128]{4,3,2,1,0:T(8,128)S(1)}, f32[4,3,40,128]{3,2,1,0:T(8,128)S(1)}, f32[4,3,40,128]{3,2,1,0:T(8,128)S(1)}) custom-call(f32[17,4,3,56,128]{4,3,2,1,0:T(8,128)S(1)} %get-tuple-element.39.v_ref.next_ref, f32[17,4,3,56,128]{4,3,2,1,0:T(8,128)S(1)} %get-tuple-element.40.next_ref.v_ref, ...), custom_call_target="tpu_custom_call" | custom-call | flops 1 | bytes 1 | tf_op jit(solution)/shard_map/pallas_call | solution.py:19
  14.7 0.1 broadcast_in_dim.4.seam_ref
  14.8 0.2 shard_map.108
  15.0 1.3 %collective-permute-start.5 = (f32[4,40,384]{2,1,0:T(8,128)S(1)}, f32[4,40,384]{2,1,0:T(8,128)S(1)}, u32[]{:S(2)}, u32[]{:S(2)}) collective-permute-start(f32[4,40,384]{2,1,0:T(8,128)S(1)} %get-tuple-element.49.lowest_ref), channel_id=1, source_target_pairs={{2,0},{4,2},{6,4},{3,1},{5,3},{7,5},{10,8},{12,10},{14,12},{11,9},... | collective-permute-start | bytes 737288 | tf_op jit(solution)/shard_map/ppermute | solution.py:675
  16.3 0.7 %collective-permute-start.3 = (f32[3,4,128]{2,1,0:T(4,128)S(1)}, f32[3,4,128]{2,1,0:T(4,128)S(1)}, u32[]{:S(2)}, u32[]{:S(2)}) collective-permute-start(f32[3,4,128]{2,1,0:T(4,128)S(1)} %get-tuple-element.52), channel_id=1, source_target_pairs={{0,8},{8,16},{16,24},{24,0},{1,9},{9,17},{17,25},{25,1},{2,10},{10... | collective-permute-start | bytes 18440 | tf_op jit(solution)/shard_map/ppermute | solution.py:670
  17.0 1.1 %collective-permute-start.4 = (f32[3,4,128]{2,1,0:T(4,128)S(1)}, f32[3,4,128]{2,1,0:T(4,128)S(1)}, u32[]{:S(2)}, u32[]{:S(2)}) collective-permute-start(f32[3,4,128]{2,1,0:T(4,128)S(1)} %get-tuple-element.53), channel_id=1, source_target_pairs={{8,0},{16,8},{24,16},{0,24},{9,1},{17,9},{25,17},{1,25},{10,2},{18... | collective-permute-start | bytes 18440 | tf_op jit(solution)/shard_map/ppermute | solution.py:670
  18.1 2.9 %shard_map.109 = (f32[16,4,3,56,128]{4,3,2,1,0:T(8,128)S(1)}, f32[3,64,128]{2,1,0:T(8,128)S(1)}, f32[3,64,128]{2,1,0:T(8,128)S(1)}, f32[4,3,40,128]{3,2,1,0:T(8,128)S(1)}) custom-call(f32[17,4,3,56,128]{4,3,2,1,0:T(8,128)S(1)} %get-tuple-element.40.next_ref.v_ref, f32[17,4,3,56,128]{4,3,2,1,0:T(8,128)S(1)} %get-tuple-element.39.v_ref.next_ref, ...), custom_call_target="tpu_custom_call" | custom-call | flops 1 | bytes 1 | tf_op jit(solution)/shard_map/pallas_call | solution.py:19
  21.0 0.0 copy-start.4
  21.1 0.2 shard_map.110
  21.3 1.1 %collective-permute-start.6 = (f32[3,68,128]{2,1,0:T(8,128)S(1)}, f32[3,68,128]{2,1,0:T(8,128)S(1)}, u32[]{:S(2)}, u32[]{:S(2)}) collective-permute-start(f32[3,68,128]{2,1,0:T(8,128)S(1)} %get-tuple-element.60), channel_id=1, source_target_pairs={{0,8},{8,16},{16,24},{24,0},{1,9},{9,17},{17,25},{25,1},{2,10},{10... | collective-permute-start | bytes 313352 | tf_op jit(solution)/shard_map/ppermute | solution.py:670
  22.4 0.7 %collective-permute-start.7 = (f32[3,68,128]{2,1,0:T(8,128)S(1)}, f32[3,68,128]{2,1,0:T(8,128)S(1)}, u32[]{:S(2)}, u32[]{:S(2)}) collective-permute-start(f32[3,68,128]{2,1,0:T(8,128)S(1)} %get-tuple-element.61), channel_id=1, source_target_pairs={{8,0},{16,8},{24,16},{0,24},{9,1},{17,9},{25,17},{1,25},{10,2},{18... | collective-permute-start | bytes 313352 | tf_op jit(solution)/shard_map/ppermute | solution.py:670
  23.1 3.2 %collective-permute-done.5.above_ref = f32[4,40,384]{2,1,0:T(8,128)S(1)} collective-permute-done((f32[4,40,384]{2,1,0:T(8,128)S(1)}, f32[4,40,384]{2,1,0:T(8,128)S(1)}, u32[]{:S(2)}, u32[]{:S(2)}) %collective-permute-start.5) | collective-permute-done | bytes 245792 | tf_op jit(solution)/shard_map/ppermute | solution.py:675
  26.3 0.2 shard_map.111
  26.5 0.1 collective-permute-start.8
  26.6 1.7 %collective-permute-start.9 = (f32[3,4,128]{2,1,0:T(4,128)S(1)}, f32[3,4,128]{2,1,0:T(4,128)S(1)}, u32[]{:S(2)}, u32[]{:S(2)}) collective-permute-start(f32[3,4,128]{2,1,0:T(4,128)S(1)} %get-tuple-element.63), channel_id=1, source_target_pairs={{8,0},{16,8},{24,16},{0,24},{9,1},{17,9},{25,17},{1,25},{10,2},{18... | collective-permute-start | bytes 18440 | tf_op jit(solution)/shard_map/ppermute | solution.py:670
  28.3 0.1 broadcast_in_dim.5.weight_ref
  28.4 2.0 %shard_map.112 = (f32[4,18,40,384]{3,2,1,0:T(8,128)}, f32[40,384]{1,0:T(8,128)S(1)}) custom-call(f32[16,4,3,56,128]{4,3,2,1,0:T(8,128)S(1)} %get-tuple-element.42.inner_ref, f32[16,4,3,56,128]{4,3,2,1,0:T(8,128)S(1)} %get-tuple-element.50.outer_ref, f32[4,3,56,128]{3,2,1,0:T(8,128)S(1)} %get-tuple-element.57.vs_ref, ...), custom_call_target="tpu_custom_call" | custom-call | flops 1 | bytes 1 | tf_op jit(solution)/shard_map/pallas_call | solution.py:19
  30.5 2.6 %shard_map.113 = (f32[4,18,40,384]{3,2,1,0:T(8,128)}, f32[4,4,2,8,128]{4,3,2,1,0:T(8,128)}) custom-call(f32[16,4,3,56,128]{4,3,2,1,0:T(8,128)S(1)} %get-tuple-element.42.inner_ref, f32[16,4,3,56,128]{4,3,2,1,0:T(8,128)S(1)} %get-tuple-element.50.outer_ref, f32[4,3,56,128]{3,2,1,0:T(8,128)S(1)} %get-tuple-element.57.vs_ref, ...), custom_call_target="tpu_custom_call", output_to_operand_aliasing={{0}: (14, {})} | custom-call | flops 1 | bytes 1 | tf_op jit(solution)/shard_map/pallas_call | solution.py:19
  33.1 5.6 %all-to-all-start = ((f32[32,8,128]{2,1,0:T(8,128)}), f32[32,8,128]{2,1,0:T(8,128)S(1)}, u32[]{:S(2)}, u32[]{:S(2)}) async-start(f32[32,8,128]{2,1,0:T(8,128)} %bitcast.2), calls=%async_computation | async-start | bytes 262144 | tf_op jit(solution)/shard_map/all_to_all | solution.py:653
  38.7 7.7 %all-to-all-done = f32[32,8,128]{2,1,0:T(8,128)S(1)} async-done(((f32[32,8,128]{2,1,0:T(8,128)}), f32[32,8,128]{2,1,0:T(8,128)S(1)}, u32[]{:S(2)}, u32[]{:S(2)}) %all-to-all-start) | async-done | bytes 131104 | tf_op jit(solution)/shard_map/all_to_all | solution.py:653
  46.4 1.1 %collective-permute-start.10 = (f32[4,8,128]{2,1,0:T(8,128)S(1)}, f32[4,8,128]{2,1,0:T(8,128)S(1)}, u32[]{:S(2)}, u32[]{:S(2)}) collective-permute-start(f32[4,8,128]{2,1,0:T(8,128)S(1)} %bitcast_reduce_fusion.refs_0_), channel_id=1, source_target_pairs={{0,2},{2,0},{4,6},{6,4},{1,3},{3,1},{5,7},{7,5},{8,10},{10,8},{12,... | collective-permute-start | bytes 49160 | tf_op jit(solution)/shard_map/ppermute | solution.py:646
  47.5 0.9 %collective-permute-start.11 = (f32[4,8,128]{2,1,0:T(8,128)S(1)}, f32[4,8,128]{2,1,0:T(8,128)S(1)}, u32[]{:S(2)}, u32[]{:S(2)}) collective-permute-start(f32[4,8,128]{2,1,0:T(8,128)S(1)} %bitcast_reduce_fusion.refs_0_), channel_id=1, source_target_pairs={{0,4},{2,6},{4,0},{6,2},{1,5},{3,7},{5,1},{7,3},{8,12},{10,14},{12... | collective-permute-start | bytes 49160 | tf_op jit(solution)/shard_map/ppermute | solution.py:646
  48.4 2.5 %collective-permute-start.12 = (f32[4,8,128]{2,1,0:T(8,128)S(1)}, f32[4,8,128]{2,1,0:T(8,128)S(1)}, u32[]{:S(2)}, u32[]{:S(2)}) collective-permute-start(f32[4,8,128]{2,1,0:T(8,128)S(1)} %bitcast_reduce_fusion.refs_0_), channel_id=1, source_target_pairs={{0,6},{2,4},{4,2},{6,0},{1,7},{3,5},{5,3},{7,1},{8,14},{10,12},{12... | collective-permute-start | bytes 49160 | tf_op jit(solution)/shard_map/ppermute | solution.py:646
  50.9 1.3 %collective-permute-done.11.refs_2_ = f32[4,8,128]{2,1,0:T(8,128)S(1)} collective-permute-done((f32[4,8,128]{2,1,0:T(8,128)S(1)}, f32[4,8,128]{2,1,0:T(8,128)S(1)}, u32[]{:S(2)}, u32[]{:S(2)}) %collective-permute-start.11) | collective-permute-done | bytes 16416 | tf_op jit(solution)/shard_map/ppermute | solution.py:646
  52.1 1.8 %collective-permute-done.12.refs_3_ = f32[4,8,128]{2,1,0:T(8,128)S(1)} collective-permute-done((f32[4,8,128]{2,1,0:T(8,128)S(1)}, f32[4,8,128]{2,1,0:T(8,128)S(1)}, u32[]{:S(2)}, u32[]{:S(2)}) %collective-permute-start.12) | collective-permute-done | bytes 16416 | tf_op jit(solution)/shard_map/ppermute | solution.py:646
  53.9 3.0 %shard_map.114 = f32[120,128]{1,0:T(8,128)} custom-call(s32[4,4,8,128]{3,2,1,0:T(8,128)S(1)} %copy_bitcast_fusion.1.cells_ref, f32[4,8,128]{2,1,0:T(8,128)S(1)} %bitcast_reduce_fusion.refs_0_, f32[4,8,128]{2,1,0:T(8,128)S(1)} %collective-permute-done.10.refs_1_, f32[4,8,128]{2,1,0:T(8,128)S(1)} %collective-permute-done.11.refs_2_, ...), custom_call_target="tpu_custom_call" | custom-call | flops 1 | bytes 1 | tf_op jit(solution)/shard_map/pallas_call | solution.py:19
  (22 shorter events, 0.1 us)
Async XLA Ops:
  0.6 3.5 %copy-start = (f32[4,18,40,384]{3,2,1,0:T(8,128)S(1)}, f32[4,18,40,384]{3,2,1,0:T(8,128)}, u32[]{:S(2)}) copy-start(f32[4,18,40,384]{3,2,1,0:T(8,128)} %f_ref.3) | copy-start | bytes 13271044
  2.7 12.0 %collective-permute-start.2 = (f32[4,40,384]{2,1,0:T(8,128)S(1)}, f32[4,40,384]{2,1,0:T(8,128)S(1)}, u32[]{:S(2)}, u32[]{:S(2)}) collective-permute-start(f32[4,40,384]{2,1,0:T(8,128)S(1)} %get-tuple-element.48), channel_id=1, source_target_pairs={{2,0},{4,2},{6,4},{3,1},{5,3},{7,5},{10,8},{12,10},{14,12},{11,9},... | collective-permute-start | bytes 737288 | tf_op jit(solution)/shard_map/ppermute | solution.py:675
  6.3 8.4 %collective-permute-start = (f32[3,68,128]{2,1,0:T(8,128)S(1)}, f32[3,68,128]{2,1,0:T(8,128)S(1)}, u32[]{:S(2)}, u32[]{:S(2)}) collective-permute-start(f32[3,68,128]{2,1,0:T(8,128)S(1)} %get-tuple-element.44), channel_id=1, source_target_pairs={{0,8},{8,16},{16,24},{24,0},{1,9},{9,17},{17,25},{25,1},{2,10},{10... | collective-permute-start | bytes 313352 | tf_op jit(solution)/shard_map/ppermute | solution.py:670
  6.8 7.9 %collective-permute-start.1 = (f32[3,68,128]{2,1,0:T(8,128)S(1)}, f32[3,68,128]{2,1,0:T(8,128)S(1)}, u32[]{:S(2)}, u32[]{:S(2)}) collective-permute-start(f32[3,68,128]{2,1,0:T(8,128)S(1)} %get-tuple-element.45), channel_id=1, source_target_pairs={{8,0},{16,8},{24,16},{0,24},{9,1},{17,9},{25,17},{1,25},{10,2},{18... | collective-permute-start | bytes 313352 | tf_op jit(solution)/shard_map/ppermute | solution.py:670
  11.3 3.4 %copy-start.3 = (s32[4,2]{0,1:T(2,128)S(1)}, s32[4,2]{0,1:T(2,128)}, u32[]{:S(2)}) copy-start(s32[4,2]{0,1:T(2,128)} %param.14) | copy-start | bytes 100
  15.0 11.3 %collective-permute-start.5 = (f32[4,40,384]{2,1,0:T(8,128)S(1)}, f32[4,40,384]{2,1,0:T(8,128)S(1)}, u32[]{:S(2)}, u32[]{:S(2)}) collective-permute-start(f32[4,40,384]{2,1,0:T(8,128)S(1)} %get-tuple-element.49.lowest_ref), channel_id=1, source_target_pairs={{2,0},{4,2},{6,4},{3,1},{5,3},{7,5},{10,8},{12,10},{14,12},{11,9},... | collective-permute-start | bytes 737288 | tf_op jit(solution)/shard_map/ppermute | solution.py:675
  16.3 4.7 %collective-permute-start.3 = (f32[3,4,128]{2,1,0:T(4,128)S(1)}, f32[3,4,128]{2,1,0:T(4,128)S(1)}, u32[]{:S(2)}, u32[]{:S(2)}) collective-permute-start(f32[3,4,128]{2,1,0:T(4,128)S(1)} %get-tuple-element.52), channel_id=1, source_target_pairs={{0,8},{8,16},{16,24},{24,0},{1,9},{9,17},{17,25},{25,1},{2,10},{10... | collective-permute-start | bytes 18440 | tf_op jit(solution)/shard_map/ppermute | solution.py:670
  17.0 4.1 %collective-permute-start.4 = (f32[3,4,128]{2,1,0:T(4,128)S(1)}, f32[3,4,128]{2,1,0:T(4,128)S(1)}, u32[]{:S(2)}, u32[]{:S(2)}) collective-permute-start(f32[3,4,128]{2,1,0:T(4,128)S(1)} %get-tuple-element.53), channel_id=1, source_target_pairs={{8,0},{16,8},{24,16},{0,24},{9,1},{17,9},{25,17},{1,25},{10,2},{18... | collective-permute-start | bytes 18440 | tf_op jit(solution)/shard_map/ppermute | solution.py:670
  21.0 7.3 %copy-start.4 = (f32[18]{0:T(128)S(1)}, f32[18]{0:T(128)}, u32[]{:S(2)}) copy-start(f32[18]{0:T(128)} %param.15) | copy-start | bytes 220
  21.0 7.4 %copy-start.1 = (f32[4,40,384]{2,1,0:T(8,128)S(1)}, f32[4,40,384]{2,1,0:T(8,128)}, u32[]{:S(2)}) copy-start(f32[4,40,384]{2,1,0:T(8,128)} %share_ref.3) | copy-start | bytes 737284
  21.3 9.1 %collective-permute-start.6 = (f32[3,68,128]{2,1,0:T(8,128)S(1)}, f32[3,68,128]{2,1,0:T(8,128)S(1)}, u32[]{:S(2)}, u32[]{:S(2)}) collective-permute-start(f32[3,68,128]{2,1,0:T(8,128)S(1)} %get-tuple-element.60), channel_id=1, source_target_pairs={{0,8},{8,16},{16,24},{24,0},{1,9},{9,17},{17,25},{25,1},{2,10},{10... | collective-permute-start | bytes 313352 | tf_op jit(solution)/shard_map/ppermute | solution.py:670
  22.4 8.0 %collective-permute-start.7 = (f32[3,68,128]{2,1,0:T(8,128)S(1)}, f32[3,68,128]{2,1,0:T(8,128)S(1)}, u32[]{:S(2)}, u32[]{:S(2)}) collective-permute-start(f32[3,68,128]{2,1,0:T(8,128)S(1)} %get-tuple-element.61), channel_id=1, source_target_pairs={{8,0},{16,8},{24,16},{0,24},{9,1},{17,9},{25,17},{1,25},{10,2},{18... | collective-permute-start | bytes 313352 | tf_op jit(solution)/shard_map/ppermute | solution.py:670
  26.5 3.9 %collective-permute-start.8 = (f32[3,4,128]{2,1,0:T(4,128)S(1)}, f32[3,4,128]{2,1,0:T(4,128)S(1)}, u32[]{:S(2)}, u32[]{:S(2)}) collective-permute-start(f32[3,4,128]{2,1,0:T(4,128)S(1)} %get-tuple-element.62), channel_id=1, source_target_pairs={{0,8},{8,16},{16,24},{24,0},{1,9},{9,17},{17,25},{25,1},{2,10},{10... | collective-permute-start | bytes 18440 | tf_op jit(solution)/shard_map/ppermute | solution.py:670
  26.6 3.9 %collective-permute-start.9 = (f32[3,4,128]{2,1,0:T(4,128)S(1)}, f32[3,4,128]{2,1,0:T(4,128)S(1)}, u32[]{:S(2)}, u32[]{:S(2)}) collective-permute-start(f32[3,4,128]{2,1,0:T(4,128)S(1)} %get-tuple-element.63), channel_id=1, source_target_pairs={{8,0},{16,8},{24,16},{0,24},{9,1},{17,9},{25,17},{1,25},{10,2},{18... | collective-permute-start | bytes 18440 | tf_op jit(solution)/shard_map/ppermute | solution.py:670
  30.4 8.2 %copy-start.2 = (s32[4,3840]{1,0:T(4,128)S(1)}, s32[4,3840]{1,0:T(4,128)}, u32[]{:S(2)}) copy-start(s32[4,3840]{1,0:T(4,128)} %param.17) | copy-start | bytes 184324
  33.1 13.3 %all-to-all-start = ((f32[32,8,128]{2,1,0:T(8,128)}), f32[32,8,128]{2,1,0:T(8,128)S(1)}, u32[]{:S(2)}, u32[]{:S(2)}) async-start(f32[32,8,128]{2,1,0:T(8,128)} %bitcast.2), calls=%async_computation | async-start | bytes 262144 | tf_op jit(solution)/shard_map/all_to_all | solution.py:653
  46.4 4.5 %collective-permute-start.10 = (f32[4,8,128]{2,1,0:T(8,128)S(1)}, f32[4,8,128]{2,1,0:T(8,128)S(1)}, u32[]{:S(2)}, u32[]{:S(2)}) collective-permute-start(f32[4,8,128]{2,1,0:T(8,128)S(1)} %bitcast_reduce_fusion.refs_0_), channel_id=1, source_target_pairs={{0,2},{2,0},{4,6},{6,4},{1,3},{3,1},{5,7},{7,5},{8,10},{10,8},{12,... | collective-permute-start | bytes 49160 | tf_op jit(solution)/shard_map/ppermute | solution.py:646
  47.5 4.6 %collective-permute-start.11 = (f32[4,8,128]{2,1,0:T(8,128)S(1)}, f32[4,8,128]{2,1,0:T(8,128)S(1)}, u32[]{:S(2)}, u32[]{:S(2)}) collective-permute-start(f32[4,8,128]{2,1,0:T(8,128)S(1)} %bitcast_reduce_fusion.refs_0_), channel_id=1, source_target_pairs={{0,4},{2,6},{4,0},{6,2},{1,5},{3,7},{5,1},{7,3},{8,12},{10,14},{12... | collective-permute-start | bytes 49160 | tf_op jit(solution)/shard_map/ppermute | solution.py:646
  48.4 5.5 %collective-permute-start.12 = (f32[4,8,128]{2,1,0:T(8,128)S(1)}, f32[4,8,128]{2,1,0:T(8,128)S(1)}, u32[]{:S(2)}, u32[]{:S(2)}) collective-permute-start(f32[4,8,128]{2,1,0:T(8,128)S(1)} %bitcast_reduce_fusion.refs_0_), channel_id=1, source_target_pairs={{0,6},{2,4},{4,2},{6,0},{1,7},{3,5},{5,3},{7,1},{8,14},{10,12},{12... | collective-permute-start | bytes 49160 | tf_op jit(solution)/shard_map/ppermute | solution.py:646

commit v14 on v12

--- a/solution.py
+++ b/solution.py
@@ -591,8 +591,7 @@
     for start in range(0, len(lines), wide):
         lefts, rights = [], []
         for part, owner, line in lines[start : start + wide]:
-            piece = jnp.bitwise_xor(rank, (group - part) % group)
-            cells = cells_ref[piece, owner, line : line + 1, :]
+            cells = cells_ref[jnp.bitwise_xor(rank, part), owner, line : line + 1, :]
             value = value_refs[part][owner, line : line + 1, :]
             coarse = value.astype(half).astype(jnp.float32)
             high = spread(jnp.right_shift(cells, 7).astype(jnp.float32)) == iota
@@ -629,7 +628,7 @@
         sent, ("tile", "lev", "sec"), split_axis=0, concat_axis=0, tiled=True
     )
     own = jnp.sum(arrived.reshape(owners, group * copies, depth, LANES), axis=1)
-    parts = [own] + [exchanged(own, "lev", group - d) for d in range(1, group)]
+    parts = [own] + [exchanged(own, "lev", d) for d in range(1, group)]
     cells = jnp.pad(flux_cell, ((0, 0), (0, group * depth * LANES - share)))
     cells = cells.reshape(owners, group, depth, LANES).transpose(1, 0, 2, 3)
     out = call(

time: 55.6 us -> 54.4 us (0.978)
  waiting for transfers between devices: 13.5 us -> 12.4 us
    ppermute x3, waiting for transfers between devices: 3.05 us -> 1.88 us  [exchanged(): return lax.ppermute(value, axis, [(i, i ^ apart) for i in range(count)])]
where the time goes in v14:
time: 54.4 us; the launch traced here: 54.2 us
  starting transfers between devices  21.1 us (39%)
  Pallas kernels  19.7 us (36%)
  waiting for transfers between devices  12.4 us (23%)
  between operations  0.85 us (2%)
    pallas_call x10, Pallas kernels, call(): pl.pallas_call(kernel, out_shape=out_shape, in_specs=in_specs, out_specs=...  19.7 us
    ppermute x8, starting transfers between devices, around(): return (lax.ppermute(last, 'tile', up), lax.ppermute(first, 'tile', down))  8.11 us
    all_to_all x1, waiting for transfers between devices, remapped(): lax.all_to_all(sent, ('tile', 'lev', 'sec'), split_axis=0, concat_axis=0,...  7.71 us
    all_to_all x1, starting transfers between devices, remapped(): lax.all_to_all(sent, ('tile', 'lev', 'sec'), split_axis=0, concat_axis=0,...  5.79 us
    ppermute x3, starting transfers between devices, exchanged(): return lax.ppermute(value, axis, [(i, i ^ apart) for i in range(count)])  4.45 us
    ppermute x2, starting transfers between devices, from_above(): return lax.ppermute(value, 'lev', [(i + 1, i) for i in range(count - 1)])  2.72 us
    ppermute x2, waiting for transfers between devices, from_above(): return lax.ppermute(value, 'lev', [(i + 1, i) for i in range(count - 1)])  2.52 us
    ppermute x3, waiting for transfers between devices, exchanged(): return lax.ppermute(value, axis, [(i, i ^ apart) for i in range(count)])  1.88 us
  transfers between devices with their start and end apart: 14, of which 6 were waited for; matrix products, arithmetic and copies ran while one was open for 0% of the time, Pallas kernels for 22%

profile of v14, /device:TPU:0, one launch (start us, length us, event | category | flops | bytes accessed | tf_op | source)
XLA Modules:
  0.0 54.2 jit_solution(5313047509007814999)
XLA Ops:
  0.6 2.0 %shard_map.104 = (f32[4,40,384]{2,1,0:T(8,128)S(1)}, bf16[18,40,384]{2,1,0:T(8,128)(2,1)S(1)}, bf16[18,40,384]{2,1,0:T(8,128)(2,1)S(1)}, s32[18,40,384]{2,1,0:T(8,128)S(1)}, bf16[18,40,384]{2,1,0:T(8,128)(2,1)S(1)}) custom-call(f32[4,18,40,384]{3,2,1,0:T(8,128)} %f_ref.1, bf16[18,40,384]{2,1,0:T(8,128)(2,1)} %mf_hbm.1, bf16[18,40,384]{2,1,0:T(8,128)(2,1)} %cy_hbm.1, ...), custom_call_target="tpu_custom_call" | custom-call | flops 1 | bytes 1 | tf_op jit(solution)/shard_map/pallas_call | solution.py:19
  2.7 1.4 %collective-permute-start.2 = (f32[4,40,384]{2,1,0:T(8,128)S(1)}, f32[4,40,384]{2,1,0:T(8,128)S(1)}, u32[]{:S(2)}, u32[]{:S(2)}) collective-permute-start(f32[4,40,384]{2,1,0:T(8,128)S(1)} %get-tuple-element.46), channel_id=1, source_target_pairs={{2,0},{4,2},{6,4},{3,1},{5,3},{7,5},{10,8},{12,10},{14,12},{11,9},... | collective-permute-start | bytes 737288 | tf_op jit(solution)/shard_map/ppermute | solution.py:649
  4.1 3.5 %shard_map.105 = (f32[17,4,3,56,128]{4,3,2,1,0:T(8,128)S(1)}, f32[3,68,128]{2,1,0:T(8,128)S(1)}, f32[3,68,128]{2,1,0:T(8,128)S(1)}, f32[4,40,384]{2,1,0:T(8,128)S(1)}) custom-call(f32[4,18,40,384]{3,2,1,0:T(8,128)S(1)} %copy-done, bf16[18,40,384]{2,1,0:T(8,128)(2,1)S(1)} %get-tuple-element.35.mf_ref, bf16[18,40,384]{2,1,0:T(8,128)(2,1)S(1)} %get-tuple-element.36.cy_ref, ...), custom_call_target="tpu_custom_call" | custom-call | flops 1 | bytes 1 | tf_op jit(solution)/shard_map/pallas_call | solution.py:19
  7.6 0.5 collective-permute-start
  8.1 2.0 %collective-permute-start.1 = (f32[3,68,128]{2,1,0:T(8,128)S(1)}, f32[3,68,128]{2,1,0:T(8,128)S(1)}, u32[]{:S(2)}, u32[]{:S(2)}) collective-permute-start(f32[3,68,128]{2,1,0:T(8,128)S(1)} %get-tuple-element.43), channel_id=1, source_target_pairs={{8,0},{16,8},{24,16},{0,24},{9,1},{17,9},{25,17},{1,25},{10,2},{18... | collective-permute-start | bytes 313352 | tf_op jit(solution)/shard_map/ppermute | solution.py:644
  10.1 3.1 %shard_map.106 = (f32[16,4,3,56,128]{4,3,2,1,0:T(8,128)S(1)}, f32[4,3,40,128]{3,2,1,0:T(8,128)S(1)}, f32[4,3,40,128]{3,2,1,0:T(8,128)S(1)}) custom-call(f32[17,4,3,56,128]{4,3,2,1,0:T(8,128)S(1)} %get-tuple-element.38.v_ref, bf16[18,40,384]{2,1,0:T(8,128)(2,1)S(1)} %get-tuple-element.39.cx_ref, bf16[18,40,384]{2,1,0:T(8,128)(2,1)S(1)} %get-tuple-element.35.mf_ref, ...), custom_call_target="tpu_custom_call" | custom-call | flops 1 | bytes 1 | tf_op jit(solution)/shard_map/pallas_call | solution.py:19
  13.2 0.2 collective-permute-done.1.right_ref
  13.5 0.2 collective-permute-done.2.above_ref
  13.7 0.1 broadcast_in_dim.4.seam_ref
  13.8 0.2 shard_map.107
  14.0 1.3 %collective-permute-start.5 = (f32[4,40,384]{2,1,0:T(8,128)S(1)}, f32[4,40,384]{2,1,0:T(8,128)S(1)}, u32[]{:S(2)}, u32[]{:S(2)}) collective-permute-start(f32[4,40,384]{2,1,0:T(8,128)S(1)} %get-tuple-element.47.lowest_ref), channel_id=1, source_target_pairs={{2,0},{4,2},{6,4},{3,1},{5,3},{7,5},{10,8},{12,10},{14,12},{11,9},... | collective-permute-start | bytes 737288 | tf_op jit(solution)/shard_map/ppermute | solution.py:649
  15.3 1.3 %collective-permute-start.3 = (f32[3,4,128]{2,1,0:T(4,128)S(1)}, f32[3,4,128]{2,1,0:T(4,128)S(1)}, u32[]{:S(2)}, u32[]{:S(2)}) collective-permute-start(f32[3,4,128]{2,1,0:T(4,128)S(1)} %get-tuple-element.50), channel_id=1, source_target_pairs={{0,8},{8,16},{16,24},{24,0},{1,9},{9,17},{17,25},{25,1},{2,10},{10... | collective-permute-start | bytes 18440 | tf_op jit(solution)/shard_map/ppermute | solution.py:644
  16.6 0.8 %collective-permute-start.4 = (f32[3,4,128]{2,1,0:T(4,128)S(1)}, f32[3,4,128]{2,1,0:T(4,128)S(1)}, u32[]{:S(2)}, u32[]{:S(2)}) collective-permute-start(f32[3,4,128]{2,1,0:T(4,128)S(1)} %get-tuple-element.51), channel_id=1, source_target_pairs={{8,0},{16,8},{24,16},{0,24},{9,1},{17,9},{25,17},{1,25},{10,2},{18... | collective-permute-start | bytes 18440 | tf_op jit(solution)/shard_map/ppermute | solution.py:644
  17.3 2.9 %shard_map.108 = (f32[16,4,3,56,128]{4,3,2,1,0:T(8,128)S(1)}, f32[3,64,128]{2,1,0:T(8,128)S(1)}, f32[3,64,128]{2,1,0:T(8,128)S(1)}, f32[4,3,40,128]{3,2,1,0:T(8,128)S(1)}) custom-call(f32[17,4,3,56,128]{4,3,2,1,0:T(8,128)S(1)} %get-tuple-element.38.v_ref, f32[4,3,40,128]{3,2,1,0:T(8,128)S(1)} %get-tuple-element.41.inner_top_ref, ...), custom_call_target="tpu_custom_call" | custom-call | flops 1 | bytes 1 | tf_op jit(solution)/shard_map/pallas_call | solution.py:19
  20.3 0.2 shard_map.109
  20.6 0.8 %collective-permute-start.6 = (f32[3,68,128]{2,1,0:T(8,128)S(1)}, f32[3,68,128]{2,1,0:T(8,128)S(1)}, u32[]{:S(2)}, u32[]{:S(2)}) collective-permute-start(f32[3,68,128]{2,1,0:T(8,128)S(1)} %get-tuple-element.58), channel_id=1, source_target_pairs={{0,8},{8,16},{16,24},{24,0},{1,9},{9,17},{17,25},{25,1},{2,10},{10... | collective-permute-start | bytes 313352 | tf_op jit(solution)/shard_map/ppermute | solution.py:644
  21.3 1.0 %collective-permute-start.7 = (f32[3,68,128]{2,1,0:T(8,128)S(1)}, f32[3,68,128]{2,1,0:T(8,128)S(1)}, u32[]{:S(2)}, u32[]{:S(2)}) collective-permute-start(f32[3,68,128]{2,1,0:T(8,128)S(1)} %get-tuple-element.59), channel_id=1, source_target_pairs={{8,0},{16,8},{24,16},{0,24},{9,1},{17,9},{25,17},{1,25},{10,2},{18... | collective-permute-start | bytes 313352 | tf_op jit(solution)/shard_map/ppermute | solution.py:644
  22.4 2.3 %collective-permute-done.5.above_ref = f32[4,40,384]{2,1,0:T(8,128)S(1)} collective-permute-done((f32[4,40,384]{2,1,0:T(8,128)S(1)}, f32[4,40,384]{2,1,0:T(8,128)S(1)}, u32[]{:S(2)}, u32[]{:S(2)}) %collective-permute-start.5) | collective-permute-done | bytes 245792 | tf_op jit(solution)/shard_map/ppermute | solution.py:649
  24.7 0.2 shard_map.110
  24.9 0.4 collective-permute-start.8
  25.3 1.3 %collective-permute-start.9 = (f32[3,4,128]{2,1,0:T(4,128)S(1)}, f32[3,4,128]{2,1,0:T(4,128)S(1)}, u32[]{:S(2)}, u32[]{:S(2)}) collective-permute-start(f32[3,4,128]{2,1,0:T(4,128)S(1)} %get-tuple-element.61), channel_id=1, source_target_pairs={{8,0},{16,8},{24,16},{0,24},{9,1},{17,9},{25,17},{1,25},{10,2},{18... | collective-permute-start | bytes 18440 | tf_op jit(solution)/shard_map/ppermute | solution.py:644
  26.7 0.1 broadcast_in_dim.5.weight_ref
  26.7 2.0 %shard_map.111 = (f32[4,18,40,384]{3,2,1,0:T(8,128)}, f32[40,384]{1,0:T(8,128)S(1)}) custom-call(f32[16,4,3,56,128]{4,3,2,1,0:T(8,128)S(1)} %get-tuple-element.40.inner_ref, f32[16,4,3,56,128]{4,3,2,1,0:T(8,128)S(1)} %get-tuple-element.48.outer_ref, f32[4,3,56,128]{3,2,1,0:T(8,128)S(1)} %get-tuple-element.55.vs_ref, ...), custom_call_target="tpu_custom_call" | custom-call | flops 1 | bytes 1 | tf_op jit(solution)/shard_map/pallas_call | solution.py:19
  28.8 2.5 %shard_map.112 = (f32[4,18,40,384]{3,2,1,0:T(8,128)}, f32[4,4,2,8,128]{4,3,2,1,0:T(8,128)}) custom-call(f32[16,4,3,56,128]{4,3,2,1,0:T(8,128)S(1)} %get-tuple-element.40.inner_ref, f32[16,4,3,56,128]{4,3,2,1,0:T(8,128)S(1)} %get-tuple-element.48.outer_ref, f32[4,3,56,128]{3,2,1,0:T(8,128)S(1)} %get-tuple-element.55.vs_ref, ...), custom_call_target="tpu_custom_call", output_to_operand_aliasing={{0}: (14, {})} | custom-call | flops 1 | bytes 1 | tf_op jit(solution)/shard_map/pallas_call | solution.py:19
  31.4 5.8 %all-to-all-start = ((f32[32,8,128]{2,1,0:T(8,128)}), f32[32,8,128]{2,1,0:T(8,128)S(1)}, u32[]{:S(2)}, u32[]{:S(2)}) async-start(f32[32,8,128]{2,1,0:T(8,128)} %bitcast.2), calls=%async_computation | async-start | bytes 262144 | tf_op jit(solution)/shard_map/all_to_all | solution.py:627
  37.2 7.7 %all-to-all-done = f32[32,8,128]{2,1,0:T(8,128)S(1)} async-done(((f32[32,8,128]{2,1,0:T(8,128)}), f32[32,8,128]{2,1,0:T(8,128)S(1)}, u32[]{:S(2)}, u32[]{:S(2)}) %all-to-all-start) | async-done | bytes 131104 | tf_op jit(solution)/shard_map/all_to_all | solution.py:627
  44.9 1.4 %collective-permute-start.12 = (f32[4,8,128]{2,1,0:T(8,128)S(1)}, f32[4,8,128]{2,1,0:T(8,128)S(1)}, u32[]{:S(2)}, u32[]{:S(2)}) collective-permute-start(f32[4,8,128]{2,1,0:T(8,128)S(1)} %bitcast_reduce_fusion.refs_0_), channel_id=1, source_target_pairs={{0,6},{2,4},{4,2},{6,0},{1,7},{3,5},{5,3},{7,1},{8,14},{10,12},{12... | collective-permute-start | bytes 49160 | tf_op jit(solution)/shard_map/ppermute | solution.py:620
  46.3 1.1 %collective-permute-start.11 = (f32[4,8,128]{2,1,0:T(8,128)S(1)}, f32[4,8,128]{2,1,0:T(8,128)S(1)}, u32[]{:S(2)}, u32[]{:S(2)}) collective-permute-start(f32[4,8,128]{2,1,0:T(8,128)S(1)} %bitcast_reduce_fusion.refs_0_), channel_id=1, source_target_pairs={{0,4},{2,6},{4,0},{6,2},{1,5},{3,7},{5,1},{7,3},{8,12},{10,14},{12... | collective-permute-start | bytes 49160 | tf_op jit(solution)/shard_map/ppermute | solution.py:620
  47.5 1.9 %collective-permute-start.10 = (f32[4,8,128]{2,1,0:T(8,128)S(1)}, f32[4,8,128]{2,1,0:T(8,128)S(1)}, u32[]{:S(2)}, u32[]{:S(2)}) collective-permute-start(f32[4,8,128]{2,1,0:T(8,128)S(1)} %bitcast_reduce_fusion.refs_0_), channel_id=1, source_target_pairs={{0,2},{2,0},{4,6},{6,4},{1,3},{3,1},{5,7},{7,5},{8,10},{10,8},{12,... | collective-permute-start | bytes 49160 | tf_op jit(solution)/shard_map/ppermute | solution.py:620
  49.4 1.1 %collective-permute-done.12.refs_3_ = f32[4,8,128]{2,1,0:T(8,128)S(1)} collective-permute-done((f32[4,8,128]{2,1,0:T(8,128)S(1)}, f32[4,8,128]{2,1,0:T(8,128)S(1)}, u32[]{:S(2)}, u32[]{:S(2)}) %collective-permute-start.12) | collective-permute-done | bytes 16416 | tf_op jit(solution)/shard_map/ppermute | solution.py:620
  50.5 0.7 %collective-permute-done.11.refs_2_ = f32[4,8,128]{2,1,0:T(8,128)S(1)} collective-permute-done((f32[4,8,128]{2,1,0:T(8,128)S(1)}, f32[4,8,128]{2,1,0:T(8,128)S(1)}, u32[]{:S(2)}, u32[]{:S(2)}) %collective-permute-start.11) | collective-permute-done | bytes 16416 | tf_op jit(solution)/shard_map/ppermute | solution.py:620
  51.3 3.0 %shard_map.113 = f32[120,128]{1,0:T(8,128)} custom-call(s32[4,4,8,128]{3,2,1,0:T(8,128)S(1)} %copy_bitcast_fusion.1.cells_ref, f32[4,8,128]{2,1,0:T(8,128)S(1)} %bitcast_reduce_fusion.refs_0_, f32[4,8,128]{2,1,0:T(8,128)S(1)} %collective-permute-done.10.refs_1_, f32[4,8,128]{2,1,0:T(8,128)S(1)} %collective-permute-done.11.refs_2_, ...), custom_call_target="tpu_custom_call" | custom-call | flops 1 | bytes 1 | tf_op jit(solution)/shard_map/pallas_call | solution.py:19
  (21 shorter events, 0.1 us)
Async XLA Ops:
  0.6 3.5 %copy-start = (f32[4,18,40,384]{3,2,1,0:T(8,128)S(1)}, f32[4,18,40,384]{3,2,1,0:T(8,128)}, u32[]{:S(2)}) copy-start(f32[4,18,40,384]{3,2,1,0:T(8,128)} %f_ref.1) | copy-start | bytes 13271044
  2.7 11.0 %collective-permute-start.2 = (f32[4,40,384]{2,1,0:T(8,128)S(1)}, f32[4,40,384]{2,1,0:T(8,128)S(1)}, u32[]{:S(2)}, u32[]{:S(2)}) collective-permute-start(f32[4,40,384]{2,1,0:T(8,128)S(1)} %get-tuple-element.46), channel_id=1, source_target_pairs={{2,0},{4,2},{6,4},{3,1},{5,3},{7,5},{10,8},{12,10},{14,12},{11,9},... | collective-permute-start | bytes 737288 | tf_op jit(solution)/shard_map/ppermute | solution.py:649
  7.6 6.1 %copy-start.3 = (s32[4,2]{0,1:T(2,128)S(1)}, s32[4,2]{0,1:T(2,128)}, u32[]{:S(2)}) copy-start(s32[4,2]{0,1:T(2,128)} %param.14) | copy-start | bytes 100
  7.6 5.6 %collective-permute-start = (f32[3,68,128]{2,1,0:T(8,128)S(1)}, f32[3,68,128]{2,1,0:T(8,128)S(1)}, u32[]{:S(2)}, u32[]{:S(2)}) collective-permute-start(f32[3,68,128]{2,1,0:T(8,128)S(1)} %get-tuple-element.42), channel_id=1, source_target_pairs={{0,8},{8,16},{16,24},{24,0},{1,9},{9,17},{17,25},{25,1},{2,10},{10... | collective-permute-start | bytes 313352 | tf_op jit(solution)/shard_map/ppermute | solution.py:644
  8.1 5.4 %collective-permute-start.1 = (f32[3,68,128]{2,1,0:T(8,128)S(1)}, f32[3,68,128]{2,1,0:T(8,128)S(1)}, u32[]{:S(2)}, u32[]{:S(2)}) collective-permute-start(f32[3,68,128]{2,1,0:T(8,128)S(1)} %get-tuple-element.43), channel_id=1, source_target_pairs={{8,0},{16,8},{24,16},{0,24},{9,1},{17,9},{25,17},{1,25},{10,2},{18... | collective-permute-start | bytes 313352 | tf_op jit(solution)/shard_map/ppermute | solution.py:644
  14.0 10.7 %collective-permute-start.5 = (f32[4,40,384]{2,1,0:T(8,128)S(1)}, f32[4,40,384]{2,1,0:T(8,128)S(1)}, u32[]{:S(2)}, u32[]{:S(2)}) collective-permute-start(f32[4,40,384]{2,1,0:T(8,128)S(1)} %get-tuple-element.47.lowest_ref), channel_id=1, source_target_pairs={{2,0},{4,2},{6,4},{3,1},{5,3},{7,5},{10,8},{12,10},{14,12},{11,9},... | collective-permute-start | bytes 737288 | tf_op jit(solution)/shard_map/ppermute | solution.py:649
  15.3 5.0 %collective-permute-start.3 = (f32[3,4,128]{2,1,0:T(4,128)S(1)}, f32[3,4,128]{2,1,0:T(4,128)S(1)}, u32[]{:S(2)}, u32[]{:S(2)}) collective-permute-start(f32[3,4,128]{2,1,0:T(4,128)S(1)} %get-tuple-element.50), channel_id=1, source_target_pairs={{0,8},{8,16},{16,24},{24,0},{1,9},{9,17},{17,25},{25,1},{2,10},{10... | collective-permute-start | bytes 18440 | tf_op jit(solution)/shard_map/ppermute | solution.py:644
  16.6 3.7 %collective-permute-start.4 = (f32[3,4,128]{2,1,0:T(4,128)S(1)}, f32[3,4,128]{2,1,0:T(4,128)S(1)}, u32[]{:S(2)}, u32[]{:S(2)}) collective-permute-start(f32[3,4,128]{2,1,0:T(4,128)S(1)} %get-tuple-element.51), channel_id=1, source_target_pairs={{8,0},{16,8},{24,16},{0,24},{9,1},{17,9},{25,17},{1,25},{10,2},{18... | collective-permute-start | bytes 18440 | tf_op jit(solution)/shard_map/ppermute | solution.py:644
  20.3 6.4 %copy-start.4 = (f32[18]{0:T(128)S(1)}, f32[18]{0:T(128)}, u32[]{:S(2)}) copy-start(f32[18]{0:T(128)} %param.15) | copy-start | bytes 220
  20.3 6.5 %copy-start.1 = (f32[4,40,384]{2,1,0:T(8,128)S(1)}, f32[4,40,384]{2,1,0:T(8,128)}, u32[]{:S(2)}) copy-start(f32[4,40,384]{2,1,0:T(8,128)} %share_ref.3) | copy-start | bytes 737284
  20.6 8.2 %collective-permute-start.6 = (f32[3,68,128]{2,1,0:T(8,128)S(1)}, f32[3,68,128]{2,1,0:T(8,128)S(1)}, u32[]{:S(2)}, u32[]{:S(2)}) collective-permute-start(f32[3,68,128]{2,1,0:T(8,128)S(1)} %get-tuple-element.58), channel_id=1, source_target_pairs={{0,8},{8,16},{16,24},{24,0},{1,9},{9,17},{17,25},{25,1},{2,10},{10... | collective-permute-start | bytes 313352 | tf_op jit(solution)/shard_map/ppermute | solution.py:644
  21.3 7.5 %collective-permute-start.7 = (f32[3,68,128]{2,1,0:T(8,128)S(1)}, f32[3,68,128]{2,1,0:T(8,128)S(1)}, u32[]{:S(2)}, u32[]{:S(2)}) collective-permute-start(f32[3,68,128]{2,1,0:T(8,128)S(1)} %get-tuple-element.59), channel_id=1, source_target_pairs={{8,0},{16,8},{24,16},{0,24},{9,1},{17,9},{25,17},{1,25},{10,2},{18... | collective-permute-start | bytes 313352 | tf_op jit(solution)/shard_map/ppermute | solution.py:644
  24.9 3.9 %collective-permute-start.8 = (f32[3,4,128]{2,1,0:T(4,128)S(1)}, f32[3,4,128]{2,1,0:T(4,128)S(1)}, u32[]{:S(2)}, u32[]{:S(2)}) collective-permute-start(f32[3,4,128]{2,1,0:T(4,128)S(1)} %get-tuple-element.60), channel_id=1, source_target_pairs={{0,8},{8,16},{16,24},{24,0},{1,9},{9,17},{17,25},{25,1},{2,10},{10... | collective-permute-start | bytes 18440 | tf_op jit(solution)/shard_map/ppermute | solution.py:644
  25.3 3.5 %collective-permute-start.9 = (f32[3,4,128]{2,1,0:T(4,128)S(1)}, f32[3,4,128]{2,1,0:T(4,128)S(1)}, u32[]{:S(2)}, u32[]{:S(2)}) collective-permute-start(f32[3,4,128]{2,1,0:T(4,128)S(1)} %get-tuple-element.61), channel_id=1, source_target_pairs={{8,0},{16,8},{24,16},{0,24},{9,1},{17,9},{25,17},{1,25},{10,2},{18... | collective-permute-start | bytes 18440 | tf_op jit(solution)/shard_map/ppermute | solution.py:644
  28.8 8.4 %copy-start.2 = (s32[4,3840]{1,0:T(4,128)S(1)}, s32[4,3840]{1,0:T(4,128)}, u32[]{:S(2)}) copy-start(s32[4,3840]{1,0:T(4,128)} %param.17) | copy-start | bytes 184324
  31.4 13.5 %all-to-all-start = ((f32[32,8,128]{2,1,0:T(8,128)}), f32[32,8,128]{2,1,0:T(8,128)S(1)}, u32[]{:S(2)}, u32[]{:S(2)}) async-start(f32[32,8,128]{2,1,0:T(8,128)} %bitcast.2), calls=%async_computation | async-start | bytes 262144 | tf_op jit(solution)/shard_map/all_to_all | solution.py:627
  44.9 5.6 %collective-permute-start.12 = (f32[4,8,128]{2,1,0:T(8,128)S(1)}, f32[4,8,128]{2,1,0:T(8,128)S(1)}, u32[]{:S(2)}, u32[]{:S(2)}) collective-permute-start(f32[4,8,128]{2,1,0:T(8,128)S(1)} %bitcast_reduce_fusion.refs_0_), channel_id=1, source_target_pairs={{0,6},{2,4},{4,2},{6,0},{1,7},{3,5},{5,3},{7,1},{8,14},{10,12},{12... | collective-permute-start | bytes 49160 | tf_op jit(solution)/shard_map/ppermute | solution.py:620
  46.3 4.9 %collective-permute-start.11 = (f32[4,8,128]{2,1,0:T(8,128)S(1)}, f32[4,8,128]{2,1,0:T(8,128)S(1)}, u32[]{:S(2)}, u32[]{:S(2)}) collective-permute-start(f32[4,8,128]{2,1,0:T(8,128)S(1)} %bitcast_reduce_fusion.refs_0_), channel_id=1, source_target_pairs={{0,4},{2,6},{4,0},{6,2},{1,5},{3,7},{5,1},{7,3},{8,12},{10,14},{12... | collective-permute-start | bytes 49160 | tf_op jit(solution)/shard_map/ppermute | solution.py:620
  47.5 3.8 %collective-permute-start.10 = (f32[4,8,128]{2,1,0:T(8,128)S(1)}, f32[4,8,128]{2,1,0:T(8,128)S(1)}, u32[]{:S(2)}, u32[]{:S(2)}) collective-permute-start(f32[4,8,128]{2,1,0:T(8,128)S(1)} %bitcast_reduce_fusion.refs_0_), channel_id=1, source_target_pairs={{0,2},{2,0},{4,6},{6,4},{1,3},{3,1},{5,7},{7,5},{8,10},{10,8},{12,... | collective-permute-start | bytes 49160 | tf_op jit(solution)/shard_map/ppermute | solution.py:620

commit v15 on v14

--- a/solution.py
+++ b/solution.py
@@ -130,7 +130,7 @@
     return seam_ref[0, pl.ds(tile, 1), :] == 1, seam_ref[1, pl.ds(tile, 1), :] == 1
 
 
-def start_kernel(f_hbm, mf_hbm, cy_hbm, code_hbm, cx_hbm, out_ref, mf_ref, cy_ref, code_ref, cx_ref, sems):
+def start_kernel(f_hbm, mf_hbm, cy_hbm, code_hbm, out_ref, mf_ref, cy_ref, code_ref, sems):
     copies = [
         pltpu.make_async_copy(source, target, sems.at[i])
         for i, (source, target) in enumerate(
@@ -139,7 +139,6 @@
                 (mf_hbm, mf_ref),
                 (cy_hbm, cy_ref),
                 (code_hbm, code_ref),
-                (cx_hbm, cx_ref),
             )
         )
     ]
@@ -667,13 +666,13 @@
     weight = jnp.broadcast_to(level_weight[:, None], (levels, LANES))
 
     narrow = pltpu.VMEM((levels, columns, width), jnp.bfloat16)
-    lowest, mass_flux, courant_y, limiter_code, courant_x = call(
+    lowest, mass_flux, courant_y, limiter_code = call(
         start_kernel,
-        (plane, narrow, narrow, pltpu.VMEM((levels, columns, width), jnp.int32), narrow),
-        [HBM] * 5,
-        [VM] * 5,
-        in_hbm(forcing, mass_flux, courant_y, limiter_code, courant_x),
-        [pltpu.SemaphoreType.DMA((5,))],
+        (plane, narrow, narrow, pltpu.VMEM((levels, columns, width), jnp.int32)),
+        [HBM] * 4,
+        [VM] * 4,
+        in_hbm(forcing, mass_flux, courant_y, limiter_code),
+        [pltpu.SemaphoreType.DMA((4,))],
     )
     above = from_above(lowest)
     v, first, last, top = call(

time: 54.4 us -> 54.3 us (level)
  no operation moved by 1% of the time
where the time goes in v15:
time: 54.3 us; the launch traced here: 54.1 us
  starting transfers between devices  21.1 us (39%)
  Pallas kernels  19.6 us (36%)
  waiting for transfers between devices  12.4 us (23%)
  between operations  0.86 us (2%)
    pallas_call x10, Pallas kernels, call(): pl.pallas_call(kernel, out_shape=out_shape, in_specs=in_specs, out_specs=...  19.6 us
    ppermute x8, starting transfers between devices, around(): return (lax.ppermute(last, 'tile', up), lax.ppermute(first, 'tile', down))  8.1 us
    all_to_all x1, waiting for transfers between devices, remapped(): lax.all_to_all(sent, ('tile', 'lev', 'sec'), split_axis=0, concat_axis=0,...  7.71 us
    all_to_all x1, starting transfers between devices, remapped(): lax.all_to_all(sent, ('tile', 'lev', 'sec'), split_axis=0, concat_axis=0,...  5.8 us
    ppermute x3, starting transfers between devices, exchanged(): return lax.ppermute(value, axis, [(i, i ^ apart) for i in range(count)])  4.45 us
    ppermute x2, starting transfers between devices, from_above(): return lax.ppermute(value, 'lev', [(i + 1, i) for i in range(count - 1)])  2.72 us
    ppermute x2, waiting for transfers between devices, from_above(): return lax.ppermute(value, 'lev', [(i + 1, i) for i in range(count - 1)])  2.53 us
    ppermute x3, waiting for transfers between devices, exchanged(): return lax.ppermute(value, axis, [(i, i ^ apart) for i in range(count)])  1.88 us
  transfers between devices with their start and end apart: 14, of which 6 were waited for; matrix products, arithmetic and copies ran while one was open for 0% of the time, Pallas kernels for 22%

profile of v15, /device:TPU:0, one launch (start us, length us, event | category | flops | bytes accessed | tf_op | source)
XLA Modules:
  0.0 54.1 jit_solution(18047077732865874204)
XLA Ops:
  0.6 1.9 %shard_map.104 = (f32[4,40,384]{2,1,0:T(8,128)S(1)}, bf16[18,40,384]{2,1,0:T(8,128)(2,1)S(1)}, bf16[18,40,384]{2,1,0:T(8,128)(2,1)S(1)}, s32[18,40,384]{2,1,0:T(8,128)S(1)}) custom-call(f32[4,18,40,384]{3,2,1,0:T(8,128)} %f_ref.1, bf16[18,40,384]{2,1,0:T(8,128)(2,1)} %mf_hbm.1, bf16[18,40,384]{2,1,0:T(8,128)(2,1)} %cy_hbm.1, s32[18,40,384]{2,1,0:T(8,128)} %code_hbm.1), custom_call_target="tpu_custom_call" | custom-call | flops 1 | bytes 1 | tf_op jit(solution)/shard_map/pallas_call | solution.py:19
  2.5 1.4 %collective-permute-start.2 = (f32[4,40,384]{2,1,0:T(8,128)S(1)}, f32[4,40,384]{2,1,0:T(8,128)S(1)}, u32[]{:S(2)}, u32[]{:S(2)}) collective-permute-start(f32[4,40,384]{2,1,0:T(8,128)S(1)} %get-tuple-element.44), channel_id=1, source_target_pairs={{2,0},{4,2},{6,4},{3,1},{5,3},{7,5},{10,8},{12,10},{14,12},{11,9},... | collective-permute-start | bytes 737288 | tf_op jit(solution)/shard_map/ppermute | solution.py:648
  4.0 3.5 %shard_map.105 = (f32[17,4,3,56,128]{4,3,2,1,0:T(8,128)S(1)}, f32[3,68,128]{2,1,0:T(8,128)S(1)}, f32[3,68,128]{2,1,0:T(8,128)S(1)}, f32[4,40,384]{2,1,0:T(8,128)S(1)}) custom-call(f32[4,18,40,384]{3,2,1,0:T(8,128)S(1)} %copy-done.1, bf16[18,40,384]{2,1,0:T(8,128)(2,1)S(1)} %get-tuple-element.34.mf_ref, bf16[18,40,384]{2,1,0:T(8,128)(2,1)S(1)} %get-tuple-element.35.cy_ref, ...), custom_call_target="tpu_custom_call" | custom-call | flops 1 | bytes 1 | tf_op jit(solution)/shard_map/pallas_call | solution.py:19
  7.5 0.5 collective-permute-start
  8.0 2.0 %collective-permute-start.1 = (f32[3,68,128]{2,1,0:T(8,128)S(1)}, f32[3,68,128]{2,1,0:T(8,128)S(1)}, u32[]{:S(2)}, u32[]{:S(2)}) collective-permute-start(f32[3,68,128]{2,1,0:T(8,128)S(1)} %get-tuple-element.41), channel_id=1, source_target_pairs={{8,0},{16,8},{24,16},{0,24},{9,1},{17,9},{25,17},{1,25},{10,2},{18... | collective-permute-start | bytes 313352 | tf_op jit(solution)/shard_map/ppermute | solution.py:643
  10.0 3.1 %shard_map.106 = (f32[16,4,3,56,128]{4,3,2,1,0:T(8,128)S(1)}, f32[4,3,40,128]{3,2,1,0:T(8,128)S(1)}, f32[4,3,40,128]{3,2,1,0:T(8,128)S(1)}) custom-call(f32[17,4,3,56,128]{4,3,2,1,0:T(8,128)S(1)} %get-tuple-element.37.v_ref, bf16[18,40,384]{2,1,0:T(8,128)(2,1)S(1)} %copy-done, bf16[18,40,384]{2,1,0:T(8,128)(2,1)S(1)} %get-tuple-element.34.mf_ref, ...), custom_call_target="tpu_custom_call" | custom-call | flops 1 | bytes 1 | tf_op jit(solution)/shard_map/pallas_call | solution.py:19
  13.1 0.2 collective-permute-done.1.right_ref
  13.3 0.2 collective-permute-done.2.above_ref
  13.6 0.1 broadcast_in_dim.4.seam_ref
  13.6 0.2 shard_map.107
  13.9 1.3 %collective-permute-start.5 = (f32[4,40,384]{2,1,0:T(8,128)S(1)}, f32[4,40,384]{2,1,0:T(8,128)S(1)}, u32[]{:S(2)}, u32[]{:S(2)}) collective-permute-start(f32[4,40,384]{2,1,0:T(8,128)S(1)} %get-tuple-element.45.lowest_ref), channel_id=1, source_target_pairs={{2,0},{4,2},{6,4},{3,1},{5,3},{7,5},{10,8},{12,10},{14,12},{11,9},... | collective-permute-start | bytes 737288 | tf_op jit(solution)/shard_map/ppermute | solution.py:648
  15.2 1.2 %collective-permute-start.3 = (f32[3,4,128]{2,1,0:T(4,128)S(1)}, f32[3,4,128]{2,1,0:T(4,128)S(1)}, u32[]{:S(2)}, u32[]{:S(2)}) collective-permute-start(f32[3,4,128]{2,1,0:T(4,128)S(1)} %get-tuple-element.48), channel_id=1, source_target_pairs={{0,8},{8,16},{16,24},{24,0},{1,9},{9,17},{17,25},{25,1},{2,10},{10... | collective-permute-start | bytes 18440 | tf_op jit(solution)/shard_map/ppermute | solution.py:643
  16.4 0.8 %collective-permute-start.4 = (f32[3,4,128]{2,1,0:T(4,128)S(1)}, f32[3,4,128]{2,1,0:T(4,128)S(1)}, u32[]{:S(2)}, u32[]{:S(2)}) collective-permute-start(f32[3,4,128]{2,1,0:T(4,128)S(1)} %get-tuple-element.49), channel_id=1, source_target_pairs={{8,0},{16,8},{24,16},{0,24},{9,1},{17,9},{25,17},{1,25},{10,2},{18... | collective-permute-start | bytes 18440 | tf_op jit(solution)/shard_map/ppermute | solution.py:643
  17.2 2.9 %shard_map.108 = (f32[16,4,3,56,128]{4,3,2,1,0:T(8,128)S(1)}, f32[3,64,128]{2,1,0:T(8,128)S(1)}, f32[3,64,128]{2,1,0:T(8,128)S(1)}, f32[4,3,40,128]{3,2,1,0:T(8,128)S(1)}) custom-call(f32[17,4,3,56,128]{4,3,2,1,0:T(8,128)S(1)} %get-tuple-element.37.v_ref, f32[4,3,40,128]{3,2,1,0:T(8,128)S(1)} %get-tuple-element.39.inner_top_ref, ...), custom_call_target="tpu_custom_call" | custom-call | flops 1 | bytes 1 | tf_op jit(solution)/shard_map/pallas_call | solution.py:19
  20.2 0.2 shard_map.109
  20.4 0.8 %collective-permute-start.6 = (f32[3,68,128]{2,1,0:T(8,128)S(1)}, f32[3,68,128]{2,1,0:T(8,128)S(1)}, u32[]{:S(2)}, u32[]{:S(2)}) collective-permute-start(f32[3,68,128]{2,1,0:T(8,128)S(1)} %get-tuple-element.56), channel_id=1, source_target_pairs={{0,8},{8,16},{16,24},{24,0},{1,9},{9,17},{17,25},{25,1},{2,10},{10... | collective-permute-start | bytes 313352 | tf_op jit(solution)/shard_map/ppermute | solution.py:643
  21.2 1.0 %collective-permute-start.7 = (f32[3,68,128]{2,1,0:T(8,128)S(1)}, f32[3,68,128]{2,1,0:T(8,128)S(1)}, u32[]{:S(2)}, u32[]{:S(2)}) collective-permute-start(f32[3,68,128]{2,1,0:T(8,128)S(1)} %get-tuple-element.57), channel_id=1, source_target_pairs={{8,0},{16,8},{24,16},{0,24},{9,1},{17,9},{25,17},{1,25},{10,2},{18... | collective-permute-start | bytes 313352 | tf_op jit(solution)/shard_map/ppermute | solution.py:643
  22.2 2.3 %collective-permute-done.5.above_ref = f32[4,40,384]{2,1,0:T(8,128)S(1)} collective-permute-done((f32[4,40,384]{2,1,0:T(8,128)S(1)}, f32[4,40,384]{2,1,0:T(8,128)S(1)}, u32[]{:S(2)}, u32[]{:S(2)}) %collective-permute-start.5) | collective-permute-done | bytes 245792 | tf_op jit(solution)/shard_map/ppermute | solution.py:648
  24.5 0.2 shard_map.110
  24.7 0.4 collective-permute-start.8
  25.2 1.3 %collective-permute-start.9 = (f32[3,4,128]{2,1,0:T(4,128)S(1)}, f32[3,4,128]{2,1,0:T(4,128)S(1)}, u32[]{:S(2)}, u32[]{:S(2)}) collective-permute-start(f32[3,4,128]{2,1,0:T(4,128)S(1)} %get-tuple-element.59), channel_id=1, source_target_pairs={{8,0},{16,8},{24,16},{0,24},{9,1},{17,9},{25,17},{1,25},{10,2},{18... | collective-permute-start | bytes 18440 | tf_op jit(solution)/shard_map/ppermute | solution.py:643
  26.5 0.1 broadcast_in_dim.5.weight_ref
  26.6 2.0 %shard_map.111 = (f32[4,18,40,384]{3,2,1,0:T(8,128)}, f32[40,384]{1,0:T(8,128)S(1)}) custom-call(f32[16,4,3,56,128]{4,3,2,1,0:T(8,128)S(1)} %get-tuple-element.38.inner_ref, f32[16,4,3,56,128]{4,3,2,1,0:T(8,128)S(1)} %get-tuple-element.46.outer_ref, f32[4,3,56,128]{3,2,1,0:T(8,128)S(1)} %get-tuple-element.53.vs_ref, bf16[18,40,384]{2,1,0:T(8,128)(2,1)S(1)} %copy-done, ...), custom_call_target="tpu_custom_call" | custom-call | flops 1 | bytes 1 | tf_op jit(solution)/shard_map/pallas_call | solution.py:19
  28.7 2.5 %shard_map.112 = (f32[4,18,40,384]{3,2,1,0:T(8,128)}, f32[4,4,2,8,128]{4,3,2,1,0:T(8,128)}) custom-call(f32[16,4,3,56,128]{4,3,2,1,0:T(8,128)S(1)} %get-tuple-element.38.inner_ref, f32[16,4,3,56,128]{4,3,2,1,0:T(8,128)S(1)} %get-tuple-element.46.outer_ref, f32[4,3,56,128]{3,2,1,0:T(8,128)S(1)} %get-tuple-element.53.vs_ref, ...), custom_call_target="tpu_custom_call", output_to_operand_aliasing={{0}: (14, {})} | custom-call | flops 1 | bytes 1 | tf_op jit(solution)/shard_map/pallas_call | solution.py:19
  31.2 5.8 %all-to-all-start = ((f32[32,8,128]{2,1,0:T(8,128)}), f32[32,8,128]{2,1,0:T(8,128)S(1)}, u32[]{:S(2)}, u32[]{:S(2)}) async-start(f32[32,8,128]{2,1,0:T(8,128)} %bitcast.2), calls=%async_computation | async-start | bytes 262144 | tf_op jit(solution)/shard_map/all_to_all | solution.py:626
  37.0 7.7 %all-to-all-done = f32[32,8,128]{2,1,0:T(8,128)S(1)} async-done(((f32[32,8,128]{2,1,0:T(8,128)}), f32[32,8,128]{2,1,0:T(8,128)S(1)}, u32[]{:S(2)}, u32[]{:S(2)}) %all-to-all-start) | async-done | bytes 131104 | tf_op jit(solution)/shard_map/all_to_all | solution.py:626
  44.8 1.4 %collective-permute-start.12 = (f32[4,8,128]{2,1,0:T(8,128)S(1)}, f32[4,8,128]{2,1,0:T(8,128)S(1)}, u32[]{:S(2)}, u32[]{:S(2)}) collective-permute-start(f32[4,8,128]{2,1,0:T(8,128)S(1)} %bitcast_reduce_fusion.refs_0_), channel_id=1, source_target_pairs={{0,6},{2,4},{4,2},{6,0},{1,7},{3,5},{5,3},{7,1},{8,14},{10,12},{12... | collective-permute-start | bytes 49160 | tf_op jit(solution)/shard_map/ppermute | solution.py:619
  46.2 1.1 %collective-permute-start.11 = (f32[4,8,128]{2,1,0:T(8,128)S(1)}, f32[4,8,128]{2,1,0:T(8,128)S(1)}, u32[]{:S(2)}, u32[]{:S(2)}) collective-permute-start(f32[4,8,128]{2,1,0:T(8,128)S(1)} %bitcast_reduce_fusion.refs_0_), channel_id=1, source_target_pairs={{0,4},{2,6},{4,0},{6,2},{1,5},{3,7},{5,1},{7,3},{8,12},{10,14},{12... | collective-permute-start | bytes 49160 | tf_op jit(solution)/shard_map/ppermute | solution.py:619
  47.3 1.9 %collective-permute-start.10 = (f32[4,8,128]{2,1,0:T(8,128)S(1)}, f32[4,8,128]{2,1,0:T(8,128)S(1)}, u32[]{:S(2)}, u32[]{:S(2)}) collective-permute-start(f32[4,8,128]{2,1,0:T(8,128)S(1)} %bitcast_reduce_fusion.refs_0_), channel_id=1, source_target_pairs={{0,2},{2,0},{4,6},{6,4},{1,3},{3,1},{5,7},{7,5},{8,10},{10,8},{12,... | collective-permute-start | bytes 49160 | tf_op jit(solution)/shard_map/ppermute | solution.py:619
  49.2 1.1 %collective-permute-done.12.refs_3_ = f32[4,8,128]{2,1,0:T(8,128)S(1)} collective-permute-done((f32[4,8,128]{2,1,0:T(8,128)S(1)}, f32[4,8,128]{2,1,0:T(8,128)S(1)}, u32[]{:S(2)}, u32[]{:S(2)}) %collective-permute-start.12) | collective-permute-done | bytes 16416 | tf_op jit(solution)/shard_map/ppermute | solution.py:619
  50.4 0.7 %collective-permute-done.11.refs_2_ = f32[4,8,128]{2,1,0:T(8,128)S(1)} collective-permute-done((f32[4,8,128]{2,1,0:T(8,128)S(1)}, f32[4,8,128]{2,1,0:T(8,128)S(1)}, u32[]{:S(2)}, u32[]{:S(2)}) %collective-permute-start.11) | collective-permute-done | bytes 16416 | tf_op jit(solution)/shard_map/ppermute | solution.py:619
  51.1 3.0 %shard_map.113 = f32[120,128]{1,0:T(8,128)} custom-call(s32[4,4,8,128]{3,2,1,0:T(8,128)S(1)} %copy_bitcast_fusion.1.cells_ref, f32[4,8,128]{2,1,0:T(8,128)S(1)} %bitcast_reduce_fusion.refs_0_, f32[4,8,128]{2,1,0:T(8,128)S(1)} %collective-permute-done.10.refs_1_, f32[4,8,128]{2,1,0:T(8,128)S(1)} %collective-permute-done.11.refs_2_, ...), custom_call_target="tpu_custom_call" | custom-call | flops 1 | bytes 1 | tf_op jit(solution)/shard_map/pallas_call | solution.py:19
  (23 shorter events, 0.1 us)
Async XLA Ops:
  0.6 3.3 %copy-start.1 = (f32[4,18,40,384]{3,2,1,0:T(8,128)S(1)}, f32[4,18,40,384]{3,2,1,0:T(8,128)}, u32[]{:S(2)}) copy-start(f32[4,18,40,384]{3,2,1,0:T(8,128)} %f_ref.1) | copy-start | bytes 13271044
  2.5 7.4 %copy-start = (bf16[18,40,384]{2,1,0:T(8,128)(2,1)S(1)}, bf16[18,40,384]{2,1,0:T(8,128)(2,1)}, u32[]{:S(2)}) copy-start(bf16[18,40,384]{2,1,0:T(8,128)(2,1)} %cx_ref.11) | copy-start | bytes 1658884
  2.5 11.0 %collective-permute-start.2 = (f32[4,40,384]{2,1,0:T(8,128)S(1)}, f32[4,40,384]{2,1,0:T(8,128)S(1)}, u32[]{:S(2)}, u32[]{:S(2)}) collective-permute-start(f32[4,40,384]{2,1,0:T(8,128)S(1)} %get-tuple-element.44), channel_id=1, source_target_pairs={{2,0},{4,2},{6,4},{3,1},{5,3},{7,5},{10,8},{12,10},{14,12},{11,9},... | collective-permute-start | bytes 737288 | tf_op jit(solution)/shard_map/ppermute | solution.py:648
  7.4 6.1 %copy-start.4 = (s32[4,2]{0,1:T(2,128)S(1)}, s32[4,2]{0,1:T(2,128)}, u32[]{:S(2)}) copy-start(s32[4,2]{0,1:T(2,128)} %param.14) | copy-start | bytes 100
  7.5 5.6 %collective-permute-start = (f32[3,68,128]{2,1,0:T(8,128)S(1)}, f32[3,68,128]{2,1,0:T(8,128)S(1)}, u32[]{:S(2)}, u32[]{:S(2)}) collective-permute-start(f32[3,68,128]{2,1,0:T(8,128)S(1)} %get-tuple-element.40), channel_id=1, source_target_pairs={{0,8},{8,16},{16,24},{24,0},{1,9},{9,17},{17,25},{25,1},{2,10},{10... | collective-permute-start | bytes 313352 | tf_op jit(solution)/shard_map/ppermute | solution.py:643
  8.0 5.4 %collective-permute-start.1 = (f32[3,68,128]{2,1,0:T(8,128)S(1)}, f32[3,68,128]{2,1,0:T(8,128)S(1)}, u32[]{:S(2)}, u32[]{:S(2)}) collective-permute-start(f32[3,68,128]{2,1,0:T(8,128)S(1)} %get-tuple-element.41), channel_id=1, source_target_pairs={{8,0},{16,8},{24,16},{0,24},{9,1},{17,9},{25,17},{1,25},{10,2},{18... | collective-permute-start | bytes 313352 | tf_op jit(solution)/shard_map/ppermute | solution.py:643
  13.9 10.6 %collective-permute-start.5 = (f32[4,40,384]{2,1,0:T(8,128)S(1)}, f32[4,40,384]{2,1,0:T(8,128)S(1)}, u32[]{:S(2)}, u32[]{:S(2)}) collective-permute-start(f32[4,40,384]{2,1,0:T(8,128)S(1)} %get-tuple-element.45.lowest_ref), channel_id=1, source_target_pairs={{2,0},{4,2},{6,4},{3,1},{5,3},{7,5},{10,8},{12,10},{14,12},{11,9},... | collective-permute-start | bytes 737288 | tf_op jit(solution)/shard_map/ppermute | solution.py:648
  15.2 5.0 %collective-permute-start.3 = (f32[3,4,128]{2,1,0:T(4,128)S(1)}, f32[3,4,128]{2,1,0:T(4,128)S(1)}, u32[]{:S(2)}, u32[]{:S(2)}) collective-permute-start(f32[3,4,128]{2,1,0:T(4,128)S(1)} %get-tuple-element.48), channel_id=1, source_target_pairs={{0,8},{8,16},{16,24},{24,0},{1,9},{9,17},{17,25},{25,1},{2,10},{10... | collective-permute-start | bytes 18440 | tf_op jit(solution)/shard_map/ppermute | solution.py:643
  16.4 3.7 %collective-permute-start.4 = (f32[3,4,128]{2,1,0:T(4,128)S(1)}, f32[3,4,128]{2,1,0:T(4,128)S(1)}, u32[]{:S(2)}, u32[]{:S(2)}) collective-permute-start(f32[3,4,128]{2,1,0:T(4,128)S(1)} %get-tuple-element.49), channel_id=1, source_target_pairs={{8,0},{16,8},{24,16},{0,24},{9,1},{17,9},{25,17},{1,25},{10,2},{18... | collective-permute-start | bytes 18440 | tf_op jit(solution)/shard_map/ppermute | solution.py:643
  20.1 6.4 %copy-start.5 = (f32[18]{0:T(128)S(1)}, f32[18]{0:T(128)}, u32[]{:S(2)}) copy-start(f32[18]{0:T(128)} %param.15) | copy-start | bytes 220
  20.1 6.5 %copy-start.2 = (f32[4,40,384]{2,1,0:T(8,128)S(1)}, f32[4,40,384]{2,1,0:T(8,128)}, u32[]{:S(2)}) copy-start(f32[4,40,384]{2,1,0:T(8,128)} %share_ref.3) | copy-start | bytes 737284
  20.4 8.2 %collective-permute-start.6 = (f32[3,68,128]{2,1,0:T(8,128)S(1)}, f32[3,68,128]{2,1,0:T(8,128)S(1)}, u32[]{:S(2)}, u32[]{:S(2)}) collective-permute-start(f32[3,68,128]{2,1,0:T(8,128)S(1)} %get-tuple-element.56), channel_id=1, source_target_pairs={{0,8},{8,16},{16,24},{24,0},{1,9},{9,17},{17,25},{25,1},{2,10},{10... | collective-permute-start | bytes 313352 | tf_op jit(solution)/shard_map/ppermute | solution.py:643
  21.2 7.5 %collective-permute-start.7 = (f32[3,68,128]{2,1,0:T(8,128)S(1)}, f32[3,68,128]{2,1,0:T(8,128)S(1)}, u32[]{:S(2)}, u32[]{:S(2)}) collective-permute-start(f32[3,68,128]{2,1,0:T(8,128)S(1)} %get-tuple-element.57), channel_id=1, source_target_pairs={{8,0},{16,8},{24,16},{0,24},{9,1},{17,9},{25,17},{1,25},{10,2},{18... | collective-permute-start | bytes 313352 | tf_op jit(solution)/shard_map/ppermute | solution.py:643
  24.7 3.9 %collective-permute-start.8 = (f32[3,4,128]{2,1,0:T(4,128)S(1)}, f32[3,4,128]{2,1,0:T(4,128)S(1)}, u32[]{:S(2)}, u32[]{:S(2)}) collective-permute-start(f32[3,4,128]{2,1,0:T(4,128)S(1)} %get-tuple-element.58), channel_id=1, source_target_pairs={{0,8},{8,16},{16,24},{24,0},{1,9},{9,17},{17,25},{25,1},{2,10},{10... | collective-permute-start | bytes 18440 | tf_op jit(solution)/shard_map/ppermute | solution.py:643
  25.2 3.5 %collective-permute-start.9 = (f32[3,4,128]{2,1,0:T(4,128)S(1)}, f32[3,4,128]{2,1,0:T(4,128)S(1)}, u32[]{:S(2)}, u32[]{:S(2)}) collective-permute-start(f32[3,4,128]{2,1,0:T(4,128)S(1)} %get-tuple-element.59), channel_id=1, source_target_pairs={{8,0},{16,8},{24,16},{0,24},{9,1},{17,9},{25,17},{1,25},{10,2},{18... | collective-permute-start | bytes 18440 | tf_op jit(solution)/shard_map/ppermute | solution.py:643
  28.7 8.4 %copy-start.3 = (s32[4,3840]{1,0:T(4,128)S(1)}, s32[4,3840]{1,0:T(4,128)}, u32[]{:S(2)}) copy-start(s32[4,3840]{1,0:T(4,128)} %param.17) | copy-start | bytes 184324
  31.2 13.5 %all-to-all-start = ((f32[32,8,128]{2,1,0:T(8,128)}), f32[32,8,128]{2,1,0:T(8,128)S(1)}, u32[]{:S(2)}, u32[]{:S(2)}) async-start(f32[32,8,128]{2,1,0:T(8,128)} %bitcast.2), calls=%async_computation | async-start | bytes 262144 | tf_op jit(solution)/shard_map/all_to_all | solution.py:626
  44.8 5.6 %collective-permute-start.12 = (f32[4,8,128]{2,1,0:T(8,128)S(1)}, f32[4,8,128]{2,1,0:T(8,128)S(1)}, u32[]{:S(2)}, u32[]{:S(2)}) collective-permute-start(f32[4,8,128]{2,1,0:T(8,128)S(1)} %bitcast_reduce_fusion.refs_0_), channel_id=1, source_target_pairs={{0,6},{2,4},{4,2},{6,0},{1,7},{3,5},{5,3},{7,1},{8,14},{10,12},{12... | collective-permute-start | bytes 49160 | tf_op jit(solution)/shard_map/ppermute | solution.py:619
  46.2 4.9 %collective-permute-start.11 = (f32[4,8,128]{2,1,0:T(8,128)S(1)}, f32[4,8,128]{2,1,0:T(8,128)S(1)}, u32[]{:S(2)}, u32[]{:S(2)}) collective-permute-start(f32[4,8,128]{2,1,0:T(8,128)S(1)} %bitcast_reduce_fusion.refs_0_), channel_id=1, source_target_pairs={{0,4},{2,6},{4,0},{6,2},{1,5},{3,7},{5,1},{7,3},{8,12},{10,14},{12... | collective-permute-start | bytes 49160 | tf_op jit(solution)/shard_map/ppermute | solution.py:619
  47.3 3.8 %collective-permute-start.10 = (f32[4,8,128]{2,1,0:T(8,128)S(1)}, f32[4,8,128]{2,1,0:T(8,128)S(1)}, u32[]{:S(2)}, u32[]{:S(2)}) collective-permute-start(f32[4,8,128]{2,1,0:T(8,128)S(1)} %bitcast_reduce_fusion.refs_0_), channel_id=1, source_target_pairs={{0,2},{2,0},{4,6},{6,4},{1,3},{3,1},{5,7},{7,5},{8,10},{10,8},{12,... | collective-permute-start | bytes 49160 | tf_op jit(solution)/shard_map/ppermute | solution.py:619
